TPU v7x, 32 devices: a whole 2x2x4 slice. The times are simulated.
32 devices in a mesh: dp: 8 (over z, y), group: 4 (over x, core).
Axes of the slice: x: 2, y: 2, z: 4, core: 2. Of those that a mesh axis runs over, the one named last changes fastest.
Arguments:
- frames: bfloat16 [4, 4608, 2048], P('group', 'dp'), may hold values from -6 to 6
- lengths: int32 [4, 24], P('group', 'dp'), may hold values from 24 to 192, as said below
- destination: int32 [4, 24], P('group', 'dp'), may hold values from 0 to 7, as said below
- offsets: int32 [4, 24], P('group', 'dp'), may hold values from 0 to 360, as said below
- norm_gain: bfloat16 [2048], P(('dp', 'group')), may hold values from 0.099609375 to 1.8984375
- weight_in: bfloat16 [2048, 4096], P(('dp', 'group')), may hold values from -0.125 to 0.125
- depth_kernel: bfloat16 [2048, 32], P(('dp', 'group')), may hold values from -1 to 1
- post_gain: bfloat16 [2048], P(('dp', 'group')), may hold values from 0.099609375 to 1.8984375
- weight_out: bfloat16 [2048, 2048], P(('dp', 'group')), may hold values from -0.125 to 0.125
Outputs:
- mixed: bfloat16 [4, 3072, 2048], P('group', 'dp')
Inputs may be any that keep to these rules, and one draw needn't show every extreme that they name: `destination`: every device of a group sends exactly one utterance to itself, one to dp index + 1 and one to dp index - 1, both taken modulo 8, within its own group index. `lengths`: every device receives utterances with 384 frames in all; one utterance of each device's receipts has exactly 192 frames; in every group some device's slots are full. `offsets`: the utterances that one device receives lie back to back without gaps or intersection over its 384 rows.
All inputs are finite; a program needn't handle non-finite values.
Results may differ from a plain program's by a relative error of at most 0.0085.
Values may be sent and summed in bfloat16 or wider, within the bound.
No kernel may reach another device: no remote copies, remote signals or barrier semaphores. Data moves between devices by JAX's collectives and lax.ppermute only.
A program may use at most 128 MiB of HBM per device.

v0:
```python
import jax
import jax.numpy as jnp
from jax import lax
from jax.sharding import PartitionSpec as P

D = 2048
KERNEL = 32
MAXLEN = 192
RCV_DEV = 384


epsilon = 1e-05


def shifted(array, axis, by):
    peers = lax.axis_size(axis)
    return lax.ppermute(array, axis, [(i, (i + by) % peers) for i in range(peers)])


def layer_norm(values, scale_gain):
    center = values - jnp.mean(values, axis=-1, keepdims=True)
    spread = jnp.mean(center * center, axis=-1, keepdims=True)
    return center * lax.rsqrt(spread + epsilon) * scale_gain.astype(jnp.float32)


def depth_pass(gated_rows, segment, depth_kernel):
    row_count = gated_rows.shape[0]
    margin = KERNEL // 2
    padded = jnp.pad(gated_rows, ((margin, margin), (0, 0)))
    labels = jnp.pad(segment, (margin, margin), constant_values=-1)
    kernel_rows = depth_kernel.astype(jnp.float32)
    depthwise = jnp.zeros_like(gated_rows)
    for column in range(KERNEL):
        inside = (labels[column : column + row_count] == segment)[:, None]
        depthwise = (
            depthwise
            + jnp.where(inside, padded[column : column + row_count], 0.0) * kernel_rows[:, column]
        )
    return depthwise


def conv_module(inputs, segment, params):
    norm_gain, weight_in, depth_kernel, post_gain, weight_out = params
    widths = inputs.shape[1]
    source = inputs.astype(jnp.float32)
    normed = layer_norm(source, norm_gain).astype(jnp.bfloat16)
    projected = jnp.dot(normed, weight_in, preferred_element_type=jnp.float32)
    gated_rows = projected[:, :widths] * jax.nn.sigmoid(projected[:, widths:])
    depthwise = depth_pass(gated_rows, segment, depth_kernel)
    normed_post = layer_norm(depthwise, post_gain)
    active = (normed_post * jax.nn.sigmoid(normed_post)).astype(jnp.bfloat16)
    return (source + jnp.dot(active, weight_out, preferred_element_type=jnp.float32)).astype(
        jnp.bfloat16
    )


def relocate(own_part, next_part, prev_part):
    from_prev = shifted((next_part[0], next_part[1]), "dp", 1)
    from_next = shifted((prev_part[0], prev_part[1]), "dp", -1)
    received = jnp.zeros((RCV_DEV + MAXLEN, D), jnp.bfloat16)
    segment = jnp.zeros((RCV_DEV,), jnp.int32)
    position = jnp.arange(RCV_DEV, dtype=jnp.int32)
    arrivals = (own_part, from_prev, from_next)
    for label_id in range(3):
        frame_rows, meta_data = arrivals[label_id]
        current = lax.dynamic_slice_in_dim(received, meta_data[1], MAXLEN, 0)
        received = lax.dynamic_update_slice_in_dim(received, current + frame_rows, meta_data[1], 0)
        inside = (position >= meta_data[1]) & (position < meta_data[1] + meta_data[0])
        segment = jnp.where(inside, label_id + 1, segment)
    return (received[:RCV_DEV], segment)


def shards(
    frames, lengths, destination, offsets, norm_gain, weight_in, depth_kernel, post_gain, weight_out
):
    dp_count = lax.axis_size("dp")
    params = (
        lax.all_gather(norm_gain, ("dp", "group"), axis=0, tiled=True),
        lax.all_gather(weight_in, ("dp", "group"), axis=0, tiled=True),
        lax.all_gather(depth_kernel, ("dp", "group"), axis=0, tiled=True),
        lax.all_gather(post_gain, ("dp", "group"), axis=0, tiled=True),
        lax.all_gather(weight_out, ("dp", "group"), axis=0, tiled=True),
    )
    my_index = lax.axis_index("dp")
    local_frames = frames[0]
    lengths_here = lengths[0]
    dest_here = destination[0]
    offsets_here = offsets[0]
    starts = jnp.cumsum(lengths_here) - lengths_here
    relative = (dest_here - my_index) % dp_count
    slot_ids = jnp.arange(3, dtype=jnp.int32)

    def pick_entry(values, which):
        return jnp.sum(jnp.where(slot_ids == which, values, 0))

    def slot_of(code):
        return jnp.sum(jnp.where(relative == code, slot_ids, 0))

    chosen = (slot_of(0), slot_of(1), slot_of(dp_count - 1))

    def cut_utterance(source_rows, which):
        start_row = pick_entry(starts, which)
        live_count = pick_entry(lengths_here, which)
        frame_rows = lax.dynamic_slice_in_dim(source_rows, start_row, MAXLEN, 0)
        keep_rows = jnp.arange(MAXLEN, dtype=jnp.int32) < live_count
        kept = jnp.where(keep_rows[:, None], frame_rows, jnp.zeros_like(frame_rows))
        return (kept, jnp.stack([live_count, pick_entry(offsets_here, which)]))

    received, segment = relocate(
        cut_utterance(local_frames, chosen[0]),
        cut_utterance(local_frames, chosen[1]),
        cut_utterance(local_frames, chosen[2]),
    )
    mixed = conv_module(received, segment, params)
    return mixed[None]


def solution(mesh):
    placed = (
        P("group", "dp", None),
        P("group", "dp"),
        P("group", "dp"),
        P("group", "dp"),
        P(("dp", "group")),
        P(("dp", "group"), None),
        P(("dp", "group"), None),
        P(("dp", "group")),
        P(("dp", "group"), None),
    )
    return jax.shard_map(
        shards, mesh=mesh, in_specs=placed, out_specs=P("group", "dp", None), check_vma=False
    )
```

profile of v0, /device:TPU:0, one launch (start us, length us, event | category | flops | bytes accessed | tf_op | source)
XLA Modules:
  0.0 237.7 jit_solution(17897894399643775131)
XLA Ops:
  6.6 0.7 all-gather.4.cloned.1.call-update
  7.3 0.7 all-gather.6.cloned.1.call-update
  8.0 0.8 reduce-window.9
  8.9 1.4 fusion.70
  10.2 3.3 %select_reduce_fusion = (s32[]{:T(128)}, s32[]{:T(128)}, s32[]{:T(128)}, s32[]{:T(128)}, s32[]{:T(128)}, /*index=5*/s32[]{:T(128)}) fusion(s32[]{:T(128)} %get-tuple-element.14, s32[1,3]{1,0:T(1,128)} %param.10, s32[3,1]{0,1:T(1,128)S(1)} %reduce-window.9, s32[]{:T(128)} %get-tuple-element.15, s32[]{:T(128)} %get-tuple-element.16), kind=kLoop, calls=%fused_computation.164 | loop fusion | flops 42 | bytes 60 | tf_op jit(solution)/shard_map/reduce_sum | solution.py:94
  19.0 0.7 iota_compare_fusion.8
  19.7 1.2 iota_compare_fusion.6
  20.9 3.6 %bitcast_select_fusion = (bf16[192,2048]{1,0:T(8,128)(2,1)}, bf16[192,2048]{1,0:T(8,128)(2,1)S(1)}, bf16[192,2048]{1,0:T(8,128)(2,1)}) fusion(bf16[1,576,2048]{2,1,0:T(8,128)(2,1)} %param.9, s32[]{:T(128)S(6)} %select_n.199, pred[192]{0:T(512)(128)(4,1)S(1)} %get-tuple-element.93, s32[]{:T(128)S(6)} %select_n.183, pred[192]{0:T(512)(128)(4,1)S(1)} %iota_compare_fusion.8, ...), kind=kLoop, calls=%fused_computation.86 | loop fusion | flops 1179648 | bytes 4719180 | tf_op jit(solution)/shard_map/jit(_where)/select_n | solution.py:106
  24.6 3.0 %collective-permute-start.1 = (bf16[192,2048]{1,0:T(8,128)(2,1)}, bf16[192,2048]{1,0:T(8,128)(2,1)}, u32[]{:S(2)}, u32[]{:S(2)}) collective-permute-start(bf16[192,2048]{1,0:T(8,128)(2,1)} %get-tuple-element.23), channel_id=1, source_target_pairs={{0,4},{4,8},{8,12},{12,16},{16,20},{20,24},{24,28},{28,0},{1,5},{5... | collective-permute-start | bytes 2359304 | tf_op jit(solution)/shard_map/ppermute | solution.py:17
  27.5 2.6 %fusion.74 = (s32[]{:T(128)}, s32[]{:T(128)}, s32[]{:T(128)}) fusion(s32[1,3]{1,0:T(1,128)S(1)} %copy-done.18, s32[]{:T(128)} %get-tuple-element.14, s32[]{:T(128)} %get-tuple-element.15, s32[]{:T(128)} %get-tuple-element.16), kind=kLoop, calls=%fused_computation.156 | loop fusion | flops 24 | bytes 36 | tf_op jit(solution)/shard_map/reduce_sum | solution.py:94
  30.1 3.1 %pad_add_fusion = (s32[2]{0:T(128)}, s32[2]{0:T(128)}) fusion(s32[1]{0:T(128)} %bitcast.7, s32[1]{0:T(128)} %bitcast.6, s32[1]{0:T(128)} %bitcast.11, s32[1]{0:T(128)} %bitcast.10), kind=kLoop, calls=%fused_computation.149 | loop fusion | flops 4 | bytes 32 | tf_op jit(solution)/shard_map/stack | solution.py:107
  33.2 1.5 collective-permute-start
  34.7 3.2 %collective-permute-start.3 = (bf16[192,2048]{1,0:T(8,128)(2,1)}, bf16[192,2048]{1,0:T(8,128)(2,1)}, u32[]{:S(2)}, u32[]{:S(2)}) collective-permute-start(bf16[192,2048]{1,0:T(8,128)(2,1)} %get-tuple-element.21), channel_id=1, source_target_pairs={{0,28},{4,0},{8,4},{12,8},{16,12},{20,16},{24,20},{28,24},{1,29},{... | collective-permute-start | bytes 2359304 | tf_op jit(solution)/shard_map/ppermute | solution.py:17
  41.3 69.8 %all-reduce.4 = (bf16[2048]{0:T(1024)(128)(2,1)S(1)}, bf16[2048]{0:T(1024)(128)(2,1)S(1)}) all-reduce(bf16[2048]{0:T(1024)(128)(2,1)S(1)} %dynamic-update-slice, bf16[2048]{0:T(1024)(128)(2,1)S(1)} %dynamic-update-slice.1), channel_id=1, replica_groups=mesh['dp'=8,'group'=4] {'dp','group'}, use_global_device_ids=true, to_apply=%add.2 | all-reduce | flops 4096 | bytes 16384
  111.1 0.6 convert_element_type.24
  111.7 42.1 %all-gather = bf16[32,64,32]{1,2,0:T(8,128)(2,1)S(1)} all-gather(bf16[1,64,32]{1,2,0:T(8,128)(2,1)S(1)} %bitcast.123), channel_id=1, replica_groups=mesh['dp'=8,'group'=4] {'dp','group'}, dimensions={0}, use_global_device_ids=true | all-gather | bytes 135168 | tf_op jit(solution)/shard_map/all_gather | solution.py:80
  155.6 4.0 %dynamic_update_slice.9 = bf16[576,2048]{1,0:T(8,128)(2,1)S(1)} dynamic-update-slice(bf16[576,2048]{1,0:T(8,128)(2,1)S(1)} %broadcast_in_dim.287, bf16[192,2048]{1,0:T(8,128)(2,1)S(1)} %get-tuple-element.22, s32[]{:T(128)S(6)} %select_n.186, s32[]{:T(128)} %constant.47.clone.1) | dynamic-update-slice | bytes 1572868 | tf_op jit(solution)/shard_map/dynamic_update_slice | solution.py:67
  159.7 0.7 fusion.81
  160.4 0.7 fusion.80
  161.1 1.4 fusion.82
  163.8 1.3 fusion.83
  166.2 1.9 select_select_fusion
  172.1 1.4 dynamic-slice_add_fusion.1
  173.6 3.9 %dynamic_update_slice.10 = bf16[576,2048]{1,0:T(8,128)(2,1)S(1)} dynamic-update-slice(bf16[576,2048]{1,0:T(8,128)(2,1)S(1)} %dynamic_update_slice.9, bf16[192,2048]{1,0:T(8,128)(2,1)S(1)} %dynamic-slice_add_fusion.1, s32[]{:T(128)S(6)} %select_n.190, s32[]{:T(128)} %constant.47.clone.1) | dynamic-update-slice | bytes 1572868 | tf_op jit(solution)/shard_map/dynamic_update_slice | solution.py:67
  177.5 1.4 dynamic-slice_add_fusion
  179.0 4.0 %dynamic_update_slice.11 = bf16[576,2048]{1,0:T(8,128)(2,1)S(1)} dynamic-update-slice(bf16[576,2048]{1,0:T(8,128)(2,1)S(1)} %dynamic_update_slice.10, bf16[192,2048]{1,0:T(8,128)(2,1)S(1)} %dynamic-slice_add_fusion, s32[]{:T(128)S(6)} %select_n.197, s32[]{:T(128)} %constant.47.clone.1) | dynamic-update-slice | bytes 1572868 | tf_op jit(solution)/shard_map/dynamic_update_slice | solution.py:67
  183.9 10.3 %fusion.55 = f32[384,4096]{1,0:T(8,128)S(1)} fusion(bf16[2048,4096]{1,0:T(8,128)(2,1)} %all-gather.4.cloned.1.call-done, f32[2048]{0:T(1024)S(1)} %copy-done.17, f32[384]{0:T(512)S(1)} %add_rsqrt_fusion.1, f32[384]{0:T(512)S(1)} %broadcast_multiply_fusion.1, bf16[576,2048]{1,0:T(8,128)(2,1)S(1)} %dynamic_update_slice.11), kind=kOutput, calls=%fused_computation.77 | convolution fusion | flops 6446383104 | bytes 24653824 | tf_op jit(solution)/shard_map/dot_general | solution.py:47
  194.4 0.8 fusion.9
  195.4 19.7 %fusion.79 = (f32[384]{0:T(512)S(1)}, f32[384,2048]{1,0:T(8,128)S(1)}) fusion(f32[2048]{0:T(1024)S(1)} %bitcast.92, pred[384]{0:T(512)(128)(4,1)S(1)} %get-tuple-element.86, f32[2048]{0:T(1024)S(1)} %bitcast.93, pred[384]{0:T(512)(128)(4,1)S(1)} %get-tuple-element.57, f32[2048]{0:T(1024)S(1)} %bitcast.94, pred[384]{0:T(512)(128)(4,1)S(1)} %get-tuple-element.58, ...), kind=kLoop, calls=%fused_computation.171 | loop fusion | flops 74710656 | bytes 6567040 | tf_op jit(solution)/shard_map/reduce_sum | solution.py:21
  215.1 1.6 copy-done
  217.2 4.5 %all-gather.6.cloned.1.call-done = bf16[2048,2048]{1,0:T(8,128)(2,1)} async-done(((bf16[64,2048]{1,0:T(8,128)(2,1)}), bf16[2048,2048]{1,0:T(8,128)(2,1)}) %all-gather.6.cloned.1.call-update) | async-done | bytes 8388624 | tf_op jit(solution)/shard_map/all_gather | solution.py:82
  221.8 9.1 %fusion.54 = bf16[1,384,2048]{2,1,0:T(8,128)(2,1)} fusion(bf16[2048,2048]{1,0:T(8,128)(2,1)} %all-gather.6.cloned.1.call-done, f32[384,2048]{1,0:T(8,128)} %copy-done, f32[2048]{0:T(1024)S(1)} %copy-done.16, f32[384]{0:T(512)S(1)} %add_rsqrt_fusion, f32[384]{0:T(512)S(1)} %broadcast_multiply_fusion, bf16[576,2048]{1,0:T(8,128)(2,1)S(1)} %dynamic_update_slice.11), kind=kOutput, calls=%fused_computation.76 | convolution fusion | flops 3229876224 | bytes 14691328 | tf_op jit(solution)/shard_map/dot_general | solution.py:52
  (68 shorter events, 3.8 us)
Async XLA Ops:
  6.5 21.0 %copy-start.18 = (s32[1,3]{1,0:T(1,128)S(1)}, s32[1,3]{1,0:T(1,128)}, u32[]{:S(2)}) copy-start(s32[1,3]{1,0:T(1,128)} %param.12) | copy-start | bytes 40
  6.5 34.2 %copy-start.19 = (bf16[64]{0:T(256)(128)(2,1)S(1)}, bf16[64]{0:T(256)(128)(2,1)}, u32[]{:S(2)}) copy-start(bf16[64]{0:T(256)(128)(2,1)} %param.13) | copy-start | bytes 388
  6.5 34.5 %copy-start.20 = (bf16[64]{0:T(256)(128)(2,1)S(1)}, bf16[64]{0:T(256)(128)(2,1)}, u32[]{:S(2)}) copy-start(bf16[64]{0:T(256)(128)(2,1)} %param.16) | copy-start | bytes 388
  6.5 105.2 %copy-start.15 = (bf16[64,32]{0,1:T(8,128)(2,1)S(1)}, bf16[64,32]{0,1:T(8,128)(2,1)}, u32[]{:S(2)}) copy-start(bf16[64,32]{0,1:T(8,128)(2,1)} %param.15) | copy-start | bytes 12292
  6.5 177.4 %all-gather.4.cloned.1.call-start = ((), (), s32[]{:S(2)}) async-start(), calls=%async_computation | async-start | bytes 17301504 | tf_op jit(solution)/shard_map/all_gather | solution.py:79
  7.3 214.5 %all-gather.6.cloned.1.call-start = ((), (), s32[]{:S(2)}) async-start(), calls=%async_computation.1 | async-start | bytes 8650752 | tf_op jit(solution)/shard_map/all_gather | solution.py:82
  24.6 147.5 %collective-permute-start.1 = (bf16[192,2048]{1,0:T(8,128)(2,1)}, bf16[192,2048]{1,0:T(8,128)(2,1)}, u32[]{:S(2)}, u32[]{:S(2)}) collective-permute-start(bf16[192,2048]{1,0:T(8,128)(2,1)} %get-tuple-element.23), channel_id=1, source_target_pairs={{0,4},{4,8},{8,12},{12,16},{16,20},{20,24},{24,28},{28,0},{1,5},{5... | collective-permute-start | bytes 2359304 | tf_op jit(solution)/shard_map/ppermute | solution.py:17
  33.2 130.6 %collective-permute-start = (s32[2]{0:T(128)}, s32[2]{0:T(128)}, u32[]{:S(2)}, u32[]{:S(2)}) collective-permute-start(s32[2]{0:T(128)} %get-tuple-element.91), channel_id=1, source_target_pairs={{0,4},{4,8},{8,12},{12,16},{16,20},{20,24},{24,28},{28,0},{1,5},{5... | collective-permute-start | bytes 32 | tf_op jit(solution)/shard_map/ppermute | solution.py:17
  34.7 142.9 %collective-permute-start.3 = (bf16[192,2048]{1,0:T(8,128)(2,1)}, bf16[192,2048]{1,0:T(8,128)(2,1)}, u32[]{:S(2)}, u32[]{:S(2)}) collective-permute-start(bf16[192,2048]{1,0:T(8,128)(2,1)} %get-tuple-element.21), channel_id=1, source_target_pairs={{0,28},{4,0},{8,4},{12,8},{16,12},{20,16},{24,20},{28,24},{1,29},{... | collective-permute-start | bytes 2359304 | tf_op jit(solution)/shard_map/ppermute | solution.py:17
  37.9 123.2 %collective-permute-start.2 = (s32[2]{0:T(128)}, s32[2]{0:T(128)}, u32[]{:S(2)}, u32[]{:S(2)}) collective-permute-start(s32[2]{0:T(128)} %get-tuple-element.92), channel_id=1, source_target_pairs={{0,28},{4,0},{8,4},{12,8},{16,12},{20,16},{24,20},{28,24},{1,29},{... | collective-permute-start | bytes 32 | tf_op jit(solution)/shard_map/ppermute | solution.py:17
  177.5 6.4 %copy-start.17 = (f32[2048]{0:T(1024)S(1)}, f32[2048]{0:T(1024)}, u32[]{:S(2)}) copy-start(f32[2048]{0:T(1024)} %convert_element_type.24) | copy-start | bytes 24580
  194.3 1.0 copy-start.1
  194.3 1.0 copy-start.2
  194.3 1.0 copy-start.3
  194.3 1.0 copy-start.4
  194.3 1.0 copy-start.5
  194.3 1.0 copy-start.6
  194.4 1.0 copy-start.7
  194.4 1.0 copy-start.8
  194.4 1.0 copy-start.9
  194.4 1.0 copy-start.10
  194.4 1.0 copy-start.11
  194.4 1.0 copy-start.12
  194.4 1.0 copy-start.13
  194.4 1.0 copy-start.14
  215.1 1.7 copy-start
  215.1 6.7 %copy-start.16 = (f32[2048]{0:T(1024)S(1)}, f32[2048]{0:T(1024)}, u32[]{:S(2)}) copy-start(f32[2048]{0:T(1024)} %convert_element_type.27) | copy-start | bytes 24580
Sparse Core Ops, SparseCore 0:
  10.2 133.2 all-gather.3
  146.4 75.3 all-gather.5
where the time goes:
time: 238 us
  blocking collectives  112 us (47%)
  other arithmetic  44.8 us (19%)
  between operations  28.8 us (12%)
  matrix products  19.5 us (8%)
  local copies, waits for them, and re-layouts  18.8 us (8%)
  starting transfers between devices  8.03 us (3%)
  waiting for transfers between devices  5.94 us (2%)
    unnamed x1, blocking collectives  69.8 us
    all_gather x1, blocking collectives, shards(): lax.all_gather(depth_kernel, ('dp', 'group'), axis=0, tiled=True)  42.1 us
    reduce_sum x2, other arithmetic, layer_norm(): center = values - jnp.mean(values, axis=-1, keepdims=True)  20 us
    dynamic_update_slice x3, local copies, waits for them, and re-layouts, relocate(): lax.dynamic_update_slice_in_dim(received, current + frame_rows, meta_data...  12 us
    dot_general x1, matrix products, conv_module(): projected = jnp.dot(normed, weight_in, preferred_element_type=jnp.float32)  10.3 us
    dot_general x1, matrix products, conv_module(): jnp.dot(active, weight_out, preferred_element_type=jnp.float32)  9.1 us
    ppermute x4, starting transfers between devices, shifted(): lax.ppermute(array, axis, [(i, (i + by) % peers) for i in range(peers)])  7.96 us
    reduce_sum x2, other arithmetic, pick_entry(): return jnp.sum(jnp.where(slot_ids == which, values, 0))  5.86 us
  transfers between devices with their start and end apart: 6, of which 1 were waited for; matrix products, arithmetic and copies ran while one was open for 30% of the time, Pallas kernels for 0%

commit v1 on v0

--- a/solution.py
+++ b/solution.py
@@ -1,6 +1,10 @@
+import functools
+
 import jax
 import jax.numpy as jnp
 from jax import lax
+from jax.experimental import pallas as pl
+from jax.experimental.pallas import tpu as pltpu
 from jax.sharding import PartitionSpec as P
 
 D = 2048
@@ -115,18 +119,377 @@
     return mixed[None]
 
 
+SWAP = ((0, 1), (1, 0))
+HOPS = {
+    "c": ("core", SWAP),
+    "x": ("x", SWAP),
+    "y": ("y", SWAP),
+    "z1": ("z", tuple((i, i ^ 1) for i in range(4))),
+    "z2": ("z", tuple((i, i ^ 2) for i in range(4))),
+}
+GAP = KERNEL // 2
+PAD = RCV_DEV + 4 * GAP
+PAIR = 2 * PAD
+LANE = 128
+BLOCKS = D // LANE
+HALF = D // 2
+CHUNK = 256
+SMALL = 48
+META = 16
+ROWS = 224
+TILE = 64
+
+
+def hop(array, name):
+    axis, pairs = HOPS[name]
+    return lax.ppermute(array, axis, pairs)
+
+
+def turn(array, by):
+    return lax.ppermute(array, ("z", "y"), [(i, (i + by) % 8) for i in range(8)])
+
+
+def stack(first, second):
+    return jnp.concatenate([first, second], 0)
+
+
+def beside(*parts):
+    return jnp.concatenate(parts, 1)
+
+
+def tie(*arrays):
+    return list(lax.optimization_barrier(arrays))
+
+
+def lanes(index):
+    return pl.ds(pl.multiple_of(index * LANE, LANE), LANE)
+
+
+def prep_kernel(where, rows_ref, small_ref, first_ref, second_ref):
+    def one(step, carry):
+        at = pl.ds(pl.multiple_of(step * LANE, LANE), LANE)
+        values = rows_ref[at, :].astype(jnp.float32)
+        center = values - jnp.mean(values, axis=-1, keepdims=True)
+        spread = jnp.mean(center * center, axis=-1, keepdims=True)
+        scaled = center * lax.rsqrt(spread + epsilon)
+        for block in range(BLOCKS):
+            gain = small_ref[KERNEL : KERNEL + 1, lanes(where[0, block])]
+            part = scaled[:, block * LANE : (block + 1) * LANE] * gain
+            part = part.astype(jnp.bfloat16)
+            first_ref[at, lanes(where[0, block])] = part
+            second_ref[at, lanes(where[1, block])] = part
+        return carry
+
+    lax.fori_loop(0, PAIR // LANE, one, 0)
+
+
+def prep(where, rows, small):
+    out = jax.ShapeDtypeStruct((PAIR, D), jnp.bfloat16)
+    vmem = pl.BlockSpec(memory_space=pltpu.VMEM)
+    return pl.pallas_call(
+        prep_kernel,
+        out_shape=(out, out),
+        in_specs=[pl.BlockSpec(memory_space=pltpu.SMEM), vmem, vmem],
+        out_specs=(vmem, vmem),
+        compiler_params=pltpu.CompilerParams(vmem_limit_bytes=32 * 2**20),
+        cost_estimate=pl.CostEstimate(
+            flops=20 * PAIR * D, bytes_accessed=6 * PAIR * D, transcendentals=PAIR
+        ),
+        name="prep",
+    )(where, rows, small)
+
+
+def conv_kernel(sub, where, rows_ref, near_ref, far_ref, small_ref, own_ref, other_ref, gated, taps):
+    tiles = CHUNK // LANE
+    half = where[4, 0]
+    for tile in range(tiles):
+        gated[tile, 0:GAP, :] = jnp.zeros((GAP, LANE), jnp.float32)
+        gated[tile, GAP + PAIR : 2 * GAP + PAIR, :] = jnp.zeros((GAP, LANE), jnp.float32)
+        taps[tile] = small_ref[0:KERNEL, lanes(where[0, half * (BLOCKS // 2) + sub + tile])]
+
+    def project(step, carry):
+        at = pl.ds(pl.multiple_of(step * ROWS, ROWS), ROWS)
+        near, far = rows_ref[at, 0:HALF], rows_ref[at, HALF:D]
+
+        def columns(low):
+            span = slice(low, low + CHUNK)
+            return jnp.dot(
+                near, near_ref[:, span], preferred_element_type=jnp.float32
+            ) + jnp.dot(far, far_ref[:, span], preferred_element_type=jnp.float32)
+
+        mixed = columns(0) * jax.nn.sigmoid(columns(CHUNK))
+        at = pl.ds(pl.multiple_of(step * ROWS + GAP, GAP), ROWS)
+        for tile in range(tiles):
+            gated[tile, at, :] = mixed[:, tile * LANE : (tile + 1) * LANE]
+        return carry
+
+    lax.fori_loop(0, PAIR // ROWS, project, 0)
+
+    def slide(out_ref, base):
+        def one(step, carry):
+            for tile in range(tiles):
+                total = jnp.zeros((TILE, LANE), jnp.float32)
+                for tap in range(KERNEL):
+                    window = gated[tile, pl.ds(base + step * TILE + tap, TILE), :]
+                    total = total + window * taps[tile, tap : tap + 1, :]
+                at = pl.ds(pl.multiple_of(step * TILE, TILE), TILE)
+                out_ref[at, tile * LANE : (tile + 1) * LANE] = total.astype(jnp.bfloat16)
+            return carry
+
+        lax.fori_loop(0, PAD // TILE, one, 0)
+
+    slide(own_ref, 0)
+    slide(other_ref, PAD)
+
+
+def conv(sub, where, rows, near, far, small):
+    out = jax.ShapeDtypeStruct((PAD, CHUNK), jnp.bfloat16)
+    vmem = pl.BlockSpec(memory_space=pltpu.VMEM)
+    return pl.pallas_call(
+        functools.partial(conv_kernel, sub),
+        out_shape=(out, out),
+        in_specs=[pl.BlockSpec(memory_space=pltpu.SMEM)] + [vmem] * 4,
+        out_specs=(vmem, vmem),
+        scratch_shapes=[
+            pltpu.VMEM((CHUNK // LANE, PAIR + 2 * GAP, LANE), jnp.float32),
+            pltpu.VMEM((CHUNK // LANE, KERNEL, LANE), jnp.float32),
+        ],
+        compiler_params=pltpu.CompilerParams(vmem_limit_bytes=32 * 2**20),
+        cost_estimate=pl.CostEstimate(
+            flops=4 * PAIR * D * CHUNK, bytes_accessed=8 * 2**20, transcendentals=PAIR * CHUNK
+        ),
+        name="conv",
+    )(where, rows, near, far, small)
+
+
+def finish_kernel(
+    where, m0, m1, m2, m3, o0, o1, o2, o3, small_ref, pick_ref, base_ref,
+    e8, er, d8, dr, f8, fr, g8, gr, out_ref, first, second,
+):
+    half = where[4, 0]
+    count = KERNEL + 1
+    pieces = [(half, (m0, m1, m2, m3)), (1 - half, (o0, o1, o2, o3))]
+    refs = [ref for _, group in pieces for ref in group]
+    total = jnp.zeros((PAD, 1), jnp.float32)
+    for ref in refs:
+        total = total + jnp.sum(ref[...].astype(jnp.float32), axis=-1, keepdims=True)
+    mean = total / D
+    total = jnp.zeros((PAD, 1), jnp.float32)
+    for ref in refs:
+        center = ref[...].astype(jnp.float32) - mean
+        total = total + jnp.sum(center * center, axis=-1, keepdims=True)
+    scale = lax.rsqrt(total / D + epsilon)
+    for side, group in pieces:
+        for place, ref in enumerate(group):
+            parts = []
+            for tile in range(CHUNK // LANE):
+                block = side * (BLOCKS // 2) + place * (CHUNK // LANE) + tile
+                gain = small_ref[count : count + 1, lanes(where[0, block])]
+                values = ref[:, tile * LANE : (tile + 1) * LANE].astype(jnp.float32)
+                post = (values - mean) * scale * gain
+                parts.append((post * jax.nn.sigmoid(post)).astype(jnp.bfloat16))
+            kept = jnp.dot(
+                pick_ref[...], beside(*parts), preferred_element_type=jnp.float32
+            ).astype(jnp.bfloat16)
+            for tile in range(CHUNK // LANE):
+                block = side * (BLOCKS // 2) + place * (CHUNK // LANE) + tile
+                part = kept[:, tile * LANE : (tile + 1) * LANE]
+                first[:, lanes(where[2, block])] = part
+                second[:, lanes(where[3, block])] = part
+    width = HALF // 2
+    for side, active, near, far, low in (
+        (half, first, e8, er, 0),
+        (half, second, d8, dr, width),
+        (1 - half, first, f8, fr, 0),
+        (1 - half, second, g8, gr, width),
+    ):
+        at = pl.ds(pl.multiple_of(side * HALF + low, width), width)
+        result = (
+            jnp.dot(active[:, 0:HALF], near[...], preferred_element_type=jnp.float32)
+            + jnp.dot(active[:, HALF:D], far[...], preferred_element_type=jnp.float32)
+            + base_ref[:, at].astype(jnp.float32)
+        )
+        out_ref[:, at] = result.astype(jnp.bfloat16)
+
+
+def finish(where, mine, others, small, pick, base, weights):
+    vmem = pl.BlockSpec(memory_space=pltpu.VMEM)
+    return pl.pallas_call(
+        finish_kernel,
+        out_shape=jax.ShapeDtypeStruct((RCV_DEV, D), jnp.bfloat16),
+        in_specs=[pl.BlockSpec(memory_space=pltpu.SMEM)] + [vmem] * 19,
+        out_specs=vmem,
+        scratch_shapes=[pltpu.VMEM((RCV_DEV, D), jnp.bfloat16)] * 2,
+        compiler_params=pltpu.CompilerParams(vmem_limit_bytes=48 * 2**20),
+        cost_estimate=pl.CostEstimate(
+            flops=2 * RCV_DEV * D * D, bytes_accessed=16 * 2**20, transcendentals=PAD * D
+        ),
+        name="finish",
+    )(where, *mine, *others, small, pick, base, *weights)
+
+
+def hot(condition):
+    return condition.astype(jnp.bfloat16)
+
+
+def take(picker, rows):
+    return jnp.dot(picker, rows, preferred_element_type=jnp.float32)
+
+
+def hyper_shards(
+    frames, lengths, destination, offsets, norm_gain, weight_in, depth_kernel, post_gain, weight_out
+):
+    core, x, y, z = (lax.axis_index(name) for name in ("core", "x", "y", "z"))
+    low = core == 0
+    per = weight_in.shape[0]
+
+    small = jnp.concatenate(
+        [depth_kernel, norm_gain[:, None], post_gain[:, None], jnp.zeros((per, LANE - KERNEL - 2), jnp.bfloat16)], 1
+    )
+    left = [weight_in[:, 0:HALF], weight_in[:, D : D + HALF], weight_out[:, 0:HALF]]
+    right = [weight_in[:, HALF:D], weight_in[:, D + HALF :], weight_out[:, HALF:]]
+    left, right = beside(*left), beside(*right)
+    kept = beside(jnp.where(low, left, right), small)
+    given = beside(jnp.where(low, right, left), small)
+    got = hop(given, "c")
+    chip = jnp.where(low, stack(kept, got), stack(got, kept))
+
+    def value_gate(start):
+        return [chip[:, start : start + CHUNK], chip[:, HALF + start : HALF + start + CHUNK]]
+
+    a = beside(*value_gate(0), *value_gate(CHUNK), chip[:, 3 * HALF :])
+    b = beside(*value_gate(2 * CHUNK), *value_gate(3 * CHUNK))
+    o = chip[:, 2 * HALF : 3 * HALF]
+
+    rows, lens, dest, offs = frames[0], lengths[0], destination[0], offsets[0]
+    starts = jnp.cumsum(lens) - lens
+    relative = (dest - (z * 2 + y)) % 8
+
+    def entry(values, code):
+        return jnp.sum(jnp.where(relative == code, values, 0))
+
+    def sent(code):
+        count, offset, start = entry(lens, code), entry(offs, code), entry(starts, code)
+        spot = jnp.arange(MAXLEN + META, dtype=jnp.int32)[:, None]
+        slot = jnp.arange(rows.shape[0], dtype=jnp.int32)[None, :]
+        picker = hot((slot == start + spot) & (spot < count))
+        note = jnp.where(spot == MAXLEN, count, 0) + jnp.where(spot == MAXLEN + 1, offset // 2, 0)
+        note = note + jnp.where(spot == MAXLEN + 2, offset % 2, 0)
+        first = take(picker, rows[:, 0:HALF]) + note.astype(jnp.float32)
+        second = take(picker[0:MAXLEN], rows[:, HALF:D])
+        return first.astype(jnp.bfloat16), second.astype(jnp.bfloat16)
+
+    up, down = sent(1), sent(7)
+    prev_first, next_first = turn(up[0], 1), turn(down[0], -1)
+    arrived = [hop(a, "z2"), hop(b, "z1"), hop(o, "x")]
+    a, b, o, prev_first, next_first, up_second, down_second = tie(
+        stack(a, arrived[0]), stack(b, arrived[1]), stack(o, arrived[2]),
+        prev_first, next_first, up[1], down[1],
+    )
+    prev_second, next_second = turn(up_second, 1), turn(down_second, -1)
+    arrived = [hop(a, "z1"), hop(b, "z2"), hop(o, "y")]
+    a, b, o, prev_second, next_second = tie(
+        stack(a, arrived[0]), stack(b, arrived[1]), stack(o, arrived[2]), prev_second, next_second
+    )
+    e, d = o[:, 0 : HALF // 2], o[:, HALF // 2 :]
+    small = a[:, 4 * CHUNK :].T[0:SMALL]
+    a = a[:, 0 : 4 * CHUNK]
+    small = beside(small, hop(small, "y"))
+    arrived = [hop(a, "y"), hop(b, "x"), hop(e, "z1"), hop(d, "z2")]
+    a, b, e, d, small = tie(
+        stack(a, arrived[0]), stack(b, arrived[1]), stack(e, arrived[2]), stack(d, arrived[3]), small
+    )
+    small = beside(small, hop(small, "x")).astype(jnp.float32)
+    e_far, d_far = hop(e, "z2"), hop(d, "z1")
+    cut = 2 * CHUNK
+    a1, a2, b1, b2 = a[:, 0:cut], a[:, cut:], b[:, 0:cut], b[:, cut:]
+    a1_far, b1_far = hop(a1, "x"), hop(b1, "y")
+    a1_far, b1_far, a2, b2 = tie(a1_far, b1_far, a2, b2)
+    a2_far, b2_far = hop(a2, "x"), hop(b2, "y")
+
+    def noted(first):
+        head = first[MAXLEN : MAXLEN + 3, 0].astype(jnp.int32)
+        return head[0], head[1] * 2 + head[2]
+
+    own = (entry(lens, 0), entry(offs, 0))
+    parts = [own, noted(prev_first), noted(next_first)]
+    order = [sum((other[1] < part[1]).astype(jnp.int32) for other in parts) for part in parts]
+    padded = jnp.arange(PAD, dtype=jnp.int32)[:, None]
+
+    def placer(part, rank, width, start):
+        source = jnp.arange(width, dtype=jnp.int32)[None, :] - start
+        inside = (source >= 0) & (source < part[0])
+        return hot((padded == GAP + part[1] + GAP * rank + source) & inside)
+
+    place_own = placer(parts[0], order[0], rows.shape[0], entry(starts, 0))
+    place_prev = placer(parts[1], order[1], MAXLEN + META, 0)
+    place_next = placer(parts[2], order[2], MAXLEN + META, 0)
+    first = take(place_own, rows[:, 0:HALF]) + take(place_prev, prev_first) + take(place_next, next_first)
+    second = (
+        take(place_own, rows[:, HALF:D])
+        + take(place_prev[:, 0:MAXLEN], prev_second)
+        + take(place_next[:, 0:MAXLEN], next_second)
+    )
+    spread_rows = beside(first, second).astype(jnp.bfloat16)
+    flat = jnp.arange(RCV_DEV, dtype=jnp.int32)[:, None]
+    rank = sum((part[1] <= flat).astype(jnp.int32) for part in parts)
+    pick = hot(jnp.arange(PAD, dtype=jnp.int32)[None, :] == flat + GAP * rank)
+    base = take(pick, spread_rows).astype(jnp.bfloat16)
+
+    block = jnp.arange(BLOCKS, dtype=jnp.int32)
+    zb2, zb1 = (block >> 3) ^ (z >> 1), ((block >> 2) & 1) ^ (z & 1)
+    yb, xb = ((block >> 1) & 1) ^ y, (block & 1) ^ x
+    where = jnp.stack(
+        [
+            xb * 8 + yb * 4 + zb1 * 2 + zb2,
+            yb * 8 + xb * 4 + zb2 * 2 + zb1,
+            zb2 * 8 + zb1 * 4 + yb * 2 + xb,
+            zb1 * 8 + zb2 * 4 + yb * 2 + xb,
+            jnp.full_like(block, core),
+        ]
+    )
+
+    both = stack(spread_rows, hop(spread_rows, "c"))
+    for_a, for_b = prep(where, both, small)
+    mine, others = [], []
+
+    def run(sub, rows_in, near, far):
+        kept_part, given_part = conv(sub, where, rows_in, near, far, small)
+        mine.append(kept_part)
+        others.append(hop(given_part, "c"))
+
+    run(0, for_a, a1, a1_far)
+    run(4, for_b, b1, b1_far)
+    e, d, e_far, d_far, a2_far, b2_far = tie(e, d, e_far, d_far, a2_far, b2_far)
+    weights = [e, e_far, d, d_far]
+    weights = weights + [hop(array, "c") for array in weights]
+    run(2, for_a, a2, a2_far)
+    run(6, for_b, b2, b2_far)
+    order = (0, 2, 1, 3)
+    mixed = finish(
+        where, [mine[i] for i in order], [others[i] for i in order], small, pick, base, weights
+    )
+    return mixed[None]
+
+
 def solution(mesh):
+    if dict(mesh.shape) == {"dp": 8, "group": 4}:
+        grid = jax.sharding.Mesh(mesh.devices.reshape(4, 2, 2, 2), ("z", "y", "x", "core"))
+        dp, group, body = ("z", "y"), ("x", "core"), hyper_shards
+    else:
+        grid, dp, group, body = mesh, ("dp",), ("group",), shards
+    every = dp + group
     placed = (
-        P("group", "dp", None),
-        P("group", "dp"),
-        P("group", "dp"),
-        P("group", "dp"),
-        P(("dp", "group")),
-        P(("dp", "group"), None),
-        P(("dp", "group"), None),
-        P(("dp", "group")),
-        P(("dp", "group"), None),
+        P(group, dp, None),
+        P(group, dp),
+        P(group, dp),
+        P(group, dp),
+        P(every),
+        P(every, None),
+        P(every, None),
+        P(every),
+        P(every, None),
     )
     return jax.shard_map(
-        shards, mesh=mesh, in_specs=placed, out_specs=P("group", "dp", None), check_vma=False
-    )
+        body, mesh=grid, in_specs=placed, out_specs=P(group, dp, None), check_vma=False
+    )

time: 238 us -> 238 us (level)
  blocking collectives: 112 us -> 0 us
  waiting for transfers between devices: 5.94 us -> 84.7 us
  Pallas kernels: 0 us -> 39.1 us
  starting transfers between devices: 8.03 us -> 46.2 us
  other arithmetic: 44.8 us -> 24.3 us
  between operations: 28.8 us -> 11.3 us
  matrix products: 19.5 us -> 16 us
  local copies, waits for them, and re-layouts: 18.8 us -> 15.3 us
    ppermute x4 -> x32, waiting for transfers between devices: 0.01 us -> 84.7 us  [the longest x28 80.5 us: hop(): return lax.ppermute(array, axis, pairs)]
    unnamed x1 -> x0, blocking collectives: 69.8 us -> none
    all_gather x1 -> x0, blocking collectives: 42.1 us -> none  [shards(): lax.all_gather(depth_kernel, ('dp', 'group'), axis=0, tiled=True)]
    pallas_call x0 -> x6, Pallas kernels: none -> 39.1 us  [the longest x4 23.4 us: conv(): pl.pallas_call(functools.partial(conv_kernel, sub), out_shape=(out, out),...]
    ppermute x4 -> x32, starting transfers between devices: 7.96 us -> 46.2 us  [the longest x28 35.8 us: hop(): return lax.ppermute(array, axis, pairs)]
    reduce_sum x7 -> x1, other arithmetic: 28.2 us -> 0.79 us  [entry(): return jnp.sum(jnp.where(relative == code, values, 0))]
    concatenate x0 -> x14, other arithmetic: none -> 14.7 us  [the longest x11 13.2 us: stack(): return jnp.concatenate([first, second], 0)]
    dynamic_update_slice x3 -> x0, local copies, waits for them, and re-layouts: 12 us -> none  [relocate(): lax.dynamic_update_slice_in_dim(received, current + frame_rows, meta_data...]
  transfers between devices with their start and end apart: 6 -> 32, of which waited for: 1 -> 9; matrix products, arithmetic and copies ran while one was open for 30% -> 17% of each run, Pallas kernels for 0% -> 12%
where the time goes in v1:
time: 238 us; the launch traced here: 237 us
  waiting for transfers between devices  84.7 us (36%)
  starting transfers between devices  46.2 us (19%)
  Pallas kernels  39.1 us (16%)
  other arithmetic  24.3 us (10%)
  matrix products  16 us (7%)
  local copies, waits for them, and re-layouts  15.3 us (6%)
  between operations  11.3 us (5%)
    ppermute x28, waiting for transfers between devices, hop(): return lax.ppermute(array, axis, pairs)  80.5 us
    ppermute x28, starting transfers between devices, hop(): return lax.ppermute(array, axis, pairs)  35.8 us
    pallas_call x4, Pallas kernels, conv(): pl.pallas_call(functools.partial(conv_kernel, sub), out_shape=(out, out),...  23.4 us
    dot_general x11, matrix products, take(): return jnp.dot(picker, rows, preferred_element_type=jnp.float32)  16 us
    concatenate x11, other arithmetic, stack(): return jnp.concatenate([first, second], 0)  13.2 us
    pallas_call x1, Pallas kernels, finish(): pl.pallas_call(finish_kernel, out_shape=jax.ShapeDtypeStruct((RCV_DEV, D)...  10.9 us
    ppermute x4, starting transfers between devices, turn(): lax.ppermute(array, ('z', 'y'), [(i, (i + by) % 8) for i in range(8)])  10.3 us
    unnamed x62, local copies, waits for them, and re-layouts  8.33 us
  transfers between devices with their start and end apart: 32, of which 9 were waited for; matrix products, arithmetic and copies ran while one was open for 17% of the time, Pallas kernels for 12%

profile of v1, /device:TPU:0, one launch (start us, length us, event | category | flops | bytes accessed | tf_op | source)
XLA Modules:
  0.0 236.8 jit_solution(7785771552082828854)
XLA Ops:
  9.9 2.6 %fusion = bf16[208,1024]{1,0:T(8,128)(2,1)} fusion(bf16[576,2048]{1,0:T(8,128)(2,1)} %bitcast.58, f32[208]{0:T(256)S(1)} %get-tuple-element.124, s32[208]{0:T(256)S(1)} %get-tuple-element.125, pred[208]{0:T(512)(128)(4,1)S(1)} %iota_compare_fusion.16), kind=kOutput, calls=%fused_computation.9 | convolution fusion | flops 246032384 | bytes 1607504 | tf_op jit(solution)/shard_map/dot_general | solution.py:336
  12.4 2.5 %collective-permute-start.4 = (bf16[208,1024]{1,0:T(8,128)(2,1)}, bf16[208,1024]{1,0:T(8,128)(2,1)S(1)}, u32[]{:S(2)}, u32[]{:S(2)}) collective-permute-start(bf16[208,1024]{1,0:T(8,128)(2,1)} %fusion), channel_id=1, source_target_pairs={{0,4},{4,8},{8,12},{12,16},{16,20},{20,24},{24,28},{28,0},{1,5},{5... | collective-permute-start | bytes 1277960 | tf_op jit(solution)/shard_map/ppermute | solution.py:149
  19.3 2.6 %fusion.1 = bf16[208,1024]{1,0:T(8,128)(2,1)} fusion(bf16[576,2048]{1,0:T(8,128)(2,1)} %bitcast.59, f32[208]{0:T(256)S(1)} %get-tuple-element.122, s32[208]{0:T(256)S(1)} %get-tuple-element.123, pred[208]{0:T(512)(128)(4,1)S(1)} %iota_compare_fusion.12), kind=kOutput, calls=%fused_computation.10 | convolution fusion | flops 246032384 | bytes 1607504 | tf_op jit(solution)/shard_map/dot_general | solution.py:336
  21.9 3.0 %collective-permute-start.5 = (bf16[208,1024]{1,0:T(8,128)(2,1)}, bf16[208,1024]{1,0:T(8,128)(2,1)S(1)}, u32[]{:S(2)}, u32[]{:S(2)}) collective-permute-start(bf16[208,1024]{1,0:T(8,128)(2,1)} %fusion.1), channel_id=1, source_target_pairs={{0,28},{4,0},{8,4},{12,8},{16,12},{20,16},{24,20},{28,24},{1,29},{... | collective-permute-start | bytes 1277960 | tf_op jit(solution)/shard_map/ppermute | solution.py:149
  25.2 2.6 %convolution_convert_fusion.2 = bf16[192,1024]{1,0:T(8,128)(2,1)} fusion(bf16[576,2048]{1,0:T(8,128)(2,1)} %bitcast.60, pred[208,576]{1,0:T(8,128)(4,1)S(1)} %fusion.18), kind=kOutput, calls=%fused_computation.12 | convolution fusion | flops 226689024 | bytes 1695744 | tf_op jit(solution)/shard_map/dot_general | solution.py:336
  29.7 1.7 collective-permute-start.3
  31.4 2.4 collective-permute-start.1
  35.6 11.3 %collective-permute-done.2 = bf16[128,1024]{1,0:T(8,128)(2,1)S(1)} collective-permute-done((bf16[128,1024]{1,0:T(8,128)(2,1)S(1)}, bf16[128,1024]{1,0:T(8,128)(2,1)S(1)}, u32[]{:S(2)}, u32[]{:S(2)}) %collective-permute-start.2) | collective-permute-done | bytes 262176 | tf_op jit(solution)/shard_map/ppermute | solution.py:145
  58.7 2.9 %collective-permute-start.7 = (bf16[256,1024]{1,0:T(8,128)(2,1)S(1)}, bf16[256,1024]{1,0:T(8,128)(2,1)}, u32[]{:S(2)}, u32[]{:S(2)}) collective-permute-start(bf16[256,1024]{1,0:T(8,128)(2,1)S(1)} %pad_maximum_fusion.10), channel_id=1, source_target_pairs={{0,16},{8,24},{16,0},{24,8},{1,17},{9,25},{17,1},{25,9},{2,18},{10... | collective-permute-start | bytes 1572872 | tf_op jit(solution)/shard_map/ppermute | solution.py:145
  62.1 2.2 fusion.5
  65.3 2.0 collective-permute-start.9
  67.3 2.7 %collective-permute-start.10 = (bf16[192,1024]{1,0:T(8,128)(2,1)S(1)}, bf16[192,1024]{1,0:T(8,128)(2,1)S(1)}, u32[]{:S(2)}, u32[]{:S(2)}) collective-permute-start(bf16[192,1024]{1,0:T(8,128)(2,1)S(1)} %copy-done.28), channel_id=1, source_target_pairs={{0,28},{4,0},{8,4},{12,8},{16,12},{20,16},{24,20},{28,24},{1,29},{... | collective-permute-start | bytes 1179656 | tf_op jit(solution)/shard_map/ppermute | solution.py:149
  70.9 13.0 %collective-permute-done.7 = bf16[256,1024]{1,0:T(8,128)(2,1)} collective-permute-done((bf16[256,1024]{1,0:T(8,128)(2,1)S(1)}, bf16[256,1024]{1,0:T(8,128)(2,1)}, u32[]{:S(2)}, u32[]{:S(2)}) %collective-permute-start.7) | collective-permute-done | bytes 524320 | tf_op jit(solution)/shard_map/ppermute | solution.py:145
  87.7 2.6 %collective-permute-done.9 = bf16[192,1024]{1,0:T(8,128)(2,1)S(1)} collective-permute-done((bf16[192,1024]{1,0:T(8,128)(2,1)S(1)}, bf16[192,1024]{1,0:T(8,128)(2,1)S(1)}, u32[]{:S(2)}, u32[]{:S(2)}) %collective-permute-start.9) | collective-permute-done | bytes 393248 | tf_op jit(solution)/shard_map/ppermute | solution.py:149
  95.8 3.7 %collective-permute-start.14 = (bf16[512,512]{1,0:T(8,128)(2,1)S(1)}, bf16[512,512]{1,0:T(8,128)(2,1)}, u32[]{:S(2)}, u32[]{:S(2)}) collective-permute-start(bf16[512,512]{1,0:T(8,128)(2,1)S(1)} %get-tuple-element.96), channel_id=1, source_target_pairs={{0,8},{8,0},{16,24},{24,16},{1,9},{9,1},{17,25},{25,17},{2,10},{10... | collective-permute-start | bytes 1572872 | tf_op jit(solution)/shard_map/ppermute | solution.py:145
  99.4 3.5 %collective-permute-start.15 = (bf16[512,512]{1,0:T(8,128)(2,1)S(1)}, bf16[512,512]{1,0:T(8,128)(2,1)}, u32[]{:S(2)}, u32[]{:S(2)}) collective-permute-start(bf16[512,512]{1,0:T(8,128)(2,1)S(1)} %get-tuple-element.95), channel_id=1, source_target_pairs={{0,16},{8,24},{16,0},{24,8},{1,17},{9,25},{17,1},{25,9},{2,18},{10... | collective-permute-start | bytes 1572872 | tf_op jit(solution)/shard_map/ppermute | solution.py:145
  103.0 1.9 collective-permute-start.16
  108.2 11.4 %collective-permute-done.16 = bf16[48,512]{0,1:T(8,128)(2,1)S(1)} collective-permute-done((bf16[48,512]{0,1:T(8,128)(2,1)S(1)}, bf16[48,512]{0,1:T(8,128)(2,1)S(1)}, u32[]{:S(2)}, u32[]{:S(2)}) %collective-permute-start.16) | collective-permute-done | bytes 49184 | tf_op jit(solution)/shard_map/ppermute | solution.py:145
  132.0 3.3 %collective-permute-start.20 = (bf16[1024,512]{1,0:T(8,128)(2,1)S(1)}, bf16[1024,512]{1,0:T(8,128)(2,1)}, u32[]{:S(2)}, u32[]{:S(2)}) collective-permute-start(bf16[1024,512]{1,0:T(8,128)(2,1)S(1)} %pad_maximum_fusion.7.e8), channel_id=1, source_target_pairs={{0,16},{8,24},{16,0},{24,8},{1,17},{9,25},{17,1},{25,9},{2,18},{10... | collective-permute-start | bytes 3145736 | tf_op jit(solution)/shard_map/ppermute | solution.py:145
  135.4 17.1 %collective-permute-done.18.far_ref = bf16[1024,512]{1,0:T(8,128)(2,1)S(1)} collective-permute-done((bf16[1024,512]{1,0:T(8,128)(2,1)S(1)}, bf16[1024,512]{1,0:T(8,128)(2,1)S(1)}, u32[]{:S(2)}, u32[]{:S(2)}) %collective-permute-start.18) | collective-permute-done | bytes 1048608 | tf_op jit(solution)/shard_map/ppermute | solution.py:145
  153.4 2.3 collective-permute-start.21
  157.9 1.7 collective-permute-start.23
  159.8 2.3 pad_maximum_fusion.rows_ref
  162.1 4.9 %prep.1 = (bf16[896,2048]{1,0:T(8,128)(2,1)S(1)}, bf16[896,2048]{1,0:T(8,128)(2,1)S(1)}) custom-call(s32[5,16]{1,0:T(8,128)S(1)} %stack.2.where, bf16[896,2048]{1,0:T(8,128)(2,1)S(1)} %pad_maximum_fusion.rows_ref, f32[48,2048]{1,0:T(8,128)S(1)} %maximum_convert_fusion.small_ref), custom_call_target="tpu_custom_call" | custom-call | flops 36700160 | bytes 11010048 | tf_op jit(solution)/shard_map/prep/pallas_call | solution.py:189
  167.0 5.4 %conv.4 = (bf16[448,256]{1,0:T(8,128)(2,1)S(1)}, bf16[448,256]{1,0:T(8,128)(2,1)S(1)}) custom-call(s32[5,16]{1,0:T(8,128)S(1)} %stack.2.where, bf16[896,2048]{1,0:T(8,128)(2,1)S(1)} %get-tuple-element.55.rows_ref, bf16[1024,512]{1,0:T(8,128)(2,1)S(1)} %copy-done.3, bf16[1024,512]{1,0:T(8,128)(2,1)S(1)} %copy-done.7, f32[48,2048]{1,0:T(8,128)S(1)} %maximum_convert_fusion.small_ref), custom_call_target="tpu_custom_call" | custom-call | flops 1879048192 | bytes 8388608 | tf_op jit(solution)/shard_map/conv/pallas_call | solution.py:248
  172.5 8.8 %collective-permute-done.20.er = bf16[1024,512]{1,0:T(8,128)(2,1)} collective-permute-done((bf16[1024,512]{1,0:T(8,128)(2,1)S(1)}, bf16[1024,512]{1,0:T(8,128)(2,1)}, u32[]{:S(2)}, u32[]{:S(2)}) %collective-permute-start.20) | collective-permute-done | bytes 1048608 | tf_op jit(solution)/shard_map/ppermute | solution.py:145
  181.3 18.6 %collective-permute-done.21.dr = bf16[1024,512]{1,0:T(8,128)(2,1)} collective-permute-done((bf16[1024,512]{1,0:T(8,128)(2,1)S(1)}, bf16[1024,512]{1,0:T(8,128)(2,1)}, u32[]{:S(2)}, u32[]{:S(2)}) %collective-permute-start.21) | collective-permute-done | bytes 1048608 | tf_op jit(solution)/shard_map/ppermute | solution.py:145
  201.0 5.4 %conv.6 = (bf16[448,256]{1,0:T(8,128)(2,1)S(1)}, bf16[448,256]{1,0:T(8,128)(2,1)S(1)}) custom-call(s32[5,16]{1,0:T(8,128)S(1)} %stack.2.where, bf16[896,2048]{1,0:T(8,128)(2,1)S(1)} %get-tuple-element.66.rows_ref, bf16[1024,512]{1,0:T(8,128)(2,1)S(1)} %copy-done.1, bf16[1024,512]{1,0:T(8,128)(2,1)S(1)} %copy-done.5, f32[48,2048]{1,0:T(8,128)S(1)} %maximum_convert_fusion.small_ref), custom_call_target="tpu_custom_call" | custom-call | flops 1879048192 | bytes 8388608 | tf_op jit(solution)/shard_map/conv/pallas_call | solution.py:248
  207.2 6.4 %conv.5 = (bf16[448,256]{1,0:T(8,128)(2,1)S(1)}, bf16[448,256]{1,0:T(8,128)(2,1)S(1)}) custom-call(s32[5,16]{1,0:T(8,128)S(1)} %stack.2.where, bf16[896,2048]{1,0:T(8,128)(2,1)S(1)} %get-tuple-element.55.rows_ref, bf16[1024,512]{1,0:T(8,128)(2,1)} %get-tuple-element.60.near_ref, bf16[1024,512]{1,0:T(8,128)(2,1)} %collective-permute-done.22.far_ref, ...), custom_call_target="tpu_custom_call" | custom-call | flops 1879048192 | bytes 8388608 | tf_op jit(solution)/shard_map/conv/pallas_call | solution.py:248
  214.2 6.2 %conv.7 = (bf16[448,256]{1,0:T(8,128)(2,1)S(1)}, bf16[448,256]{1,0:T(8,128)(2,1)S(1)}) custom-call(s32[5,16]{1,0:T(8,128)S(1)} %stack.2.where, bf16[896,2048]{1,0:T(8,128)(2,1)S(1)} %get-tuple-element.66.rows_ref, bf16[1024,512]{1,0:T(8,128)(2,1)S(1)} %get-tuple-element.63.near_ref, bf16[1024,512]{1,0:T(8,128)(2,1)} %collective-permute-done.23.far_ref, ...), custom_call_target="tpu_custom_call" | custom-call | flops 1879048192 | bytes 8388608 | tf_op jit(solution)/shard_map/conv/pallas_call | solution.py:248
  220.6 2.2 convolution_convert_fusion.base_ref
  225.9 10.9 %finish.1 = bf16[384,2048]{1,0:T(8,128)(2,1)} custom-call(s32[5,16]{1,0:T(8,128)S(1)} %stack.2.where, bf16[448,256]{1,0:T(8,128)(2,1)S(1)} %get-tuple-element.59.m0, bf16[448,256]{1,0:T(8,128)(2,1)S(1)} %get-tuple-element.65.m1, bf16[448,256]{1,0:T(8,128)(2,1)S(1)} %get-tuple-element.68.m2, bf16[448,256]{1,0:T(8,128)(2,1)S(1)} %get-tuple-element.70.m3, ...), custom_call_target="tpu_custom_call" | custom-call | flops 3221225472 | bytes 16777216 | tf_op jit(solution)/shard_map/finish/pallas_call | solution.py:317
  (170 shorter events, 55.2 us)
Async XLA Ops:
  3.9 25.4 %collective-permute-start = (bf16[64,3200]{1,0:T(8,128)(2,1)S(1)}, bf16[64,3200]{1,0:T(8,128)(2,1)S(1)}, u32[]{:S(2)}, u32[]{:S(2)}) collective-permute-start(bf16[64,3200]{1,0:T(8,128)(2,1)S(1)} %concatenate.73), channel_id=1, source_target_pairs={{0,1},{1,0},{2,3},{3,2},{4,5},{5,4},{6,7},{7,6},{8,9},{9,8},{10,11... | collective-permute-start | bytes 1228808 | tf_op jit(solution)/shard_map/ppermute | solution.py:145
  12.4 36.4 %collective-permute-start.4 = (bf16[208,1024]{1,0:T(8,128)(2,1)}, bf16[208,1024]{1,0:T(8,128)(2,1)S(1)}, u32[]{:S(2)}, u32[]{:S(2)}) collective-permute-start(bf16[208,1024]{1,0:T(8,128)(2,1)} %fusion), channel_id=1, source_target_pairs={{0,4},{4,8},{8,12},{12,16},{16,20},{20,24},{24,28},{28,0},{1,5},{5... | collective-permute-start | bytes 1277960 | tf_op jit(solution)/shard_map/ppermute | solution.py:149
  21.9 26.9 %collective-permute-start.5 = (bf16[208,1024]{1,0:T(8,128)(2,1)}, bf16[208,1024]{1,0:T(8,128)(2,1)S(1)}, u32[]{:S(2)}, u32[]{:S(2)}) collective-permute-start(bf16[208,1024]{1,0:T(8,128)(2,1)} %fusion.1), channel_id=1, source_target_pairs={{0,28},{4,0},{8,4},{12,8},{16,12},{20,16},{24,20},{28,24},{1,29},{... | collective-permute-start | bytes 1277960 | tf_op jit(solution)/shard_map/ppermute | solution.py:149
  29.6 17.4 %collective-permute-start.2 = (bf16[128,1024]{1,0:T(8,128)(2,1)S(1)}, bf16[128,1024]{1,0:T(8,128)(2,1)S(1)}, u32[]{:S(2)}, u32[]{:S(2)}) collective-permute-start(bf16[128,1024]{1,0:T(8,128)(2,1)S(1)} %pad_maximum_fusion.14), channel_id=1, source_target_pairs={{0,8},{8,0},{16,24},{24,16},{1,9},{9,1},{17,25},{25,17},{2,10},{10... | collective-permute-start | bytes 786440 | tf_op jit(solution)/shard_map/ppermute | solution.py:145
  29.7 17.4 %collective-permute-start.3 = (bf16[128,1024]{1,0:T(8,128)(2,1)S(1)}, bf16[128,1024]{1,0:T(8,128)(2,1)S(1)}, u32[]{:S(2)}, u32[]{:S(2)}) collective-permute-start(bf16[128,1024]{1,0:T(8,128)(2,1)S(1)} %slice.175), channel_id=1, source_target_pairs={{0,2},{2,0},{1,3},{3,1},{4,6},{6,4},{5,7},{7,5},{8,10},{10,8},{9,1... | collective-permute-start | bytes 786440 | tf_op jit(solution)/shard_map/ppermute | solution.py:145
  31.4 16.5 %collective-permute-start.1 = (bf16[128,1152]{1,0:T(8,128)(2,1)S(1)}, bf16[128,1152]{1,0:T(8,128)(2,1)S(1)}, u32[]{:S(2)}, u32[]{:S(2)}) collective-permute-start(bf16[128,1152]{1,0:T(8,128)(2,1)S(1)} %slice_dynamic-update-slice_fusion.4), channel_id=1, source_target_pairs={{0,16},{8,24},{16,0},{24,8},{1,17},{9,25},{17,1},{25,9},{2,18},{10... | collective-permute-start | bytes 884744 | tf_op jit(solution)/shard_map/ppermute | solution.py:145
  57.0 29.4 %collective-permute-start.6 = (bf16[256,1152]{1,0:T(8,128)(2,1)}, bf16[256,1152]{1,0:T(8,128)(2,1)}, u32[]{:S(2)}, u32[]{:S(2)}) collective-permute-start(bf16[256,1152]{1,0:T(8,128)(2,1)} %pad_maximum_fusion.9), channel_id=1, source_target_pairs={{0,8},{8,0},{16,24},{24,16},{1,9},{9,1},{17,25},{25,17},{2,10},{10... | collective-permute-start | bytes 1769480 | tf_op jit(solution)/shard_map/ppermute | solution.py:145
  58.7 25.3 %collective-permute-start.7 = (bf16[256,1024]{1,0:T(8,128)(2,1)S(1)}, bf16[256,1024]{1,0:T(8,128)(2,1)}, u32[]{:S(2)}, u32[]{:S(2)}) collective-permute-start(bf16[256,1024]{1,0:T(8,128)(2,1)S(1)} %pad_maximum_fusion.10), channel_id=1, source_target_pairs={{0,16},{8,24},{16,0},{24,8},{1,17},{9,25},{17,1},{25,9},{2,18},{10... | collective-permute-start | bytes 1572872 | tf_op jit(solution)/shard_map/ppermute | solution.py:145
  61.5 23.5 %collective-permute-start.8 = (bf16[256,1024]{1,0:T(8,128)(2,1)}, bf16[256,1024]{1,0:T(8,128)(2,1)}, u32[]{:S(2)}, u32[]{:S(2)}) collective-permute-start(bf16[256,1024]{1,0:T(8,128)(2,1)} %pad_maximum_fusion.11), channel_id=1, source_target_pairs={{0,4},{4,0},{1,5},{5,1},{2,6},{6,2},{3,7},{7,3},{8,12},{12,8},{9,1... | collective-permute-start | bytes 1572872 | tf_op jit(solution)/shard_map/ppermute | solution.py:145
  65.3 25.0 %collective-permute-start.9 = (bf16[192,1024]{1,0:T(8,128)(2,1)S(1)}, bf16[192,1024]{1,0:T(8,128)(2,1)S(1)}, u32[]{:S(2)}, u32[]{:S(2)}) collective-permute-start(bf16[192,1024]{1,0:T(8,128)(2,1)S(1)} %copy-done.27), channel_id=1, source_target_pairs={{0,4},{4,8},{8,12},{12,16},{16,20},{20,24},{24,28},{28,0},{1,5},{5... | collective-permute-start | bytes 1179656 | tf_op jit(solution)/shard_map/ppermute | solution.py:149
  67.3 24.6 %collective-permute-start.10 = (bf16[192,1024]{1,0:T(8,128)(2,1)S(1)}, bf16[192,1024]{1,0:T(8,128)(2,1)S(1)}, u32[]{:S(2)}, u32[]{:S(2)}) collective-permute-start(bf16[192,1024]{1,0:T(8,128)(2,1)S(1)} %copy-done.28), channel_id=1, source_target_pairs={{0,28},{4,0},{8,4},{12,8},{16,12},{20,16},{24,20},{28,24},{1,29},{... | collective-permute-start | bytes 1179656 | tf_op jit(solution)/shard_map/ppermute | solution.py:149
  93.0 29.2 %collective-permute-start.12 = (bf16[512,1024]{1,0:T(8,128)(2,1)}, bf16[512,1024]{1,0:T(8,128)(2,1)}, u32[]{:S(2)}, u32[]{:S(2)}) collective-permute-start(bf16[512,1024]{1,0:T(8,128)(2,1)} %slice.157), channel_id=1, source_target_pairs={{0,4},{4,0},{1,5},{5,1},{2,6},{6,2},{3,7},{7,3},{8,12},{12,8},{9,1... | collective-permute-start | bytes 3145736 | tf_op jit(solution)/shard_map/ppermute | solution.py:145
  94.2 29.8 %collective-permute-start.13 = (bf16[512,1024]{1,0:T(8,128)(2,1)S(1)}, bf16[512,1024]{1,0:T(8,128)(2,1)}, u32[]{:S(2)}, u32[]{:S(2)}) collective-permute-start(bf16[512,1024]{1,0:T(8,128)(2,1)S(1)} %pad_maximum_fusion.5), channel_id=1, source_target_pairs={{0,2},{2,0},{1,3},{3,1},{4,6},{6,4},{5,7},{7,5},{8,10},{10,8},{9,1... | collective-permute-start | bytes 3145736 | tf_op jit(solution)/shard_map/ppermute | solution.py:145
  95.8 24.2 %collective-permute-start.14 = (bf16[512,512]{1,0:T(8,128)(2,1)S(1)}, bf16[512,512]{1,0:T(8,128)(2,1)}, u32[]{:S(2)}, u32[]{:S(2)}) collective-permute-start(bf16[512,512]{1,0:T(8,128)(2,1)S(1)} %get-tuple-element.96), channel_id=1, source_target_pairs={{0,8},{8,0},{16,24},{24,16},{1,9},{9,1},{17,25},{25,17},{2,10},{10... | collective-permute-start | bytes 1572872 | tf_op jit(solution)/shard_map/ppermute | solution.py:145
  99.4 21.6 %collective-permute-start.15 = (bf16[512,512]{1,0:T(8,128)(2,1)S(1)}, bf16[512,512]{1,0:T(8,128)(2,1)}, u32[]{:S(2)}, u32[]{:S(2)}) collective-permute-start(bf16[512,512]{1,0:T(8,128)(2,1)S(1)} %get-tuple-element.95), channel_id=1, source_target_pairs={{0,16},{8,24},{16,0},{24,8},{1,17},{9,25},{17,1},{25,9},{2,18},{10... | collective-permute-start | bytes 1572872 | tf_op jit(solution)/shard_map/ppermute | solution.py:145
  103.0 16.7 %collective-permute-start.16 = (bf16[48,512]{0,1:T(8,128)(2,1)S(1)}, bf16[48,512]{0,1:T(8,128)(2,1)S(1)}, u32[]{:S(2)}, u32[]{:S(2)}) collective-permute-start(bf16[48,512]{0,1:T(8,128)(2,1)S(1)} %bitcast.53), channel_id=1, source_target_pairs={{0,4},{4,0},{1,5},{5,1},{2,6},{6,2},{3,7},{7,3},{8,12},{12,8},{9,1... | collective-permute-start | bytes 147464 | tf_op jit(solution)/shard_map/ppermute | solution.py:145
  119.7 40.1 %collective-permute-start.11 = (bf16[448,2048]{1,0:T(8,128)(2,1)}, bf16[448,2048]{1,0:T(8,128)(2,1)}, u32[]{:S(2)}, u32[]{:S(2)}) collective-permute-start(bf16[448,2048]{1,0:T(8,128)(2,1)} %pad_maximum_fusion.3), channel_id=1, source_target_pairs={{0,1},{1,0},{2,3},{3,2},{4,5},{5,4},{6,7},{7,6},{8,9},{9,8},{10,11... | collective-permute-start | bytes 5505032 | tf_op jit(solution)/shard_map/ppermute | solution.py:145
  126.5 26.0 %collective-permute-start.18 = (bf16[1024,512]{1,0:T(8,128)(2,1)S(1)}, bf16[1024,512]{1,0:T(8,128)(2,1)S(1)}, u32[]{:S(2)}, u32[]{:S(2)}) collective-permute-start(bf16[1024,512]{1,0:T(8,128)(2,1)S(1)} %get-tuple-element.94.near_ref), channel_id=1, source_target_pairs={{0,2},{2,0},{1,3},{3,1},{4,6},{6,4},{5,7},{7,5},{8,10},{10,8},{9,1... | collective-permute-start | bytes 3145736 | tf_op jit(solution)/shard_map/ppermute | solution.py:145
  128.0 27.7 %collective-permute-start.19 = (bf16[1024,512]{1,0:T(8,128)(2,1)S(1)}, bf16[1024,512]{1,0:T(8,128)(2,1)S(1)}, u32[]{:S(2)}, u32[]{:S(2)}) collective-permute-start(bf16[1024,512]{1,0:T(8,128)(2,1)S(1)} %get-tuple-element.92.near_ref), channel_id=1, source_target_pairs={{0,4},{4,0},{1,5},{5,1},{2,6},{6,2},{3,7},{7,3},{8,12},{12,8},{9,1... | collective-permute-start | bytes 3145736 | tf_op jit(solution)/shard_map/ppermute | solution.py:145
  130.8 27.1 %collective-permute-start.17 = (bf16[48,1024]{1,0:T(8,128)(2,1)S(1)}, bf16[48,1024]{1,0:T(8,128)(2,1)S(1)}, u32[]{:S(2)}, u32[]{:S(2)}) collective-permute-start(bf16[48,1024]{1,0:T(8,128)(2,1)S(1)} %pad_maximum_fusion.15), channel_id=1, source_target_pairs={{0,2},{2,0},{1,3},{3,1},{4,6},{6,4},{5,7},{7,5},{8,10},{10,8},{9,1... | collective-permute-start | bytes 294920 | tf_op jit(solution)/shard_map/ppermute | solution.py:145
  132.0 49.3 %collective-permute-start.20 = (bf16[1024,512]{1,0:T(8,128)(2,1)S(1)}, bf16[1024,512]{1,0:T(8,128)(2,1)}, u32[]{:S(2)}, u32[]{:S(2)}) collective-permute-start(bf16[1024,512]{1,0:T(8,128)(2,1)S(1)} %pad_maximum_fusion.7.e8), channel_id=1, source_target_pairs={{0,16},{8,24},{16,0},{24,8},{1,17},{9,25},{17,1},{25,9},{2,18},{10... | collective-permute-start | bytes 3145736 | tf_op jit(solution)/shard_map/ppermute | solution.py:145
  153.4 46.6 %collective-permute-start.21 = (bf16[1024,512]{1,0:T(8,128)(2,1)S(1)}, bf16[1024,512]{1,0:T(8,128)(2,1)}, u32[]{:S(2)}, u32[]{:S(2)}) collective-permute-start(bf16[1024,512]{1,0:T(8,128)(2,1)S(1)} %pad_maximum_fusion.8.d8), channel_id=1, source_target_pairs={{0,8},{8,0},{16,24},{24,16},{1,9},{9,1},{17,25},{25,17},{2,10},{10... | collective-permute-start | bytes 3145736 | tf_op jit(solution)/shard_map/ppermute | solution.py:145
  156.7 43.3 %collective-permute-start.22 = (bf16[1024,512]{1,0:T(8,128)(2,1)}, bf16[1024,512]{1,0:T(8,128)(2,1)}, u32[]{:S(2)}, u32[]{:S(2)}) collective-permute-start(bf16[1024,512]{1,0:T(8,128)(2,1)} %get-tuple-element.60.near_ref), channel_id=1, source_target_pairs={{0,2},{2,0},{1,3},{3,1},{4,6},{6,4},{5,7},{7,5},{8,10},{10,8},{9,1... | collective-permute-start | bytes 3145736 | tf_op jit(solution)/shard_map/ppermute | solution.py:145
  157.9 42.1 %collective-permute-start.23 = (bf16[1024,512]{1,0:T(8,128)(2,1)S(1)}, bf16[1024,512]{1,0:T(8,128)(2,1)}, u32[]{:S(2)}, u32[]{:S(2)}) collective-permute-start(bf16[1024,512]{1,0:T(8,128)(2,1)S(1)} %get-tuple-element.63.near_ref), channel_id=1, source_target_pairs={{0,4},{4,0},{1,5},{5,1},{2,6},{6,2},{3,7},{7,3},{8,12},{12,8},{9,1... | collective-permute-start | bytes 3145736 | tf_op jit(solution)/shard_map/ppermute | solution.py:145
  172.4 34.0 %collective-permute-start.24 = (bf16[448,256]{1,0:T(8,128)(2,1)S(1)}, bf16[448,256]{1,0:T(8,128)(2,1)S(1)}, u32[]{:S(2)}, u32[]{:S(2)}) collective-permute-start(bf16[448,256]{1,0:T(8,128)(2,1)S(1)} %get-tuple-element.71), channel_id=1, source_target_pairs={{0,1},{1,0},{2,3},{3,2},{4,5},{5,4},{6,7},{7,6},{8,9},{9,8},{10,11... | collective-permute-start | bytes 688136 | tf_op jit(solution)/shard_map/ppermute | solution.py:145
  200.0 22.8 %collective-permute-start.28 = (bf16[1024,512]{1,0:T(8,128)(2,1)S(1)}, bf16[1024,512]{1,0:T(8,128)(2,1)S(1)}, u32[]{:S(2)}, u32[]{:S(2)}) collective-permute-start(bf16[1024,512]{1,0:T(8,128)(2,1)S(1)} %pad_maximum_fusion.7.e8), channel_id=1, source_target_pairs={{0,1},{1,0},{2,3},{3,2},{4,5},{5,4},{6,7},{7,6},{8,9},{9,8},{10,11... | collective-permute-start | bytes 3145736 | tf_op jit(solution)/shard_map/ppermute | solution.py:145
  200.0 22.8 %collective-permute-start.29 = (bf16[1024,512]{1,0:T(8,128)(2,1)}, bf16[1024,512]{1,0:T(8,128)(2,1)S(1)}, u32[]{:S(2)}, u32[]{:S(2)}) collective-permute-start(bf16[1024,512]{1,0:T(8,128)(2,1)} %collective-permute-done.20.er), channel_id=1, source_target_pairs={{0,1},{1,0},{2,3},{3,2},{4,5},{5,4},{6,7},{7,6},{8,9},{9,8},{10,11... | collective-permute-start | bytes 3145736 | tf_op jit(solution)/shard_map/ppermute | solution.py:145
  200.5 22.3 %collective-permute-start.30 = (bf16[1024,512]{1,0:T(8,128)(2,1)S(1)}, bf16[1024,512]{1,0:T(8,128)(2,1)S(1)}, u32[]{:S(2)}, u32[]{:S(2)}) collective-permute-start(bf16[1024,512]{1,0:T(8,128)(2,1)S(1)} %pad_maximum_fusion.8.d8), channel_id=1, source_target_pairs={{0,1},{1,0},{2,3},{3,2},{4,5},{5,4},{6,7},{7,6},{8,9},{9,8},{10,11... | collective-permute-start | bytes 3145736 | tf_op jit(solution)/shard_map/ppermute | solution.py:145
  200.6 23.3 %collective-permute-start.31 = (bf16[1024,512]{1,0:T(8,128)(2,1)}, bf16[1024,512]{1,0:T(8,128)(2,1)S(1)}, u32[]{:S(2)}, u32[]{:S(2)}) collective-permute-start(bf16[1024,512]{1,0:T(8,128)(2,1)} %collective-permute-done.21.dr), channel_id=1, source_target_pairs={{0,1},{1,0},{2,3},{3,2},{4,5},{5,4},{6,7},{7,6},{8,9},{9,8},{10,11... | collective-permute-start | bytes 3145736 | tf_op jit(solution)/shard_map/ppermute | solution.py:145
  206.4 7.1 %collective-permute-start.26 = (bf16[448,256]{1,0:T(8,128)(2,1)S(1)}, bf16[448,256]{1,0:T(8,128)(2,1)S(1)}, u32[]{:S(2)}, u32[]{:S(2)}) collective-permute-start(bf16[448,256]{1,0:T(8,128)(2,1)S(1)} %get-tuple-element.73), channel_id=1, source_target_pairs={{0,1},{1,0},{2,3},{3,2},{4,5},{5,4},{6,7},{7,6},{8,9},{9,8},{10,11... | collective-permute-start | bytes 688136 | tf_op jit(solution)/shard_map/ppermute | solution.py:145
  213.6 6.8 %collective-permute-start.25 = (bf16[448,256]{1,0:T(8,128)(2,1)S(1)}, bf16[448,256]{1,0:T(8,128)(2,1)S(1)}, u32[]{:S(2)}, u32[]{:S(2)}) collective-permute-start(bf16[448,256]{1,0:T(8,128)(2,1)S(1)} %get-tuple-element.72), channel_id=1, source_target_pairs={{0,1},{1,0},{2,3},{3,2},{4,5},{5,4},{6,7},{7,6},{8,9},{9,8},{10,11... | collective-permute-start | bytes 688136 | tf_op jit(solution)/shard_map/ppermute | solution.py:145
  220.4 2.4 collective-permute-start.27
  (29 other events, 226.4 us)

commit v2 on v1

--- a/solution.py
+++ b/solution.py
@@ -165,38 +165,160 @@
     return pl.ds(pl.multiple_of(index * LANE, LANE), LANE)
 
 
-def prep_kernel(where, rows_ref, small_ref, first_ref, second_ref):
-    def one(step, carry):
-        at = pl.ds(pl.multiple_of(step * LANE, LANE), LANE)
-        values = rows_ref[at, :].astype(jnp.float32)
-        center = values - jnp.mean(values, axis=-1, keepdims=True)
-        spread = jnp.mean(center * center, axis=-1, keepdims=True)
-        scaled = center * lax.rsqrt(spread + epsilon)
-        for block in range(BLOCKS):
-            gain = small_ref[KERNEL : KERNEL + 1, lanes(where[0, block])]
-            part = scaled[:, block * LANE : (block + 1) * LANE] * gain
-            part = part.astype(jnp.bfloat16)
-            first_ref[at, lanes(where[0, block])] = part
-            second_ref[at, lanes(where[1, block])] = part
-        return carry
-
-    lax.fori_loop(0, PAIR // LANE, one, 0)
-
-
-def prep(where, rows, small):
-    out = jax.ShapeDtypeStruct((PAIR, D), jnp.bfloat16)
-    vmem = pl.BlockSpec(memory_space=pltpu.VMEM)
+def local(lens, dest, offs, where, code):
+    count, offset, start, before = 0, 0, 0, 0
+    for slot in range(3):
+        match = (dest[0, slot] - where[4, 3] + 8) % 8 == code
+        count = jnp.where(match, lens[0, slot], count)
+        offset = jnp.where(match, offs[0, slot], offset)
+        start = jnp.where(match, before, start)
+        before = before + lens[0, slot]
+    return count, offset, start
+
+
+def hot(condition):
+    return jnp.where(condition, 1.0, 0.0).astype(jnp.bfloat16)
+
+
+def take(picker, rows):
+    return jnp.dot(picker, rows, preferred_element_type=jnp.float32)
+
+
+def grid_of(rows, columns):
+    shape = (rows, columns)
+    return lax.broadcasted_iota(jnp.int32, shape, 0), lax.broadcasted_iota(jnp.int32, shape, 1)
+
+
+def cut_kernel(where, lens, dest, offs, rows_ref, up0, up1, down0, down1):
+    for code, first_ref, second_ref in ((1, up0, up1), (7, down0, down1)):
+        count, offset, start = local(lens, dest, offs, where, code)
+        spot, slot = grid_of(MAXLEN + META, rows_ref.shape[0])
+        picker = hot((slot == start + spot) & (spot < count))
+        spot, _ = grid_of(MAXLEN + META, HALF)
+        note = jnp.where(spot == MAXLEN, count, 0) + jnp.where(spot == MAXLEN + 1, offset // 2, 0)
+        note = note + jnp.where(spot == MAXLEN + 2, offset % 2, 0)
+        first = take(picker, rows_ref[:, 0:HALF]) + note.astype(jnp.float32)
+        first_ref[...] = first.astype(jnp.bfloat16)
+        second_ref[...] = take(picker[0:MAXLEN], rows_ref[:, HALF:D]).astype(jnp.bfloat16)
+
+
+def smem(count):
+    return [pl.BlockSpec(memory_space=pltpu.SMEM)] * count
+
+
+def vmem(count):
+    return [pl.BlockSpec(memory_space=pltpu.VMEM)] * count
+
+
+def shape(rows, columns, dtype=jnp.bfloat16):
+    return jax.ShapeDtypeStruct((rows, columns), dtype)
+
+
+def limits(mebibytes):
+    return pltpu.CompilerParams(vmem_limit_bytes=mebibytes * 2**20)
+
+
+def cut(where, lens, dest, offs, rows):
+    first, second = shape(MAXLEN + META, HALF), shape(MAXLEN, HALF)
+    return pl.pallas_call(
+        cut_kernel,
+        out_shape=(first, second, first, second),
+        in_specs=smem(4) + vmem(1),
+        out_specs=tuple(vmem(4)),
+        compiler_params=limits(16),
+        cost_estimate=pl.CostEstimate(
+            flops=4 * (MAXLEN + META) * rows.shape[0] * D, bytes_accessed=5 * 2**20, transcendentals=0
+        ),
+        name="cut",
+    )(where, lens, dest, offs, rows)
+
+
+def place_kernel(where, lens, dest, offs, rows_ref, p0, p1, n0, n1, spread_ref, base_ref, pick_ref):
+    count, offset, start = local(lens, dest, offs, where, 0)
+    ones = jnp.ones((1, 1), jnp.int32)
+
+    def noted(ref):
+        head = ref[MAXLEN : MAXLEN + META, 0:LANE].astype(jnp.float32).astype(jnp.int32)
+        return head[0:1, 0:1], head[1:2, 0:1] * 2 + head[2:3, 0:1]
+
+    parts = [(count * ones, offset * ones), noted(p0), noted(n0)]
+
+    def placer(which, width, first):
+        mine = parts[which]
+        rank = sum((other[1] < mine[1]).astype(jnp.int32) for other in parts)
+        spot, slot = grid_of(PAD, width)
+        source = slot - first
+        inside = (source >= 0) & (source < mine[0])
+        return hot((spot == GAP + mine[1] + GAP * rank + source) & inside)
+
+    from_own = placer(0, rows_ref.shape[0], start)
+    from_prev = placer(1, MAXLEN + META, 0)
+    from_next = placer(2, MAXLEN + META, 0)
+    first = take(from_own, rows_ref[:, 0:HALF]) + take(from_prev, p0[...]) + take(from_next, n0[...])
+    spread_ref[:, 0:HALF] = first.astype(jnp.bfloat16)
+    second = (
+        take(from_own, rows_ref[:, HALF:D])
+        + take(from_prev[:, 0:MAXLEN], p1[...])
+        + take(from_next[:, 0:MAXLEN], n1[...])
+    )
+    spread_ref[:, HALF:D] = second.astype(jnp.bfloat16)
+    flat, spot = grid_of(RCV_DEV, PAD)
+    rank = sum((part[1] <= flat).astype(jnp.int32) for part in parts)
+    pick = hot(spot == flat + GAP * rank)
+    pick_ref[...] = pick
+    base_ref[...] = take(pick, spread_ref[...]).astype(jnp.bfloat16)
+
+
+def place(where, lens, dest, offs, rows, arrived):
+    return pl.pallas_call(
+        place_kernel,
+        out_shape=(shape(PAD, D), shape(RCV_DEV, D), shape(RCV_DEV, PAD)),
+        in_specs=smem(4) + vmem(5),
+        out_specs=tuple(vmem(3)),
+        compiler_params=limits(24),
+        cost_estimate=pl.CostEstimate(flops=4 * 2**30, bytes_accessed=10 * 2**20, transcendentals=0),
+        name="place",
+    )(where, lens, dest, offs, rows, *arrived)
+
+
+def prep_kernel(where, mine_ref, other_ref, notes_ref, first_ref, second_ref, small_ref):
+    for block in range(BLOCKS):
+        at = pl.ds(pl.multiple_of(where[5, block] * META, META), META)
+        for part in range(SMALL // META):
+            tile = notes_ref[at, lanes(where[6, block] * (SMALL // META) + part)]
+            small_ref[part * META : (part + 1) * META, block * LANE : (block + 1) * LANE] = tile.astype(
+                jnp.float32
+            )
+    for base, rows_ref in ((0, mine_ref), (PAD, other_ref)):
+
+        def one(step, carry):
+            values = rows_ref[pl.ds(pl.multiple_of(step * TILE, TILE), TILE), :].astype(jnp.float32)
+            center = values - jnp.mean(values, axis=-1, keepdims=True)
+            spread = jnp.mean(center * center, axis=-1, keepdims=True)
+            scaled = center * lax.rsqrt(spread + epsilon) * small_ref[KERNEL : KERNEL + 1, :]
+            scaled = scaled.astype(jnp.bfloat16)
+            at = pl.ds(pl.multiple_of(base + step * TILE, TILE), TILE)
+            for block in range(BLOCKS):
+                part = scaled[:, block * LANE : (block + 1) * LANE]
+                first_ref[at, lanes(where[0, block])] = part
+                second_ref[at, lanes(where[1, block])] = part
+            return carry
+
+        lax.fori_loop(0, PAD // TILE, one, 0)
+
+
+def prep(where, mine, other, notes):
     return pl.pallas_call(
         prep_kernel,
-        out_shape=(out, out),
-        in_specs=[pl.BlockSpec(memory_space=pltpu.SMEM), vmem, vmem],
-        out_specs=(vmem, vmem),
-        compiler_params=pltpu.CompilerParams(vmem_limit_bytes=32 * 2**20),
+        out_shape=(shape(PAIR, D), shape(PAIR, D), shape(SMALL, D, jnp.float32)),
+        in_specs=smem(1) + vmem(3),
+        out_specs=tuple(vmem(3)),
+        compiler_params=limits(20),
         cost_estimate=pl.CostEstimate(
             flops=20 * PAIR * D, bytes_accessed=6 * PAIR * D, transcendentals=PAIR
         ),
         name="prep",
-    )(where, rows, small)
+    )(where, mine, other, notes)
 
 
 def conv_kernel(sub, where, rows_ref, near_ref, far_ref, small_ref, own_ref, other_ref, gated, taps):
@@ -205,7 +327,7 @@
     for tile in range(tiles):
         gated[tile, 0:GAP, :] = jnp.zeros((GAP, LANE), jnp.float32)
         gated[tile, GAP + PAIR : 2 * GAP + PAIR, :] = jnp.zeros((GAP, LANE), jnp.float32)
-        taps[tile] = small_ref[0:KERNEL, lanes(where[0, half * (BLOCKS // 2) + sub + tile])]
+        taps[tile] = small_ref[0:KERNEL, lanes(half * (BLOCKS // 2) + sub + tile)]
 
     def project(step, carry):
         at = pl.ds(pl.multiple_of(step * ROWS, ROWS), ROWS)
@@ -243,18 +365,17 @@
 
 
 def conv(sub, where, rows, near, far, small):
-    out = jax.ShapeDtypeStruct((PAD, CHUNK), jnp.bfloat16)
-    vmem = pl.BlockSpec(memory_space=pltpu.VMEM)
+    out = shape(PAD, CHUNK)
     return pl.pallas_call(
         functools.partial(conv_kernel, sub),
         out_shape=(out, out),
-        in_specs=[pl.BlockSpec(memory_space=pltpu.SMEM)] + [vmem] * 4,
-        out_specs=(vmem, vmem),
+        in_specs=smem(1) + vmem(4),
+        out_specs=tuple(vmem(2)),
         scratch_shapes=[
             pltpu.VMEM((CHUNK // LANE, PAIR + 2 * GAP, LANE), jnp.float32),
             pltpu.VMEM((CHUNK // LANE, KERNEL, LANE), jnp.float32),
         ],
-        compiler_params=pltpu.CompilerParams(vmem_limit_bytes=32 * 2**20),
+        compiler_params=limits(16),
         cost_estimate=pl.CostEstimate(
             flops=4 * PAIR * D * CHUNK, bytes_accessed=8 * 2**20, transcendentals=PAIR * CHUNK
         ),
@@ -284,7 +405,7 @@
             parts = []
             for tile in range(CHUNK // LANE):
                 block = side * (BLOCKS // 2) + place * (CHUNK // LANE) + tile
-                gain = small_ref[count : count + 1, lanes(where[0, block])]
+                gain = small_ref[count : count + 1, lanes(block)]
                 values = ref[:, tile * LANE : (tile + 1) * LANE].astype(jnp.float32)
                 post = (values - mean) * scale * gain
                 parts.append((post * jax.nn.sigmoid(post)).astype(jnp.bfloat16))
@@ -313,27 +434,18 @@
 
 
 def finish(where, mine, others, small, pick, base, weights):
-    vmem = pl.BlockSpec(memory_space=pltpu.VMEM)
     return pl.pallas_call(
         finish_kernel,
-        out_shape=jax.ShapeDtypeStruct((RCV_DEV, D), jnp.bfloat16),
-        in_specs=[pl.BlockSpec(memory_space=pltpu.SMEM)] + [vmem] * 19,
-        out_specs=vmem,
+        out_shape=shape(RCV_DEV, D),
+        in_specs=smem(1) + vmem(19),
+        out_specs=vmem(1)[0],
         scratch_shapes=[pltpu.VMEM((RCV_DEV, D), jnp.bfloat16)] * 2,
-        compiler_params=pltpu.CompilerParams(vmem_limit_bytes=48 * 2**20),
+        compiler_params=limits(28),
         cost_estimate=pl.CostEstimate(
             flops=2 * RCV_DEV * D * D, bytes_accessed=16 * 2**20, transcendentals=PAD * D
         ),
         name="finish",
     )(where, *mine, *others, small, pick, base, *weights)
-
-
-def hot(condition):
-    return condition.astype(jnp.bfloat16)
-
-
-def take(picker, rows):
-    return jnp.dot(picker, rows, preferred_element_type=jnp.float32)
 
 
 def hyper_shards(
@@ -343,132 +455,90 @@
     low = core == 0
     per = weight_in.shape[0]
 
-    small = jnp.concatenate(
-        [depth_kernel, norm_gain[:, None], post_gain[:, None], jnp.zeros((per, LANE - KERNEL - 2), jnp.bfloat16)], 1
-    )
-    left = [weight_in[:, 0:HALF], weight_in[:, D : D + HALF], weight_out[:, 0:HALF]]
-    right = [weight_in[:, HALF:D], weight_in[:, D + HALF :], weight_out[:, HALF:]]
-    left, right = beside(*left), beside(*right)
-    kept = beside(jnp.where(low, left, right), small)
-    given = beside(jnp.where(low, right, left), small)
-    got = hop(given, "c")
-    chip = jnp.where(low, stack(kept, got), stack(got, kept))
-
-    def value_gate(start):
-        return [chip[:, start : start + CHUNK], chip[:, HALF + start : HALF + start + CHUNK]]
-
-    a = beside(*value_gate(0), *value_gate(CHUNK), chip[:, 3 * HALF :])
-    b = beside(*value_gate(2 * CHUNK), *value_gate(3 * CHUNK))
-    o = chip[:, 2 * HALF : 3 * HALF]
-
-    rows, lens, dest, offs = frames[0], lengths[0], destination[0], offsets[0]
-    starts = jnp.cumsum(lens) - lens
-    relative = (dest - (z * 2 + y)) % 8
-
-    def entry(values, code):
-        return jnp.sum(jnp.where(relative == code, values, 0))
-
-    def sent(code):
-        count, offset, start = entry(lens, code), entry(offs, code), entry(starts, code)
-        spot = jnp.arange(MAXLEN + META, dtype=jnp.int32)[:, None]
-        slot = jnp.arange(rows.shape[0], dtype=jnp.int32)[None, :]
-        picker = hot((slot == start + spot) & (spot < count))
-        note = jnp.where(spot == MAXLEN, count, 0) + jnp.where(spot == MAXLEN + 1, offset // 2, 0)
-        note = note + jnp.where(spot == MAXLEN + 2, offset % 2, 0)
-        first = take(picker, rows[:, 0:HALF]) + note.astype(jnp.float32)
-        second = take(picker[0:MAXLEN], rows[:, HALF:D])
-        return first.astype(jnp.bfloat16), second.astype(jnp.bfloat16)
-
-    up, down = sent(1), sent(7)
-    prev_first, next_first = turn(up[0], 1), turn(down[0], -1)
-    arrived = [hop(a, "z2"), hop(b, "z1"), hop(o, "x")]
-    a, b, o, prev_first, next_first, up_second, down_second = tie(
-        stack(a, arrived[0]), stack(b, arrived[1]), stack(o, arrived[2]),
-        prev_first, next_first, up[1], down[1],
-    )
-    prev_second, next_second = turn(up_second, 1), turn(down_second, -1)
-    arrived = [hop(a, "z1"), hop(b, "z2"), hop(o, "y")]
-    a, b, o, prev_second, next_second = tie(
-        stack(a, arrived[0]), stack(b, arrived[1]), stack(o, arrived[2]), prev_second, next_second
-    )
-    e, d = o[:, 0 : HALF // 2], o[:, HALF // 2 :]
-    small = a[:, 4 * CHUNK :].T[0:SMALL]
-    a = a[:, 0 : 4 * CHUNK]
-    small = beside(small, hop(small, "y"))
-    arrived = [hop(a, "y"), hop(b, "x"), hop(e, "z1"), hop(d, "z2")]
-    a, b, e, d, small = tie(
-        stack(a, arrived[0]), stack(b, arrived[1]), stack(e, arrived[2]), stack(d, arrived[3]), small
-    )
-    small = beside(small, hop(small, "x")).astype(jnp.float32)
-    e_far, d_far = hop(e, "z2"), hop(d, "z1")
-    cut = 2 * CHUNK
-    a1, a2, b1, b2 = a[:, 0:cut], a[:, cut:], b[:, 0:cut], b[:, cut:]
-    a1_far, b1_far = hop(a1, "x"), hop(b1, "y")
-    a1_far, b1_far, a2, b2 = tie(a1_far, b1_far, a2, b2)
-    a2_far, b2_far = hop(a2, "x"), hop(b2, "y")
-
-    def noted(first):
-        head = first[MAXLEN : MAXLEN + 3, 0].astype(jnp.int32)
-        return head[0], head[1] * 2 + head[2]
-
-    own = (entry(lens, 0), entry(offs, 0))
-    parts = [own, noted(prev_first), noted(next_first)]
-    order = [sum((other[1] < part[1]).astype(jnp.int32) for other in parts) for part in parts]
-    padded = jnp.arange(PAD, dtype=jnp.int32)[:, None]
-
-    def placer(part, rank, width, start):
-        source = jnp.arange(width, dtype=jnp.int32)[None, :] - start
-        inside = (source >= 0) & (source < part[0])
-        return hot((padded == GAP + part[1] + GAP * rank + source) & inside)
-
-    place_own = placer(parts[0], order[0], rows.shape[0], entry(starts, 0))
-    place_prev = placer(parts[1], order[1], MAXLEN + META, 0)
-    place_next = placer(parts[2], order[2], MAXLEN + META, 0)
-    first = take(place_own, rows[:, 0:HALF]) + take(place_prev, prev_first) + take(place_next, next_first)
-    second = (
-        take(place_own, rows[:, HALF:D])
-        + take(place_prev[:, 0:MAXLEN], prev_second)
-        + take(place_next[:, 0:MAXLEN], next_second)
-    )
-    spread_rows = beside(first, second).astype(jnp.bfloat16)
-    flat = jnp.arange(RCV_DEV, dtype=jnp.int32)[:, None]
-    rank = sum((part[1] <= flat).astype(jnp.int32) for part in parts)
-    pick = hot(jnp.arange(PAD, dtype=jnp.int32)[None, :] == flat + GAP * rank)
-    base = take(pick, spread_rows).astype(jnp.bfloat16)
-
     block = jnp.arange(BLOCKS, dtype=jnp.int32)
     zb2, zb1 = (block >> 3) ^ (z >> 1), ((block >> 2) & 1) ^ (z & 1)
     yb, xb = ((block >> 1) & 1) ^ y, (block & 1) ^ x
+    info = jnp.where(block == 3, z * 2 + y, core)
     where = jnp.stack(
         [
             xb * 8 + yb * 4 + zb1 * 2 + zb2,
             yb * 8 + xb * 4 + zb2 * 2 + zb1,
             zb2 * 8 + zb1 * 4 + yb * 2 + xb,
             zb1 * 8 + zb2 * 4 + yb * 2 + xb,
-            jnp.full_like(block, core),
+            info,
+            yb * 4 + zb1 * 2 + zb2,
+            xb,
         ]
     )
 
-    both = stack(spread_rows, hop(spread_rows, "c"))
-    for_a, for_b = prep(where, both, small)
-    mine, others = [], []
+    left = beside(weight_in[:, 0:HALF], weight_in[:, D : D + HALF], weight_out[:, 0:HALF])
+    right = beside(weight_in[:, HALF:D], weight_in[:, D + HALF :], weight_out[:, HALF:])
+    kept, given = jnp.where(low, left, right), jnp.where(low, right, left)
+    got = hop(given, "c")
+    chip = jnp.where(low, stack(kept, got), stack(got, kept))
+
+    notes = jnp.concatenate(
+        [depth_kernel.T, norm_gain[None], post_gain[None], jnp.zeros((SMALL - KERNEL - 2, per), jnp.bfloat16)], 0
+    )
+    blank = jnp.zeros_like(notes)
+    notes = jnp.where(low, beside(notes, blank), beside(blank, notes))
+    notes = notes + hop(notes, "c")
+    pair = [notes, hop(notes, "x")]
+    tiles = [one[low_row : low_row + META] for one in pair for low_row in range(0, SMALL, META)]
+    notes = beside(*tiles, jnp.zeros((META, 4 * CHUNK - 2 * LANE * SMALL // META), jnp.bfloat16))
+
+    def value_gate(start):
+        return [chip[:, start : start + CHUNK], chip[:, HALF + start : HALF + start + CHUNK]]
+
+    a = beside(*value_gate(0), *value_gate(CHUNK))
+    b = beside(*value_gate(2 * CHUNK), *value_gate(3 * CHUNK))
+    o = chip[:, 2 * HALF : 3 * HALF]
+
+    def grow(array, extra, name):
+        size = array.shape[0]
+        arrived = hop(stack(array, extra), name)
+        return stack(array, arrived[0:size]), stack(extra, arrived[size:])
+
+    rows = frames[0]
+    up0, up1, down0, down1 = cut(where, lengths, destination, offsets, rows)
+    prev0, next0 = turn(up0, 1), turn(down0, -1)
+    (a, notes), b_far, o_far = grow(a, notes, "z2"), hop(b, "z1"), hop(o, "x")
+    a, notes, b, o, prev0, next0, up1, down1 = tie(
+        a, notes, stack(b, b_far), stack(o, o_far), prev0, next0, up1, down1
+    )
+    prev1, next1 = turn(up1, 1), turn(down1, -1)
+    (a, notes), b_far, o_far = grow(a, notes, "z1"), hop(b, "z2"), hop(o, "y")
+    a, notes, b, o, prev1, next1 = tie(a, notes, stack(b, b_far), stack(o, o_far), prev1, next1)
+    e, d = o[:, 0 : HALF // 2], o[:, HALF // 2 :]
+    spread, base, pick = place(
+        where, lengths, destination, offsets, rows, (prev0, prev1, next0, next1)
+    )
+    spread_other = hop(spread, "c")
+    (a, notes), b_far, e_far, d_far = grow(a, notes, "y"), hop(b, "x"), hop(e, "z1"), hop(d, "z2")
+    a, notes, b, e, d, spread, spread_other, base, pick = tie(
+        a, notes, stack(b, b_far), stack(e, e_far), stack(d, d_far), spread, spread_other, base, pick
+    )
+    e_far, d_far = hop(e, "z2"), hop(d, "z1")
+    cut_at = 2 * CHUNK
+    a1, a2, b1, b2 = a[:, 0:cut_at], a[:, cut_at:], b[:, 0:cut_at], b[:, cut_at:]
+    a1_far, b1_far = hop(a1, "x"), hop(b1, "y")
+    a1_far, b1_far, a2, b2 = tie(a1_far, b1_far, a2, b2)
+    a2_far, b2_far = hop(a2, "x"), hop(b2, "y")
+
+    for_a, for_b, small = prep(where, spread, spread_other, notes)
 
     def run(sub, rows_in, near, far):
-        kept_part, given_part = conv(sub, where, rows_in, near, far, small)
-        mine.append(kept_part)
-        others.append(hop(given_part, "c"))
-
-    run(0, for_a, a1, a1_far)
-    run(4, for_b, b1, b1_far)
-    e, d, e_far, d_far, a2_far, b2_far = tie(e, d, e_far, d_far, a2_far, b2_far)
+        mine, given_part = conv(sub, where, rows_in, near, far, small)
+        return mine, hop(given_part, "c")
+
+    m0, o0 = run(0, for_a, a1, a1_far)
+    m2, o2 = run(4, for_b, b1, b1_far)
+    e, d, e_far, d_far, a2_far, b2_far, m0, m2 = tie(e, d, e_far, d_far, a2_far, b2_far, m0, m2)
     weights = [e, e_far, d, d_far]
     weights = weights + [hop(array, "c") for array in weights]
-    run(2, for_a, a2, a2_far)
-    run(6, for_b, b2, b2_far)
-    order = (0, 2, 1, 3)
-    mixed = finish(
-        where, [mine[i] for i in order], [others[i] for i in order], small, pick, base, weights
-    )
+    m1, o1 = run(2, for_a, a2, a2_far)
+    m3, o3 = run(6, for_b, b2, b2_far)
+    mixed = finish(where, (m0, m1, m2, m3), (o0, o1, o2, o3), small, pick, base, weights)
     return mixed[None]
 
 

time: 238 us -> 185 us (0.78)
  other arithmetic: 24.3 us -> 1.6 us
  waiting for transfers between devices: 84.7 us -> 104 us
  matrix products: 16 us -> 0 us
  local copies, waits for them, and re-layouts: 15.3 us -> 2.06 us
  starting transfers between devices: 46.2 us -> 33.7 us
  between operations: 11.3 us -> 0.41 us
  Pallas kernels: 39.1 us -> 42.2 us
    dot_general x11 -> x0, matrix products: 16 us -> none  [take(): return jnp.dot(picker, rows, preferred_element_type=jnp.float32)]
    concatenate x11 -> x16, other arithmetic: 13.2 us -> 1 us  [stack(): return jnp.concatenate([first, second], 0)]
    ppermute x28, starting transfers between devices: 35.8 us -> 24.2 us  [hop(): return lax.ppermute(array, axis, pairs)]
    ppermute x4, waiting for transfers between devices: 4.21 us -> 14.8 us  [turn(): lax.ppermute(array, ('z', 'y'), [(i, (i + by) % 8) for i in range(8)])]
    ppermute x28, waiting for transfers between devices: 80.5 us -> 89.6 us  [hop(): return lax.ppermute(array, axis, pairs)]
    unnamed x62 -> x20, local copies, waits for them, and re-layouts: 8.33 us -> 0.07 us
    pallas_call x2 -> x4, Pallas kernels: 15.8 us -> 20.6 us  [the longest x1 8.48 us: finish(): pl.pallas_call(finish_kernel, out_shape=shape(RCV_DEV, D), in_specs=smem(...]
    slice x6 -> x8, local copies, waits for them, and re-layouts: 3.7 us -> 0.46 us  [the longest x1 0.16 us: hyper_shards(): a[:, cut_at:]]
  transfers between devices with their start and end apart: 32 -> 32, of which waited for: 9 -> 16; matrix products, arithmetic and copies ran while one was open for 17% -> 1% of each run, Pallas kernels for 12% -> 16%
where the time goes in v2:
time: 185 us; the launch traced here: 184 us
  waiting for transfers between devices  104 us (56%)
  Pallas kernels  42.2 us (23%)
  starting transfers between devices  33.7 us (18%)
  local copies, waits for them, and re-layouts  2.06 us (1%)
    ppermute x28, waiting for transfers between devices, hop(): return lax.ppermute(array, axis, pairs)  89.6 us
    ppermute x28, starting transfers between devices, hop(): return lax.ppermute(array, axis, pairs)  24.2 us
    pallas_call x4, Pallas kernels, conv(): pl.pallas_call(functools.partial(conv_kernel, sub), out_shape=(out, out),...  21.6 us
    ppermute x4, waiting for transfers between devices, turn(): lax.ppermute(array, ('z', 'y'), [(i, (i + by) % 8) for i in range(8)])  14.8 us
    ppermute x4, starting transfers between devices, turn(): lax.ppermute(array, ('z', 'y'), [(i, (i + by) % 8) for i in range(8)])  9.5 us
    pallas_call x1, Pallas kernels, finish(): pl.pallas_call(finish_kernel, out_shape=shape(RCV_DEV, D), in_specs=smem(...  8.48 us
    pallas_call x1, Pallas kernels, prep(): pl.pallas_call(prep_kernel, out_shape=(shape(PAIR, D), shape(PAIR, D), sh...  5.92 us
    pallas_call x1, Pallas kernels, place(): pl.pallas_call(place_kernel, out_shape=(shape(PAD, D), shape(RCV_DEV, D),...  4.12 us
  transfers between devices with their start and end apart: 32, of which 16 were waited for; matrix products, arithmetic and copies ran while one was open for 1% of the time, Pallas kernels for 16%

profile of v2, /device:TPU:0, one launch (start us, length us, event | category | flops | bytes accessed | tf_op | source)
XLA Modules:
  0.0 184.4 jit_solution(12010133267097199958)
XLA Ops:
  3.5 2.8 %collective-permute-start.2 = (bf16[48,128]{1,0:T(8,128)(2,1)S(1)}, bf16[48,128]{1,0:T(8,128)(2,1)S(1)}, u32[]{:S(2)}, u32[]{:S(2)}) collective-permute-start(bf16[48,128]{1,0:T(8,128)(2,1)S(1)} %fusion.6), channel_id=1, source_target_pairs={{0,2},{2,0},{1,3},{3,1},{4,6},{6,4},{5,7},{7,5},{8,10},{10,8},{9,1... | collective-permute-start | bytes 36872 | tf_op jit(solution)/shard_map/ppermute | solution.py:145
  6.3 1.7 collective-permute-done.2
  8.3 2.2 %collective-permute-start.4 = (bf16[128,1024]{1,0:T(8,128)(2,1)S(1)}, bf16[128,1024]{1,0:T(8,128)(2,1)S(1)}, u32[]{:S(2)}, u32[]{:S(2)}) collective-permute-start(bf16[128,1024]{1,0:T(8,128)(2,1)S(1)} %pad_maximum_fusion.15), channel_id=1, source_target_pairs={{0,8},{8,0},{16,24},{24,16},{1,9},{9,1},{17,25},{25,17},{2,10},{10... | collective-permute-start | bytes 786440 | tf_op jit(solution)/shard_map/ppermute | solution.py:145
  10.5 1.6 collective-permute-start.5
  12.1 2.7 %collective-permute-start.3 = (bf16[144,1024]{1,0:T(8,128)(2,1)S(1)}, bf16[144,1024]{1,0:T(8,128)(2,1)S(1)}, u32[]{:S(2)}, u32[]{:S(2)}) collective-permute-start(bf16[144,1024]{1,0:T(8,128)(2,1)S(1)} %pad_maximum_fusion.14), channel_id=1, source_target_pairs={{0,16},{8,24},{16,0},{24,8},{1,17},{9,25},{17,1},{25,9},{2,18},{10... | collective-permute-start | bytes 884744 | tf_op jit(solution)/shard_map/ppermute | solution.py:145
  14.7 2.1 %cut.1 = (bf16[208,1024]{1,0:T(8,128)(2,1)S(1)}, bf16[192,1024]{1,0:T(8,128)(2,1)S(1)}, bf16[208,1024]{1,0:T(8,128)(2,1)S(1)}, bf16[192,1024]{1,0:T(8,128)(2,1)S(1)}) custom-call(s32[7,16]{1,0:T(8,128)S(1)} %stack.2.where, s32[1,3]{1,0:T(1,128)S(1)} %copy-done.1, s32[1,3]{1,0:T(1,128)S(1)} %copy-done.2, s32[1,3]{1,0:T(1,128)S(1)} %copy-done.3, ...), custom_call_target="tpu_custom_call" | custom-call | flops 981467136 | bytes 5242880 | tf_op jit(solution)/shard_map/cut/pallas_call | solution.py:223
  16.8 1.6 collective-permute-start.6
  18.4 3.2 %collective-permute-start.7 = (bf16[208,1024]{1,0:T(8,128)(2,1)S(1)}, bf16[208,1024]{1,0:T(8,128)(2,1)S(1)}, u32[]{:S(2)}, u32[]{:S(2)}) collective-permute-start(bf16[208,1024]{1,0:T(8,128)(2,1)S(1)} %get-tuple-element.59), channel_id=1, source_target_pairs={{0,28},{4,0},{8,4},{12,8},{16,12},{20,16},{24,20},{28,24},{1,29},{... | collective-permute-start | bytes 1277960 | tf_op jit(solution)/shard_map/ppermute | solution.py:149
  21.7 7.4 %collective-permute-done.3 = bf16[144,1024]{1,0:T(8,128)(2,1)S(1)} collective-permute-done((bf16[144,1024]{1,0:T(8,128)(2,1)S(1)}, bf16[144,1024]{1,0:T(8,128)(2,1)S(1)}, u32[]{:S(2)}, u32[]{:S(2)}) %collective-permute-start.3) | collective-permute-done | bytes 294944 | tf_op jit(solution)/shard_map/ppermute | solution.py:145
  29.2 5.8 %collective-permute-done.6.p0 = bf16[208,1024]{1,0:T(8,128)(2,1)S(1)} collective-permute-done((bf16[208,1024]{1,0:T(8,128)(2,1)S(1)}, bf16[208,1024]{1,0:T(8,128)(2,1)S(1)}, u32[]{:S(2)}, u32[]{:S(2)}) %collective-permute-start.6) | collective-permute-done | bytes 426016 | tf_op jit(solution)/shard_map/ppermute | solution.py:149
  35.0 3.2 %collective-permute-done.7.n0 = bf16[208,1024]{1,0:T(8,128)(2,1)S(1)} collective-permute-done((bf16[208,1024]{1,0:T(8,128)(2,1)S(1)}, bf16[208,1024]{1,0:T(8,128)(2,1)S(1)}, u32[]{:S(2)}, u32[]{:S(2)}) %collective-permute-start.7) | collective-permute-done | bytes 426016 | tf_op jit(solution)/shard_map/ppermute | solution.py:149
  39.9 2.0 %collective-permute-start.11 = (bf16[192,1024]{1,0:T(8,128)(2,1)S(1)}, bf16[192,1024]{1,0:T(8,128)(2,1)S(1)}, u32[]{:S(2)}, u32[]{:S(2)}) collective-permute-start(bf16[192,1024]{1,0:T(8,128)(2,1)S(1)} %get-tuple-element.66), channel_id=1, source_target_pairs={{0,4},{4,8},{8,12},{12,16},{16,20},{20,24},{24,28},{28,0},{1,5},{5... | collective-permute-start | bytes 1179656 | tf_op jit(solution)/shard_map/ppermute | solution.py:149
  41.9 2.7 %collective-permute-start.12 = (bf16[192,1024]{1,0:T(8,128)(2,1)S(1)}, bf16[192,1024]{1,0:T(8,128)(2,1)S(1)}, u32[]{:S(2)}, u32[]{:S(2)}) collective-permute-start(bf16[192,1024]{1,0:T(8,128)(2,1)S(1)} %get-tuple-element.67), channel_id=1, source_target_pairs={{0,28},{4,0},{8,4},{12,8},{16,12},{20,16},{24,20},{28,24},{1,29},{... | collective-permute-start | bytes 1179656 | tf_op jit(solution)/shard_map/ppermute | solution.py:149
  44.6 8.0 %collective-permute-done.10 = bf16[256,1024]{1,0:T(8,128)(2,1)S(1)} collective-permute-done((bf16[256,1024]{1,0:T(8,128)(2,1)S(1)}, bf16[256,1024]{1,0:T(8,128)(2,1)S(1)}, u32[]{:S(2)}, u32[]{:S(2)}) %collective-permute-start.10) | collective-permute-done | bytes 524320 | tf_op jit(solution)/shard_map/ppermute | solution.py:145
  52.7 8.3 %collective-permute-done.9 = bf16[256,1024]{1,0:T(8,128)(2,1)S(1)} collective-permute-done((bf16[256,1024]{1,0:T(8,128)(2,1)S(1)}, bf16[256,1024]{1,0:T(8,128)(2,1)S(1)}, u32[]{:S(2)}, u32[]{:S(2)}) %collective-permute-start.9) | collective-permute-done | bytes 524320 | tf_op jit(solution)/shard_map/ppermute | solution.py:145
  61.1 4.9 %collective-permute-done.8 = bf16[288,1024]{1,0:T(8,128)(2,1)S(1)} collective-permute-done((bf16[288,1024]{1,0:T(8,128)(2,1)S(1)}, bf16[288,1024]{1,0:T(8,128)(2,1)S(1)}, u32[]{:S(2)}, u32[]{:S(2)}) %collective-permute-start.8) | collective-permute-done | bytes 589856 | tf_op jit(solution)/shard_map/ppermute | solution.py:145
  66.1 5.8 %collective-permute-done.11.p1 = bf16[192,1024]{1,0:T(8,128)(2,1)S(1)} collective-permute-done((bf16[192,1024]{1,0:T(8,128)(2,1)S(1)}, bf16[192,1024]{1,0:T(8,128)(2,1)S(1)}, u32[]{:S(2)}, u32[]{:S(2)}) %collective-permute-start.11) | collective-permute-done | bytes 393248 | tf_op jit(solution)/shard_map/ppermute | solution.py:149
  71.9 4.1 %place.1 = (bf16[448,2048]{1,0:T(8,128)(2,1)S(1)}, bf16[384,2048]{1,0:T(8,128)(2,1)S(1)}, bf16[384,448]{1,0:T(8,128)(2,1)S(1)}) custom-call(s32[7,16]{1,0:T(8,128)S(1)} %stack.2.where, s32[1,3]{1,0:T(1,128)S(1)} %copy-done.1, s32[1,3]{1,0:T(1,128)S(1)} %copy-done.2, s32[1,3]{1,0:T(1,128)S(1)} %copy-done.3, bf16[576,2048]{1,0:T(8,128)(2,1)S(1)} %bitcast.6, ...), custom_call_target="tpu_custom_call" | custom-call | flops 4294967296 | bytes 10485760 | tf_op jit(solution)/shard_map/place/pallas_call | solution.py:273
  76.3 1.4 collective-permute-start.13
  77.9 2.3 %collective-permute-start.15 = (bf16[512,512]{1,0:T(8,128)(2,1)S(1)}, bf16[512,512]{1,0:T(8,128)(2,1)S(1)}, u32[]{:S(2)}, u32[]{:S(2)}) collective-permute-start(bf16[512,512]{1,0:T(8,128)(2,1)S(1)} %get-tuple-element.116), channel_id=1, source_target_pairs={{0,8},{8,0},{16,24},{24,16},{1,9},{9,1},{17,25},{25,17},{2,10},{10... | collective-permute-start | bytes 1572872 | tf_op jit(solution)/shard_map/ppermute | solution.py:145
  80.2 23.1 %collective-permute-done.16 = bf16[512,512]{1,0:T(8,128)(2,1)S(1)} collective-permute-done((bf16[512,512]{1,0:T(8,128)(2,1)S(1)}, bf16[512,512]{1,0:T(8,128)(2,1)S(1)}, u32[]{:S(2)}, u32[]{:S(2)}) %collective-permute-start.16) | collective-permute-done | bytes 524320 | tf_op jit(solution)/shard_map/ppermute | solution.py:145
  105.1 1.8 collective-permute-start.20
  108.5 2.3 %collective-permute-start.19 = (bf16[1024,512]{1,0:T(8,128)(2,1)S(1)}, bf16[1024,512]{1,0:T(8,128)(2,1)S(1)}, u32[]{:S(2)}, u32[]{:S(2)}) collective-permute-start(bf16[1024,512]{1,0:T(8,128)(2,1)S(1)} %pad_maximum_fusion.7.d8), channel_id=1, source_target_pairs={{0,8},{8,0},{16,24},{24,16},{1,9},{9,1},{17,25},{25,17},{2,10},{10... | collective-permute-start | bytes 3145736 | tf_op jit(solution)/shard_map/ppermute | solution.py:145
  110.8 19.1 %collective-permute-done.20.far_ref = bf16[1024,512]{1,0:T(8,128)(2,1)S(1)} collective-permute-done((bf16[1024,512]{1,0:T(8,128)(2,1)S(1)}, bf16[1024,512]{1,0:T(8,128)(2,1)S(1)}, u32[]{:S(2)}, u32[]{:S(2)}) %collective-permute-start.20) | collective-permute-done | bytes 1048608 | tf_op jit(solution)/shard_map/ppermute | solution.py:145
  132.7 5.9 %prep.1 = (bf16[896,2048]{1,0:T(8,128)(2,1)S(1)}, bf16[896,2048]{1,0:T(8,128)(2,1)S(1)}, f32[48,2048]{1,0:T(8,128)S(1)}) custom-call(s32[7,16]{1,0:T(8,128)S(1)} %stack.2.where, bf16[448,2048]{1,0:T(8,128)(2,1)S(1)} %get-tuple-element.85.mine_ref, bf16[448,2048]{1,0:T(8,128)(2,1)S(1)} %collective-permute-done.17.other_ref, ...), custom_call_target="tpu_custom_call" | custom-call | flops 36700160 | bytes 11010048 | tf_op jit(solution)/shard_map/prep/pallas_call | solution.py:311
  138.6 5.4 %conv.5 = (bf16[448,256]{1,0:T(8,128)(2,1)S(1)}, bf16[448,256]{1,0:T(8,128)(2,1)S(1)}) custom-call(s32[7,16]{1,0:T(8,128)S(1)} %stack.2.where, bf16[896,2048]{1,0:T(8,128)(2,1)S(1)} %get-tuple-element.92.rows_ref, bf16[1024,512]{1,0:T(8,128)(2,1)S(1)} %get-tuple-element.112.near_ref, bf16[1024,512]{1,0:T(8,128)(2,1)S(1)} %collective-permute-done.21.far_ref, ...), custom_call_target="tpu_custom_call" | custom-call | flops 1879048192 | bytes 8388608 | tf_op jit(solution)/shard_map/conv/pallas_call | solution.py:369
  144.0 5.4 %conv.4 = (bf16[448,256]{1,0:T(8,128)(2,1)S(1)}, bf16[448,256]{1,0:T(8,128)(2,1)S(1)}) custom-call(s32[7,16]{1,0:T(8,128)S(1)} %stack.2.where, bf16[896,2048]{1,0:T(8,128)(2,1)S(1)} %get-tuple-element.88.rows_ref, bf16[1024,512]{1,0:T(8,128)(2,1)S(1)} %get-tuple-element.114.near_ref, bf16[1024,512]{1,0:T(8,128)(2,1)S(1)} %collective-permute-done.20.far_ref, ...), custom_call_target="tpu_custom_call" | custom-call | flops 1879048192 | bytes 8388608 | tf_op jit(solution)/shard_map/conv/pallas_call | solution.py:369
  149.4 5.9 %collective-permute-done.18.er = bf16[1024,512]{1,0:T(8,128)(2,1)S(1)} collective-permute-done((bf16[1024,512]{1,0:T(8,128)(2,1)S(1)}, bf16[1024,512]{1,0:T(8,128)(2,1)S(1)}, u32[]{:S(2)}, u32[]{:S(2)}) %collective-permute-start.18) | collective-permute-done | bytes 1048608 | tf_op jit(solution)/shard_map/ppermute | solution.py:145
  156.6 6.4 %collective-permute-done.26.o2 = bf16[448,256]{1,0:T(8,128)(2,1)S(1)} collective-permute-done((bf16[448,256]{1,0:T(8,128)(2,1)S(1)}, bf16[448,256]{1,0:T(8,128)(2,1)S(1)}, u32[]{:S(2)}, u32[]{:S(2)}) %collective-permute-start.26) | collective-permute-done | bytes 229408 | tf_op jit(solution)/shard_map/ppermute | solution.py:145
  163.1 5.4 %conv.7 = (bf16[448,256]{1,0:T(8,128)(2,1)S(1)}, bf16[448,256]{1,0:T(8,128)(2,1)S(1)}) custom-call(s32[7,16]{1,0:T(8,128)S(1)} %stack.2.where, bf16[896,2048]{1,0:T(8,128)(2,1)S(1)} %get-tuple-element.92.rows_ref, bf16[1024,512]{1,0:T(8,128)(2,1)S(1)} %get-tuple-element.84.near_ref, bf16[1024,512]{1,0:T(8,128)(2,1)S(1)} %collective-permute-done.23.far_ref, ...), custom_call_target="tpu_custom_call" | custom-call | flops 1879048192 | bytes 8388608 | tf_op jit(solution)/shard_map/conv/pallas_call | solution.py:369
  168.9 5.4 %conv.6 = (bf16[448,256]{1,0:T(8,128)(2,1)S(1)}, bf16[448,256]{1,0:T(8,128)(2,1)S(1)}) custom-call(s32[7,16]{1,0:T(8,128)S(1)} %stack.2.where, bf16[896,2048]{1,0:T(8,128)(2,1)S(1)} %get-tuple-element.88.rows_ref, bf16[1024,512]{1,0:T(8,128)(2,1)S(1)} %get-tuple-element.83.near_ref, bf16[1024,512]{1,0:T(8,128)(2,1)S(1)} %collective-permute-done.22.far_ref, ...), custom_call_target="tpu_custom_call" | custom-call | flops 1879048192 | bytes 8388608 | tf_op jit(solution)/shard_map/conv/pallas_call | solution.py:369
  175.9 8.5 %finish.1 = bf16[384,2048]{1,0:T(8,128)(2,1)} custom-call(s32[7,16]{1,0:T(8,128)S(1)} %stack.2.where, bf16[448,256]{1,0:T(8,128)(2,1)S(1)} %get-tuple-element.95.m0, bf16[448,256]{1,0:T(8,128)(2,1)S(1)} %get-tuple-element.97.m1, bf16[448,256]{1,0:T(8,128)(2,1)S(1)} %get-tuple-element.98.m2, bf16[448,256]{1,0:T(8,128)(2,1)S(1)} %get-tuple-element.100.m3, ...), custom_call_target="tpu_custom_call" | custom-call | flops 3221225472 | bytes 16777216 | tf_op jit(solution)/shard_map/finish/pallas_call | solution.py:437
  (102 shorter events, 15.5 us)
Async XLA Ops:
  1.5 6.6 %collective-permute-start = (bf16[64,3072]{1,0:T(8,128)(2,1)S(1)}, bf16[64,3072]{1,0:T(8,128)(2,1)S(1)}, u32[]{:S(2)}, u32[]{:S(2)}) collective-permute-start(bf16[64,3072]{1,0:T(8,128)(2,1)S(1)} %get-tuple-element.126), channel_id=1, source_target_pairs={{0,1},{1,0},{2,3},{3,2},{4,5},{5,4},{6,7},{7,6},{8,9},{9,8},{10,11... | collective-permute-start | bytes 1179656 | tf_op jit(solution)/shard_map/ppermute | solution.py:145
  2.2 1.2 collective-permute-start.1
  3.5 4.5 %collective-permute-start.2 = (bf16[48,128]{1,0:T(8,128)(2,1)S(1)}, bf16[48,128]{1,0:T(8,128)(2,1)S(1)}, u32[]{:S(2)}, u32[]{:S(2)}) collective-permute-start(bf16[48,128]{1,0:T(8,128)(2,1)S(1)} %fusion.6), channel_id=1, source_target_pairs={{0,2},{2,0},{1,3},{3,1},{4,6},{6,4},{5,7},{7,5},{8,10},{10,8},{9,1... | collective-permute-start | bytes 36872 | tf_op jit(solution)/shard_map/ppermute | solution.py:145
  8.3 13.3 %collective-permute-start.4 = (bf16[128,1024]{1,0:T(8,128)(2,1)S(1)}, bf16[128,1024]{1,0:T(8,128)(2,1)S(1)}, u32[]{:S(2)}, u32[]{:S(2)}) collective-permute-start(bf16[128,1024]{1,0:T(8,128)(2,1)S(1)} %pad_maximum_fusion.15), channel_id=1, source_target_pairs={{0,8},{8,0},{16,24},{24,16},{1,9},{9,1},{17,25},{25,17},{2,10},{10... | collective-permute-start | bytes 786440 | tf_op jit(solution)/shard_map/ppermute | solution.py:145
  10.5 11.2 %collective-permute-start.5 = (bf16[128,1024]{1,0:T(8,128)(2,1)S(1)}, bf16[128,1024]{1,0:T(8,128)(2,1)S(1)}, u32[]{:S(2)}, u32[]{:S(2)}) collective-permute-start(bf16[128,1024]{1,0:T(8,128)(2,1)S(1)} %slice.148), channel_id=1, source_target_pairs={{0,2},{2,0},{1,3},{3,1},{4,6},{6,4},{5,7},{7,5},{8,10},{10,8},{9,1... | collective-permute-start | bytes 786440 | tf_op jit(solution)/shard_map/ppermute | solution.py:145
  12.1 17.0 %collective-permute-start.3 = (bf16[144,1024]{1,0:T(8,128)(2,1)S(1)}, bf16[144,1024]{1,0:T(8,128)(2,1)S(1)}, u32[]{:S(2)}, u32[]{:S(2)}) collective-permute-start(bf16[144,1024]{1,0:T(8,128)(2,1)S(1)} %pad_maximum_fusion.14), channel_id=1, source_target_pairs={{0,16},{8,24},{16,0},{24,8},{1,17},{9,25},{17,1},{25,9},{2,18},{10... | collective-permute-start | bytes 884744 | tf_op jit(solution)/shard_map/ppermute | solution.py:145
  16.8 18.2 %collective-permute-start.6 = (bf16[208,1024]{1,0:T(8,128)(2,1)S(1)}, bf16[208,1024]{1,0:T(8,128)(2,1)S(1)}, u32[]{:S(2)}, u32[]{:S(2)}) collective-permute-start(bf16[208,1024]{1,0:T(8,128)(2,1)S(1)} %get-tuple-element.58), channel_id=1, source_target_pairs={{0,4},{4,8},{8,12},{12,16},{16,20},{20,24},{24,28},{28,0},{1,5},{5... | collective-permute-start | bytes 1277960 | tf_op jit(solution)/shard_map/ppermute | solution.py:149
  18.4 19.8 %collective-permute-start.7 = (bf16[208,1024]{1,0:T(8,128)(2,1)S(1)}, bf16[208,1024]{1,0:T(8,128)(2,1)S(1)}, u32[]{:S(2)}, u32[]{:S(2)}) collective-permute-start(bf16[208,1024]{1,0:T(8,128)(2,1)S(1)} %get-tuple-element.59), channel_id=1, source_target_pairs={{0,28},{4,0},{8,4},{12,8},{16,12},{20,16},{24,20},{28,24},{1,29},{... | collective-permute-start | bytes 1277960 | tf_op jit(solution)/shard_map/ppermute | solution.py:149
  38.2 14.4 %collective-permute-start.10 = (bf16[256,1024]{1,0:T(8,128)(2,1)S(1)}, bf16[256,1024]{1,0:T(8,128)(2,1)S(1)}, u32[]{:S(2)}, u32[]{:S(2)}) collective-permute-start(bf16[256,1024]{1,0:T(8,128)(2,1)S(1)} %pad_maximum_fusion.11), channel_id=1, source_target_pairs={{0,4},{4,0},{1,5},{5,1},{2,6},{6,2},{3,7},{7,3},{8,12},{12,8},{9,1... | collective-permute-start | bytes 1572872 | tf_op jit(solution)/shard_map/ppermute | solution.py:145
  38.2 22.8 %collective-permute-start.9 = (bf16[256,1024]{1,0:T(8,128)(2,1)S(1)}, bf16[256,1024]{1,0:T(8,128)(2,1)S(1)}, u32[]{:S(2)}, u32[]{:S(2)}) collective-permute-start(bf16[256,1024]{1,0:T(8,128)(2,1)S(1)} %pad_maximum_fusion.10), channel_id=1, source_target_pairs={{0,16},{8,24},{16,0},{24,8},{1,17},{9,25},{17,1},{25,9},{2,18},{10... | collective-permute-start | bytes 1572872 | tf_op jit(solution)/shard_map/ppermute | solution.py:145
  38.5 27.5 %collective-permute-start.8 = (bf16[288,1024]{1,0:T(8,128)(2,1)S(1)}, bf16[288,1024]{1,0:T(8,128)(2,1)S(1)}, u32[]{:S(2)}, u32[]{:S(2)}) collective-permute-start(bf16[288,1024]{1,0:T(8,128)(2,1)S(1)} %pad_maximum_fusion.8), channel_id=1, source_target_pairs={{0,8},{8,0},{16,24},{24,16},{1,9},{9,1},{17,25},{25,17},{2,10},{10... | collective-permute-start | bytes 1769480 | tf_op jit(solution)/shard_map/ppermute | solution.py:145
  39.9 32.0 %collective-permute-start.11 = (bf16[192,1024]{1,0:T(8,128)(2,1)S(1)}, bf16[192,1024]{1,0:T(8,128)(2,1)S(1)}, u32[]{:S(2)}, u32[]{:S(2)}) collective-permute-start(bf16[192,1024]{1,0:T(8,128)(2,1)S(1)} %get-tuple-element.66), channel_id=1, source_target_pairs={{0,4},{4,8},{8,12},{12,16},{16,20},{20,24},{24,28},{28,0},{1,5},{5... | collective-permute-start | bytes 1179656 | tf_op jit(solution)/shard_map/ppermute | solution.py:149
  41.9 30.0 %collective-permute-start.12 = (bf16[192,1024]{1,0:T(8,128)(2,1)S(1)}, bf16[192,1024]{1,0:T(8,128)(2,1)S(1)}, u32[]{:S(2)}, u32[]{:S(2)}) collective-permute-start(bf16[192,1024]{1,0:T(8,128)(2,1)S(1)} %get-tuple-element.67), channel_id=1, source_target_pairs={{0,28},{4,0},{8,4},{12,8},{16,12},{20,16},{24,20},{28,24},{1,29},{... | collective-permute-start | bytes 1179656 | tf_op jit(solution)/shard_map/ppermute | solution.py:149
  76.0 28.9 %collective-permute-start.17 = (bf16[448,2048]{1,0:T(8,128)(2,1)S(1)}, bf16[448,2048]{1,0:T(8,128)(2,1)S(1)}, u32[]{:S(2)}, u32[]{:S(2)}) collective-permute-start(bf16[448,2048]{1,0:T(8,128)(2,1)S(1)} %get-tuple-element.85.mine_ref), channel_id=1, source_target_pairs={{0,1},{1,0},{2,3},{3,2},{4,5},{5,4},{6,7},{7,6},{8,9},{9,8},{10,11... | collective-permute-start | bytes 5505032 | tf_op jit(solution)/shard_map/ppermute | solution.py:145
  76.1 27.4 %collective-permute-start.14 = (bf16[512,1024]{1,0:T(8,128)(2,1)S(1)}, bf16[512,1024]{1,0:T(8,128)(2,1)S(1)}, u32[]{:S(2)}, u32[]{:S(2)}) collective-permute-start(bf16[512,1024]{1,0:T(8,128)(2,1)S(1)} %pad_maximum_fusion.4), channel_id=1, source_target_pairs={{0,2},{2,0},{1,3},{3,1},{4,6},{6,4},{5,7},{7,5},{8,10},{10,8},{9,1... | collective-permute-start | bytes 3145736 | tf_op jit(solution)/shard_map/ppermute | solution.py:145
  76.3 28.4 %collective-permute-start.13 = (bf16[576,1024]{1,0:T(8,128)(2,1)S(1)}, bf16[576,1024]{1,0:T(8,128)(2,1)S(1)}, u32[]{:S(2)}, u32[]{:S(2)}) collective-permute-start(bf16[576,1024]{1,0:T(8,128)(2,1)S(1)} %pad_maximum_fusion.2), channel_id=1, source_target_pairs={{0,4},{4,0},{1,5},{5,1},{2,6},{6,2},{3,7},{7,3},{8,12},{12,8},{9,1... | collective-permute-start | bytes 3538952 | tf_op jit(solution)/shard_map/ppermute | solution.py:145
  77.8 25.5 %collective-permute-start.16 = (bf16[512,512]{1,0:T(8,128)(2,1)S(1)}, bf16[512,512]{1,0:T(8,128)(2,1)S(1)}, u32[]{:S(2)}, u32[]{:S(2)}) collective-permute-start(bf16[512,512]{1,0:T(8,128)(2,1)S(1)} %get-tuple-element.115), channel_id=1, source_target_pairs={{0,16},{8,24},{16,0},{24,8},{1,17},{9,25},{17,1},{25,9},{2,18},{10... | collective-permute-start | bytes 1572872 | tf_op jit(solution)/shard_map/ppermute | solution.py:145
  77.9 25.5 %collective-permute-start.15 = (bf16[512,512]{1,0:T(8,128)(2,1)S(1)}, bf16[512,512]{1,0:T(8,128)(2,1)S(1)}, u32[]{:S(2)}, u32[]{:S(2)}) collective-permute-start(bf16[512,512]{1,0:T(8,128)(2,1)S(1)} %get-tuple-element.116), channel_id=1, source_target_pairs={{0,8},{8,0},{16,24},{24,16},{1,9},{9,1},{17,25},{25,17},{2,10},{10... | collective-permute-start | bytes 1572872 | tf_op jit(solution)/shard_map/ppermute | solution.py:145
  105.1 24.8 %collective-permute-start.20 = (bf16[1024,512]{1,0:T(8,128)(2,1)S(1)}, bf16[1024,512]{1,0:T(8,128)(2,1)S(1)}, u32[]{:S(2)}, u32[]{:S(2)}) collective-permute-start(bf16[1024,512]{1,0:T(8,128)(2,1)S(1)} %get-tuple-element.114.near_ref), channel_id=1, source_target_pairs={{0,2},{2,0},{1,3},{3,1},{4,6},{6,4},{5,7},{7,5},{8,10},{10,8},{9,1... | collective-permute-start | bytes 3145736 | tf_op jit(solution)/shard_map/ppermute | solution.py:145
  107.1 24.2 %collective-permute-start.21 = (bf16[1024,512]{1,0:T(8,128)(2,1)S(1)}, bf16[1024,512]{1,0:T(8,128)(2,1)S(1)}, u32[]{:S(2)}, u32[]{:S(2)}) collective-permute-start(bf16[1024,512]{1,0:T(8,128)(2,1)S(1)} %get-tuple-element.112.near_ref), channel_id=1, source_target_pairs={{0,4},{4,0},{1,5},{5,1},{2,6},{6,2},{3,7},{7,3},{8,12},{12,8},{9,1... | collective-permute-start | bytes 3145736 | tf_op jit(solution)/shard_map/ppermute | solution.py:145
  108.2 47.2 %collective-permute-start.18 = (bf16[1024,512]{1,0:T(8,128)(2,1)S(1)}, bf16[1024,512]{1,0:T(8,128)(2,1)S(1)}, u32[]{:S(2)}, u32[]{:S(2)}) collective-permute-start(bf16[1024,512]{1,0:T(8,128)(2,1)S(1)} %pad_maximum_fusion.6.e8), channel_id=1, source_target_pairs={{0,16},{8,24},{16,0},{24,8},{1,17},{9,25},{17,1},{25,9},{2,18},{10... | collective-permute-start | bytes 3145736 | tf_op jit(solution)/shard_map/ppermute | solution.py:145
  108.5 46.9 %collective-permute-start.19 = (bf16[1024,512]{1,0:T(8,128)(2,1)S(1)}, bf16[1024,512]{1,0:T(8,128)(2,1)S(1)}, u32[]{:S(2)}, u32[]{:S(2)}) collective-permute-start(bf16[1024,512]{1,0:T(8,128)(2,1)S(1)} %pad_maximum_fusion.7.d8), channel_id=1, source_target_pairs={{0,8},{8,0},{16,24},{24,16},{1,9},{9,1},{17,25},{25,17},{2,10},{10... | collective-permute-start | bytes 3145736 | tf_op jit(solution)/shard_map/ppermute | solution.py:145
  131.3 24.1 %collective-permute-start.22 = (bf16[1024,512]{1,0:T(8,128)(2,1)S(1)}, bf16[1024,512]{1,0:T(8,128)(2,1)S(1)}, u32[]{:S(2)}, u32[]{:S(2)}) collective-permute-start(bf16[1024,512]{1,0:T(8,128)(2,1)S(1)} %get-tuple-element.83.near_ref), channel_id=1, source_target_pairs={{0,2},{2,0},{1,3},{3,1},{4,6},{6,4},{5,7},{7,5},{8,10},{10,8},{9,1... | collective-permute-start | bytes 3145736 | tf_op jit(solution)/shard_map/ppermute | solution.py:145
  131.9 23.5 %collective-permute-start.23 = (bf16[1024,512]{1,0:T(8,128)(2,1)S(1)}, bf16[1024,512]{1,0:T(8,128)(2,1)S(1)}, u32[]{:S(2)}, u32[]{:S(2)}) collective-permute-start(bf16[1024,512]{1,0:T(8,128)(2,1)S(1)} %get-tuple-element.84.near_ref), channel_id=1, source_target_pairs={{0,4},{4,0},{1,5},{5,1},{2,6},{6,2},{3,7},{7,3},{8,12},{12,8},{9,1... | collective-permute-start | bytes 3145736 | tf_op jit(solution)/shard_map/ppermute | solution.py:145
  155.4 20.5 %collective-permute-start.28 = (bf16[1024,512]{1,0:T(8,128)(2,1)S(1)}, bf16[1024,512]{1,0:T(8,128)(2,1)S(1)}, u32[]{:S(2)}, u32[]{:S(2)}) collective-permute-start(bf16[1024,512]{1,0:T(8,128)(2,1)S(1)} %pad_maximum_fusion.6.e8), channel_id=1, source_target_pairs={{0,1},{1,0},{2,3},{3,2},{4,5},{5,4},{6,7},{7,6},{8,9},{9,8},{10,11... | collective-permute-start | bytes 3145736 | tf_op jit(solution)/shard_map/ppermute | solution.py:145
  155.5 20.4 %collective-permute-start.29 = (bf16[1024,512]{1,0:T(8,128)(2,1)S(1)}, bf16[1024,512]{1,0:T(8,128)(2,1)S(1)}, u32[]{:S(2)}, u32[]{:S(2)}) collective-permute-start(bf16[1024,512]{1,0:T(8,128)(2,1)S(1)} %collective-permute-done.18.er), channel_id=1, source_target_pairs={{0,1},{1,0},{2,3},{3,2},{4,5},{5,4},{6,7},{7,6},{8,9},{9,8},{10,11... | collective-permute-start | bytes 3145736 | tf_op jit(solution)/shard_map/ppermute | solution.py:145
  156.0 20.0 %collective-permute-start.30 = (bf16[1024,512]{1,0:T(8,128)(2,1)S(1)}, bf16[1024,512]{1,0:T(8,128)(2,1)S(1)}, u32[]{:S(2)}, u32[]{:S(2)}) collective-permute-start(bf16[1024,512]{1,0:T(8,128)(2,1)S(1)} %pad_maximum_fusion.7.d8), channel_id=1, source_target_pairs={{0,1},{1,0},{2,3},{3,2},{4,5},{5,4},{6,7},{7,6},{8,9},{9,8},{10,11... | collective-permute-start | bytes 3145736 | tf_op jit(solution)/shard_map/ppermute | solution.py:145
  156.0 19.9 %collective-permute-start.31 = (bf16[1024,512]{1,0:T(8,128)(2,1)S(1)}, bf16[1024,512]{1,0:T(8,128)(2,1)S(1)}, u32[]{:S(2)}, u32[]{:S(2)}) collective-permute-start(bf16[1024,512]{1,0:T(8,128)(2,1)S(1)} %collective-permute-done.19.dr), channel_id=1, source_target_pairs={{0,1},{1,0},{2,3},{3,2},{4,5},{5,4},{6,7},{7,6},{8,9},{9,8},{10,11... | collective-permute-start | bytes 3145736 | tf_op jit(solution)/shard_map/ppermute | solution.py:145
  156.5 6.5 %collective-permute-start.26 = (bf16[448,256]{1,0:T(8,128)(2,1)S(1)}, bf16[448,256]{1,0:T(8,128)(2,1)S(1)}, u32[]{:S(2)}, u32[]{:S(2)}) collective-permute-start(bf16[448,256]{1,0:T(8,128)(2,1)S(1)} %get-tuple-element.103), channel_id=1, source_target_pairs={{0,1},{1,0},{2,3},{3,2},{4,5},{5,4},{6,7},{7,6},{8,9},{9,8},{10,11... | collective-permute-start | bytes 688136 | tf_op jit(solution)/shard_map/ppermute | solution.py:145
  162.9 5.5 %collective-permute-start.24 = (bf16[448,256]{1,0:T(8,128)(2,1)S(1)}, bf16[448,256]{1,0:T(8,128)(2,1)S(1)}, u32[]{:S(2)}, u32[]{:S(2)}) collective-permute-start(bf16[448,256]{1,0:T(8,128)(2,1)S(1)} %get-tuple-element.101), channel_id=1, source_target_pairs={{0,1},{1,0},{2,3},{3,2},{4,5},{5,4},{6,7},{7,6},{8,9},{9,8},{10,11... | collective-permute-start | bytes 688136 | tf_op jit(solution)/shard_map/ppermute | solution.py:145
  168.5 5.9 %collective-permute-start.27 = (bf16[448,256]{1,0:T(8,128)(2,1)S(1)}, bf16[448,256]{1,0:T(8,128)(2,1)S(1)}, u32[]{:S(2)}, u32[]{:S(2)}) collective-permute-start(bf16[448,256]{1,0:T(8,128)(2,1)S(1)} %get-tuple-element.104), channel_id=1, source_target_pairs={{0,1},{1,0},{2,3},{3,2},{4,5},{5,4},{6,7},{7,6},{8,9},{9,8},{10,11... | collective-permute-start | bytes 688136 | tf_op jit(solution)/shard_map/ppermute | solution.py:145
  174.4 1.6 collective-permute-start.25
  (7 other events, 33.0 us)

commit v3 on v2

--- a/solution.py
+++ b/solution.py
@@ -133,10 +133,10 @@
 LANE = 128
 BLOCKS = D // LANE
 HALF = D // 2
-CHUNK = 256
+FIRST = 384
 SMALL = 48
 META = 16
-ROWS = 224
+ROWS = PAIR
 TILE = 64
 
 
@@ -161,14 +161,47 @@
     return list(lax.optimization_barrier(arrays))
 
 
+def coordinates():
+    return [lax.axis_index(name) for name in ("z", "y", "x", "core")]
+
+
+def bits(block):
+    z, y, x, _ = coordinates()
+    return (block >> 3) ^ (z >> 1), ((block >> 2) & 1) ^ (z & 1), ((block >> 1) & 1) ^ y, (block & 1) ^ x
+
+
+def spot_a(block):
+    z2, z1, y, x = bits(block)
+    return x * 8 + y * 4 + z1 * 2 + z2
+
+
+def spot_b(block):
+    z2, z1, y, x = bits(block)
+    return y * 8 + x * 4 + z2 * 2 + z1
+
+
+def spot_e(block):
+    z2, z1, y, x = bits(block)
+    return z2 * 8 + z1 * 4 + y * 2 + x
+
+
+def spot_d(block):
+    z2, z1, y, x = bits(block)
+    return z1 * 8 + z2 * 4 + y * 2 + x
+
+
 def lanes(index):
     return pl.ds(pl.multiple_of(index * LANE, LANE), LANE)
 
 
-def local(lens, dest, offs, where, code):
+COST = pl.CostEstimate(flops=2**20, bytes_accessed=2**16, transcendentals=0)
+
+
+def local(lens, dest, offs, code):
+    z, y, _, _ = coordinates()
     count, offset, start, before = 0, 0, 0, 0
     for slot in range(3):
-        match = (dest[0, slot] - where[4, 3] + 8) % 8 == code
+        match = (dest[0, slot] - (z * 2 + y) + 8) % 8 == code
         count = jnp.where(match, lens[0, slot], count)
         offset = jnp.where(match, offs[0, slot], offset)
         start = jnp.where(match, before, start)
@@ -189,9 +222,9 @@
     return lax.broadcasted_iota(jnp.int32, shape, 0), lax.broadcasted_iota(jnp.int32, shape, 1)
 
 
-def cut_kernel(where, lens, dest, offs, rows_ref, up0, up1, down0, down1):
+def cut_kernel(lens, dest, offs, rows_ref, up0, up1, down0, down1):
     for code, first_ref, second_ref in ((1, up0, up1), (7, down0, down1)):
-        count, offset, start = local(lens, dest, offs, where, code)
+        count, offset, start = local(lens, dest, offs, code)
         spot, slot = grid_of(MAXLEN + META, rows_ref.shape[0])
         picker = hot((slot == start + spot) & (spot < count))
         spot, _ = grid_of(MAXLEN + META, HALF)
@@ -218,23 +251,21 @@
     return pltpu.CompilerParams(vmem_limit_bytes=mebibytes * 2**20)
 
 
-def cut(where, lens, dest, offs, rows):
+def cut(lens, dest, offs, rows):
     first, second = shape(MAXLEN + META, HALF), shape(MAXLEN, HALF)
     return pl.pallas_call(
         cut_kernel,
         out_shape=(first, second, first, second),
-        in_specs=smem(4) + vmem(1),
+        in_specs=smem(3) + vmem(1),
         out_specs=tuple(vmem(4)),
         compiler_params=limits(16),
-        cost_estimate=pl.CostEstimate(
-            flops=4 * (MAXLEN + META) * rows.shape[0] * D, bytes_accessed=5 * 2**20, transcendentals=0
-        ),
+        cost_estimate=COST,
         name="cut",
-    )(where, lens, dest, offs, rows)
-
-
-def place_kernel(where, lens, dest, offs, rows_ref, p0, p1, n0, n1, spread_ref, base_ref, pick_ref):
-    count, offset, start = local(lens, dest, offs, where, 0)
+    )(lens, dest, offs, rows)
+
+
+def place_kernel(lens, dest, offs, rows_ref, p0, p1, n0, n1, spread_ref, base_ref, pick_ref):
+    count, offset, start = local(lens, dest, offs, 0)
     ones = jnp.ones((1, 1), jnp.int32)
 
     def noted(ref):
@@ -269,23 +300,24 @@
     base_ref[...] = take(pick, spread_ref[...]).astype(jnp.bfloat16)
 
 
-def place(where, lens, dest, offs, rows, arrived):
+def place(lens, dest, offs, rows, arrived):
     return pl.pallas_call(
         place_kernel,
         out_shape=(shape(PAD, D), shape(RCV_DEV, D), shape(RCV_DEV, PAD)),
-        in_specs=smem(4) + vmem(5),
+        in_specs=smem(3) + vmem(5),
         out_specs=tuple(vmem(3)),
         compiler_params=limits(24),
-        cost_estimate=pl.CostEstimate(flops=4 * 2**30, bytes_accessed=10 * 2**20, transcendentals=0),
+        cost_estimate=COST,
         name="place",
-    )(where, lens, dest, offs, rows, *arrived)
-
-
-def prep_kernel(where, mine_ref, other_ref, notes_ref, first_ref, second_ref, small_ref):
+    )(lens, dest, offs, rows, *arrived)
+
+
+def prep_kernel(mine_ref, other_ref, notes_ref, first_ref, second_ref, small_ref):
     for block in range(BLOCKS):
-        at = pl.ds(pl.multiple_of(where[5, block] * META, META), META)
+        spot = spot_a(block)
+        at = pl.ds(pl.multiple_of((spot & 7) * META, META), META)
         for part in range(SMALL // META):
-            tile = notes_ref[at, lanes(where[6, block] * (SMALL // META) + part)]
+            tile = notes_ref[at, lanes((spot >> 3) * (SMALL // META) + part)]
             small_ref[part * META : (part + 1) * META, block * LANE : (block + 1) * LANE] = tile.astype(
                 jnp.float32
             )
@@ -300,52 +332,51 @@
             at = pl.ds(pl.multiple_of(base + step * TILE, TILE), TILE)
             for block in range(BLOCKS):
                 part = scaled[:, block * LANE : (block + 1) * LANE]
-                first_ref[at, lanes(where[0, block])] = part
-                second_ref[at, lanes(where[1, block])] = part
+                first_ref[at, lanes(spot_a(block))] = part
+                second_ref[at, lanes(spot_b(block))] = part
             return carry
 
         lax.fori_loop(0, PAD // TILE, one, 0)
 
 
-def prep(where, mine, other, notes):
+def prep(mine, other, notes):
     return pl.pallas_call(
         prep_kernel,
         out_shape=(shape(PAIR, D), shape(PAIR, D), shape(SMALL, D, jnp.float32)),
-        in_specs=smem(1) + vmem(3),
+        in_specs=vmem(3),
         out_specs=tuple(vmem(3)),
         compiler_params=limits(20),
-        cost_estimate=pl.CostEstimate(
-            flops=20 * PAIR * D, bytes_accessed=6 * PAIR * D, transcendentals=PAIR
-        ),
+        cost_estimate=COST,
         name="prep",
-    )(where, mine, other, notes)
-
-
-def conv_kernel(sub, where, rows_ref, near_ref, far_ref, small_ref, own_ref, other_ref, gated, taps):
-    tiles = CHUNK // LANE
-    half = where[4, 0]
+    )(mine, other, notes)
+
+
+def conv_kernel(sub, rows_hbm, near_hbm, far_hbm, small_ref, own_ref, other_ref, gated, taps, rows_ref, near_ref, far_ref, done):
+    width = own_ref.shape[1]
+    tiles = width // LANE
+    steps = PAIR // ROWS
+    spans = [pl.ds(step * ROWS, ROWS) for step in range(steps)]
+    loads = [
+        pltpu.make_async_copy(near_hbm, near_ref, done.at[0]),
+        pltpu.make_async_copy(far_hbm, far_ref, done.at[1]),
+    ]
+    for step, span in enumerate(spans):
+        loads.append(pltpu.make_async_copy(rows_hbm.at[span, :], rows_ref.at[span, :], done.at[2 + step]))
+    for load in loads:
+        load.start()
+    half = lax.axis_index("core")
     for tile in range(tiles):
         gated[tile, 0:GAP, :] = jnp.zeros((GAP, LANE), jnp.float32)
         gated[tile, GAP + PAIR : 2 * GAP + PAIR, :] = jnp.zeros((GAP, LANE), jnp.float32)
         taps[tile] = small_ref[0:KERNEL, lanes(half * (BLOCKS // 2) + sub + tile)]
-
-    def project(step, carry):
-        at = pl.ds(pl.multiple_of(step * ROWS, ROWS), ROWS)
-        near, far = rows_ref[at, 0:HALF], rows_ref[at, HALF:D]
-
-        def columns(low):
-            span = slice(low, low + CHUNK)
-            return jnp.dot(
-                near, near_ref[:, span], preferred_element_type=jnp.float32
-            ) + jnp.dot(far, far_ref[:, span], preferred_element_type=jnp.float32)
-
-        mixed = columns(0) * jax.nn.sigmoid(columns(CHUNK))
-        at = pl.ds(pl.multiple_of(step * ROWS + GAP, GAP), ROWS)
+    loads[0].wait()
+    loads[1].wait()
+    for step, span in enumerate(spans):
+        loads[2 + step].wait()
+        both = take(rows_ref[span, 0:HALF], near_ref[...]) + take(rows_ref[span, HALF:D], far_ref[...])
+        mixed = both[:, 0:width] * jax.nn.sigmoid(both[:, width:])
         for tile in range(tiles):
-            gated[tile, at, :] = mixed[:, tile * LANE : (tile + 1) * LANE]
-        return carry
-
-    lax.fori_loop(0, PAIR // ROWS, project, 0)
+            gated[tile, pl.ds(GAP + step * ROWS, ROWS), :] = mixed[:, tile * LANE : (tile + 1) * LANE]
 
     def slide(out_ref, base):
         def one(step, carry):
@@ -364,30 +395,45 @@
     slide(other_ref, PAD)
 
 
-def conv(sub, where, rows, near, far, small):
-    out = shape(PAD, CHUNK)
+def anywhere(count):
+    return [pl.BlockSpec(memory_space=pl.ANY)] * count
+
+
+def conv(sub, rows, near, far, small):
+    width = near.shape[1] // 2
+    out = shape(PAD, width)
+    weight = pltpu.VMEM(near.shape, near.dtype)
     return pl.pallas_call(
         functools.partial(conv_kernel, sub),
         out_shape=(out, out),
-        in_specs=smem(1) + vmem(4),
+        in_specs=anywhere(3) + vmem(1),
         out_specs=tuple(vmem(2)),
         scratch_shapes=[
-            pltpu.VMEM((CHUNK // LANE, PAIR + 2 * GAP, LANE), jnp.float32),
-            pltpu.VMEM((CHUNK // LANE, KERNEL, LANE), jnp.float32),
+            pltpu.VMEM((width // LANE, PAIR + 2 * GAP, LANE), jnp.float32),
+            pltpu.VMEM((width // LANE, KERNEL, LANE), jnp.float32),
+            pltpu.VMEM((PAIR, D), jnp.bfloat16),
+            weight,
+            weight,
+            pltpu.SemaphoreType.DMA((2 + PAIR // ROWS,)),
         ],
         compiler_params=limits(16),
-        cost_estimate=pl.CostEstimate(
-            flops=4 * PAIR * D * CHUNK, bytes_accessed=8 * 2**20, transcendentals=PAIR * CHUNK
-        ),
+        cost_estimate=COST,
         name="conv",
-    )(where, rows, near, far, small)
+    )(rows, near, far, small)
 
 
 def finish_kernel(
-    where, m0, m1, m2, m3, o0, o1, o2, o3, small_ref, pick_ref, base_ref,
-    e8, er, d8, dr, f8, fr, g8, gr, out_ref, first, second,
+    m0, m1, m2, m3, o0, o1, o2, o3, small_ref, pick_ref, base_ref,
+    e8, er, d8, dr, f8, fr, g8, gr, out_ref, first, second, weights, done,
 ):
-    half = where[4, 0]
+    sources = (e8, er, d8, dr, f8, fr, g8, gr)
+    loads = [
+        pltpu.make_async_copy(source, weights.at[index], done.at[index])
+        for index, source in enumerate(sources)
+    ]
+    for load in loads:
+        load.start()
+    half = lax.axis_index("core")
     count = KERNEL + 1
     pieces = [(half, (m0, m1, m2, m3)), (1 - half, (o0, o1, o2, o3))]
     refs = [ref for _, group in pieces for ref in group]
@@ -401,97 +447,82 @@
         total = total + jnp.sum(center * center, axis=-1, keepdims=True)
     scale = lax.rsqrt(total / D + epsilon)
     for side, group in pieces:
-        for place, ref in enumerate(group):
+        place = side * (BLOCKS // 2)
+        for ref in group:
+            blocks = [place + tile for tile in range(ref.shape[1] // LANE)]
+            place = place + len(blocks)
             parts = []
-            for tile in range(CHUNK // LANE):
-                block = side * (BLOCKS // 2) + place * (CHUNK // LANE) + tile
+            for tile, block in enumerate(blocks):
                 gain = small_ref[count : count + 1, lanes(block)]
                 values = ref[:, tile * LANE : (tile + 1) * LANE].astype(jnp.float32)
                 post = (values - mean) * scale * gain
                 parts.append((post * jax.nn.sigmoid(post)).astype(jnp.bfloat16))
-            kept = jnp.dot(
-                pick_ref[...], beside(*parts), preferred_element_type=jnp.float32
-            ).astype(jnp.bfloat16)
-            for tile in range(CHUNK // LANE):
-                block = side * (BLOCKS // 2) + place * (CHUNK // LANE) + tile
+            kept = take(pick_ref[...], beside(*parts) if len(parts) > 1 else parts[0])
+            kept = kept.astype(jnp.bfloat16)
+            for tile, block in enumerate(blocks):
                 part = kept[:, tile * LANE : (tile + 1) * LANE]
-                first[:, lanes(where[2, block])] = part
-                second[:, lanes(where[3, block])] = part
+                first[:, lanes(spot_e(block))] = part
+                second[:, lanes(spot_d(block))] = part
     width = HALF // 2
-    for side, active, near, far, low in (
-        (half, first, e8, er, 0),
-        (half, second, d8, dr, width),
-        (1 - half, first, f8, fr, 0),
-        (1 - half, second, g8, gr, width),
+    for turn_index, (side, active, edge) in enumerate(
+        ((half, first, 0), (half, second, width), (1 - half, first, 0), (1 - half, second, width))
     ):
-        at = pl.ds(pl.multiple_of(side * HALF + low, width), width)
+        at = pl.ds(pl.multiple_of(side * HALF + edge, width), width)
+        loads[2 * turn_index].wait()
+        loads[2 * turn_index + 1].wait()
         result = (
-            jnp.dot(active[:, 0:HALF], near[...], preferred_element_type=jnp.float32)
-            + jnp.dot(active[:, HALF:D], far[...], preferred_element_type=jnp.float32)
+            take(active[:, 0:HALF], weights[2 * turn_index])
+            + take(active[:, HALF:D], weights[2 * turn_index + 1])
             + base_ref[:, at].astype(jnp.float32)
         )
         out_ref[:, at] = result.astype(jnp.bfloat16)
 
 
-def finish(where, mine, others, small, pick, base, weights):
+def finish(mine, others, small, pick, base, weights):
     return pl.pallas_call(
         finish_kernel,
         out_shape=shape(RCV_DEV, D),
-        in_specs=smem(1) + vmem(19),
+        in_specs=vmem(11) + anywhere(8),
         out_specs=vmem(1)[0],
-        scratch_shapes=[pltpu.VMEM((RCV_DEV, D), jnp.bfloat16)] * 2,
+        scratch_shapes=[pltpu.VMEM((RCV_DEV, D), jnp.bfloat16)] * 2
+        + [pltpu.VMEM((8, HALF, HALF // 2), jnp.bfloat16), pltpu.SemaphoreType.DMA((8,))],
         compiler_params=limits(28),
-        cost_estimate=pl.CostEstimate(
-            flops=2 * RCV_DEV * D * D, bytes_accessed=16 * 2**20, transcendentals=PAD * D
-        ),
+        cost_estimate=COST,
         name="finish",
-    )(where, *mine, *others, small, pick, base, *weights)
+    )(*mine, *others, small, pick, base, *weights)
 
 
 def hyper_shards(
     frames, lengths, destination, offsets, norm_gain, weight_in, depth_kernel, post_gain, weight_out
 ):
-    core, x, y, z = (lax.axis_index(name) for name in ("core", "x", "y", "z"))
-    low = core == 0
+    low = lax.axis_index("core") == 0
     per = weight_in.shape[0]
-
-    block = jnp.arange(BLOCKS, dtype=jnp.int32)
-    zb2, zb1 = (block >> 3) ^ (z >> 1), ((block >> 2) & 1) ^ (z & 1)
-    yb, xb = ((block >> 1) & 1) ^ y, (block & 1) ^ x
-    info = jnp.where(block == 3, z * 2 + y, core)
-    where = jnp.stack(
-        [
-            xb * 8 + yb * 4 + zb1 * 2 + zb2,
-            yb * 8 + xb * 4 + zb2 * 2 + zb1,
-            zb2 * 8 + zb1 * 4 + yb * 2 + xb,
-            zb1 * 8 + zb2 * 4 + yb * 2 + xb,
-            info,
-            yb * 4 + zb1 * 2 + zb2,
-            xb,
-        ]
-    )
 
     left = beside(weight_in[:, 0:HALF], weight_in[:, D : D + HALF], weight_out[:, 0:HALF])
     right = beside(weight_in[:, HALF:D], weight_in[:, D + HALF :], weight_out[:, HALF:])
     kept, given = jnp.where(low, left, right), jnp.where(low, right, left)
     got = hop(given, "c")
+    rows = frames[0]
+    up0, up1, down0, down1 = cut(lengths, destination, offsets, rows)
     chip = jnp.where(low, stack(kept, got), stack(got, kept))
+    chip, up1, down1 = tie(chip, up1, down1)
 
     notes = jnp.concatenate(
         [depth_kernel.T, norm_gain[None], post_gain[None], jnp.zeros((SMALL - KERNEL - 2, per), jnp.bfloat16)], 0
     )
     blank = jnp.zeros_like(notes)
-    notes = jnp.where(low, beside(notes, blank), beside(blank, notes))
-    notes = notes + hop(notes, "c")
-    pair = [notes, hop(notes, "x")]
-    tiles = [one[low_row : low_row + META] for one in pair for low_row in range(0, SMALL, META)]
-    notes = beside(*tiles, jnp.zeros((META, 4 * CHUNK - 2 * LANE * SMALL // META), jnp.bfloat16))
-
-    def value_gate(start):
-        return [chip[:, start : start + CHUNK], chip[:, HALF + start : HALF + start + CHUNK]]
-
-    a = beside(*value_gate(0), *value_gate(CHUNK))
-    b = beside(*value_gate(2 * CHUNK), *value_gate(3 * CHUNK))
+    pair = [jnp.where(low, beside(one, blank), beside(blank, one)) for one in (notes, hop(notes, "x"))]
+    pair = stack(*pair)
+    pair = pair + hop(pair, "c")
+    tiles = [pair[low_row : low_row + META] for low_row in range(0, 2 * SMALL, META)]
+    notes = beside(*tiles, jnp.zeros((META, HALF - 2 * LANE * SMALL // META), jnp.bfloat16))
+
+    def stream(start):
+        edges = (start, start + FIRST, start + HALF // 2)
+        spans = [(low_edge + gate, high_edge + gate) for low_edge, high_edge in zip(edges, edges[1:]) for gate in (0, HALF)]
+        return beside(*[chip[:, low_edge:high_edge] for low_edge, high_edge in spans])
+
+    a, b = stream(0), stream(HALF // 2)
     o = chip[:, 2 * HALF : 3 * HALF]
 
     def grow(array, extra, name):
@@ -499,46 +530,42 @@
         arrived = hop(stack(array, extra), name)
         return stack(array, arrived[0:size]), stack(extra, arrived[size:])
 
-    rows = frames[0]
-    up0, up1, down0, down1 = cut(where, lengths, destination, offsets, rows)
     prev0, next0 = turn(up0, 1), turn(down0, -1)
     (a, notes), b_far, o_far = grow(a, notes, "z2"), hop(b, "z1"), hop(o, "x")
-    a, notes, b, o, prev0, next0, up1, down1 = tie(
-        a, notes, stack(b, b_far), stack(o, o_far), prev0, next0, up1, down1
+    prev0, next0, a, notes, b, o, up1, down1 = tie(
+        prev0, next0, a, notes, stack(b, b_far), stack(o, o_far), up1, down1
     )
     prev1, next1 = turn(up1, 1), turn(down1, -1)
     (a, notes), b_far, o_far = grow(a, notes, "z1"), hop(b, "z2"), hop(o, "y")
-    a, notes, b, o, prev1, next1 = tie(a, notes, stack(b, b_far), stack(o, o_far), prev1, next1)
+    prev1, next1, a, notes, b, o = tie(prev1, next1, a, notes, stack(b, b_far), stack(o, o_far))
     e, d = o[:, 0 : HALF // 2], o[:, HALF // 2 :]
-    spread, base, pick = place(
-        where, lengths, destination, offsets, rows, (prev0, prev1, next0, next1)
-    )
-    spread_other = hop(spread, "c")
+    spread, base, pick = place(lengths, destination, offsets, rows, (prev0, prev1, next0, next1))
     (a, notes), b_far, e_far, d_far = grow(a, notes, "y"), hop(b, "x"), hop(e, "z1"), hop(d, "z2")
-    a, notes, b, e, d, spread, spread_other, base, pick = tie(
-        a, notes, stack(b, b_far), stack(e, e_far), stack(d, d_far), spread, spread_other, base, pick
+    a, notes, b, e, d, spread, base, pick = tie(
+        a, notes, stack(b, b_far), stack(e, e_far), stack(d, d_far), spread, base, pick
     )
     e_far, d_far = hop(e, "z2"), hop(d, "z1")
-    cut_at = 2 * CHUNK
+    cut_at = 2 * FIRST
     a1, a2, b1, b2 = a[:, 0:cut_at], a[:, cut_at:], b[:, 0:cut_at], b[:, cut_at:]
     a1_far, b1_far = hop(a1, "x"), hop(b1, "y")
-    a1_far, b1_far, a2, b2 = tie(a1_far, b1_far, a2, b2)
+    for_a, for_b, small = prep(spread, hop(spread, "c"), notes)
+    a1_far, b1_far, a2, b2, small = tie(a1_far, b1_far, a2, b2, small)
     a2_far, b2_far = hop(a2, "x"), hop(b2, "y")
 
-    for_a, for_b, small = prep(where, spread, spread_other, notes)
-
     def run(sub, rows_in, near, far):
-        mine, given_part = conv(sub, where, rows_in, near, far, small)
+        mine, given_part = conv(sub, rows_in, near, far, small)
         return mine, hop(given_part, "c")
 
     m0, o0 = run(0, for_a, a1, a1_far)
-    m2, o2 = run(4, for_b, b1, b1_far)
-    e, d, e_far, d_far, a2_far, b2_far, m0, m2 = tie(e, d, e_far, d_far, a2_far, b2_far, m0, m2)
+    m2, o2 = run(BLOCKS // 4, for_b, b1, b1_far)
+    e, d, e_far, d_far, a2_far, b2_far, m0, o0, m2, o2 = tie(
+        e, d, e_far, d_far, a2_far, b2_far, m0, o0, m2, o2
+    )
     weights = [e, e_far, d, d_far]
     weights = weights + [hop(array, "c") for array in weights]
-    m1, o1 = run(2, for_a, a2, a2_far)
-    m3, o3 = run(6, for_b, b2, b2_far)
-    mixed = finish(where, (m0, m1, m2, m3), (o0, o1, o2, o3), small, pick, base, weights)
+    m1, o1 = run(FIRST // LANE, for_a, a2, a2_far)
+    m3, o3 = run(BLOCKS // 4 + FIRST // LANE, for_b, b2, b2_far)
+    mixed = finish((m0, m1, m2, m3), (o0, o1, o2, o3), small, pick, base, weights)
     return mixed[None]
 
 

time: 185 us -> 173 us (0.935)
  waiting for transfers between devices: 104 us -> 89.9 us
  starting transfers between devices: 33.7 us -> 38.7 us
  Pallas kernels: 42.2 us -> 39.3 us
    ppermute x28, waiting for transfers between devices: 89.6 us -> 77.8 us  [hop(): return lax.ppermute(array, axis, pairs)]
    ppermute x28, starting transfers between devices: 24.2 us -> 29.3 us  [hop(): return lax.ppermute(array, axis, pairs)]
    pallas_call x4, Pallas kernels: 21.6 us -> 18.7 us  [conv(): pl.pallas_call(functools.partial(conv_kernel, sub), out_shape=(out, out),...]
    ppermute x4, waiting for transfers between devices: 14.8 us -> 12.1 us  [turn(): lax.ppermute(array, ('z', 'y'), [(i, (i + by) % 8) for i in range(8)])]
  transfers between devices with their start and end apart: 32 -> 32, of which waited for: 16 -> 16; matrix products, arithmetic and copies ran while one was open for 1% -> 2% of each run, Pallas kernels for 16% -> 17%
where the time goes in v3:
time: 173 us
  waiting for transfers between devices  89.9 us (52%)
  Pallas kernels  39.3 us (23%)
  starting transfers between devices  38.7 us (22%)
  other arithmetic  2.46 us (1%)
  local copies, waits for them, and re-layouts  2.13 us (1%)
    ppermute x28, waiting for transfers between devices, hop(): return lax.ppermute(array, axis, pairs)  77.8 us
    ppermute x28, starting transfers between devices, hop(): return lax.ppermute(array, axis, pairs)  29.3 us
    pallas_call x4, Pallas kernels, conv(): pl.pallas_call(functools.partial(conv_kernel, sub), out_shape=(out, out),...  18.7 us
    ppermute x4, waiting for transfers between devices, turn(): lax.ppermute(array, ('z', 'y'), [(i, (i + by) % 8) for i in range(8)])  12.1 us
    ppermute x4, starting transfers between devices, turn(): lax.ppermute(array, ('z', 'y'), [(i, (i + by) % 8) for i in range(8)])  9.45 us
    pallas_call x1, Pallas kernels, finish(): pl.pallas_call(finish_kernel, out_shape=shape(RCV_DEV, D), in_specs=vmem(...  9.17 us
    pallas_call x1, Pallas kernels, prep(): pl.pallas_call(prep_kernel, out_shape=(shape(PAIR, D), shape(PAIR, D), sh...  5.39 us
    pallas_call x1, Pallas kernels, place(): pl.pallas_call(place_kernel, out_shape=(shape(PAD, D), shape(RCV_DEV, D),...  4.06 us
  transfers between devices with their start and end apart: 32, of which 16 were waited for; matrix products, arithmetic and copies ran while one was open for 2% of the time, Pallas kernels for 17%

profile of v3, /device:TPU:0, one launch (start us, length us, event | category | flops | bytes accessed | tf_op | source)
XLA Modules:
  0.0 173.1 jit_solution(7169371850286361757)
XLA Ops:
  1.0 3.0 %collective-permute-start.3 = (bf16[48,64]{1,0:T(8,128)(2,1)S(1)}, bf16[48,64]{1,0:T(8,128)(2,1)S(1)}, u32[]{:S(2)}, u32[]{:S(2)}) collective-permute-start(bf16[48,64]{1,0:T(8,128)(2,1)S(1)} %maximum_maximum_fusion), channel_id=1, source_target_pairs={{0,2},{2,0},{1,3},{3,1},{4,6},{6,4},{5,7},{7,5},{8,10},{10,8},{9,1... | collective-permute-start | bytes 18440 | tf_op jit(solution)/shard_map/ppermute | solution.py:145
  6.5 2.0 %cut.1 = (bf16[208,1024]{1,0:T(8,128)(2,1)S(1)}, bf16[192,1024]{1,0:T(8,128)(2,1)S(1)}, bf16[208,1024]{1,0:T(8,128)(2,1)S(1)}, bf16[192,1024]{1,0:T(8,128)(2,1)S(1)}) custom-call(s32[1,3]{1,0:T(1,128)S(1)} %copy-done.1, s32[1,3]{1,0:T(1,128)S(1)} %copy-done.2, s32[1,3]{1,0:T(1,128)S(1)} %copy-done.3, bf16[576,2048]{1,0:T(8,128)(2,1)S(1)} %bitcast.5), custom_call_target="tpu_custom_call" | custom-call | flops 1048576 | bytes 65536 | tf_op jit(solution)/shard_map/cut/pallas_call | solution.py:256
  8.9 2.2 %collective-permute-start.6 = (bf16[128,1024]{1,0:T(8,128)(2,1)S(1)}, bf16[128,1024]{1,0:T(8,128)(2,1)S(1)}, u32[]{:S(2)}, u32[]{:S(2)}) collective-permute-start(bf16[128,1024]{1,0:T(8,128)(2,1)S(1)} %pad_maximum_fusion.15), channel_id=1, source_target_pairs={{0,8},{8,0},{16,24},{24,16},{1,9},{9,1},{17,25},{25,17},{2,10},{10... | collective-permute-start | bytes 786440 | tf_op jit(solution)/shard_map/ppermute | solution.py:145
  11.1 1.6 collective-permute-start.7
  12.7 2.6 %collective-permute-start.5 = (bf16[144,1024]{1,0:T(8,128)(2,1)S(1)}, bf16[144,1024]{1,0:T(8,128)(2,1)S(1)}, u32[]{:S(2)}, u32[]{:S(2)}) collective-permute-start(bf16[144,1024]{1,0:T(8,128)(2,1)S(1)} %pad_maximum_fusion.14), channel_id=1, source_target_pairs={{0,16},{8,24},{16,0},{24,8},{1,17},{9,25},{17,1},{25,9},{2,18},{10... | collective-permute-start | bytes 884744 | tf_op jit(solution)/shard_map/ppermute | solution.py:145
  15.3 1.5 collective-permute-start
  16.9 3.2 %collective-permute-start.1 = (bf16[208,1024]{1,0:T(8,128)(2,1)S(1)}, bf16[208,1024]{1,0:T(8,128)(2,1)S(1)}, u32[]{:S(2)}, u32[]{:S(2)}) collective-permute-start(bf16[208,1024]{1,0:T(8,128)(2,1)S(1)} %get-tuple-element.64), channel_id=1, source_target_pairs={{0,28},{4,0},{8,4},{12,8},{16,12},{20,16},{24,20},{28,24},{1,29},{... | collective-permute-start | bytes 1277960 | tf_op jit(solution)/shard_map/ppermute | solution.py:149
  20.1 2.2 %collective-permute-done.6 = bf16[128,1024]{1,0:T(8,128)(2,1)S(1)} collective-permute-done((bf16[128,1024]{1,0:T(8,128)(2,1)S(1)}, bf16[128,1024]{1,0:T(8,128)(2,1)S(1)}, u32[]{:S(2)}, u32[]{:S(2)}) %collective-permute-start.6) | collective-permute-done | bytes 262176 | tf_op jit(solution)/shard_map/ppermute | solution.py:145
  22.4 7.5 %collective-permute-done.5 = bf16[144,1024]{1,0:T(8,128)(2,1)S(1)} collective-permute-done((bf16[144,1024]{1,0:T(8,128)(2,1)S(1)}, bf16[144,1024]{1,0:T(8,128)(2,1)S(1)}, u32[]{:S(2)}, u32[]{:S(2)}) %collective-permute-start.5) | collective-permute-done | bytes 294944 | tf_op jit(solution)/shard_map/ppermute | solution.py:145
  30.0 6.4 %collective-permute-done.p0 = bf16[208,1024]{1,0:T(8,128)(2,1)S(1)} collective-permute-done((bf16[208,1024]{1,0:T(8,128)(2,1)S(1)}, bf16[208,1024]{1,0:T(8,128)(2,1)S(1)}, u32[]{:S(2)}, u32[]{:S(2)}) %collective-permute-start) | collective-permute-done | bytes 426016 | tf_op jit(solution)/shard_map/ppermute | solution.py:149
  36.6 2.7 %collective-permute-start.12 = (bf16[256,1024]{1,0:T(8,128)(2,1)S(1)}, bf16[256,1024]{1,0:T(8,128)(2,1)S(1)}, u32[]{:S(2)}, u32[]{:S(2)}) collective-permute-start(bf16[256,1024]{1,0:T(8,128)(2,1)S(1)} %pad_maximum_fusion.11), channel_id=1, source_target_pairs={{0,4},{4,0},{1,5},{5,1},{2,6},{6,2},{3,7},{7,3},{8,12},{12,8},{9,1... | collective-permute-start | bytes 1572872 | tf_op jit(solution)/shard_map/ppermute | solution.py:145
  41.0 1.9 %collective-permute-start.8 = (bf16[192,1024]{1,0:T(8,128)(2,1)S(1)}, bf16[192,1024]{1,0:T(8,128)(2,1)S(1)}, u32[]{:S(2)}, u32[]{:S(2)}) collective-permute-start(bf16[192,1024]{1,0:T(8,128)(2,1)S(1)} %get-tuple-element.70), channel_id=1, source_target_pairs={{0,4},{4,8},{8,12},{12,16},{16,20},{20,24},{24,28},{28,0},{1,5},{5... | collective-permute-start | bytes 1179656 | tf_op jit(solution)/shard_map/ppermute | solution.py:149
  42.9 2.8 %collective-permute-start.9 = (bf16[192,1024]{1,0:T(8,128)(2,1)S(1)}, bf16[192,1024]{1,0:T(8,128)(2,1)S(1)}, u32[]{:S(2)}, u32[]{:S(2)}) collective-permute-start(bf16[192,1024]{1,0:T(8,128)(2,1)S(1)} %get-tuple-element.71), channel_id=1, source_target_pairs={{0,28},{4,0},{8,4},{12,8},{16,12},{20,16},{24,20},{28,24},{1,29},{... | collective-permute-start | bytes 1179656 | tf_op jit(solution)/shard_map/ppermute | solution.py:149
  45.7 6.5 %collective-permute-done.12 = bf16[256,1024]{1,0:T(8,128)(2,1)S(1)} collective-permute-done((bf16[256,1024]{1,0:T(8,128)(2,1)S(1)}, bf16[256,1024]{1,0:T(8,128)(2,1)S(1)}, u32[]{:S(2)}, u32[]{:S(2)}) %collective-permute-start.12) | collective-permute-done | bytes 524320 | tf_op jit(solution)/shard_map/ppermute | solution.py:145
  52.2 11.2 %collective-permute-done.11 = bf16[256,1024]{1,0:T(8,128)(2,1)S(1)} collective-permute-done((bf16[256,1024]{1,0:T(8,128)(2,1)S(1)}, bf16[256,1024]{1,0:T(8,128)(2,1)S(1)}, u32[]{:S(2)}, u32[]{:S(2)}) %collective-permute-start.11) | collective-permute-done | bytes 524320 | tf_op jit(solution)/shard_map/ppermute | solution.py:145
  63.5 4.1 %collective-permute-done.10 = bf16[288,1024]{1,0:T(8,128)(2,1)S(1)} collective-permute-done((bf16[288,1024]{1,0:T(8,128)(2,1)S(1)}, bf16[288,1024]{1,0:T(8,128)(2,1)S(1)}, u32[]{:S(2)}, u32[]{:S(2)}) %collective-permute-start.10) | collective-permute-done | bytes 589856 | tf_op jit(solution)/shard_map/ppermute | solution.py:145
  67.8 5.5 %collective-permute-done.8.p1 = bf16[192,1024]{1,0:T(8,128)(2,1)S(1)} collective-permute-done((bf16[192,1024]{1,0:T(8,128)(2,1)S(1)}, bf16[192,1024]{1,0:T(8,128)(2,1)S(1)}, u32[]{:S(2)}, u32[]{:S(2)}) %collective-permute-start.8) | collective-permute-done | bytes 393248 | tf_op jit(solution)/shard_map/ppermute | solution.py:149
  73.9 2.1 %collective-permute-start.13 = (bf16[576,1024]{1,0:T(8,128)(2,1)S(1)}, bf16[576,1024]{1,0:T(8,128)(2,1)S(1)}, u32[]{:S(2)}, u32[]{:S(2)}) collective-permute-start(bf16[576,1024]{1,0:T(8,128)(2,1)S(1)} %pad_maximum_fusion.2), channel_id=1, source_target_pairs={{0,4},{4,0},{1,5},{5,1},{2,6},{6,2},{3,7},{7,3},{8,12},{12,8},{9,1... | collective-permute-start | bytes 3538952 | tf_op jit(solution)/shard_map/ppermute | solution.py:145
  76.1 2.2 %collective-permute-start.15 = (bf16[512,512]{1,0:T(8,128)(2,1)S(1)}, bf16[512,512]{1,0:T(8,128)(2,1)S(1)}, u32[]{:S(2)}, u32[]{:S(2)}) collective-permute-start(bf16[512,512]{1,0:T(8,128)(2,1)S(1)} %get-tuple-element.122), channel_id=1, source_target_pairs={{0,8},{8,0},{16,24},{24,16},{1,9},{9,1},{17,25},{25,17},{2,10},{10... | collective-permute-start | bytes 1572872 | tf_op jit(solution)/shard_map/ppermute | solution.py:145
  78.3 4.1 %place.1 = (bf16[448,2048]{1,0:T(8,128)(2,1)S(1)}, bf16[384,2048]{1,0:T(8,128)(2,1)S(1)}, bf16[384,448]{1,0:T(8,128)(2,1)S(1)}) custom-call(s32[1,3]{1,0:T(1,128)S(1)} %copy-done.1, s32[1,3]{1,0:T(1,128)S(1)} %copy-done.2, s32[1,3]{1,0:T(1,128)S(1)} %copy-done.3, bf16[576,2048]{1,0:T(8,128)(2,1)S(1)} %bitcast.6, ...), custom_call_target="tpu_custom_call" | custom-call | flops 1048576 | bytes 65536 | tf_op jit(solution)/shard_map/place/pallas_call | solution.py:304
  82.4 16.0 %collective-permute-done.16 = bf16[512,512]{1,0:T(8,128)(2,1)S(1)} collective-permute-done((bf16[512,512]{1,0:T(8,128)(2,1)S(1)}, bf16[512,512]{1,0:T(8,128)(2,1)S(1)}, u32[]{:S(2)}, u32[]{:S(2)}) %collective-permute-start.16) | collective-permute-done | bytes 524320 | tf_op jit(solution)/shard_map/ppermute | solution.py:145
  99.7 1.5 collective-permute-start.19
  101.4 1.5 collective-permute-start.20
  103.5 2.2 %collective-permute-start.18 = (bf16[1024,512]{1,0:T(8,128)(2,1)S(1)}, bf16[1024,512]{1,0:T(8,128)(2,1)S(1)}, u32[]{:S(2)}, u32[]{:S(2)}) collective-permute-start(bf16[1024,512]{1,0:T(8,128)(2,1)S(1)} %pad_maximum_fusion.7.d8), channel_id=1, source_target_pairs={{0,8},{8,0},{16,24},{24,16},{1,9},{9,1},{17,25},{25,17},{2,10},{10... | collective-permute-start | bytes 3145736 | tf_op jit(solution)/shard_map/ppermute | solution.py:145
  105.9 5.4 %prep.1 = (bf16[896,2048]{1,0:T(8,128)(2,1)S(1)}, bf16[896,2048]{1,0:T(8,128)(2,1)S(1)}, f32[48,2048]{1,0:T(8,128)S(1)}) custom-call(bf16[448,2048]{1,0:T(8,128)(2,1)S(1)} %get-tuple-element.91.mine_ref, bf16[448,2048]{1,0:T(8,128)(2,1)S(1)} %collective-permute-done.21.other_ref, bf16[128,1024]{1,0:T(8,128)(2,1)S(1)} %pad_maximum_fusion.16.notes_ref), custom_call_target="tpu_custom_call" | custom-call | flops 1048576 | bytes 65536 | tf_op jit(solution)/shard_map/prep/pallas_call | solution.py:343
  111.3 25.3 %collective-permute-done.19.far_hbm = bf16[1024,768]{1,0:T(8,128)(2,1)S(1)} collective-permute-done((bf16[1024,768]{1,0:T(8,128)(2,1)S(1)}, bf16[1024,768]{1,0:T(8,128)(2,1)S(1)}, u32[]{:S(2)}, u32[]{:S(2)}) %collective-permute-start.19) | collective-permute-done | bytes 1572896 | tf_op jit(solution)/shard_map/ppermute | solution.py:145
  136.6 1.4 collective-permute-done.20.far_hbm
  139.7 6.7 %conv.5 = (bf16[448,384]{1,0:T(8,128)(2,1)S(1)}, bf16[448,384]{1,0:T(8,128)(2,1)S(1)}) custom-call(bf16[896,2048]{1,0:T(8,128)(2,1)S(1)} %get-tuple-element.101.rows_hbm, bf16[1024,768]{1,0:T(8,128)(2,1)S(1)} %slice.129.near_hbm, bf16[1024,768]{1,0:T(8,128)(2,1)S(1)} %collective-permute-done.20.far_hbm, f32[48,2048]{1,0:T(8,128)S(1)} %get-tuple-element.98.small_ref), custom_call_target="tpu_custom_call" | custom-call | flops 1048576 | bytes 65536 | tf_op jit(solution)/shard_map/conv/pallas_call | solution.py:406
  146.5 6.7 %conv.4 = (bf16[448,384]{1,0:T(8,128)(2,1)S(1)}, bf16[448,384]{1,0:T(8,128)(2,1)S(1)}) custom-call(bf16[896,2048]{1,0:T(8,128)(2,1)S(1)} %get-tuple-element.96.rows_hbm, bf16[1024,768]{1,0:T(8,128)(2,1)S(1)} %slice.128.near_hbm, bf16[1024,768]{1,0:T(8,128)(2,1)S(1)} %collective-permute-done.19.far_hbm, f32[48,2048]{1,0:T(8,128)S(1)} %get-tuple-element.98.small_ref), custom_call_target="tpu_custom_call" | custom-call | flops 1048576 | bytes 65536 | tf_op jit(solution)/shard_map/conv/pallas_call | solution.py:406
  156.0 2.7 %conv.7 = (bf16[448,128]{1,0:T(8,128)(2,1)S(1)}, bf16[448,128]{1,0:T(8,128)(2,1)S(1)}) custom-call(bf16[896,2048]{1,0:T(8,128)(2,1)S(1)} %get-tuple-element.101.rows_hbm, bf16[1024,256]{1,0:T(8,128)(2,1)S(1)} %slice.131.near_hbm, bf16[1024,256]{1,0:T(8,128)(2,1)S(1)} %collective-permute-done.23.far_hbm, f32[48,2048]{1,0:T(8,128)S(1)} %get-tuple-element.98.small_ref), custom_call_target="tpu_custom_call" | custom-call | flops 1048576 | bytes 65536 | tf_op jit(solution)/shard_map/conv/pallas_call | solution.py:406
  159.2 2.7 %conv.6 = (bf16[448,128]{1,0:T(8,128)(2,1)S(1)}, bf16[448,128]{1,0:T(8,128)(2,1)S(1)}) custom-call(bf16[896,2048]{1,0:T(8,128)(2,1)S(1)} %get-tuple-element.96.rows_hbm, bf16[1024,256]{1,0:T(8,128)(2,1)S(1)} %slice.130.near_hbm, bf16[1024,256]{1,0:T(8,128)(2,1)S(1)} %collective-permute-done.22.far_hbm, f32[48,2048]{1,0:T(8,128)S(1)} %get-tuple-element.98.small_ref), custom_call_target="tpu_custom_call" | custom-call | flops 1048576 | bytes 65536 | tf_op jit(solution)/shard_map/conv/pallas_call | solution.py:406
  163.7 9.2 %finish.1 = bf16[384,2048]{1,0:T(8,128)(2,1)} custom-call(bf16[448,384]{1,0:T(8,128)(2,1)S(1)} %get-tuple-element.105.m0, bf16[448,128]{1,0:T(8,128)(2,1)S(1)} %get-tuple-element.107.m1, bf16[448,384]{1,0:T(8,128)(2,1)S(1)} %get-tuple-element.108.m2, bf16[448,128]{1,0:T(8,128)(2,1)S(1)} %get-tuple-element.110.m3, ...), custom_call_target="tpu_custom_call" | custom-call | flops 1048576 | bytes 65536 | tf_op jit(solution)/shard_map/finish/pallas_call | solution.py:482
  (96 shorter events, 16.1 us)
Async XLA Ops:
  1.0 4.6 %collective-permute-start.3 = (bf16[48,64]{1,0:T(8,128)(2,1)S(1)}, bf16[48,64]{1,0:T(8,128)(2,1)S(1)}, u32[]{:S(2)}, u32[]{:S(2)}) collective-permute-start(bf16[48,64]{1,0:T(8,128)(2,1)S(1)} %maximum_maximum_fusion), channel_id=1, source_target_pairs={{0,2},{2,0},{1,3},{3,1},{4,6},{6,4},{5,7},{7,5},{8,10},{10,8},{9,1... | collective-permute-start | bytes 18440 | tf_op jit(solution)/shard_map/ppermute | solution.py:145
  5.8 2.8 %collective-permute-start.4 = (bf16[96,128]{1,0:T(8,128)(2,1)S(1)}, bf16[96,128]{1,0:T(8,128)(2,1)S(1)}, u32[]{:S(2)}, u32[]{:S(2)}) collective-permute-start(bf16[96,128]{1,0:T(8,128)(2,1)S(1)} %pad_maximum_fusion.19), channel_id=1, source_target_pairs={{0,1},{1,0},{2,3},{3,2},{4,5},{5,4},{6,7},{7,6},{8,9},{9,8},{10,11... | collective-permute-start | bytes 73736 | tf_op jit(solution)/shard_map/ppermute | solution.py:145
  5.9 2.7 %collective-permute-start.2 = (bf16[64,3072]{1,0:T(8,128)(2,1)S(1)}, bf16[64,3072]{1,0:T(8,128)(2,1)S(1)}, u32[]{:S(2)}, u32[]{:S(2)}) collective-permute-start(bf16[64,3072]{1,0:T(8,128)(2,1)S(1)} %get-tuple-element.132), channel_id=1, source_target_pairs={{0,1},{1,0},{2,3},{3,2},{4,5},{5,4},{6,7},{7,6},{8,9},{9,8},{10,11... | collective-permute-start | bytes 1179656 | tf_op jit(solution)/shard_map/ppermute | solution.py:145
  8.9 13.4 %collective-permute-start.6 = (bf16[128,1024]{1,0:T(8,128)(2,1)S(1)}, bf16[128,1024]{1,0:T(8,128)(2,1)S(1)}, u32[]{:S(2)}, u32[]{:S(2)}) collective-permute-start(bf16[128,1024]{1,0:T(8,128)(2,1)S(1)} %pad_maximum_fusion.15), channel_id=1, source_target_pairs={{0,8},{8,0},{16,24},{24,16},{1,9},{9,1},{17,25},{25,17},{2,10},{10... | collective-permute-start | bytes 786440 | tf_op jit(solution)/shard_map/ppermute | solution.py:145
  11.1 11.3 %collective-permute-start.7 = (bf16[128,1024]{1,0:T(8,128)(2,1)S(1)}, bf16[128,1024]{1,0:T(8,128)(2,1)S(1)}, u32[]{:S(2)}, u32[]{:S(2)}) collective-permute-start(bf16[128,1024]{1,0:T(8,128)(2,1)S(1)} %slice.121), channel_id=1, source_target_pairs={{0,2},{2,0},{1,3},{3,1},{4,6},{6,4},{5,7},{7,5},{8,10},{10,8},{9,1... | collective-permute-start | bytes 786440 | tf_op jit(solution)/shard_map/ppermute | solution.py:145
  12.7 17.2 %collective-permute-start.5 = (bf16[144,1024]{1,0:T(8,128)(2,1)S(1)}, bf16[144,1024]{1,0:T(8,128)(2,1)S(1)}, u32[]{:S(2)}, u32[]{:S(2)}) collective-permute-start(bf16[144,1024]{1,0:T(8,128)(2,1)S(1)} %pad_maximum_fusion.14), channel_id=1, source_target_pairs={{0,16},{8,24},{16,0},{24,8},{1,17},{9,25},{17,1},{25,9},{2,18},{10... | collective-permute-start | bytes 884744 | tf_op jit(solution)/shard_map/ppermute | solution.py:145
  15.3 21.1 %collective-permute-start = (bf16[208,1024]{1,0:T(8,128)(2,1)S(1)}, bf16[208,1024]{1,0:T(8,128)(2,1)S(1)}, u32[]{:S(2)}, u32[]{:S(2)}) collective-permute-start(bf16[208,1024]{1,0:T(8,128)(2,1)S(1)} %get-tuple-element.63), channel_id=1, source_target_pairs={{0,4},{4,8},{8,12},{12,16},{16,20},{20,24},{24,28},{28,0},{1,5},{5... | collective-permute-start | bytes 1277960 | tf_op jit(solution)/shard_map/ppermute | solution.py:149
  16.9 19.8 %collective-permute-start.1 = (bf16[208,1024]{1,0:T(8,128)(2,1)S(1)}, bf16[208,1024]{1,0:T(8,128)(2,1)S(1)}, u32[]{:S(2)}, u32[]{:S(2)}) collective-permute-start(bf16[208,1024]{1,0:T(8,128)(2,1)S(1)} %get-tuple-element.64), channel_id=1, source_target_pairs={{0,28},{4,0},{8,4},{12,8},{16,12},{20,16},{24,20},{28,24},{1,29},{... | collective-permute-start | bytes 1277960 | tf_op jit(solution)/shard_map/ppermute | solution.py:149
  36.6 15.5 %collective-permute-start.12 = (bf16[256,1024]{1,0:T(8,128)(2,1)S(1)}, bf16[256,1024]{1,0:T(8,128)(2,1)S(1)}, u32[]{:S(2)}, u32[]{:S(2)}) collective-permute-start(bf16[256,1024]{1,0:T(8,128)(2,1)S(1)} %pad_maximum_fusion.11), channel_id=1, source_target_pairs={{0,4},{4,0},{1,5},{5,1},{2,6},{6,2},{3,7},{7,3},{8,12},{12,8},{9,1... | collective-permute-start | bytes 1572872 | tf_op jit(solution)/shard_map/ppermute | solution.py:145
  39.3 24.1 %collective-permute-start.11 = (bf16[256,1024]{1,0:T(8,128)(2,1)S(1)}, bf16[256,1024]{1,0:T(8,128)(2,1)S(1)}, u32[]{:S(2)}, u32[]{:S(2)}) collective-permute-start(bf16[256,1024]{1,0:T(8,128)(2,1)S(1)} %pad_maximum_fusion.10), channel_id=1, source_target_pairs={{0,16},{8,24},{16,0},{24,8},{1,17},{9,25},{17,1},{25,9},{2,18},{10... | collective-permute-start | bytes 1572872 | tf_op jit(solution)/shard_map/ppermute | solution.py:145
  40.2 27.5 %collective-permute-start.10 = (bf16[288,1024]{1,0:T(8,128)(2,1)S(1)}, bf16[288,1024]{1,0:T(8,128)(2,1)S(1)}, u32[]{:S(2)}, u32[]{:S(2)}) collective-permute-start(bf16[288,1024]{1,0:T(8,128)(2,1)S(1)} %pad_maximum_fusion.8), channel_id=1, source_target_pairs={{0,8},{8,0},{16,24},{24,16},{1,9},{9,1},{17,25},{25,17},{2,10},{10... | collective-permute-start | bytes 1769480 | tf_op jit(solution)/shard_map/ppermute | solution.py:145
  41.0 32.3 %collective-permute-start.8 = (bf16[192,1024]{1,0:T(8,128)(2,1)S(1)}, bf16[192,1024]{1,0:T(8,128)(2,1)S(1)}, u32[]{:S(2)}, u32[]{:S(2)}) collective-permute-start(bf16[192,1024]{1,0:T(8,128)(2,1)S(1)} %get-tuple-element.70), channel_id=1, source_target_pairs={{0,4},{4,8},{8,12},{12,16},{16,20},{20,24},{24,28},{28,0},{1,5},{5... | collective-permute-start | bytes 1179656 | tf_op jit(solution)/shard_map/ppermute | solution.py:149
  42.9 30.3 %collective-permute-start.9 = (bf16[192,1024]{1,0:T(8,128)(2,1)S(1)}, bf16[192,1024]{1,0:T(8,128)(2,1)S(1)}, u32[]{:S(2)}, u32[]{:S(2)}) collective-permute-start(bf16[192,1024]{1,0:T(8,128)(2,1)S(1)} %get-tuple-element.71), channel_id=1, source_target_pairs={{0,28},{4,0},{8,4},{12,8},{16,12},{20,16},{24,20},{28,24},{1,29},{... | collective-permute-start | bytes 1179656 | tf_op jit(solution)/shard_map/ppermute | solution.py:149
  73.2 25.3 %collective-permute-start.14 = (bf16[512,1024]{1,0:T(8,128)(2,1)S(1)}, bf16[512,1024]{1,0:T(8,128)(2,1)S(1)}, u32[]{:S(2)}, u32[]{:S(2)}) collective-permute-start(bf16[512,1024]{1,0:T(8,128)(2,1)S(1)} %pad_maximum_fusion.4), channel_id=1, source_target_pairs={{0,2},{2,0},{1,3},{3,1},{4,6},{6,4},{5,7},{7,5},{8,10},{10,8},{9,1... | collective-permute-start | bytes 3145736 | tf_op jit(solution)/shard_map/ppermute | solution.py:145
  73.9 25.3 %collective-permute-start.13 = (bf16[576,1024]{1,0:T(8,128)(2,1)S(1)}, bf16[576,1024]{1,0:T(8,128)(2,1)S(1)}, u32[]{:S(2)}, u32[]{:S(2)}) collective-permute-start(bf16[576,1024]{1,0:T(8,128)(2,1)S(1)} %pad_maximum_fusion.2), channel_id=1, source_target_pairs={{0,4},{4,0},{1,5},{5,1},{2,6},{6,2},{3,7},{7,3},{8,12},{12,8},{9,1... | collective-permute-start | bytes 3538952 | tf_op jit(solution)/shard_map/ppermute | solution.py:145
  76.1 22.3 %collective-permute-start.16 = (bf16[512,512]{1,0:T(8,128)(2,1)S(1)}, bf16[512,512]{1,0:T(8,128)(2,1)S(1)}, u32[]{:S(2)}, u32[]{:S(2)}) collective-permute-start(bf16[512,512]{1,0:T(8,128)(2,1)S(1)} %get-tuple-element.121), channel_id=1, source_target_pairs={{0,16},{8,24},{16,0},{24,8},{1,17},{9,25},{17,1},{25,9},{2,18},{10... | collective-permute-start | bytes 1572872 | tf_op jit(solution)/shard_map/ppermute | solution.py:145
  76.1 22.3 %collective-permute-start.15 = (bf16[512,512]{1,0:T(8,128)(2,1)S(1)}, bf16[512,512]{1,0:T(8,128)(2,1)S(1)}, u32[]{:S(2)}, u32[]{:S(2)}) collective-permute-start(bf16[512,512]{1,0:T(8,128)(2,1)S(1)} %get-tuple-element.122), channel_id=1, source_target_pairs={{0,8},{8,0},{16,24},{24,16},{1,9},{9,1},{17,25},{25,17},{2,10},{10... | collective-permute-start | bytes 1572872 | tf_op jit(solution)/shard_map/ppermute | solution.py:145
  99.5 6.4 %collective-permute-start.21 = (bf16[448,2048]{1,0:T(8,128)(2,1)S(1)}, bf16[448,2048]{1,0:T(8,128)(2,1)S(1)}, u32[]{:S(2)}, u32[]{:S(2)}) collective-permute-start(bf16[448,2048]{1,0:T(8,128)(2,1)S(1)} %get-tuple-element.91.mine_ref), channel_id=1, source_target_pairs={{0,1},{1,0},{2,3},{3,2},{4,5},{5,4},{6,7},{7,6},{8,9},{9,8},{10,11... | collective-permute-start | bytes 5505032 | tf_op jit(solution)/shard_map/ppermute | solution.py:145
  99.7 36.9 %collective-permute-start.19 = (bf16[1024,768]{1,0:T(8,128)(2,1)S(1)}, bf16[1024,768]{1,0:T(8,128)(2,1)S(1)}, u32[]{:S(2)}, u32[]{:S(2)}) collective-permute-start(bf16[1024,768]{1,0:T(8,128)(2,1)S(1)} %slice.128.near_hbm), channel_id=1, source_target_pairs={{0,2},{2,0},{1,3},{3,1},{4,6},{6,4},{5,7},{7,5},{8,10},{10,8},{9,1... | collective-permute-start | bytes 4718600 | tf_op jit(solution)/shard_map/ppermute | solution.py:145
  101.4 36.6 %collective-permute-start.20 = (bf16[1024,768]{1,0:T(8,128)(2,1)S(1)}, bf16[1024,768]{1,0:T(8,128)(2,1)S(1)}, u32[]{:S(2)}, u32[]{:S(2)}) collective-permute-start(bf16[1024,768]{1,0:T(8,128)(2,1)S(1)} %slice.129.near_hbm), channel_id=1, source_target_pairs={{0,4},{4,0},{1,5},{5,1},{2,6},{6,2},{3,7},{7,3},{8,12},{12,8},{9,1... | collective-permute-start | bytes 4718600 | tf_op jit(solution)/shard_map/ppermute | solution.py:145
  102.9 50.3 %collective-permute-start.17 = (bf16[1024,512]{1,0:T(8,128)(2,1)S(1)}, bf16[1024,512]{1,0:T(8,128)(2,1)S(1)}, u32[]{:S(2)}, u32[]{:S(2)}) collective-permute-start(bf16[1024,512]{1,0:T(8,128)(2,1)S(1)} %pad_maximum_fusion.6.e8), channel_id=1, source_target_pairs={{0,16},{8,24},{16,0},{24,8},{1,17},{9,25},{17,1},{25,9},{2,18},{10... | collective-permute-start | bytes 3145736 | tf_op jit(solution)/shard_map/ppermute | solution.py:145
  103.5 50.2 %collective-permute-start.18 = (bf16[1024,512]{1,0:T(8,128)(2,1)S(1)}, bf16[1024,512]{1,0:T(8,128)(2,1)S(1)}, u32[]{:S(2)}, u32[]{:S(2)}) collective-permute-start(bf16[1024,512]{1,0:T(8,128)(2,1)S(1)} %pad_maximum_fusion.7.d8), channel_id=1, source_target_pairs={{0,8},{8,0},{16,24},{24,16},{1,9},{9,1},{17,25},{25,17},{2,10},{10... | collective-permute-start | bytes 3145736 | tf_op jit(solution)/shard_map/ppermute | solution.py:145
  138.0 17.0 %collective-permute-start.22 = (bf16[1024,256]{1,0:T(8,128)(2,1)S(1)}, bf16[1024,256]{1,0:T(8,128)(2,1)S(1)}, u32[]{:S(2)}, u32[]{:S(2)}) collective-permute-start(bf16[1024,256]{1,0:T(8,128)(2,1)S(1)} %slice.130.near_hbm), channel_id=1, source_target_pairs={{0,2},{2,0},{1,3},{3,1},{4,6},{6,4},{5,7},{7,5},{8,10},{10,8},{9,1... | collective-permute-start | bytes 1572872 | tf_op jit(solution)/shard_map/ppermute | solution.py:145
  138.5 16.5 %collective-permute-start.23 = (bf16[1024,256]{1,0:T(8,128)(2,1)S(1)}, bf16[1024,256]{1,0:T(8,128)(2,1)S(1)}, u32[]{:S(2)}, u32[]{:S(2)}) collective-permute-start(bf16[1024,256]{1,0:T(8,128)(2,1)S(1)} %slice.131.near_hbm), channel_id=1, source_target_pairs={{0,4},{4,0},{1,5},{5,1},{2,6},{6,2},{3,7},{7,3},{8,12},{12,8},{9,1... | collective-permute-start | bytes 1572872 | tf_op jit(solution)/shard_map/ppermute | solution.py:145
  146.4 7.3 %collective-permute-start.25 = (bf16[448,384]{1,0:T(8,128)(2,1)S(1)}, bf16[448,384]{1,0:T(8,128)(2,1)S(1)}, u32[]{:S(2)}, u32[]{:S(2)}) collective-permute-start(bf16[448,384]{1,0:T(8,128)(2,1)S(1)} %get-tuple-element.104), channel_id=1, source_target_pairs={{0,1},{1,0},{2,3},{3,2},{4,5},{5,4},{6,7},{7,6},{8,9},{9,8},{10,11... | collective-permute-start | bytes 1032200 | tf_op jit(solution)/shard_map/ppermute | solution.py:145
  153.2 1.8 %collective-permute-start.24 = (bf16[448,384]{1,0:T(8,128)(2,1)S(1)}, bf16[448,384]{1,0:T(8,128)(2,1)S(1)}, u32[]{:S(2)}, u32[]{:S(2)}) collective-permute-start(bf16[448,384]{1,0:T(8,128)(2,1)S(1)} %get-tuple-element.100), channel_id=1, source_target_pairs={{0,1},{1,0},{2,3},{3,2},{4,5},{5,4},{6,7},{7,6},{8,9},{9,8},{10,11... | collective-permute-start | bytes 1032200 | tf_op jit(solution)/shard_map/ppermute | solution.py:145
  155.0 8.7 %collective-permute-start.28 = (bf16[1024,512]{1,0:T(8,128)(2,1)S(1)}, bf16[1024,512]{1,0:T(8,128)(2,1)S(1)}, u32[]{:S(2)}, u32[]{:S(2)}) collective-permute-start(bf16[1024,512]{1,0:T(8,128)(2,1)S(1)} %pad_maximum_fusion.6.e8), channel_id=1, source_target_pairs={{0,1},{1,0},{2,3},{3,2},{4,5},{5,4},{6,7},{7,6},{8,9},{9,8},{10,11... | collective-permute-start | bytes 3145736 | tf_op jit(solution)/shard_map/ppermute | solution.py:145
  155.4 8.3 %collective-permute-start.29 = (bf16[1024,512]{1,0:T(8,128)(2,1)S(1)}, bf16[1024,512]{1,0:T(8,128)(2,1)S(1)}, u32[]{:S(2)}, u32[]{:S(2)}) collective-permute-start(bf16[1024,512]{1,0:T(8,128)(2,1)S(1)} %collective-permute-done.17.er), channel_id=1, source_target_pairs={{0,1},{1,0},{2,3},{3,2},{4,5},{5,4},{6,7},{7,6},{8,9},{9,8},{10,11... | collective-permute-start | bytes 3145736 | tf_op jit(solution)/shard_map/ppermute | solution.py:145
  155.5 8.2 %collective-permute-start.30 = (bf16[1024,512]{1,0:T(8,128)(2,1)S(1)}, bf16[1024,512]{1,0:T(8,128)(2,1)S(1)}, u32[]{:S(2)}, u32[]{:S(2)}) collective-permute-start(bf16[1024,512]{1,0:T(8,128)(2,1)S(1)} %pad_maximum_fusion.7.d8), channel_id=1, source_target_pairs={{0,1},{1,0},{2,3},{3,2},{4,5},{5,4},{6,7},{7,6},{8,9},{9,8},{10,11... | collective-permute-start | bytes 3145736 | tf_op jit(solution)/shard_map/ppermute | solution.py:145
  155.9 7.8 %collective-permute-start.31 = (bf16[1024,512]{1,0:T(8,128)(2,1)S(1)}, bf16[1024,512]{1,0:T(8,128)(2,1)S(1)}, u32[]{:S(2)}, u32[]{:S(2)}) collective-permute-start(bf16[1024,512]{1,0:T(8,128)(2,1)S(1)} %collective-permute-done.18.dr), channel_id=1, source_target_pairs={{0,1},{1,0},{2,3},{3,2},{4,5},{5,4},{6,7},{7,6},{8,9},{9,8},{10,11... | collective-permute-start | bytes 3145736 | tf_op jit(solution)/shard_map/ppermute | solution.py:145
  158.7 3.6 %collective-permute-start.27 = (bf16[448,128]{1,0:T(8,128)(2,1)S(1)}, bf16[448,128]{1,0:T(8,128)(2,1)S(1)}, u32[]{:S(2)}, u32[]{:S(2)}) collective-permute-start(bf16[448,128]{1,0:T(8,128)(2,1)S(1)} %get-tuple-element.114), channel_id=1, source_target_pairs={{0,1},{1,0},{2,3},{3,2},{4,5},{5,4},{6,7},{7,6},{8,9},{9,8},{10,11... | collective-permute-start | bytes 344072 | tf_op jit(solution)/shard_map/ppermute | solution.py:145
  162.3 1.3 collective-permute-start.26
  (4 other events, 26.0 us)

commit v4 on v3

--- a/solution.py
+++ b/solution.py
@@ -133,10 +133,13 @@
 LANE = 128
 BLOCKS = D // LANE
 HALF = D // 2
-FIRST = 384
+PART = 256
+IN1, IN2 = ("z1", "y", "z2", "x"), ("z2", "z1", "y", "x")
+IN3, IN4 = ("z1", "z2", "x", "y"), ("z2", "x", "z1", "y")
+OUT1, OUT2 = ("z2", "x", "y", "z1"), ("z1", "y", "x", "z2")
+NOTES = ("x", "z1", "z2", "y")
 SMALL = 48
 META = 16
-ROWS = PAIR
 TILE = 64
 
 
@@ -165,29 +168,10 @@
     return [lax.axis_index(name) for name in ("z", "y", "x", "core")]
 
 
-def bits(block):
+def spot(order, block):
     z, y, x, _ = coordinates()
-    return (block >> 3) ^ (z >> 1), ((block >> 2) & 1) ^ (z & 1), ((block >> 1) & 1) ^ y, (block & 1) ^ x
-
-
-def spot_a(block):
-    z2, z1, y, x = bits(block)
-    return x * 8 + y * 4 + z1 * 2 + z2
-
-
-def spot_b(block):
-    z2, z1, y, x = bits(block)
-    return y * 8 + x * 4 + z2 * 2 + z1
-
-
-def spot_e(block):
-    z2, z1, y, x = bits(block)
-    return z2 * 8 + z1 * 4 + y * 2 + x
-
-
-def spot_d(block):
-    z2, z1, y, x = bits(block)
-    return z1 * 8 + z2 * 4 + y * 2 + x
+    bit = {"z2": (block >> 3) ^ (z >> 1), "z1": ((block >> 2) & 1) ^ (z & 1), "y": ((block >> 1) & 1) ^ y, "x": (block & 1) ^ x}
+    return sum(bit[name] << place for place, name in enumerate(order))
 
 
 def lanes(index):
@@ -222,17 +206,15 @@
     return lax.broadcasted_iota(jnp.int32, shape, 0), lax.broadcasted_iota(jnp.int32, shape, 1)
 
 
-def cut_kernel(lens, dest, offs, rows_ref, up0, up1, down0, down1):
-    for code, first_ref, second_ref in ((1, up0, up1), (7, down0, down1)):
+def cut_kernel(lens, dest, offs, rows_ref, up_ref, down_ref):
+    for code, out_ref in ((1, up_ref), (7, down_ref)):
         count, offset, start = local(lens, dest, offs, code)
         spot, slot = grid_of(MAXLEN + META, rows_ref.shape[0])
         picker = hot((slot == start + spot) & (spot < count))
-        spot, _ = grid_of(MAXLEN + META, HALF)
+        spot, _ = grid_of(MAXLEN + META, D)
         note = jnp.where(spot == MAXLEN, count, 0) + jnp.where(spot == MAXLEN + 1, offset // 2, 0)
         note = note + jnp.where(spot == MAXLEN + 2, offset % 2, 0)
-        first = take(picker, rows_ref[:, 0:HALF]) + note.astype(jnp.float32)
-        first_ref[...] = first.astype(jnp.bfloat16)
-        second_ref[...] = take(picker[0:MAXLEN], rows_ref[:, HALF:D]).astype(jnp.bfloat16)
+        out_ref[...] = (take(picker, rows_ref[...]) + note.astype(jnp.float32)).astype(jnp.bfloat16)
 
 
 def smem(count):
@@ -243,6 +225,10 @@
     return [pl.BlockSpec(memory_space=pltpu.VMEM)] * count
 
 
+def anywhere(count):
+    return [pl.BlockSpec(memory_space=pl.ANY)] * count
+
+
 def shape(rows, columns, dtype=jnp.bfloat16):
     return jax.ShapeDtypeStruct((rows, columns), dtype)
 
@@ -252,19 +238,19 @@
 
 
 def cut(lens, dest, offs, rows):
-    first, second = shape(MAXLEN + META, HALF), shape(MAXLEN, HALF)
+    sent = shape(MAXLEN + META, D)
     return pl.pallas_call(
         cut_kernel,
-        out_shape=(first, second, first, second),
+        out_shape=(sent, sent),
         in_specs=smem(3) + vmem(1),
-        out_specs=tuple(vmem(4)),
+        out_specs=tuple(vmem(2)),
         compiler_params=limits(16),
         cost_estimate=COST,
         name="cut",
     )(lens, dest, offs, rows)
 
 
-def place_kernel(lens, dest, offs, rows_ref, p0, p1, n0, n1, spread_ref, base_ref, pick_ref):
+def place_kernel(lens, dest, offs, rows_ref, prev_ref, next_ref, spread_ref, base_ref, pick_ref):
     count, offset, start = local(lens, dest, offs, 0)
     ones = jnp.ones((1, 1), jnp.int32)
 
@@ -272,7 +258,7 @@
         head = ref[MAXLEN : MAXLEN + META, 0:LANE].astype(jnp.float32).astype(jnp.int32)
         return head[0:1, 0:1], head[1:2, 0:1] * 2 + head[2:3, 0:1]
 
-    parts = [(count * ones, offset * ones), noted(p0), noted(n0)]
+    parts = [(count * ones, offset * ones), noted(prev_ref), noted(next_ref)]
 
     def placer(which, width, first):
         mine = parts[which]
@@ -285,14 +271,8 @@
     from_own = placer(0, rows_ref.shape[0], start)
     from_prev = placer(1, MAXLEN + META, 0)
     from_next = placer(2, MAXLEN + META, 0)
-    first = take(from_own, rows_ref[:, 0:HALF]) + take(from_prev, p0[...]) + take(from_next, n0[...])
-    spread_ref[:, 0:HALF] = first.astype(jnp.bfloat16)
-    second = (
-        take(from_own, rows_ref[:, HALF:D])
-        + take(from_prev[:, 0:MAXLEN], p1[...])
-        + take(from_next[:, 0:MAXLEN], n1[...])
-    )
-    spread_ref[:, HALF:D] = second.astype(jnp.bfloat16)
+    found = take(from_own, rows_ref[...]) + take(from_prev, prev_ref[...]) + take(from_next, next_ref[...])
+    spread_ref[...] = found.astype(jnp.bfloat16)
     flat, spot = grid_of(RCV_DEV, PAD)
     rank = sum((part[1] <= flat).astype(jnp.int32) for part in parts)
     pick = hot(spot == flat + GAP * rank)
@@ -304,7 +284,7 @@
     return pl.pallas_call(
         place_kernel,
         out_shape=(shape(PAD, D), shape(RCV_DEV, D), shape(RCV_DEV, PAD)),
-        in_specs=smem(3) + vmem(5),
+        in_specs=smem(3) + vmem(3),
         out_specs=tuple(vmem(3)),
         compiler_params=limits(24),
         cost_estimate=COST,
@@ -312,15 +292,10 @@
     )(lens, dest, offs, rows, *arrived)
 
 
-def prep_kernel(mine_ref, other_ref, notes_ref, first_ref, second_ref, small_ref):
+def prep_kernel(mine_ref, other_ref, notes_ref, out1, out2, out3, out4, small_ref):
     for block in range(BLOCKS):
-        spot = spot_a(block)
-        at = pl.ds(pl.multiple_of((spot & 7) * META, META), META)
-        for part in range(SMALL // META):
-            tile = notes_ref[at, lanes((spot >> 3) * (SMALL // META) + part)]
-            small_ref[part * META : (part + 1) * META, block * LANE : (block + 1) * LANE] = tile.astype(
-                jnp.float32
-            )
+        tile = notes_ref[:, lanes(spot(NOTES, block))]
+        small_ref[:, block * LANE : (block + 1) * LANE] = tile.astype(jnp.float32)
     for base, rows_ref in ((0, mine_ref), (PAD, other_ref)):
 
         def one(step, carry):
@@ -332,8 +307,9 @@
             at = pl.ds(pl.multiple_of(base + step * TILE, TILE), TILE)
             for block in range(BLOCKS):
                 part = scaled[:, block * LANE : (block + 1) * LANE]
-                first_ref[at, lanes(spot_a(block))] = part
-                second_ref[at, lanes(spot_b(block))] = part
+                for order, out_ref in ((IN1, out1), (IN2, out2), (IN3, out3), (IN4, out4)):
+                    place = spot(order, block)
+                    out_ref[place >> 3, at, lanes(place & 7)] = part
             return carry
 
         lax.fori_loop(0, PAD // TILE, one, 0)
@@ -342,26 +318,43 @@
 def prep(mine, other, notes):
     return pl.pallas_call(
         prep_kernel,
-        out_shape=(shape(PAIR, D), shape(PAIR, D), shape(SMALL, D, jnp.float32)),
+        out_shape=(jax.ShapeDtypeStruct((2, PAIR, HALF), jnp.bfloat16),) * 4 + (shape(SMALL, D, jnp.float32),),
         in_specs=vmem(3),
-        out_specs=tuple(vmem(3)),
-        compiler_params=limits(20),
+        out_specs=tuple(vmem(5)),
+        compiler_params=limits(28),
         cost_estimate=COST,
         name="prep",
     )(mine, other, notes)
 
 
-def conv_kernel(sub, rows_hbm, near_hbm, far_hbm, small_ref, own_ref, other_ref, gated, taps, rows_ref, near_ref, far_ref, done):
+def early_kernel(rows_hbm, near_ref, out_ref, rows_ref, done):
+    load = pltpu.make_async_copy(rows_hbm.at[0], rows_ref, done)
+    load.start()
+    load.wait()
+    out_ref[...] = take(rows_ref[...], near_ref[...])
+
+
+def early(rows, near):
+    return pl.pallas_call(
+        early_kernel,
+        out_shape=shape(PAIR, near.shape[1], jnp.float32),
+        in_specs=anywhere(1) + vmem(1),
+        out_specs=vmem(1)[0],
+        scratch_shapes=[pltpu.VMEM((PAIR, HALF), jnp.bfloat16), pltpu.SemaphoreType.DMA],
+        compiler_params=limits(12),
+        cost_estimate=COST,
+        name="early",
+    )(rows, near)
+
+
+def conv_kernel(sub, rows_hbm, part_hbm, far_hbm, small_ref, own_ref, other_ref, gated, taps, rows_ref, part_ref, far_ref, done):
     width = own_ref.shape[1]
     tiles = width // LANE
-    steps = PAIR // ROWS
-    spans = [pl.ds(step * ROWS, ROWS) for step in range(steps)]
     loads = [
-        pltpu.make_async_copy(near_hbm, near_ref, done.at[0]),
+        pltpu.make_async_copy(rows_hbm.at[1], rows_ref, done.at[0]),
         pltpu.make_async_copy(far_hbm, far_ref, done.at[1]),
+        pltpu.make_async_copy(part_hbm, part_ref, done.at[2]),
     ]
-    for step, span in enumerate(spans):
-        loads.append(pltpu.make_async_copy(rows_hbm.at[span, :], rows_ref.at[span, :], done.at[2 + step]))
     for load in loads:
         load.start()
     half = lax.axis_index("core")
@@ -369,14 +362,12 @@
         gated[tile, 0:GAP, :] = jnp.zeros((GAP, LANE), jnp.float32)
         gated[tile, GAP + PAIR : 2 * GAP + PAIR, :] = jnp.zeros((GAP, LANE), jnp.float32)
         taps[tile] = small_ref[0:KERNEL, lanes(half * (BLOCKS // 2) + sub + tile)]
-    loads[0].wait()
-    loads[1].wait()
-    for step, span in enumerate(spans):
-        loads[2 + step].wait()
-        both = take(rows_ref[span, 0:HALF], near_ref[...]) + take(rows_ref[span, HALF:D], far_ref[...])
-        mixed = both[:, 0:width] * jax.nn.sigmoid(both[:, width:])
-        for tile in range(tiles):
-            gated[tile, pl.ds(GAP + step * ROWS, ROWS), :] = mixed[:, tile * LANE : (tile + 1) * LANE]
+    for load in loads:
+        load.wait()
+    both = part_ref[...] + take(rows_ref[...], far_ref[...])
+    mixed = both[:, 0:width] * jax.nn.sigmoid(both[:, width:])
+    for tile in range(tiles):
+        gated[tile, GAP : GAP + PAIR, :] = mixed[:, tile * LANE : (tile + 1) * LANE]
 
     def slide(out_ref, base):
         def one(step, carry):
@@ -395,14 +386,9 @@
     slide(other_ref, PAD)
 
 
-def anywhere(count):
-    return [pl.BlockSpec(memory_space=pl.ANY)] * count
-
-
-def conv(sub, rows, near, far, small):
-    width = near.shape[1] // 2
+def conv(sub, rows, part, far, small):
+    width = far.shape[1] // 2
     out = shape(PAD, width)
-    weight = pltpu.VMEM(near.shape, near.dtype)
     return pl.pallas_call(
         functools.partial(conv_kernel, sub),
         out_shape=(out, out),
@@ -411,26 +397,29 @@
         scratch_shapes=[
             pltpu.VMEM((width // LANE, PAIR + 2 * GAP, LANE), jnp.float32),
             pltpu.VMEM((width // LANE, KERNEL, LANE), jnp.float32),
-            pltpu.VMEM((PAIR, D), jnp.bfloat16),
-            weight,
-            weight,
-            pltpu.SemaphoreType.DMA((2 + PAIR // ROWS,)),
+            pltpu.VMEM((PAIR, HALF), jnp.bfloat16),
+            pltpu.VMEM(part.shape, part.dtype),
+            pltpu.VMEM(far.shape, far.dtype),
+            pltpu.SemaphoreType.DMA((3,)),
         ],
         compiler_params=limits(16),
         cost_estimate=COST,
         name="conv",
-    )(rows, near, far, small)
+    )(rows, part, far, small)
 
 
 def finish_kernel(
-    m0, m1, m2, m3, o0, o1, o2, o3, small_ref, pick_ref, base_ref,
-    e8, er, d8, dr, f8, fr, g8, gr, out_ref, first, second, weights, done,
+    m0, m1, m2, m3, o0, o1, o2, o3, small_ref, pick_ref, base_hbm,
+    e8, er, d8, dr, f8, fr, g8, gr, out_hbm, first, second, weights, base, result, done, sent,
 ):
     sources = (e8, er, d8, dr, f8, fr, g8, gr)
     loads = [
-        pltpu.make_async_copy(source, weights.at[index], done.at[index])
+        pltpu.make_async_copy(
+            source, weights.at[index // 2, pl.ds(index % 2 * HALF, HALF), :], done.at[index]
+        )
         for index, source in enumerate(sources)
     ]
+    loads.append(pltpu.make_async_copy(base_hbm, base, done.at[len(sources)]))
     for load in loads:
         load.start()
     half = lax.axis_index("core")
@@ -461,31 +450,39 @@
             kept = kept.astype(jnp.bfloat16)
             for tile, block in enumerate(blocks):
                 part = kept[:, tile * LANE : (tile + 1) * LANE]
-                first[:, lanes(spot_e(block))] = part
-                second[:, lanes(spot_d(block))] = part
+                first[:, lanes(spot(OUT1, block))] = part
+                second[:, lanes(spot(OUT2, block))] = part
     width = HALF // 2
+    loads[len(sources)].wait()
+    stores = []
     for turn_index, (side, active, edge) in enumerate(
         ((half, first, 0), (half, second, width), (1 - half, first, 0), (1 - half, second, width))
     ):
         at = pl.ds(pl.multiple_of(side * HALF + edge, width), width)
         loads[2 * turn_index].wait()
         loads[2 * turn_index + 1].wait()
-        result = (
-            take(active[:, 0:HALF], weights[2 * turn_index])
-            + take(active[:, HALF:D], weights[2 * turn_index + 1])
-            + base_ref[:, at].astype(jnp.float32)
-        )
-        out_ref[:, at] = result.astype(jnp.bfloat16)
+        mixed = take(active[...], weights[turn_index]) + base[:, at].astype(jnp.float32)
+        result[turn_index] = mixed.astype(jnp.bfloat16)
+        stores.append(pltpu.make_async_copy(result.at[turn_index], out_hbm.at[:, at], sent.at[turn_index]))
+        stores[-1].start()
+    for store in stores:
+        store.wait()
 
 
 def finish(mine, others, small, pick, base, weights):
     return pl.pallas_call(
         finish_kernel,
         out_shape=shape(RCV_DEV, D),
-        in_specs=vmem(11) + anywhere(8),
-        out_specs=vmem(1)[0],
+        in_specs=vmem(10) + anywhere(9),
+        out_specs=anywhere(1)[0],
         scratch_shapes=[pltpu.VMEM((RCV_DEV, D), jnp.bfloat16)] * 2
-        + [pltpu.VMEM((8, HALF, HALF // 2), jnp.bfloat16), pltpu.SemaphoreType.DMA((8,))],
+        + [
+            pltpu.VMEM((4, D, HALF // 2), jnp.bfloat16),
+            pltpu.VMEM((RCV_DEV, D), jnp.bfloat16),
+            pltpu.VMEM((4, RCV_DEV, HALF // 2), jnp.bfloat16),
+            pltpu.SemaphoreType.DMA((9,)),
+            pltpu.SemaphoreType.DMA((4,)),
+        ],
         compiler_params=limits(28),
         cost_estimate=COST,
         name="finish",
@@ -498,73 +495,78 @@
     low = lax.axis_index("core") == 0
     per = weight_in.shape[0]
 
+    rows = frames[0]
+    up, down = cut(lengths, destination, offsets, rows)
     left = beside(weight_in[:, 0:HALF], weight_in[:, D : D + HALF], weight_out[:, 0:HALF])
     right = beside(weight_in[:, HALF:D], weight_in[:, D + HALF :], weight_out[:, HALF:])
     kept, given = jnp.where(low, left, right), jnp.where(low, right, left)
     got = hop(given, "c")
-    rows = frames[0]
-    up0, up1, down0, down1 = cut(lengths, destination, offsets, rows)
     chip = jnp.where(low, stack(kept, got), stack(got, kept))
-    chip, up1, down1 = tie(chip, up1, down1)
+    chip, up, down = tie(chip, up, down)
 
     notes = jnp.concatenate(
         [depth_kernel.T, norm_gain[None], post_gain[None], jnp.zeros((SMALL - KERNEL - 2, per), jnp.bfloat16)], 0
     )
     blank = jnp.zeros_like(notes)
-    pair = [jnp.where(low, beside(one, blank), beside(blank, one)) for one in (notes, hop(notes, "x"))]
-    pair = stack(*pair)
-    pair = pair + hop(pair, "c")
-    tiles = [pair[low_row : low_row + META] for low_row in range(0, 2 * SMALL, META)]
-    notes = beside(*tiles, jnp.zeros((META, HALF - 2 * LANE * SMALL // META), jnp.bfloat16))
-
-    def stream(start):
-        edges = (start, start + FIRST, start + HALF // 2)
-        spans = [(low_edge + gate, high_edge + gate) for low_edge, high_edge in zip(edges, edges[1:]) for gate in (0, HALF)]
-        return beside(*[chip[:, low_edge:high_edge] for low_edge, high_edge in spans])
-
-    a, b = stream(0), stream(HALF // 2)
-    o = chip[:, 2 * HALF : 3 * HALF]
-
-    def grow(array, extra, name):
-        size = array.shape[0]
-        arrived = hop(stack(array, extra), name)
-        return stack(array, arrived[0:size]), stack(extra, arrived[size:])
-
-    prev0, next0 = turn(up0, 1), turn(down0, -1)
-    (a, notes), b_far, o_far = grow(a, notes, "z2"), hop(b, "z1"), hop(o, "x")
-    prev0, next0, a, notes, b, o, up1, down1 = tie(
-        prev0, next0, a, notes, stack(b, b_far), stack(o, o_far), up1, down1
-    )
-    prev1, next1 = turn(up1, 1), turn(down1, -1)
-    (a, notes), b_far, o_far = grow(a, notes, "z1"), hop(b, "z2"), hop(o, "y")
-    prev1, next1, a, notes, b, o = tie(prev1, next1, a, notes, stack(b, b_far), stack(o, o_far))
-    e, d = o[:, 0 : HALF // 2], o[:, HALF // 2 :]
-    spread, base, pick = place(lengths, destination, offsets, rows, (prev0, prev1, next0, next1))
-    (a, notes), b_far, e_far, d_far = grow(a, notes, "y"), hop(b, "x"), hop(e, "z1"), hop(d, "z2")
-    a, notes, b, e, d, spread, base, pick = tie(
-        a, notes, stack(b, b_far), stack(e, e_far), stack(d, d_far), spread, base, pick
-    )
-    e_far, d_far = hop(e, "z2"), hop(d, "z1")
-    cut_at = 2 * FIRST
-    a1, a2, b1, b2 = a[:, 0:cut_at], a[:, cut_at:], b[:, 0:cut_at], b[:, cut_at:]
-    a1_far, b1_far = hop(a1, "x"), hop(b1, "y")
-    for_a, for_b, small = prep(spread, hop(spread, "c"), notes)
-    a1_far, b1_far, a2, b2, small = tie(a1_far, b1_far, a2, b2, small)
-    a2_far, b2_far = hop(a2, "x"), hop(b2, "y")
-
-    def run(sub, rows_in, near, far):
-        mine, given_part = conv(sub, rows_in, near, far, small)
+    notes = jnp.where(low, beside(notes, blank), beside(blank, notes))
+    notes = notes + hop(notes, "c")
+
+    def span(which):
+        if which >= 4:
+            return [chip[:, 2 * HALF + (which - 4) * 2 * PART : 2 * HALF + (which - 3) * 2 * PART]]
+        return [chip[:, gate + which * PART : gate + (which + 1) * PART] for gate in (0, HALF)]
+
+    def streams(*which):
+        return beside(*[piece for one in which for piece in span(one)])
+
+    def wide(notes, name):
+        return beside(notes, hop(notes, name))
+
+    size = 2 * PART
+
+    prev, next_ = turn(up, 1), turn(down, -1)
+    one, two = streams(0, 5, 2), streams(3, 4, 1)
+    one_far, two_far = hop(one, "z1"), hop(two, "z2")
+    one, two, notes = tie(stack(one, one_far), stack(two, two_far), wide(notes, NOTES[0]))
+
+    in1_out2, in3, in4_out1, in2 = one[:, 0 : 2 * size], one[:, 2 * size :], two[:, 0 : 2 * size], two[:, 2 * size :]
+    far = [hop(in3, "z2"), hop(in4_out1, "x"), hop(in2, "z1")]
+    in1_out2, notes, prev, next_ = tie(in1_out2, notes, prev, next_)
+    far = [hop(in1_out2, "y")] + far
+    in1_out2, in3, in4_out1, in2, notes = tie(
+        stack(in1_out2, far[0]), stack(in3, far[1]), stack(in4_out1, far[2]), stack(in2, far[3]), wide(wide(notes, NOTES[1]), NOTES[2])
+    )
+    spread, base, pick = place(lengths, destination, offsets, rows, (prev, next_))
+
+    in1, in4 = in1_out2[:, 0:size], in4_out1[:, 0:size]
+    in3_out2, in2_out1 = beside(in3, in1_out2[:, size:]), beside(in2, in4_out1[:, size:])
+    far = hop(in1, "z2"), hop(in3_out2, "x"), hop(in2_out1, "y"), hop(in4, "z1")
+    in1, in3_out2, in2_out1, in4, notes, spread, base, pick = tie(
+        stack(in1, far[0]), stack(in3_out2, far[1]), stack(in2_out1, far[2]), stack(in4, far[3]), wide(notes, NOTES[3]),
+        spread, base, pick,
+    )
+
+    in2, out1, in3, out2 = in2_out1[:, 0:size], in2_out1[:, size:], in3_out2[:, 0:size], in3_out2[:, size:]
+    out1_far, out2_far = hop(out1, "z1"), hop(out2, "z2")
+    in1_far, in3_far = hop(in1, "x"), hop(in3, "y")
+    n1, n2, n3, n4, small = prep(spread, hop(spread, "c"), notes)
+    part1, part2, part3, part4 = early(n1, in1), early(n2, in2), early(n3, in3), early(n4, in4)
+    in2, in4, small, part1, part2, part3, part4 = tie(in2, in4, small, part1, part2, part3, part4)
+    in2_far, in4_far = hop(in2, "x"), hop(in4, "y")
+
+    def run(normed, which, part, far):
+        mine, given_part = conv(which * PART // LANE, normed, part, far, small)
         return mine, hop(given_part, "c")
 
-    m0, o0 = run(0, for_a, a1, a1_far)
-    m2, o2 = run(BLOCKS // 4, for_b, b1, b1_far)
-    e, d, e_far, d_far, a2_far, b2_far, m0, o0, m2, o2 = tie(
-        e, d, e_far, d_far, a2_far, b2_far, m0, o0, m2, o2
-    )
-    weights = [e, e_far, d, d_far]
+    m0, o0 = run(n1, 0, part1, in1_far)
+    m2, o2 = run(n3, 2, part3, in3_far)
+    out1, out2, out1_far, out2_far, in2_far, in4_far, m0, o0, m2, o2 = tie(
+        out1, out2, out1_far, out2_far, in2_far, in4_far, m0, o0, m2, o2
+    )
+    weights = [out1, out1_far, out2, out2_far]
     weights = weights + [hop(array, "c") for array in weights]
-    m1, o1 = run(FIRST // LANE, for_a, a2, a2_far)
-    m3, o3 = run(BLOCKS // 4 + FIRST // LANE, for_b, b2, b2_far)
+    m1, o1 = run(n2, 1, part2, in2_far)
+    m3, o3 = run(n4, 3, part4, in4_far)
     mixed = finish((m0, m1, m2, m3), (o0, o1, o2, o3), small, pick, base, weights)
     return mixed[None]
 

time: 173 us -> 164 us (0.948)
  waiting for transfers between devices: 89.9 us -> 83.3 us
  starting transfers between devices: 38.7 us -> 34.6 us
  Pallas kernels: 39.3 us -> 41.3 us
    ppermute x28 -> x31, waiting for transfers between devices: 77.8 us -> 64.5 us  [hop(): return lax.ppermute(array, axis, pairs)]
    ppermute x4 -> x2, waiting for transfers between devices: 12.1 us -> 18.9 us  [turn(): lax.ppermute(array, ('z', 'y'), [(i, (i + by) % 8) for i in range(8)])]
    pallas_call x2 -> x6, Pallas kernels: 7.39 us -> 13.8 us  [the longest x1 6.71 us: prep(): pl.pallas_call(prep_kernel, out_shape=(jax.ShapeDtypeStruct((2, PAIR, HAL...]
    ppermute x4 -> x2, starting transfers between devices: 9.45 us -> 4.72 us  [turn(): lax.ppermute(array, ('z', 'y'), [(i, (i + by) % 8) for i in range(8)])]
    pallas_call x4, Pallas kernels: 18.7 us -> 14.7 us  [conv(): pl.pallas_call(functools.partial(conv_kernel, sub), out_shape=(out, out),...]
    ppermute x28 -> x31, starting transfers between devices: 29.3 us -> 29.9 us  [hop(): return lax.ppermute(array, axis, pairs)]
  transfers between devices with their start and end apart: 32 -> 33, of which waited for: 16 -> 14; matrix products, arithmetic and copies ran while one was open for 2% -> 1% of each run, Pallas kernels for 17% -> 20%
where the time goes in v4:
time: 164 us
  waiting for transfers between devices  83.3 us (51%)
  Pallas kernels  41.3 us (25%)
  starting transfers between devices  34.6 us (21%)
  local copies, waits for them, and re-layouts  2.23 us (1%)
  other arithmetic  1.7 us (1%)
    ppermute x31, waiting for transfers between devices, hop(): return lax.ppermute(array, axis, pairs)  64.5 us
    ppermute x31, starting transfers between devices, hop(): return lax.ppermute(array, axis, pairs)  29.9 us
    ppermute x2, waiting for transfers between devices, turn(): lax.ppermute(array, ('z', 'y'), [(i, (i + by) % 8) for i in range(8)])  18.9 us
    pallas_call x4, Pallas kernels, conv(): pl.pallas_call(functools.partial(conv_kernel, sub), out_shape=(out, out),...  14.7 us
    pallas_call x1, Pallas kernels, finish(): pl.pallas_call(finish_kernel, out_shape=shape(RCV_DEV, D), in_specs=vmem(...  8.7 us
    pallas_call x1, Pallas kernels, prep(): pl.pallas_call(prep_kernel, out_shape=(jax.ShapeDtypeStruct((2, PAIR, HAL...  6.71 us
    pallas_call x4, Pallas kernels, early(): pl.pallas_call(early_kernel, out_shape=shape(PAIR, near.shape[1], jnp.flo...  5.01 us
    ppermute x2, starting transfers between devices, turn(): lax.ppermute(array, ('z', 'y'), [(i, (i + by) % 8) for i in range(8)])  4.72 us
  transfers between devices with their start and end apart: 33, of which 14 were waited for; matrix products, arithmetic and copies ran while one was open for 1% of the time, Pallas kernels for 20%

profile of v4, /device:TPU:0, one launch (start us, length us, event | category | flops | bytes accessed | tf_op | source)
XLA Modules:
  0.0 163.9 jit_solution(17593254360510790198)
XLA Ops:
  0.0 1.4 fusion.5
  2.3 2.1 %cut.1 = (bf16[208,2048]{1,0:T(8,128)(2,1)S(1)}, bf16[208,2048]{1,0:T(8,128)(2,1)S(1)}) custom-call(s32[1,3]{1,0:T(1,128)S(1)} %copy-done.1, s32[1,3]{1,0:T(1,128)S(1)} %copy-done.2, s32[1,3]{1,0:T(1,128)S(1)} %copy-done.3, bf16[576,2048]{1,0:T(8,128)(2,1)S(1)} %bitcast.5), custom_call_target="tpu_custom_call" | custom-call | flops 1048576 | bytes 65536 | tf_op jit(solution)/shard_map/cut/pallas_call | solution.py:242
  4.8 3.9 %collective-permute-start.2 = (bf16[128,1536]{1,0:T(8,128)(2,1)S(1)}, bf16[128,1536]{1,0:T(8,128)(2,1)S(1)}, u32[]{:S(2)}, u32[]{:S(2)}) collective-permute-start(bf16[128,1536]{1,0:T(8,128)(2,1)S(1)} %pad_maximum_fusion.14), channel_id=1, source_target_pairs={{0,16},{8,24},{16,0},{24,8},{1,17},{9,25},{17,1},{25,9},{2,18},{10... | collective-permute-start | bytes 1179656 | tf_op jit(solution)/shard_map/ppermute | solution.py:148
  8.7 1.6 collective-permute-start.1
  10.4 1.5 collective-permute-start.4
  11.9 1.5 collective-permute-start.5
  13.4 3.2 %collective-permute-start.6 = (bf16[208,2048]{1,0:T(8,128)(2,1)S(1)}, bf16[208,2048]{1,0:T(8,128)(2,1)S(1)}, u32[]{:S(2)}, u32[]{:S(2)}) collective-permute-start(bf16[208,2048]{1,0:T(8,128)(2,1)S(1)} %get-tuple-element.69), channel_id=1, source_target_pairs={{0,28},{4,0},{8,4},{12,8},{16,12},{20,16},{24,20},{28,24},{1,29},{... | collective-permute-start | bytes 2555912 | tf_op jit(solution)/shard_map/ppermute | solution.py:152
  16.7 10.3 %collective-permute-done.2 = bf16[128,1536]{1,0:T(8,128)(2,1)S(1)} collective-permute-done((bf16[128,1536]{1,0:T(8,128)(2,1)S(1)}, bf16[128,1536]{1,0:T(8,128)(2,1)S(1)}, u32[]{:S(2)}, u32[]{:S(2)}) %collective-permute-start.2) | collective-permute-done | bytes 393248 | tf_op jit(solution)/shard_map/ppermute | solution.py:148
  29.2 1.6 collective-permute-start.9
  30.8 2.4 %collective-permute-start.8 = (bf16[256,512]{1,0:T(8,128)(2,1)S(1)}, bf16[256,512]{1,0:T(8,128)(2,1)S(1)}, u32[]{:S(2)}, u32[]{:S(2)}) collective-permute-start(bf16[256,512]{1,0:T(8,128)(2,1)S(1)} %slice.99), channel_id=1, source_target_pairs={{0,16},{8,24},{16,0},{24,8},{1,17},{9,25},{17,1},{25,9},{2,18},{10... | collective-permute-start | bytes 786440 | tf_op jit(solution)/shard_map/ppermute | solution.py:148
  33.3 15.9 %collective-permute-done.5.prev_ref = bf16[208,2048]{1,0:T(8,128)(2,1)S(1)} collective-permute-done((bf16[208,2048]{1,0:T(8,128)(2,1)S(1)}, bf16[208,2048]{1,0:T(8,128)(2,1)S(1)}, u32[]{:S(2)}, u32[]{:S(2)}) %collective-permute-start.5) | collective-permute-done | bytes 852000 | tf_op jit(solution)/shard_map/ppermute | solution.py:152
  49.2 2.9 %collective-permute-done.6.next_ref = bf16[208,2048]{1,0:T(8,128)(2,1)S(1)} collective-permute-done((bf16[208,2048]{1,0:T(8,128)(2,1)S(1)}, bf16[208,2048]{1,0:T(8,128)(2,1)S(1)}, u32[]{:S(2)}, u32[]{:S(2)}) %collective-permute-start.6) | collective-permute-done | bytes 852000 | tf_op jit(solution)/shard_map/ppermute | solution.py:152
  53.3 3.7 %collective-permute-done.10 = bf16[256,512]{1,0:T(8,128)(2,1)S(1)} collective-permute-done((bf16[256,512]{1,0:T(8,128)(2,1)S(1)}, bf16[256,512]{1,0:T(8,128)(2,1)S(1)}, u32[]{:S(2)}, u32[]{:S(2)}) %collective-permute-start.10) | collective-permute-done | bytes 262176 | tf_op jit(solution)/shard_map/ppermute | solution.py:148
  57.2 3.8 %collective-permute-done.11 = bf16[48,256]{1,0:T(8,128)(2,1)S(1)} collective-permute-done((bf16[48,256]{1,0:T(8,128)(2,1)S(1)}, bf16[48,256]{1,0:T(8,128)(2,1)S(1)}, u32[]{:S(2)}, u32[]{:S(2)}) %collective-permute-start.11) | collective-permute-done | bytes 24608 | tf_op jit(solution)/shard_map/ppermute | solution.py:148
  62.3 4.0 %collective-permute-done.12 = bf16[48,512]{1,0:T(8,128)(2,1)S(1)} collective-permute-done((bf16[48,512]{1,0:T(8,128)(2,1)S(1)}, bf16[48,512]{1,0:T(8,128)(2,1)S(1)}, u32[]{:S(2)}, u32[]{:S(2)}) %collective-permute-start.12) | collective-permute-done | bytes 49184 | tf_op jit(solution)/shard_map/ppermute | solution.py:148
  66.6 1.5 collective-permute-start.15
  68.3 1.6 collective-permute-start.14
  69.8 2.9 %collective-permute-start.13 = (bf16[512,512]{1,0:T(8,128)(2,1)S(1)}, bf16[512,512]{1,0:T(8,128)(2,1)S(1)}, u32[]{:S(2)}, u32[]{:S(2)}) collective-permute-start(bf16[512,512]{1,0:T(8,128)(2,1)S(1)} %get-tuple-element.128), channel_id=1, source_target_pairs={{0,16},{8,24},{16,0},{24,8},{1,17},{9,25},{17,1},{25,9},{2,18},{10... | collective-permute-start | bytes 1572872 | tf_op jit(solution)/shard_map/ppermute | solution.py:148
  73.4 4.1 %place.1 = (bf16[448,2048]{1,0:T(8,128)(2,1)S(1)}, bf16[384,2048]{1,0:T(8,128)(2,1)S(1)}, bf16[384,448]{1,0:T(8,128)(2,1)S(1)}) custom-call(s32[1,3]{1,0:T(1,128)S(1)} %copy-done.1, s32[1,3]{1,0:T(1,128)S(1)} %copy-done.2, s32[1,3]{1,0:T(1,128)S(1)} %copy-done.3, bf16[576,2048]{1,0:T(8,128)(2,1)S(1)} %bitcast.6, ...), custom_call_target="tpu_custom_call" | custom-call | flops 1048576 | bytes 65536 | tf_op jit(solution)/shard_map/place/pallas_call | solution.py:284
  77.5 14.3 %collective-permute-done.17 = bf16[48,1024]{1,0:T(8,128)(2,1)S(1)} collective-permute-done((bf16[48,1024]{1,0:T(8,128)(2,1)S(1)}, bf16[48,1024]{1,0:T(8,128)(2,1)S(1)}, u32[]{:S(2)}, u32[]{:S(2)}) %collective-permute-start.17) | collective-permute-done | bytes 98336 | tf_op jit(solution)/shard_map/ppermute | solution.py:148
  92.1 1.5 collective-permute-done.13
  96.3 2.5 %collective-permute-start.19 = (bf16[1024,512]{1,0:T(8,128)(2,1)S(1)}, bf16[1024,512]{1,0:T(8,128)(2,1)S(1)}, u32[]{:S(2)}, u32[]{:S(2)}) collective-permute-start(bf16[1024,512]{1,0:T(8,128)(2,1)S(1)} %get-tuple-element.119.d8), channel_id=1, source_target_pairs={{0,16},{8,24},{16,0},{24,8},{1,17},{9,25},{17,1},{25,9},{2,18},{10... | collective-permute-start | bytes 3145736 | tf_op jit(solution)/shard_map/ppermute | solution.py:148
  98.7 6.7 %prep.1 = (bf16[2,896,1024]{2,1,0:T(8,128)(2,1)S(1)}, bf16[2,896,1024]{2,1,0:T(8,128)(2,1)S(1)}, bf16[2,896,1024]{2,1,0:T(8,128)(2,1)S(1)}, bf16[2,896,1024]{2,1,0:T(8,128)(2,1)S(1)}, f32[48,2048]{1,0:T(8,128)S(1)}) custom-call(bf16[448,2048]{1,0:T(8,128)(2,1)S(1)} %get-tuple-element.86.mine_ref, bf16[448,2048]{1,0:T(8,128)(2,1)S(1)} %collective-permute-done.20.other_ref, ...), custom_call_target="tpu_custom_call" | custom-call | flops 1048576 | bytes 65536 | tf_op jit(solution)/shard_map/prep/pallas_call | solution.py:319
  110.5 1.5 collective-permute-start.21
  112.0 8.0 %collective-permute-done.25.far_hbm = bf16[1024,512]{1,0:T(8,128)(2,1)S(1)} collective-permute-done((bf16[1024,512]{1,0:T(8,128)(2,1)S(1)}, bf16[1024,512]{1,0:T(8,128)(2,1)S(1)}, u32[]{:S(2)}, u32[]{:S(2)}) %collective-permute-start.25) | collective-permute-done | bytes 1048608 | tf_op jit(solution)/shard_map/ppermute | solution.py:148
  120.6 3.7 %conv.5 = (bf16[448,256]{1,0:T(8,128)(2,1)S(1)}, bf16[448,256]{1,0:T(8,128)(2,1)S(1)}) custom-call(bf16[2,896,1024]{2,1,0:T(8,128)(2,1)S(1)} %get-tuple-element.92.rows_hbm, f32[896,512]{1,0:T(8,128)S(1)} %early.6.part_hbm, bf16[1024,512]{1,0:T(8,128)(2,1)S(1)} %collective-permute-done.25.far_hbm, f32[48,2048]{1,0:T(8,128)S(1)} %get-tuple-element.97.small_ref), custom_call_target="tpu_custom_call" | custom-call | flops 1048576 | bytes 65536 | tf_op jit(solution)/shard_map/conv/pallas_call | solution.py:392
  124.4 3.7 %conv.4 = (bf16[448,256]{1,0:T(8,128)(2,1)S(1)}, bf16[448,256]{1,0:T(8,128)(2,1)S(1)}) custom-call(bf16[2,896,1024]{2,1,0:T(8,128)(2,1)S(1)} %get-tuple-element.89.rows_hbm, f32[896,512]{1,0:T(8,128)S(1)} %early.4.part_hbm, bf16[1024,512]{1,0:T(8,128)(2,1)S(1)} %collective-permute-done.23.far_hbm, f32[48,2048]{1,0:T(8,128)S(1)} %get-tuple-element.97.small_ref), custom_call_target="tpu_custom_call" | custom-call | flops 1048576 | bytes 65536 | tf_op jit(solution)/shard_map/conv/pallas_call | solution.py:392
  128.1 14.9 %collective-permute-done.18.er = bf16[1024,512]{1,0:T(8,128)(2,1)S(1)} collective-permute-done((bf16[1024,512]{1,0:T(8,128)(2,1)S(1)}, bf16[1024,512]{1,0:T(8,128)(2,1)S(1)}, u32[]{:S(2)}, u32[]{:S(2)}) %collective-permute-start.18) | collective-permute-done | bytes 1048608 | tf_op jit(solution)/shard_map/ppermute | solution.py:148
  143.0 1.7 %collective-permute-done.19.dr = bf16[1024,512]{1,0:T(8,128)(2,1)S(1)} collective-permute-done((bf16[1024,512]{1,0:T(8,128)(2,1)S(1)}, bf16[1024,512]{1,0:T(8,128)(2,1)S(1)}, u32[]{:S(2)}, u32[]{:S(2)}) %collective-permute-start.19) | collective-permute-done | bytes 1048608 | tf_op jit(solution)/shard_map/ppermute | solution.py:148
  145.8 3.7 %conv.7 = (bf16[448,256]{1,0:T(8,128)(2,1)S(1)}, bf16[448,256]{1,0:T(8,128)(2,1)S(1)}) custom-call(bf16[2,896,1024]{2,1,0:T(8,128)(2,1)S(1)} %get-tuple-element.93.rows_hbm, f32[896,512]{1,0:T(8,128)S(1)} %early.7.part_hbm, bf16[1024,512]{1,0:T(8,128)(2,1)S(1)} %collective-permute-done.22.far_hbm, f32[48,2048]{1,0:T(8,128)S(1)} %get-tuple-element.97.small_ref), custom_call_target="tpu_custom_call" | custom-call | flops 1048576 | bytes 65536 | tf_op jit(solution)/shard_map/conv/pallas_call | solution.py:392
  149.6 3.7 %conv.6 = (bf16[448,256]{1,0:T(8,128)(2,1)S(1)}, bf16[448,256]{1,0:T(8,128)(2,1)S(1)}) custom-call(bf16[2,896,1024]{2,1,0:T(8,128)(2,1)S(1)} %get-tuple-element.91.rows_hbm, f32[896,512]{1,0:T(8,128)S(1)} %early.5.part_hbm, bf16[1024,512]{1,0:T(8,128)(2,1)S(1)} %collective-permute-done.21.far_hbm, f32[48,2048]{1,0:T(8,128)S(1)} %get-tuple-element.97.small_ref), custom_call_target="tpu_custom_call" | custom-call | flops 1048576 | bytes 65536 | tf_op jit(solution)/shard_map/conv/pallas_call | solution.py:392
  155.0 8.7 %finish.1 = bf16[384,2048]{1,0:T(8,128)(2,1)} custom-call(bf16[448,256]{1,0:T(8,128)(2,1)S(1)} %get-tuple-element.103.m0, bf16[448,256]{1,0:T(8,128)(2,1)S(1)} %get-tuple-element.106.m1, bf16[448,256]{1,0:T(8,128)(2,1)S(1)} %get-tuple-element.107.m2, bf16[448,256]{1,0:T(8,128)(2,1)S(1)} %get-tuple-element.110.m3, ...), custom_call_target="tpu_custom_call" | custom-call | flops 1048576 | bytes 65536 | tf_op jit(solution)/shard_map/finish/pallas_call | solution.py:473
  (99 shorter events, 18.9 us)
Async XLA Ops:
  1.6 2.8 %collective-permute-start = (bf16[64,3072]{1,0:T(8,128)(2,1)S(1)}, bf16[64,3072]{1,0:T(8,128)(2,1)S(1)}, u32[]{:S(2)}, u32[]{:S(2)}) collective-permute-start(bf16[64,3072]{1,0:T(8,128)(2,1)S(1)} %get-tuple-element.134), channel_id=1, source_target_pairs={{0,1},{1,0},{2,3},{3,2},{4,5},{5,4},{6,7},{7,6},{8,9},{9,8},{10,11... | collective-permute-start | bytes 1179656 | tf_op jit(solution)/shard_map/ppermute | solution.py:148
  4.8 22.2 %collective-permute-start.2 = (bf16[128,1536]{1,0:T(8,128)(2,1)S(1)}, bf16[128,1536]{1,0:T(8,128)(2,1)S(1)}, u32[]{:S(2)}, u32[]{:S(2)}) collective-permute-start(bf16[128,1536]{1,0:T(8,128)(2,1)S(1)} %pad_maximum_fusion.14), channel_id=1, source_target_pairs={{0,16},{8,24},{16,0},{24,8},{1,17},{9,25},{17,1},{25,9},{2,18},{10... | collective-permute-start | bytes 1179656 | tf_op jit(solution)/shard_map/ppermute | solution.py:148
  8.7 1.7 %collective-permute-start.3 = (bf16[48,128]{1,0:T(8,128)(2,1)S(1)}, bf16[48,128]{1,0:T(8,128)(2,1)S(1)}, u32[]{:S(2)}, u32[]{:S(2)}) collective-permute-start(bf16[48,128]{1,0:T(8,128)(2,1)S(1)} %pad_select_fusion), channel_id=1, source_target_pairs={{0,1},{1,0},{2,3},{3,2},{4,5},{5,4},{6,7},{7,6},{8,9},{9,8},{10,11... | collective-permute-start | bytes 36872 | tf_op jit(solution)/shard_map/ppermute | solution.py:148
  8.7 19.2 %collective-permute-start.1 = (bf16[128,1536]{1,0:T(8,128)(2,1)S(1)}, bf16[128,1536]{1,0:T(8,128)(2,1)S(1)}, u32[]{:S(2)}, u32[]{:S(2)}) collective-permute-start(bf16[128,1536]{1,0:T(8,128)(2,1)S(1)} %get-tuple-element.132), channel_id=1, source_target_pairs={{0,8},{8,0},{16,24},{24,16},{1,9},{9,1},{17,25},{25,17},{2,10},{10... | collective-permute-start | bytes 1179656 | tf_op jit(solution)/shard_map/ppermute | solution.py:148
  10.4 6.2 %collective-permute-start.4 = (bf16[48,128]{1,0:T(8,128)(2,1)S(1)}, bf16[48,128]{1,0:T(8,128)(2,1)S(1)}, u32[]{:S(2)}, u32[]{:S(2)}) collective-permute-start(bf16[48,128]{1,0:T(8,128)(2,1)S(1)} %fusion.7), channel_id=1, source_target_pairs={{0,2},{2,0},{1,3},{3,1},{4,6},{6,4},{5,7},{7,5},{8,10},{10,8},{9,1... | collective-permute-start | bytes 36872 | tf_op jit(solution)/shard_map/ppermute | solution.py:148
  11.9 37.3 %collective-permute-start.5 = (bf16[208,2048]{1,0:T(8,128)(2,1)S(1)}, bf16[208,2048]{1,0:T(8,128)(2,1)S(1)}, u32[]{:S(2)}, u32[]{:S(2)}) collective-permute-start(bf16[208,2048]{1,0:T(8,128)(2,1)S(1)} %get-tuple-element.68), channel_id=1, source_target_pairs={{0,4},{4,8},{8,12},{12,16},{16,20},{20,24},{24,28},{28,0},{1,5},{5... | collective-permute-start | bytes 2555912 | tf_op jit(solution)/shard_map/ppermute | solution.py:152
  13.4 38.7 %collective-permute-start.6 = (bf16[208,2048]{1,0:T(8,128)(2,1)S(1)}, bf16[208,2048]{1,0:T(8,128)(2,1)S(1)}, u32[]{:S(2)}, u32[]{:S(2)}) collective-permute-start(bf16[208,2048]{1,0:T(8,128)(2,1)S(1)} %get-tuple-element.69), channel_id=1, source_target_pairs={{0,28},{4,0},{8,4},{12,8},{16,12},{20,16},{24,20},{28,24},{1,29},{... | collective-permute-start | bytes 2555912 | tf_op jit(solution)/shard_map/ppermute | solution.py:152
  28.0 29.0 %collective-permute-start.10 = (bf16[256,512]{1,0:T(8,128)(2,1)S(1)}, bf16[256,512]{1,0:T(8,128)(2,1)S(1)}, u32[]{:S(2)}, u32[]{:S(2)}) collective-permute-start(bf16[256,512]{1,0:T(8,128)(2,1)S(1)} %slice.101), channel_id=1, source_target_pairs={{0,8},{8,0},{16,24},{24,16},{1,9},{9,1},{17,25},{25,17},{2,10},{10... | collective-permute-start | bytes 786440 | tf_op jit(solution)/shard_map/ppermute | solution.py:148
  29.2 33.0 %collective-permute-start.9 = (bf16[256,1024]{1,0:T(8,128)(2,1)S(1)}, bf16[256,1024]{1,0:T(8,128)(2,1)S(1)}, u32[]{:S(2)}, u32[]{:S(2)}) collective-permute-start(bf16[256,1024]{1,0:T(8,128)(2,1)S(1)} %slice.100), channel_id=1, source_target_pairs={{0,2},{2,0},{1,3},{3,1},{4,6},{6,4},{5,7},{7,5},{8,10},{10,8},{9,1... | collective-permute-start | bytes 1572872 | tf_op jit(solution)/shard_map/ppermute | solution.py:148
  30.8 26.4 %collective-permute-start.8 = (bf16[256,512]{1,0:T(8,128)(2,1)S(1)}, bf16[256,512]{1,0:T(8,128)(2,1)S(1)}, u32[]{:S(2)}, u32[]{:S(2)}) collective-permute-start(bf16[256,512]{1,0:T(8,128)(2,1)S(1)} %slice.99), channel_id=1, source_target_pairs={{0,16},{8,24},{16,0},{24,8},{1,17},{9,25},{17,1},{25,9},{2,18},{10... | collective-permute-start | bytes 786440 | tf_op jit(solution)/shard_map/ppermute | solution.py:148
  52.2 14.1 %collective-permute-start.7 = (bf16[256,1024]{1,0:T(8,128)(2,1)S(1)}, bf16[256,1024]{1,0:T(8,128)(2,1)S(1)}, u32[]{:S(2)}, u32[]{:S(2)}) collective-permute-start(bf16[256,1024]{1,0:T(8,128)(2,1)S(1)} %slice.98), channel_id=1, source_target_pairs={{0,4},{4,0},{1,5},{5,1},{2,6},{6,2},{3,7},{7,3},{8,12},{12,8},{9,1... | collective-permute-start | bytes 1572872 | tf_op jit(solution)/shard_map/ppermute | solution.py:148
  57.1 3.9 %collective-permute-start.11 = (bf16[48,256]{1,0:T(8,128)(2,1)S(1)}, bf16[48,256]{1,0:T(8,128)(2,1)S(1)}, u32[]{:S(2)}, u32[]{:S(2)}) collective-permute-start(bf16[48,256]{1,0:T(8,128)(2,1)S(1)} %pad_maximum_fusion.18), channel_id=1, source_target_pairs={{0,8},{8,0},{16,24},{24,16},{1,9},{9,1},{17,25},{25,17},{2,10},{10... | collective-permute-start | bytes 73736 | tf_op jit(solution)/shard_map/ppermute | solution.py:148
  61.0 5.3 %collective-permute-start.12 = (bf16[48,512]{1,0:T(8,128)(2,1)S(1)}, bf16[48,512]{1,0:T(8,128)(2,1)S(1)}, u32[]{:S(2)}, u32[]{:S(2)}) collective-permute-start(bf16[48,512]{1,0:T(8,128)(2,1)S(1)} %pad_maximum_fusion.17), channel_id=1, source_target_pairs={{0,16},{8,24},{16,0},{24,8},{1,17},{9,25},{17,1},{25,9},{2,18},{10... | collective-permute-start | bytes 147464 | tf_op jit(solution)/shard_map/ppermute | solution.py:148
  66.6 27.1 %collective-permute-start.15 = (bf16[512,1024]{1,0:T(8,128)(2,1)S(1)}, bf16[512,1024]{1,0:T(8,128)(2,1)S(1)}, u32[]{:S(2)}, u32[]{:S(2)}) collective-permute-start(bf16[512,1024]{1,0:T(8,128)(2,1)S(1)} %pad_maximum_fusion.6), channel_id=1, source_target_pairs={{0,4},{4,0},{1,5},{5,1},{2,6},{6,2},{3,7},{7,3},{8,12},{12,8},{9,1... | collective-permute-start | bytes 3145736 | tf_op jit(solution)/shard_map/ppermute | solution.py:148
  68.3 25.6 %collective-permute-start.14 = (bf16[512,1024]{1,0:T(8,128)(2,1)S(1)}, bf16[512,1024]{1,0:T(8,128)(2,1)S(1)}, u32[]{:S(2)}, u32[]{:S(2)}) collective-permute-start(bf16[512,1024]{1,0:T(8,128)(2,1)S(1)} %pad_maximum_fusion.5), channel_id=1, source_target_pairs={{0,2},{2,0},{1,3},{3,1},{4,6},{6,4},{5,7},{7,5},{8,10},{10,8},{9,1... | collective-permute-start | bytes 3145736 | tf_op jit(solution)/shard_map/ppermute | solution.py:148
  69.8 22.2 %collective-permute-start.16 = (bf16[512,512]{1,0:T(8,128)(2,1)S(1)}, bf16[512,512]{1,0:T(8,128)(2,1)S(1)}, u32[]{:S(2)}, u32[]{:S(2)}) collective-permute-start(bf16[512,512]{1,0:T(8,128)(2,1)S(1)} %get-tuple-element.125), channel_id=1, source_target_pairs={{0,8},{8,0},{16,24},{24,16},{1,9},{9,1},{17,25},{25,17},{2,10},{10... | collective-permute-start | bytes 1572872 | tf_op jit(solution)/shard_map/ppermute | solution.py:148
  69.8 23.8 %collective-permute-start.13 = (bf16[512,512]{1,0:T(8,128)(2,1)S(1)}, bf16[512,512]{1,0:T(8,128)(2,1)S(1)}, u32[]{:S(2)}, u32[]{:S(2)}) collective-permute-start(bf16[512,512]{1,0:T(8,128)(2,1)S(1)} %get-tuple-element.128), channel_id=1, source_target_pairs={{0,16},{8,24},{16,0},{24,8},{1,17},{9,25},{17,1},{25,9},{2,18},{10... | collective-permute-start | bytes 1572872 | tf_op jit(solution)/shard_map/ppermute | solution.py:148
  72.7 19.1 %collective-permute-start.17 = (bf16[48,1024]{1,0:T(8,128)(2,1)S(1)}, bf16[48,1024]{1,0:T(8,128)(2,1)S(1)}, u32[]{:S(2)}, u32[]{:S(2)}) collective-permute-start(bf16[48,1024]{1,0:T(8,128)(2,1)S(1)} %pad_maximum_fusion.16), channel_id=1, source_target_pairs={{0,4},{4,0},{1,5},{5,1},{2,6},{6,2},{3,7},{7,3},{8,12},{12,8},{9,1... | collective-permute-start | bytes 294920 | tf_op jit(solution)/shard_map/ppermute | solution.py:148
  94.1 4.6 %collective-permute-start.20 = (bf16[448,2048]{1,0:T(8,128)(2,1)S(1)}, bf16[448,2048]{1,0:T(8,128)(2,1)S(1)}, u32[]{:S(2)}, u32[]{:S(2)}) collective-permute-start(bf16[448,2048]{1,0:T(8,128)(2,1)S(1)} %get-tuple-element.86.mine_ref), channel_id=1, source_target_pairs={{0,1},{1,0},{2,3},{3,2},{4,5},{5,4},{6,7},{7,6},{8,9},{9,8},{10,11... | collective-permute-start | bytes 5505032 | tf_op jit(solution)/shard_map/ppermute | solution.py:148
  94.3 25.6 %collective-permute-start.25 = (bf16[1024,512]{1,0:T(8,128)(2,1)S(1)}, bf16[1024,512]{1,0:T(8,128)(2,1)S(1)}, u32[]{:S(2)}, u32[]{:S(2)}) collective-permute-start(bf16[1024,512]{1,0:T(8,128)(2,1)S(1)} %get-tuple-element.121.near_ref), channel_id=1, source_target_pairs={{0,4},{4,0},{1,5},{5,1},{2,6},{6,2},{3,7},{7,3},{8,12},{12,8},{9,1... | collective-permute-start | bytes 3145736 | tf_op jit(solution)/shard_map/ppermute | solution.py:148
  95.0 29.3 %collective-permute-start.23 = (bf16[1024,512]{1,0:T(8,128)(2,1)S(1)}, bf16[1024,512]{1,0:T(8,128)(2,1)S(1)}, u32[]{:S(2)}, u32[]{:S(2)}) collective-permute-start(bf16[1024,512]{1,0:T(8,128)(2,1)S(1)} %pad_maximum_fusion.4.near_ref), channel_id=1, source_target_pairs={{0,2},{2,0},{1,3},{3,1},{4,6},{6,4},{5,7},{7,5},{8,10},{10,8},{9,1... | collective-permute-start | bytes 3145736 | tf_op jit(solution)/shard_map/ppermute | solution.py:148
  96.1 46.8 %collective-permute-start.18 = (bf16[1024,512]{1,0:T(8,128)(2,1)S(1)}, bf16[1024,512]{1,0:T(8,128)(2,1)S(1)}, u32[]{:S(2)}, u32[]{:S(2)}) collective-permute-start(bf16[1024,512]{1,0:T(8,128)(2,1)S(1)} %get-tuple-element.117.e8), channel_id=1, source_target_pairs={{0,8},{8,0},{16,24},{24,16},{1,9},{9,1},{17,25},{25,17},{2,10},{10... | collective-permute-start | bytes 3145736 | tf_op jit(solution)/shard_map/ppermute | solution.py:148
  96.3 48.4 %collective-permute-start.19 = (bf16[1024,512]{1,0:T(8,128)(2,1)S(1)}, bf16[1024,512]{1,0:T(8,128)(2,1)S(1)}, u32[]{:S(2)}, u32[]{:S(2)}) collective-permute-start(bf16[1024,512]{1,0:T(8,128)(2,1)S(1)} %get-tuple-element.119.d8), channel_id=1, source_target_pairs={{0,16},{8,24},{16,0},{24,8},{1,17},{9,25},{17,1},{25,9},{2,18},{10... | collective-permute-start | bytes 3145736 | tf_op jit(solution)/shard_map/ppermute | solution.py:148
  110.5 34.2 %collective-permute-start.21 = (bf16[1024,512]{1,0:T(8,128)(2,1)S(1)}, bf16[1024,512]{1,0:T(8,128)(2,1)S(1)}, u32[]{:S(2)}, u32[]{:S(2)}) collective-permute-start(bf16[1024,512]{1,0:T(8,128)(2,1)S(1)} %get-tuple-element.94.near_ref), channel_id=1, source_target_pairs={{0,2},{2,0},{1,3},{3,1},{4,6},{6,4},{5,7},{7,5},{8,10},{10,8},{9,1... | collective-permute-start | bytes 3145736 | tf_op jit(solution)/shard_map/ppermute | solution.py:148
  120.0 24.8 %collective-permute-start.22 = (bf16[1024,512]{1,0:T(8,128)(2,1)S(1)}, bf16[1024,512]{1,0:T(8,128)(2,1)S(1)}, u32[]{:S(2)}, u32[]{:S(2)}) collective-permute-start(bf16[1024,512]{1,0:T(8,128)(2,1)S(1)} %pad_maximum_fusion.7.near_ref), channel_id=1, source_target_pairs={{0,4},{4,0},{1,5},{5,1},{2,6},{6,2},{3,7},{7,3},{8,12},{12,8},{9,1... | collective-permute-start | bytes 3145736 | tf_op jit(solution)/shard_map/ppermute | solution.py:148
  124.3 20.4 %collective-permute-start.26 = (bf16[448,256]{1,0:T(8,128)(2,1)S(1)}, bf16[448,256]{1,0:T(8,128)(2,1)S(1)}, u32[]{:S(2)}, u32[]{:S(2)}) collective-permute-start(bf16[448,256]{1,0:T(8,128)(2,1)S(1)} %get-tuple-element.102), channel_id=1, source_target_pairs={{0,1},{1,0},{2,3},{3,2},{4,5},{5,4},{6,7},{7,6},{8,9},{9,8},{10,11... | collective-permute-start | bytes 688136 | tf_op jit(solution)/shard_map/ppermute | solution.py:148
  143.0 1.7 %collective-permute-start.24 = (bf16[448,256]{1,0:T(8,128)(2,1)S(1)}, bf16[448,256]{1,0:T(8,128)(2,1)S(1)}, u32[]{:S(2)}, u32[]{:S(2)}) collective-permute-start(bf16[448,256]{1,0:T(8,128)(2,1)S(1)} %get-tuple-element.99), channel_id=1, source_target_pairs={{0,1},{1,0},{2,3},{3,2},{4,5},{5,4},{6,7},{7,6},{8,9},{9,8},{10,11... | collective-permute-start | bytes 688136 | tf_op jit(solution)/shard_map/ppermute | solution.py:148
  144.8 10.2 %collective-permute-start.29 = (bf16[1024,512]{1,0:T(8,128)(2,1)S(1)}, bf16[1024,512]{1,0:T(8,128)(2,1)S(1)}, u32[]{:S(2)}, u32[]{:S(2)}) collective-permute-start(bf16[1024,512]{1,0:T(8,128)(2,1)S(1)} %get-tuple-element.117.e8), channel_id=1, source_target_pairs={{0,1},{1,0},{2,3},{3,2},{4,5},{5,4},{6,7},{7,6},{8,9},{9,8},{10,11... | collective-permute-start | bytes 3145736 | tf_op jit(solution)/shard_map/ppermute | solution.py:148
  144.8 10.2 %collective-permute-start.30 = (bf16[1024,512]{1,0:T(8,128)(2,1)S(1)}, bf16[1024,512]{1,0:T(8,128)(2,1)S(1)}, u32[]{:S(2)}, u32[]{:S(2)}) collective-permute-start(bf16[1024,512]{1,0:T(8,128)(2,1)S(1)} %collective-permute-done.18.er), channel_id=1, source_target_pairs={{0,1},{1,0},{2,3},{3,2},{4,5},{5,4},{6,7},{7,6},{8,9},{9,8},{10,11... | collective-permute-start | bytes 3145736 | tf_op jit(solution)/shard_map/ppermute | solution.py:148
  145.3 9.7 %collective-permute-start.31 = (bf16[1024,512]{1,0:T(8,128)(2,1)S(1)}, bf16[1024,512]{1,0:T(8,128)(2,1)S(1)}, u32[]{:S(2)}, u32[]{:S(2)}) collective-permute-start(bf16[1024,512]{1,0:T(8,128)(2,1)S(1)} %get-tuple-element.119.d8), channel_id=1, source_target_pairs={{0,1},{1,0},{2,3},{3,2},{4,5},{5,4},{6,7},{7,6},{8,9},{9,8},{10,11... | collective-permute-start | bytes 3145736 | tf_op jit(solution)/shard_map/ppermute | solution.py:148
  145.4 9.6 %collective-permute-start.32 = (bf16[1024,512]{1,0:T(8,128)(2,1)S(1)}, bf16[1024,512]{1,0:T(8,128)(2,1)S(1)}, u32[]{:S(2)}, u32[]{:S(2)}) collective-permute-start(bf16[1024,512]{1,0:T(8,128)(2,1)S(1)} %collective-permute-done.19.dr), channel_id=1, source_target_pairs={{0,1},{1,0},{2,3},{3,2},{4,5},{5,4},{6,7},{7,6},{8,9},{9,8},{10,11... | collective-permute-start | bytes 3145736 | tf_op jit(solution)/shard_map/ppermute | solution.py:148
  149.5 3.8 %collective-permute-start.28 = (bf16[448,256]{1,0:T(8,128)(2,1)S(1)}, bf16[448,256]{1,0:T(8,128)(2,1)S(1)}, u32[]{:S(2)}, u32[]{:S(2)}) collective-permute-start(bf16[448,256]{1,0:T(8,128)(2,1)S(1)} %get-tuple-element.114), channel_id=1, source_target_pairs={{0,1},{1,0},{2,3},{3,2},{4,5},{5,4},{6,7},{7,6},{8,9},{9,8},{10,11... | collective-permute-start | bytes 688136 | tf_op jit(solution)/shard_map/ppermute | solution.py:148
  (8 other events, 19.2 us)

commit v5 on v4

--- a/solution.py
+++ b/solution.py
@@ -137,9 +137,8 @@
 IN1, IN2 = ("z1", "y", "z2", "x"), ("z2", "z1", "y", "x")
 IN3, IN4 = ("z1", "z2", "x", "y"), ("z2", "x", "z1", "y")
 OUT1, OUT2 = ("z2", "x", "y", "z1"), ("z1", "y", "x", "z2")
-NOTES = ("x", "z1", "z2", "y")
+NOTES = ("z1", "z2", "y", "x")
 SMALL = 48
-META = 16
 TILE = 64
 
 
@@ -206,15 +205,21 @@
     return lax.broadcasted_iota(jnp.int32, shape, 0), lax.broadcasted_iota(jnp.int32, shape, 1)
 
 
-def cut_kernel(lens, dest, offs, rows_ref, up_ref, down_ref):
-    for code, out_ref in ((1, up_ref), (7, down_ref)):
-        count, offset, start = local(lens, dest, offs, code)
-        spot, slot = grid_of(MAXLEN + META, rows_ref.shape[0])
-        picker = hot((slot == start + spot) & (spot < count))
-        spot, _ = grid_of(MAXLEN + META, D)
-        note = jnp.where(spot == MAXLEN, count, 0) + jnp.where(spot == MAXLEN + 1, offset // 2, 0)
-        note = note + jnp.where(spot == MAXLEN + 2, offset % 2, 0)
-        out_ref[...] = (take(picker, rows_ref[...]) + note.astype(jnp.float32)).astype(jnp.bfloat16)
+def cut_kernel(lens, dest, offs, rows_ref, notes_ref, up_ref, down_ref, out_ref):
+    row, lane = grid_of(SMALL, LANE)
+    slot = lane - lax.axis_index("core") * (LANE // 2)
+    notes = notes_ref[...].astype(jnp.float32)
+    for which in range(3):
+        facts = (lens[0, which], dest[0, which], offs[0, which] // 2, offs[0, which] % 2)
+        for place, fact in enumerate(facts):
+            here = (slot == which) & (row == KERNEL + 2 + place)
+            notes = jnp.where(here, fact.astype(jnp.float32), notes)
+    out_ref[...] = notes.astype(jnp.bfloat16)
+    for code, sent_ref in ((1, up_ref), (7, down_ref)):
+        count, _, start = local(lens, dest, offs, code)
+        step, slot = grid_of(MAXLEN, rows_ref.shape[0])
+        picker = hot((slot == start + step) & (step < count))
+        sent_ref[...] = take(picker, rows_ref[...]).astype(jnp.bfloat16)
 
 
 def smem(count):
@@ -237,59 +242,70 @@
     return pltpu.CompilerParams(vmem_limit_bytes=mebibytes * 2**20)
 
 
-def cut(lens, dest, offs, rows):
-    sent = shape(MAXLEN + META, D)
+def cut(lens, dest, offs, rows, notes):
+    sent = shape(MAXLEN, D)
     return pl.pallas_call(
         cut_kernel,
-        out_shape=(sent, sent),
-        in_specs=smem(3) + vmem(1),
-        out_specs=tuple(vmem(2)),
+        out_shape=(sent, sent, shape(SMALL, LANE)),
+        in_specs=smem(3) + vmem(2),
+        out_specs=tuple(vmem(3)),
         compiler_params=limits(16),
         cost_estimate=COST,
         name="cut",
-    )(lens, dest, offs, rows)
-
-
-def place_kernel(lens, dest, offs, rows_ref, prev_ref, next_ref, spread_ref, base_ref, pick_ref):
+    )(lens, dest, offs, rows, notes)
+
+
+def place_kernel(lens, dest, offs, rows_ref, prev_ref, next_ref, notes_ref, spread_ref, base_ref, pick_ref):
     count, offset, start = local(lens, dest, offs, 0)
+    z, y, x, core = coordinates()
+    here = z * 2 + y
     ones = jnp.ones((1, 1), jnp.int32)
 
-    def noted(ref):
-        head = ref[MAXLEN : MAXLEN + META, 0:LANE].astype(jnp.float32).astype(jnp.int32)
-        return head[0:1, 0:1], head[1:2, 0:1] * 2 + head[2:3, 0:1]
-
-    parts = [(count * ones, offset * ones), noted(prev_ref), noted(next_ref)]
+    def noted(place):
+        block = (place >> 1) * 4 + (place & 1) * 2 + x
+        note = notes_ref[32:SMALL, lanes(spot(NOTES[0:3], block))].astype(jnp.float32)
+        _, lane = grid_of(1, LANE)
+        slot = lane - core * (LANE // 2)
+        ours = (slot >= 0) & (slot < 3) & (note[3:4].astype(jnp.int32) == here)
+
+        def chosen(row):
+            found = jnp.sum(jnp.where(ours, note[row : row + 1], 0.0), axis=-1, keepdims=True)
+            return found.astype(jnp.int32)
+
+        return chosen(2), chosen(4) * 2 + chosen(5)
+
+    parts = [(count * ones, offset * ones), noted((here + 7) & 7), noted((here + 1) & 7)]
 
     def placer(which, width, first):
         mine = parts[which]
         rank = sum((other[1] < mine[1]).astype(jnp.int32) for other in parts)
-        spot, slot = grid_of(PAD, width)
+        step, slot = grid_of(PAD, width)
         source = slot - first
         inside = (source >= 0) & (source < mine[0])
-        return hot((spot == GAP + mine[1] + GAP * rank + source) & inside)
+        return hot((step == GAP + mine[1] + GAP * rank + source) & inside)
 
     from_own = placer(0, rows_ref.shape[0], start)
-    from_prev = placer(1, MAXLEN + META, 0)
-    from_next = placer(2, MAXLEN + META, 0)
+    from_prev = placer(1, MAXLEN, 0)
+    from_next = placer(2, MAXLEN, 0)
     found = take(from_own, rows_ref[...]) + take(from_prev, prev_ref[...]) + take(from_next, next_ref[...])
     spread_ref[...] = found.astype(jnp.bfloat16)
-    flat, spot = grid_of(RCV_DEV, PAD)
+    flat, step = grid_of(RCV_DEV, PAD)
     rank = sum((part[1] <= flat).astype(jnp.int32) for part in parts)
-    pick = hot(spot == flat + GAP * rank)
+    pick = hot(step == flat + GAP * rank)
     pick_ref[...] = pick
     base_ref[...] = take(pick, spread_ref[...]).astype(jnp.bfloat16)
 
 
-def place(lens, dest, offs, rows, arrived):
+def place(lens, dest, offs, rows, prev, next_, notes):
     return pl.pallas_call(
         place_kernel,
         out_shape=(shape(PAD, D), shape(RCV_DEV, D), shape(RCV_DEV, PAD)),
-        in_specs=smem(3) + vmem(3),
+        in_specs=smem(3) + vmem(4),
         out_specs=tuple(vmem(3)),
         compiler_params=limits(24),
         cost_estimate=COST,
         name="place",
-    )(lens, dest, offs, rows, *arrived)
+    )(lens, dest, offs, rows, prev, next_, notes)
 
 
 def prep_kernel(mine_ref, other_ref, notes_ref, out1, out2, out3, out4, small_ref):
@@ -423,35 +439,30 @@
     for load in loads:
         load.start()
     half = lax.axis_index("core")
-    count = KERNEL + 1
-    pieces = [(half, (m0, m1, m2, m3)), (1 - half, (o0, o1, o2, o3))]
-    refs = [ref for _, group in pieces for ref in group]
-    total = jnp.zeros((PAD, 1), jnp.float32)
-    for ref in refs:
-        total = total + jnp.sum(ref[...].astype(jnp.float32), axis=-1, keepdims=True)
-    mean = total / D
-    total = jnp.zeros((PAD, 1), jnp.float32)
-    for ref in refs:
-        center = ref[...].astype(jnp.float32) - mean
-        total = total + jnp.sum(center * center, axis=-1, keepdims=True)
-    scale = lax.rsqrt(total / D + epsilon)
-    for side, group in pieces:
-        place = side * (BLOCKS // 2)
+    pieces = []
+    for side, group in ((half, (m0, m1, m2, m3)), (1 - half, (o0, o1, o2, o3))):
+        block = side * (BLOCKS // 2)
         for ref in group:
-            blocks = [place + tile for tile in range(ref.shape[1] // LANE)]
-            place = place + len(blocks)
-            parts = []
-            for tile, block in enumerate(blocks):
-                gain = small_ref[count : count + 1, lanes(block)]
-                values = ref[:, tile * LANE : (tile + 1) * LANE].astype(jnp.float32)
-                post = (values - mean) * scale * gain
-                parts.append((post * jax.nn.sigmoid(post)).astype(jnp.bfloat16))
-            kept = take(pick_ref[...], beside(*parts) if len(parts) > 1 else parts[0])
-            kept = kept.astype(jnp.bfloat16)
-            for tile, block in enumerate(blocks):
-                part = kept[:, tile * LANE : (tile + 1) * LANE]
-                first[:, lanes(spot(OUT1, block))] = part
-                second[:, lanes(spot(OUT2, block))] = part
+            for tile in range(ref.shape[1] // LANE):
+                pieces.append((block, ref[:, tile * LANE : (tile + 1) * LANE].astype(jnp.float32)))
+                block = block + 1
+    mean = jnp.sum(sum(values for _, values in pieces), axis=-1, keepdims=True) / D
+    total = jnp.zeros((PAD, LANE), jnp.float32)
+    for _, values in pieces:
+        center = values - mean
+        total = total + center * center
+    scale = lax.rsqrt(jnp.sum(total, axis=-1, keepdims=True) / D + epsilon)
+    for place in range(0, BLOCKS, 2):
+        parts = []
+        for block, values in pieces[place : place + 2]:
+            gain = small_ref[KERNEL + 1 : KERNEL + 2, lanes(block)]
+            post = (values - mean) * scale * gain
+            parts.append((post * jax.nn.sigmoid(post)).astype(jnp.bfloat16))
+        kept = take(pick_ref[...], beside(*parts)).astype(jnp.bfloat16)
+        for tile, (block, _) in enumerate(pieces[place : place + 2]):
+            part = kept[:, tile * LANE : (tile + 1) * LANE]
+            first[:, lanes(spot(OUT1, block))] = part
+            second[:, lanes(spot(OUT2, block))] = part
     width = HALF // 2
     loads[len(sources)].wait()
     stores = []
@@ -496,7 +507,12 @@
     per = weight_in.shape[0]
 
     rows = frames[0]
-    up, down = cut(lengths, destination, offsets, rows)
+    notes = jnp.concatenate(
+        [depth_kernel.T, norm_gain[None], post_gain[None], jnp.zeros((SMALL - KERNEL - 2, per), jnp.bfloat16)], 0
+    )
+    blank = jnp.zeros_like(notes)
+    notes = jnp.where(low, beside(notes, blank), beside(blank, notes))
+    up, down, notes = cut(lengths, destination, offsets, rows, notes)
     left = beside(weight_in[:, 0:HALF], weight_in[:, D : D + HALF], weight_out[:, 0:HALF])
     right = beside(weight_in[:, HALF:D], weight_in[:, D + HALF :], weight_out[:, HALF:])
     kept, given = jnp.where(low, left, right), jnp.where(low, right, left)
@@ -504,11 +520,6 @@
     chip = jnp.where(low, stack(kept, got), stack(got, kept))
     chip, up, down = tie(chip, up, down)
 
-    notes = jnp.concatenate(
-        [depth_kernel.T, norm_gain[None], post_gain[None], jnp.zeros((SMALL - KERNEL - 2, per), jnp.bfloat16)], 0
-    )
-    blank = jnp.zeros_like(notes)
-    notes = jnp.where(low, beside(notes, blank), beside(blank, notes))
     notes = notes + hop(notes, "c")
 
     def span(which):
@@ -536,7 +547,7 @@
     in1_out2, in3, in4_out1, in2, notes = tie(
         stack(in1_out2, far[0]), stack(in3, far[1]), stack(in4_out1, far[2]), stack(in2, far[3]), wide(wide(notes, NOTES[1]), NOTES[2])
     )
-    spread, base, pick = place(lengths, destination, offsets, rows, (prev, next_))
+    spread, base, pick = place(lengths, destination, offsets, rows, prev, next_, notes)
 
     in1, in4 = in1_out2[:, 0:size], in4_out1[:, 0:size]
     in3_out2, in2_out1 = beside(in3, in1_out2[:, size:]), beside(in2, in4_out1[:, size:])

time: 164 us -> 161 us (0.982)
  waiting for transfers between devices: 83.3 us -> 79.3 us
    ppermute x2, waiting for transfers between devices: 18.9 us -> 16.3 us  [turn(): lax.ppermute(array, ('z', 'y'), [(i, (i + by) % 8) for i in range(8)])]
  transfers between devices with their start and end apart: 33 -> 33, of which waited for: 14 -> 13; matrix products, arithmetic and copies ran while one was open for 1% -> 1% of each run, Pallas kernels for 20% -> 20%
where the time goes in v5:
time: 161 us
  waiting for transfers between devices  79.3 us (49%)
  Pallas kernels  40.9 us (25%)
  starting transfers between devices  36.1 us (22%)
  local copies, waits for them, and re-layouts  2.23 us (1%)
  other arithmetic  1.65 us (1%)
    ppermute x31, waiting for transfers between devices, hop(): return lax.ppermute(array, axis, pairs)  63 us
    ppermute x31, starting transfers between devices, hop(): return lax.ppermute(array, axis, pairs)  31.4 us
    ppermute x2, waiting for transfers between devices, turn(): lax.ppermute(array, ('z', 'y'), [(i, (i + by) % 8) for i in range(8)])  16.3 us
    pallas_call x4, Pallas kernels, conv(): pl.pallas_call(functools.partial(conv_kernel, sub), out_shape=(out, out),...  14.7 us
    pallas_call x1, Pallas kernels, finish(): pl.pallas_call(finish_kernel, out_shape=shape(RCV_DEV, D), in_specs=vmem(...  8.36 us
    pallas_call x1, Pallas kernels, prep(): pl.pallas_call(prep_kernel, out_shape=(jax.ShapeDtypeStruct((2, PAIR, HAL...  6.71 us
    pallas_call x4, Pallas kernels, early(): pl.pallas_call(early_kernel, out_shape=shape(PAIR, near.shape[1], jnp.flo...  4.99 us
    ppermute x2, starting transfers between devices, turn(): lax.ppermute(array, ('z', 'y'), [(i, (i + by) % 8) for i in range(8)])  4.72 us
  transfers between devices with their start and end apart: 33, of which 13 were waited for; matrix products, arithmetic and copies ran while one was open for 1% of the time, Pallas kernels for 20%

profile of v5, /device:TPU:0, one launch (start us, length us, event | category | flops | bytes accessed | tf_op | source)
XLA Modules:
  0.0 160.8 jit_solution(14987762843813563303)
XLA Ops:
  0.0 1.4 fusion.5
  2.4 2.0 %cut.1 = (bf16[192,2048]{1,0:T(8,128)(2,1)S(1)}, bf16[192,2048]{1,0:T(8,128)(2,1)S(1)}, bf16[48,128]{1,0:T(8,128)(2,1)S(1)}) custom-call(s32[1,3]{1,0:T(1,128)S(1)} %copy-done.1, s32[1,3]{1,0:T(1,128)S(1)} %copy-done.2, s32[1,3]{1,0:T(1,128)S(1)} %copy-done.3, bf16[576,2048]{1,0:T(8,128)(2,1)S(1)} %bitcast.5, bf16[48,128]{1,0:T(8,128)(2,1)S(1)} %pad_select_fusion.notes_ref), custom_call_target="tpu_custom_call" | custom-call | flops 1048576 | bytes 65536 | tf_op jit(solution)/shard_map/cut/pallas_call | solution.py:247
  4.7 3.7 %collective-permute-start.2 = (bf16[128,1536]{1,0:T(8,128)(2,1)S(1)}, bf16[128,1536]{1,0:T(8,128)(2,1)S(1)}, u32[]{:S(2)}, u32[]{:S(2)}) collective-permute-start(bf16[128,1536]{1,0:T(8,128)(2,1)S(1)} %pad_maximum_fusion.14), channel_id=1, source_target_pairs={{0,16},{8,24},{16,0},{24,8},{1,17},{9,25},{17,1},{25,9},{2,18},{10... | collective-permute-start | bytes 1179656 | tf_op jit(solution)/shard_map/ppermute | solution.py:147
  8.5 1.6 collective-permute-start.1
  11.7 1.5 collective-permute-start.5
  13.2 3.2 %collective-permute-start.6 = (bf16[192,2048]{1,0:T(8,128)(2,1)S(1)}, bf16[192,2048]{1,0:T(8,128)(2,1)S(1)}, u32[]{:S(2)}, u32[]{:S(2)}) collective-permute-start(bf16[192,2048]{1,0:T(8,128)(2,1)S(1)} %get-tuple-element.71), channel_id=1, source_target_pairs={{0,28},{4,0},{8,4},{12,8},{16,12},{20,16},{24,20},{28,24},{1,29},{... | collective-permute-start | bytes 2359304 | tf_op jit(solution)/shard_map/ppermute | solution.py:151
  16.5 11.5 %collective-permute-done.4 = bf16[48,128]{1,0:T(8,128)(2,1)S(1)} collective-permute-done((bf16[48,128]{1,0:T(8,128)(2,1)S(1)}, bf16[48,128]{1,0:T(8,128)(2,1)S(1)}, u32[]{:S(2)}, u32[]{:S(2)}) %collective-permute-start.4) | collective-permute-done | bytes 12320 | tf_op jit(solution)/shard_map/ppermute | solution.py:147
  29.4 1.6 collective-permute-start.9
  31.0 1.8 %collective-permute-start.8 = (bf16[256,512]{1,0:T(8,128)(2,1)S(1)}, bf16[256,512]{1,0:T(8,128)(2,1)S(1)}, u32[]{:S(2)}, u32[]{:S(2)}) collective-permute-start(bf16[256,512]{1,0:T(8,128)(2,1)S(1)} %slice.99), channel_id=1, source_target_pairs={{0,16},{8,24},{16,0},{24,8},{1,17},{9,25},{17,1},{25,9},{2,18},{10... | collective-permute-start | bytes 786440 | tf_op jit(solution)/shard_map/ppermute | solution.py:147
  32.8 13.6 %collective-permute-done.5.prev_ref = bf16[192,2048]{1,0:T(8,128)(2,1)S(1)} collective-permute-done((bf16[192,2048]{1,0:T(8,128)(2,1)S(1)}, bf16[192,2048]{1,0:T(8,128)(2,1)S(1)}, u32[]{:S(2)}, u32[]{:S(2)}) %collective-permute-start.5) | collective-permute-done | bytes 786464 | tf_op jit(solution)/shard_map/ppermute | solution.py:151
  46.4 2.7 %collective-permute-done.6.next_ref = bf16[192,2048]{1,0:T(8,128)(2,1)S(1)} collective-permute-done((bf16[192,2048]{1,0:T(8,128)(2,1)S(1)}, bf16[192,2048]{1,0:T(8,128)(2,1)S(1)}, u32[]{:S(2)}, u32[]{:S(2)}) %collective-permute-start.6) | collective-permute-done | bytes 786464 | tf_op jit(solution)/shard_map/ppermute | solution.py:151
  49.4 2.5 %collective-permute-start.7 = (bf16[256,1024]{1,0:T(8,128)(2,1)S(1)}, bf16[256,1024]{1,0:T(8,128)(2,1)S(1)}, u32[]{:S(2)}, u32[]{:S(2)}) collective-permute-start(bf16[256,1024]{1,0:T(8,128)(2,1)S(1)} %slice.98), channel_id=1, source_target_pairs={{0,4},{4,0},{1,5},{5,1},{2,6},{6,2},{3,7},{7,3},{8,12},{12,8},{9,1... | collective-permute-start | bytes 1572872 | tf_op jit(solution)/shard_map/ppermute | solution.py:147
  51.9 3.5 %collective-permute-done.10 = bf16[256,512]{1,0:T(8,128)(2,1)S(1)} collective-permute-done((bf16[256,512]{1,0:T(8,128)(2,1)S(1)}, bf16[256,512]{1,0:T(8,128)(2,1)S(1)}, u32[]{:S(2)}, u32[]{:S(2)}) %collective-permute-start.10) | collective-permute-done | bytes 262176 | tf_op jit(solution)/shard_map/ppermute | solution.py:147
  55.4 1.7 %collective-permute-done.11 = bf16[48,256]{1,0:T(8,128)(2,1)S(1)} collective-permute-done((bf16[48,256]{1,0:T(8,128)(2,1)S(1)}, bf16[48,256]{1,0:T(8,128)(2,1)S(1)}, u32[]{:S(2)}, u32[]{:S(2)}) %collective-permute-start.11) | collective-permute-done | bytes 24608 | tf_op jit(solution)/shard_map/ppermute | solution.py:147
  57.2 1.6 collective-permute-start.12
  58.8 3.9 %collective-permute-done.12 = bf16[48,512]{1,0:T(8,128)(2,1)S(1)} collective-permute-done((bf16[48,512]{1,0:T(8,128)(2,1)S(1)}, bf16[48,512]{1,0:T(8,128)(2,1)S(1)}, u32[]{:S(2)}, u32[]{:S(2)}) %collective-permute-start.12) | collective-permute-done | bytes 49184 | tf_op jit(solution)/shard_map/ppermute | solution.py:147
  64.4 1.6 collective-permute-start.14
  66.0 2.7 %collective-permute-start.16 = (bf16[512,512]{1,0:T(8,128)(2,1)S(1)}, bf16[512,512]{1,0:T(8,128)(2,1)S(1)}, u32[]{:S(2)}, u32[]{:S(2)}) collective-permute-start(bf16[512,512]{1,0:T(8,128)(2,1)S(1)} %get-tuple-element.127), channel_id=1, source_target_pairs={{0,8},{8,0},{16,24},{24,16},{1,9},{9,1},{17,25},{25,17},{2,10},{10... | collective-permute-start | bytes 1572872 | tf_op jit(solution)/shard_map/ppermute | solution.py:147
  70.2 4.1 %place.1 = (bf16[448,2048]{1,0:T(8,128)(2,1)S(1)}, bf16[384,2048]{1,0:T(8,128)(2,1)S(1)}, bf16[384,448]{1,0:T(8,128)(2,1)S(1)}) custom-call(s32[1,3]{1,0:T(1,128)S(1)} %copy-done.1, s32[1,3]{1,0:T(1,128)S(1)} %copy-done.2, s32[1,3]{1,0:T(1,128)S(1)} %copy-done.3, bf16[576,2048]{1,0:T(8,128)(2,1)S(1)} %bitcast.6, ...), custom_call_target="tpu_custom_call" | custom-call | flops 1048576 | bytes 65536 | tf_op jit(solution)/shard_map/place/pallas_call | solution.py:300
  74.4 15.8 %collective-permute-done.17 = bf16[48,1024]{1,0:T(8,128)(2,1)S(1)} collective-permute-done((bf16[48,1024]{1,0:T(8,128)(2,1)S(1)}, bf16[48,1024]{1,0:T(8,128)(2,1)S(1)}, u32[]{:S(2)}, u32[]{:S(2)}) %collective-permute-start.17) | collective-permute-done | bytes 98336 | tf_op jit(solution)/shard_map/ppermute | solution.py:147
  91.0 1.6 collective-permute-start.25
  93.4 3.1 %collective-permute-start.19 = (bf16[1024,512]{1,0:T(8,128)(2,1)S(1)}, bf16[1024,512]{1,0:T(8,128)(2,1)S(1)}, u32[]{:S(2)}, u32[]{:S(2)}) collective-permute-start(bf16[1024,512]{1,0:T(8,128)(2,1)S(1)} %get-tuple-element.121.d8), channel_id=1, source_target_pairs={{0,16},{8,24},{16,0},{24,8},{1,17},{9,25},{17,1},{25,9},{2,18},{10... | collective-permute-start | bytes 3145736 | tf_op jit(solution)/shard_map/ppermute | solution.py:147
  96.5 6.7 %prep.1 = (bf16[2,896,1024]{2,1,0:T(8,128)(2,1)S(1)}, bf16[2,896,1024]{2,1,0:T(8,128)(2,1)S(1)}, bf16[2,896,1024]{2,1,0:T(8,128)(2,1)S(1)}, bf16[2,896,1024]{2,1,0:T(8,128)(2,1)S(1)}, f32[48,2048]{1,0:T(8,128)S(1)}) custom-call(bf16[448,2048]{1,0:T(8,128)(2,1)S(1)} %get-tuple-element.88.mine_ref, bf16[448,2048]{1,0:T(8,128)(2,1)S(1)} %collective-permute-done.20.other_ref, ...), custom_call_target="tpu_custom_call" | custom-call | flops 1048576 | bytes 65536 | tf_op jit(solution)/shard_map/prep/pallas_call | solution.py:335
  108.8 7.9 %collective-permute-done.25.far_hbm = bf16[1024,512]{1,0:T(8,128)(2,1)S(1)} collective-permute-done((bf16[1024,512]{1,0:T(8,128)(2,1)S(1)}, bf16[1024,512]{1,0:T(8,128)(2,1)S(1)}, u32[]{:S(2)}, u32[]{:S(2)}) %collective-permute-start.25) | collective-permute-done | bytes 1048608 | tf_op jit(solution)/shard_map/ppermute | solution.py:147
  116.6 1.5 collective-permute-start.22
  118.1 3.7 %conv.5 = (bf16[448,256]{1,0:T(8,128)(2,1)S(1)}, bf16[448,256]{1,0:T(8,128)(2,1)S(1)}) custom-call(bf16[2,896,1024]{2,1,0:T(8,128)(2,1)S(1)} %get-tuple-element.94.rows_hbm, f32[896,512]{1,0:T(8,128)S(1)} %early.6.part_hbm, bf16[1024,512]{1,0:T(8,128)(2,1)S(1)} %collective-permute-done.25.far_hbm, f32[48,2048]{1,0:T(8,128)S(1)} %get-tuple-element.99.small_ref), custom_call_target="tpu_custom_call" | custom-call | flops 1048576 | bytes 65536 | tf_op jit(solution)/shard_map/conv/pallas_call | solution.py:408
  121.9 3.7 %conv.4 = (bf16[448,256]{1,0:T(8,128)(2,1)S(1)}, bf16[448,256]{1,0:T(8,128)(2,1)S(1)}) custom-call(bf16[2,896,1024]{2,1,0:T(8,128)(2,1)S(1)} %get-tuple-element.91.rows_hbm, f32[896,512]{1,0:T(8,128)S(1)} %early.4.part_hbm, bf16[1024,512]{1,0:T(8,128)(2,1)S(1)} %collective-permute-done.23.far_hbm, f32[48,2048]{1,0:T(8,128)S(1)} %get-tuple-element.99.small_ref), custom_call_target="tpu_custom_call" | custom-call | flops 1048576 | bytes 65536 | tf_op jit(solution)/shard_map/conv/pallas_call | solution.py:408
  125.6 15.0 %collective-permute-done.18.er = bf16[1024,512]{1,0:T(8,128)(2,1)S(1)} collective-permute-done((bf16[1024,512]{1,0:T(8,128)(2,1)S(1)}, bf16[1024,512]{1,0:T(8,128)(2,1)S(1)}, u32[]{:S(2)}, u32[]{:S(2)}) %collective-permute-start.18) | collective-permute-done | bytes 1048608 | tf_op jit(solution)/shard_map/ppermute | solution.py:147
  140.6 1.3 collective-permute-done.19.dr
  143.1 3.7 %conv.7 = (bf16[448,256]{1,0:T(8,128)(2,1)S(1)}, bf16[448,256]{1,0:T(8,128)(2,1)S(1)}) custom-call(bf16[2,896,1024]{2,1,0:T(8,128)(2,1)S(1)} %get-tuple-element.95.rows_hbm, f32[896,512]{1,0:T(8,128)S(1)} %early.7.part_hbm, bf16[1024,512]{1,0:T(8,128)(2,1)S(1)} %collective-permute-done.22.far_hbm, f32[48,2048]{1,0:T(8,128)S(1)} %get-tuple-element.99.small_ref), custom_call_target="tpu_custom_call" | custom-call | flops 1048576 | bytes 65536 | tf_op jit(solution)/shard_map/conv/pallas_call | solution.py:408
  147.0 3.7 %conv.6 = (bf16[448,256]{1,0:T(8,128)(2,1)S(1)}, bf16[448,256]{1,0:T(8,128)(2,1)S(1)}) custom-call(bf16[2,896,1024]{2,1,0:T(8,128)(2,1)S(1)} %get-tuple-element.93.rows_hbm, f32[896,512]{1,0:T(8,128)S(1)} %early.5.part_hbm, bf16[1024,512]{1,0:T(8,128)(2,1)S(1)} %collective-permute-done.21.far_hbm, f32[48,2048]{1,0:T(8,128)S(1)} %get-tuple-element.99.small_ref), custom_call_target="tpu_custom_call" | custom-call | flops 1048576 | bytes 65536 | tf_op jit(solution)/shard_map/conv/pallas_call | solution.py:408
  152.3 8.4 %finish.1 = bf16[384,2048]{1,0:T(8,128)(2,1)} custom-call(bf16[448,256]{1,0:T(8,128)(2,1)S(1)} %get-tuple-element.105.m0, bf16[448,256]{1,0:T(8,128)(2,1)S(1)} %get-tuple-element.108.m1, bf16[448,256]{1,0:T(8,128)(2,1)S(1)} %get-tuple-element.109.m2, bf16[448,256]{1,0:T(8,128)(2,1)S(1)} %get-tuple-element.112.m3, ...), custom_call_target="tpu_custom_call" | custom-call | flops 1048576 | bytes 65536 | tf_op jit(solution)/shard_map/finish/pallas_call | solution.py:484
  (99 shorter events, 18.2 us)
Async XLA Ops:
  1.6 2.8 %collective-permute-start = (bf16[64,3072]{1,0:T(8,128)(2,1)S(1)}, bf16[64,3072]{1,0:T(8,128)(2,1)S(1)}, u32[]{:S(2)}, u32[]{:S(2)}) collective-permute-start(bf16[64,3072]{1,0:T(8,128)(2,1)S(1)} %get-tuple-element.136), channel_id=1, source_target_pairs={{0,1},{1,0},{2,3},{3,2},{4,5},{5,4},{6,7},{7,6},{8,9},{9,8},{10,11... | collective-permute-start | bytes 1179656 | tf_op jit(solution)/shard_map/ppermute | solution.py:147
  4.7 23.2 %collective-permute-start.2 = (bf16[128,1536]{1,0:T(8,128)(2,1)S(1)}, bf16[128,1536]{1,0:T(8,128)(2,1)S(1)}, u32[]{:S(2)}, u32[]{:S(2)}) collective-permute-start(bf16[128,1536]{1,0:T(8,128)(2,1)S(1)} %pad_maximum_fusion.14), channel_id=1, source_target_pairs={{0,16},{8,24},{16,0},{24,8},{1,17},{9,25},{17,1},{25,9},{2,18},{10... | collective-permute-start | bytes 1179656 | tf_op jit(solution)/shard_map/ppermute | solution.py:147
  8.5 19.6 %collective-permute-start.1 = (bf16[128,1536]{1,0:T(8,128)(2,1)S(1)}, bf16[128,1536]{1,0:T(8,128)(2,1)S(1)}, u32[]{:S(2)}, u32[]{:S(2)}) collective-permute-start(bf16[128,1536]{1,0:T(8,128)(2,1)S(1)} %get-tuple-element.134), channel_id=1, source_target_pairs={{0,8},{8,0},{16,24},{24,16},{1,9},{9,1},{17,25},{25,17},{2,10},{10... | collective-permute-start | bytes 1179656 | tf_op jit(solution)/shard_map/ppermute | solution.py:147
  11.2 16.7 %collective-permute-start.4 = (bf16[48,128]{1,0:T(8,128)(2,1)S(1)}, bf16[48,128]{1,0:T(8,128)(2,1)S(1)}, u32[]{:S(2)}, u32[]{:S(2)}) collective-permute-start(bf16[48,128]{1,0:T(8,128)(2,1)S(1)} %add.7), channel_id=1, source_target_pairs={{0,8},{8,0},{16,24},{24,16},{1,9},{9,1},{17,25},{25,17},{2,10},{10... | collective-permute-start | bytes 36872 | tf_op jit(solution)/shard_map/ppermute | solution.py:147
  11.7 34.7 %collective-permute-start.5 = (bf16[192,2048]{1,0:T(8,128)(2,1)S(1)}, bf16[192,2048]{1,0:T(8,128)(2,1)S(1)}, u32[]{:S(2)}, u32[]{:S(2)}) collective-permute-start(bf16[192,2048]{1,0:T(8,128)(2,1)S(1)} %get-tuple-element.70), channel_id=1, source_target_pairs={{0,4},{4,8},{8,12},{12,16},{16,20},{20,24},{24,28},{28,0},{1,5},{5... | collective-permute-start | bytes 2359304 | tf_op jit(solution)/shard_map/ppermute | solution.py:151
  13.2 35.8 %collective-permute-start.6 = (bf16[192,2048]{1,0:T(8,128)(2,1)S(1)}, bf16[192,2048]{1,0:T(8,128)(2,1)S(1)}, u32[]{:S(2)}, u32[]{:S(2)}) collective-permute-start(bf16[192,2048]{1,0:T(8,128)(2,1)S(1)} %get-tuple-element.71), channel_id=1, source_target_pairs={{0,28},{4,0},{8,4},{12,8},{16,12},{20,16},{24,20},{28,24},{1,29},{... | collective-permute-start | bytes 2359304 | tf_op jit(solution)/shard_map/ppermute | solution.py:151
  28.1 27.3 %collective-permute-start.10 = (bf16[256,512]{1,0:T(8,128)(2,1)S(1)}, bf16[256,512]{1,0:T(8,128)(2,1)S(1)}, u32[]{:S(2)}, u32[]{:S(2)}) collective-permute-start(bf16[256,512]{1,0:T(8,128)(2,1)S(1)} %slice.101), channel_id=1, source_target_pairs={{0,8},{8,0},{16,24},{24,16},{1,9},{9,1},{17,25},{25,17},{2,10},{10... | collective-permute-start | bytes 786440 | tf_op jit(solution)/shard_map/ppermute | solution.py:147
  29.4 33.3 %collective-permute-start.9 = (bf16[256,1024]{1,0:T(8,128)(2,1)S(1)}, bf16[256,1024]{1,0:T(8,128)(2,1)S(1)}, u32[]{:S(2)}, u32[]{:S(2)}) collective-permute-start(bf16[256,1024]{1,0:T(8,128)(2,1)S(1)} %slice.100), channel_id=1, source_target_pairs={{0,2},{2,0},{1,3},{3,1},{4,6},{6,4},{5,7},{7,5},{8,10},{10,8},{9,1... | collective-permute-start | bytes 1572872 | tf_op jit(solution)/shard_map/ppermute | solution.py:147
  31.0 27.8 %collective-permute-start.8 = (bf16[256,512]{1,0:T(8,128)(2,1)S(1)}, bf16[256,512]{1,0:T(8,128)(2,1)S(1)}, u32[]{:S(2)}, u32[]{:S(2)}) collective-permute-start(bf16[256,512]{1,0:T(8,128)(2,1)S(1)} %slice.99), channel_id=1, source_target_pairs={{0,16},{8,24},{16,0},{24,8},{1,17},{9,25},{17,1},{25,9},{2,18},{10... | collective-permute-start | bytes 786440 | tf_op jit(solution)/shard_map/ppermute | solution.py:147
  49.1 8.1 %collective-permute-start.11 = (bf16[48,256]{1,0:T(8,128)(2,1)S(1)}, bf16[48,256]{1,0:T(8,128)(2,1)S(1)}, u32[]{:S(2)}, u32[]{:S(2)}) collective-permute-start(bf16[48,256]{1,0:T(8,128)(2,1)S(1)} %pad_maximum_fusion.18), channel_id=1, source_target_pairs={{0,16},{8,24},{16,0},{24,8},{1,17},{9,25},{17,1},{25,9},{2,18},{10... | collective-permute-start | bytes 73736 | tf_op jit(solution)/shard_map/ppermute | solution.py:147
  49.4 13.3 %collective-permute-start.7 = (bf16[256,1024]{1,0:T(8,128)(2,1)S(1)}, bf16[256,1024]{1,0:T(8,128)(2,1)S(1)}, u32[]{:S(2)}, u32[]{:S(2)}) collective-permute-start(bf16[256,1024]{1,0:T(8,128)(2,1)S(1)} %slice.98), channel_id=1, source_target_pairs={{0,4},{4,0},{1,5},{5,1},{2,6},{6,2},{3,7},{7,3},{8,12},{12,8},{9,1... | collective-permute-start | bytes 1572872 | tf_op jit(solution)/shard_map/ppermute | solution.py:147
  57.2 5.5 %collective-permute-start.12 = (bf16[48,512]{1,0:T(8,128)(2,1)S(1)}, bf16[48,512]{1,0:T(8,128)(2,1)S(1)}, u32[]{:S(2)}, u32[]{:S(2)}) collective-permute-start(bf16[48,512]{1,0:T(8,128)(2,1)S(1)} %pad_maximum_fusion.17), channel_id=1, source_target_pairs={{0,4},{4,0},{1,5},{5,1},{2,6},{6,2},{3,7},{7,3},{8,12},{12,8},{9,1... | collective-permute-start | bytes 147464 | tf_op jit(solution)/shard_map/ppermute | solution.py:147
  63.1 27.2 %collective-permute-start.15 = (bf16[512,1024]{1,0:T(8,128)(2,1)S(1)}, bf16[512,1024]{1,0:T(8,128)(2,1)S(1)}, u32[]{:S(2)}, u32[]{:S(2)}) collective-permute-start(bf16[512,1024]{1,0:T(8,128)(2,1)S(1)} %pad_maximum_fusion.6), channel_id=1, source_target_pairs={{0,4},{4,0},{1,5},{5,1},{2,6},{6,2},{3,7},{7,3},{8,12},{12,8},{9,1... | collective-permute-start | bytes 3145736 | tf_op jit(solution)/shard_map/ppermute | solution.py:147
  64.4 26.1 %collective-permute-start.14 = (bf16[512,1024]{1,0:T(8,128)(2,1)S(1)}, bf16[512,1024]{1,0:T(8,128)(2,1)S(1)}, u32[]{:S(2)}, u32[]{:S(2)}) collective-permute-start(bf16[512,1024]{1,0:T(8,128)(2,1)S(1)} %pad_maximum_fusion.5), channel_id=1, source_target_pairs={{0,2},{2,0},{1,3},{3,1},{4,6},{6,4},{5,7},{7,5},{8,10},{10,8},{9,1... | collective-permute-start | bytes 3145736 | tf_op jit(solution)/shard_map/ppermute | solution.py:147
  66.0 24.1 %collective-permute-start.16 = (bf16[512,512]{1,0:T(8,128)(2,1)S(1)}, bf16[512,512]{1,0:T(8,128)(2,1)S(1)}, u32[]{:S(2)}, u32[]{:S(2)}) collective-permute-start(bf16[512,512]{1,0:T(8,128)(2,1)S(1)} %get-tuple-element.127), channel_id=1, source_target_pairs={{0,8},{8,0},{16,24},{24,16},{1,9},{9,1},{17,25},{25,17},{2,10},{10... | collective-permute-start | bytes 1572872 | tf_op jit(solution)/shard_map/ppermute | solution.py:147
  68.7 21.5 %collective-permute-start.13 = (bf16[512,512]{1,0:T(8,128)(2,1)S(1)}, bf16[512,512]{1,0:T(8,128)(2,1)S(1)}, u32[]{:S(2)}, u32[]{:S(2)}) collective-permute-start(bf16[512,512]{1,0:T(8,128)(2,1)S(1)} %get-tuple-element.130), channel_id=1, source_target_pairs={{0,16},{8,24},{16,0},{24,8},{1,17},{9,25},{17,1},{25,9},{2,18},{10... | collective-permute-start | bytes 1572872 | tf_op jit(solution)/shard_map/ppermute | solution.py:147
  69.7 20.4 %collective-permute-start.17 = (bf16[48,1024]{1,0:T(8,128)(2,1)S(1)}, bf16[48,1024]{1,0:T(8,128)(2,1)S(1)}, u32[]{:S(2)}, u32[]{:S(2)}) collective-permute-start(bf16[48,1024]{1,0:T(8,128)(2,1)S(1)} %pad_maximum_fusion.16.notes_ref), channel_id=1, source_target_pairs={{0,2},{2,0},{1,3},{3,1},{4,6},{6,4},{5,7},{7,5},{8,10},{10,8},{9,1... | collective-permute-start | bytes 294920 | tf_op jit(solution)/shard_map/ppermute | solution.py:147
  90.8 5.7 %collective-permute-start.20 = (bf16[448,2048]{1,0:T(8,128)(2,1)S(1)}, bf16[448,2048]{1,0:T(8,128)(2,1)S(1)}, u32[]{:S(2)}, u32[]{:S(2)}) collective-permute-start(bf16[448,2048]{1,0:T(8,128)(2,1)S(1)} %get-tuple-element.88.mine_ref), channel_id=1, source_target_pairs={{0,1},{1,0},{2,3},{3,2},{4,5},{5,4},{6,7},{7,6},{8,9},{9,8},{10,11... | collective-permute-start | bytes 5505032 | tf_op jit(solution)/shard_map/ppermute | solution.py:147
  91.0 25.6 %collective-permute-start.25 = (bf16[1024,512]{1,0:T(8,128)(2,1)S(1)}, bf16[1024,512]{1,0:T(8,128)(2,1)S(1)}, u32[]{:S(2)}, u32[]{:S(2)}) collective-permute-start(bf16[1024,512]{1,0:T(8,128)(2,1)S(1)} %get-tuple-element.123.near_ref), channel_id=1, source_target_pairs={{0,4},{4,0},{1,5},{5,1},{2,6},{6,2},{3,7},{7,3},{8,12},{12,8},{9,1... | collective-permute-start | bytes 3145736 | tf_op jit(solution)/shard_map/ppermute | solution.py:147
  92.6 29.3 %collective-permute-start.23 = (bf16[1024,512]{1,0:T(8,128)(2,1)S(1)}, bf16[1024,512]{1,0:T(8,128)(2,1)S(1)}, u32[]{:S(2)}, u32[]{:S(2)}) collective-permute-start(bf16[1024,512]{1,0:T(8,128)(2,1)S(1)} %pad_maximum_fusion.4.near_ref), channel_id=1, source_target_pairs={{0,2},{2,0},{1,3},{3,1},{4,6},{6,4},{5,7},{7,5},{8,10},{10,8},{9,1... | collective-permute-start | bytes 3145736 | tf_op jit(solution)/shard_map/ppermute | solution.py:147
  93.3 47.3 %collective-permute-start.18 = (bf16[1024,512]{1,0:T(8,128)(2,1)S(1)}, bf16[1024,512]{1,0:T(8,128)(2,1)S(1)}, u32[]{:S(2)}, u32[]{:S(2)}) collective-permute-start(bf16[1024,512]{1,0:T(8,128)(2,1)S(1)} %get-tuple-element.119.e8), channel_id=1, source_target_pairs={{0,8},{8,0},{16,24},{24,16},{1,9},{9,1},{17,25},{25,17},{2,10},{10... | collective-permute-start | bytes 3145736 | tf_op jit(solution)/shard_map/ppermute | solution.py:147
  93.4 48.6 %collective-permute-start.19 = (bf16[1024,512]{1,0:T(8,128)(2,1)S(1)}, bf16[1024,512]{1,0:T(8,128)(2,1)S(1)}, u32[]{:S(2)}, u32[]{:S(2)}) collective-permute-start(bf16[1024,512]{1,0:T(8,128)(2,1)S(1)} %get-tuple-element.121.d8), channel_id=1, source_target_pairs={{0,16},{8,24},{16,0},{24,8},{1,17},{9,25},{17,1},{25,9},{2,18},{10... | collective-permute-start | bytes 3145736 | tf_op jit(solution)/shard_map/ppermute | solution.py:147
  108.2 33.9 %collective-permute-start.21 = (bf16[1024,512]{1,0:T(8,128)(2,1)S(1)}, bf16[1024,512]{1,0:T(8,128)(2,1)S(1)}, u32[]{:S(2)}, u32[]{:S(2)}) collective-permute-start(bf16[1024,512]{1,0:T(8,128)(2,1)S(1)} %get-tuple-element.96.near_ref), channel_id=1, source_target_pairs={{0,2},{2,0},{1,3},{3,1},{4,6},{6,4},{5,7},{7,5},{8,10},{10,8},{9,1... | collective-permute-start | bytes 3145736 | tf_op jit(solution)/shard_map/ppermute | solution.py:147
  116.6 25.5 %collective-permute-start.22 = (bf16[1024,512]{1,0:T(8,128)(2,1)S(1)}, bf16[1024,512]{1,0:T(8,128)(2,1)S(1)}, u32[]{:S(2)}, u32[]{:S(2)}) collective-permute-start(bf16[1024,512]{1,0:T(8,128)(2,1)S(1)} %pad_maximum_fusion.7.near_ref), channel_id=1, source_target_pairs={{0,4},{4,0},{1,5},{5,1},{2,6},{6,2},{3,7},{7,3},{8,12},{12,8},{9,1... | collective-permute-start | bytes 3145736 | tf_op jit(solution)/shard_map/ppermute | solution.py:147
  121.8 20.1 %collective-permute-start.26 = (bf16[448,256]{1,0:T(8,128)(2,1)S(1)}, bf16[448,256]{1,0:T(8,128)(2,1)S(1)}, u32[]{:S(2)}, u32[]{:S(2)}) collective-permute-start(bf16[448,256]{1,0:T(8,128)(2,1)S(1)} %get-tuple-element.104), channel_id=1, source_target_pairs={{0,1},{1,0},{2,3},{3,2},{4,5},{5,4},{6,7},{7,6},{8,9},{9,8},{10,11... | collective-permute-start | bytes 688136 | tf_op jit(solution)/shard_map/ppermute | solution.py:147
  140.6 1.5 collective-permute-start.24
  142.1 10.2 %collective-permute-start.29 = (bf16[1024,512]{1,0:T(8,128)(2,1)S(1)}, bf16[1024,512]{1,0:T(8,128)(2,1)S(1)}, u32[]{:S(2)}, u32[]{:S(2)}) collective-permute-start(bf16[1024,512]{1,0:T(8,128)(2,1)S(1)} %get-tuple-element.119.e8), channel_id=1, source_target_pairs={{0,1},{1,0},{2,3},{3,2},{4,5},{5,4},{6,7},{7,6},{8,9},{9,8},{10,11... | collective-permute-start | bytes 3145736 | tf_op jit(solution)/shard_map/ppermute | solution.py:147
  142.2 10.0 %collective-permute-start.30 = (bf16[1024,512]{1,0:T(8,128)(2,1)S(1)}, bf16[1024,512]{1,0:T(8,128)(2,1)S(1)}, u32[]{:S(2)}, u32[]{:S(2)}) collective-permute-start(bf16[1024,512]{1,0:T(8,128)(2,1)S(1)} %collective-permute-done.18.er), channel_id=1, source_target_pairs={{0,1},{1,0},{2,3},{3,2},{4,5},{5,4},{6,7},{7,6},{8,9},{9,8},{10,11... | collective-permute-start | bytes 3145736 | tf_op jit(solution)/shard_map/ppermute | solution.py:147
  142.6 9.7 %collective-permute-start.31 = (bf16[1024,512]{1,0:T(8,128)(2,1)S(1)}, bf16[1024,512]{1,0:T(8,128)(2,1)S(1)}, u32[]{:S(2)}, u32[]{:S(2)}) collective-permute-start(bf16[1024,512]{1,0:T(8,128)(2,1)S(1)} %get-tuple-element.121.d8), channel_id=1, source_target_pairs={{0,1},{1,0},{2,3},{3,2},{4,5},{5,4},{6,7},{7,6},{8,9},{9,8},{10,11... | collective-permute-start | bytes 3145736 | tf_op jit(solution)/shard_map/ppermute | solution.py:147
  142.8 9.5 %collective-permute-start.32 = (bf16[1024,512]{1,0:T(8,128)(2,1)S(1)}, bf16[1024,512]{1,0:T(8,128)(2,1)S(1)}, u32[]{:S(2)}, u32[]{:S(2)}) collective-permute-start(bf16[1024,512]{1,0:T(8,128)(2,1)S(1)} %collective-permute-done.19.dr), channel_id=1, source_target_pairs={{0,1},{1,0},{2,3},{3,2},{4,5},{5,4},{6,7},{7,6},{8,9},{9,8},{10,11... | collective-permute-start | bytes 3145736 | tf_op jit(solution)/shard_map/ppermute | solution.py:147
  146.8 3.9 %collective-permute-start.28 = (bf16[448,256]{1,0:T(8,128)(2,1)S(1)}, bf16[448,256]{1,0:T(8,128)(2,1)S(1)}, u32[]{:S(2)}, u32[]{:S(2)}) collective-permute-start(bf16[448,256]{1,0:T(8,128)(2,1)S(1)} %get-tuple-element.116), channel_id=1, source_target_pairs={{0,1},{1,0},{2,3},{3,2},{4,5},{5,4},{6,7},{7,6},{8,9},{9,8},{10,11... | collective-permute-start | bytes 688136 | tf_op jit(solution)/shard_map/ppermute | solution.py:147
  150.7 1.6 collective-permute-start.27
  (8 other events, 17.6 us)

commit v6 on v5

--- a/solution.py
+++ b/solution.py
@@ -343,44 +343,31 @@
     )(mine, other, notes)
 
 
-def early_kernel(rows_hbm, near_ref, out_ref, rows_ref, done):
-    load = pltpu.make_async_copy(rows_hbm.at[0], rows_ref, done)
-    load.start()
-    load.wait()
-    out_ref[...] = take(rows_ref[...], near_ref[...])
+def early_kernel(rows_ref, near_ref, out_ref):
+    out_ref[...] = take(rows_ref[0], near_ref[...])
 
 
 def early(rows, near):
     return pl.pallas_call(
         early_kernel,
         out_shape=shape(PAIR, near.shape[1], jnp.float32),
-        in_specs=anywhere(1) + vmem(1),
+        in_specs=vmem(2),
         out_specs=vmem(1)[0],
-        scratch_shapes=[pltpu.VMEM((PAIR, HALF), jnp.bfloat16), pltpu.SemaphoreType.DMA],
         compiler_params=limits(12),
         cost_estimate=COST,
         name="early",
     )(rows, near)
 
 
-def conv_kernel(sub, rows_hbm, part_hbm, far_hbm, small_ref, own_ref, other_ref, gated, taps, rows_ref, part_ref, far_ref, done):
+def conv_kernel(sub, rows_ref, part_ref, far_ref, small_ref, own_ref, other_ref, gated, taps):
     width = own_ref.shape[1]
     tiles = width // LANE
-    loads = [
-        pltpu.make_async_copy(rows_hbm.at[1], rows_ref, done.at[0]),
-        pltpu.make_async_copy(far_hbm, far_ref, done.at[1]),
-        pltpu.make_async_copy(part_hbm, part_ref, done.at[2]),
-    ]
-    for load in loads:
-        load.start()
     half = lax.axis_index("core")
     for tile in range(tiles):
         gated[tile, 0:GAP, :] = jnp.zeros((GAP, LANE), jnp.float32)
         gated[tile, GAP + PAIR : 2 * GAP + PAIR, :] = jnp.zeros((GAP, LANE), jnp.float32)
         taps[tile] = small_ref[0:KERNEL, lanes(half * (BLOCKS // 2) + sub + tile)]
-    for load in loads:
-        load.wait()
-    both = part_ref[...] + take(rows_ref[...], far_ref[...])
+    both = part_ref[...] + take(rows_ref[1], far_ref[...])
     mixed = both[:, 0:width] * jax.nn.sigmoid(both[:, width:])
     for tile in range(tiles):
         gated[tile, GAP : GAP + PAIR, :] = mixed[:, tile * LANE : (tile + 1) * LANE]
@@ -408,15 +395,11 @@
     return pl.pallas_call(
         functools.partial(conv_kernel, sub),
         out_shape=(out, out),
-        in_specs=anywhere(3) + vmem(1),
+        in_specs=vmem(4),
         out_specs=tuple(vmem(2)),
         scratch_shapes=[
             pltpu.VMEM((width // LANE, PAIR + 2 * GAP, LANE), jnp.float32),
             pltpu.VMEM((width // LANE, KERNEL, LANE), jnp.float32),
-            pltpu.VMEM((PAIR, HALF), jnp.bfloat16),
-            pltpu.VMEM(part.shape, part.dtype),
-            pltpu.VMEM(far.shape, far.dtype),
-            pltpu.SemaphoreType.DMA((3,)),
         ],
         compiler_params=limits(16),
         cost_estimate=COST,
@@ -425,19 +408,10 @@
 
 
 def finish_kernel(
-    m0, m1, m2, m3, o0, o1, o2, o3, small_ref, pick_ref, base_hbm,
-    e8, er, d8, dr, f8, fr, g8, gr, out_hbm, first, second, weights, base, result, done, sent,
+    m0, m1, m2, m3, o0, o1, o2, o3, small_ref, pick_ref, base,
+    e8, er, d8, dr, f8, fr, g8, gr, out_hbm, first, second, result, sent,
 ):
     sources = (e8, er, d8, dr, f8, fr, g8, gr)
-    loads = [
-        pltpu.make_async_copy(
-            source, weights.at[index // 2, pl.ds(index % 2 * HALF, HALF), :], done.at[index]
-        )
-        for index, source in enumerate(sources)
-    ]
-    loads.append(pltpu.make_async_copy(base_hbm, base, done.at[len(sources)]))
-    for load in loads:
-        load.start()
     half = lax.axis_index("core")
     pieces = []
     for side, group in ((half, (m0, m1, m2, m3)), (1 - half, (o0, o1, o2, o3))):
@@ -464,15 +438,13 @@
             first[:, lanes(spot(OUT1, block))] = part
             second[:, lanes(spot(OUT2, block))] = part
     width = HALF // 2
-    loads[len(sources)].wait()
     stores = []
     for turn_index, (side, active, edge) in enumerate(
         ((half, first, 0), (half, second, width), (1 - half, first, 0), (1 - half, second, width))
     ):
         at = pl.ds(pl.multiple_of(side * HALF + edge, width), width)
-        loads[2 * turn_index].wait()
-        loads[2 * turn_index + 1].wait()
-        mixed = take(active[...], weights[turn_index]) + base[:, at].astype(jnp.float32)
+        near, far = sources[2 * turn_index], sources[2 * turn_index + 1]
+        mixed = take(active[:, 0:HALF], near[...]) + take(active[:, HALF:D], far[...]) + base[:, at].astype(jnp.float32)
         result[turn_index] = mixed.astype(jnp.bfloat16)
         stores.append(pltpu.make_async_copy(result.at[turn_index], out_hbm.at[:, at], sent.at[turn_index]))
         stores[-1].start()
@@ -484,14 +456,11 @@
     return pl.pallas_call(
         finish_kernel,
         out_shape=shape(RCV_DEV, D),
-        in_specs=vmem(10) + anywhere(9),
+        in_specs=vmem(19),
         out_specs=anywhere(1)[0],
         scratch_shapes=[pltpu.VMEM((RCV_DEV, D), jnp.bfloat16)] * 2
         + [
-            pltpu.VMEM((4, D, HALF // 2), jnp.bfloat16),
-            pltpu.VMEM((RCV_DEV, D), jnp.bfloat16),
             pltpu.VMEM((4, RCV_DEV, HALF // 2), jnp.bfloat16),
-            pltpu.SemaphoreType.DMA((9,)),
             pltpu.SemaphoreType.DMA((4,)),
         ],
         compiler_params=limits(28),

time: 161 us -> 159 us (0.988)
  Pallas kernels: 40.9 us -> 37.6 us
  transfers between devices with their start and end apart: 33 -> 33, of which waited for: 13 -> 13; matrix products, arithmetic and copies ran while one was open for 1% -> 1% of each run, Pallas kernels for 20% -> 19%
where the time goes in v6:
time: 159 us
  waiting for transfers between devices  80.6 us (51%)
  Pallas kernels  37.6 us (24%)
  starting transfers between devices  36.1 us (23%)
  local copies, waits for them, and re-layouts  2.23 us (1%)
  other arithmetic  1.65 us (1%)
    ppermute x31, waiting for transfers between devices, hop(): return lax.ppermute(array, axis, pairs)  64.3 us
    ppermute x31, starting transfers between devices, hop(): return lax.ppermute(array, axis, pairs)  31.4 us
    ppermute x2, waiting for transfers between devices, turn(): lax.ppermute(array, ('z', 'y'), [(i, (i + by) % 8) for i in range(8)])  16.3 us
    pallas_call x4, Pallas kernels, conv(): pl.pallas_call(functools.partial(conv_kernel, sub), out_shape=(out, out),...  13.5 us
    pallas_call x1, Pallas kernels, finish(): pl.pallas_call(finish_kernel, out_shape=shape(RCV_DEV, D), in_specs=vmem(...  6.84 us
    pallas_call x1, Pallas kernels, prep(): pl.pallas_call(prep_kernel, out_shape=(jax.ShapeDtypeStruct((2, PAIR, HAL...  6.71 us
    ppermute x2, starting transfers between devices, turn(): lax.ppermute(array, ('z', 'y'), [(i, (i + by) % 8) for i in range(8)])  4.72 us
    pallas_call x4, Pallas kernels, early(): pl.pallas_call(early_kernel, out_shape=shape(PAIR, near.shape[1], jnp.flo...  4.44 us
  transfers between devices with their start and end apart: 33, of which 13 were waited for; matrix products, arithmetic and copies ran while one was open for 1% of the time, Pallas kernels for 19%

profile of v6, /device:TPU:0, one launch (start us, length us, event | category | flops | bytes accessed | tf_op | source)
XLA Modules:
  0.0 158.8 jit_solution(16188644891522098420)
XLA Ops:
  0.0 1.4 fusion.5
  2.4 2.0 %cut.1 = (bf16[192,2048]{1,0:T(8,128)(2,1)S(1)}, bf16[192,2048]{1,0:T(8,128)(2,1)S(1)}, bf16[48,128]{1,0:T(8,128)(2,1)S(1)}) custom-call(s32[1,3]{1,0:T(1,128)S(1)} %copy-done.1, s32[1,3]{1,0:T(1,128)S(1)} %copy-done.2, s32[1,3]{1,0:T(1,128)S(1)} %copy-done.3, bf16[576,2048]{1,0:T(8,128)(2,1)S(1)} %bitcast.5, bf16[48,128]{1,0:T(8,128)(2,1)S(1)} %pad_select_fusion.notes_ref), custom_call_target="tpu_custom_call" | custom-call | flops 1048576 | bytes 65536 | tf_op jit(solution)/shard_map/cut/pallas_call | solution.py:247
  4.7 3.7 %collective-permute-start.2 = (bf16[128,1536]{1,0:T(8,128)(2,1)S(1)}, bf16[128,1536]{1,0:T(8,128)(2,1)S(1)}, u32[]{:S(2)}, u32[]{:S(2)}) collective-permute-start(bf16[128,1536]{1,0:T(8,128)(2,1)S(1)} %pad_maximum_fusion.14), channel_id=1, source_target_pairs={{0,16},{8,24},{16,0},{24,8},{1,17},{9,25},{17,1},{25,9},{2,18},{10... | collective-permute-start | bytes 1179656 | tf_op jit(solution)/shard_map/ppermute | solution.py:147
  8.5 1.6 collective-permute-start.1
  11.7 1.5 collective-permute-start.5
  13.2 3.2 %collective-permute-start.6 = (bf16[192,2048]{1,0:T(8,128)(2,1)S(1)}, bf16[192,2048]{1,0:T(8,128)(2,1)S(1)}, u32[]{:S(2)}, u32[]{:S(2)}) collective-permute-start(bf16[192,2048]{1,0:T(8,128)(2,1)S(1)} %get-tuple-element.71), channel_id=1, source_target_pairs={{0,28},{4,0},{8,4},{12,8},{16,12},{20,16},{24,20},{28,24},{1,29},{... | collective-permute-start | bytes 2359304 | tf_op jit(solution)/shard_map/ppermute | solution.py:151
  16.5 11.5 %collective-permute-done.4 = bf16[48,128]{1,0:T(8,128)(2,1)S(1)} collective-permute-done((bf16[48,128]{1,0:T(8,128)(2,1)S(1)}, bf16[48,128]{1,0:T(8,128)(2,1)S(1)}, u32[]{:S(2)}, u32[]{:S(2)}) %collective-permute-start.4) | collective-permute-done | bytes 12320 | tf_op jit(solution)/shard_map/ppermute | solution.py:147
  29.4 1.6 collective-permute-start.9
  31.0 1.8 %collective-permute-start.8 = (bf16[256,512]{1,0:T(8,128)(2,1)S(1)}, bf16[256,512]{1,0:T(8,128)(2,1)S(1)}, u32[]{:S(2)}, u32[]{:S(2)}) collective-permute-start(bf16[256,512]{1,0:T(8,128)(2,1)S(1)} %slice.99), channel_id=1, source_target_pairs={{0,16},{8,24},{16,0},{24,8},{1,17},{9,25},{17,1},{25,9},{2,18},{10... | collective-permute-start | bytes 786440 | tf_op jit(solution)/shard_map/ppermute | solution.py:147
  32.8 13.6 %collective-permute-done.5.prev_ref = bf16[192,2048]{1,0:T(8,128)(2,1)S(1)} collective-permute-done((bf16[192,2048]{1,0:T(8,128)(2,1)S(1)}, bf16[192,2048]{1,0:T(8,128)(2,1)S(1)}, u32[]{:S(2)}, u32[]{:S(2)}) %collective-permute-start.5) | collective-permute-done | bytes 786464 | tf_op jit(solution)/shard_map/ppermute | solution.py:151
  46.4 2.7 %collective-permute-done.6.next_ref = bf16[192,2048]{1,0:T(8,128)(2,1)S(1)} collective-permute-done((bf16[192,2048]{1,0:T(8,128)(2,1)S(1)}, bf16[192,2048]{1,0:T(8,128)(2,1)S(1)}, u32[]{:S(2)}, u32[]{:S(2)}) %collective-permute-start.6) | collective-permute-done | bytes 786464 | tf_op jit(solution)/shard_map/ppermute | solution.py:151
  49.4 2.5 %collective-permute-start.7 = (bf16[256,1024]{1,0:T(8,128)(2,1)S(1)}, bf16[256,1024]{1,0:T(8,128)(2,1)S(1)}, u32[]{:S(2)}, u32[]{:S(2)}) collective-permute-start(bf16[256,1024]{1,0:T(8,128)(2,1)S(1)} %slice.98), channel_id=1, source_target_pairs={{0,4},{4,0},{1,5},{5,1},{2,6},{6,2},{3,7},{7,3},{8,12},{12,8},{9,1... | collective-permute-start | bytes 1572872 | tf_op jit(solution)/shard_map/ppermute | solution.py:147
  51.9 3.5 %collective-permute-done.10 = bf16[256,512]{1,0:T(8,128)(2,1)S(1)} collective-permute-done((bf16[256,512]{1,0:T(8,128)(2,1)S(1)}, bf16[256,512]{1,0:T(8,128)(2,1)S(1)}, u32[]{:S(2)}, u32[]{:S(2)}) %collective-permute-start.10) | collective-permute-done | bytes 262176 | tf_op jit(solution)/shard_map/ppermute | solution.py:147
  55.4 1.7 %collective-permute-done.11 = bf16[48,256]{1,0:T(8,128)(2,1)S(1)} collective-permute-done((bf16[48,256]{1,0:T(8,128)(2,1)S(1)}, bf16[48,256]{1,0:T(8,128)(2,1)S(1)}, u32[]{:S(2)}, u32[]{:S(2)}) %collective-permute-start.11) | collective-permute-done | bytes 24608 | tf_op jit(solution)/shard_map/ppermute | solution.py:147
  57.2 1.6 collective-permute-start.12
  58.8 3.9 %collective-permute-done.12 = bf16[48,512]{1,0:T(8,128)(2,1)S(1)} collective-permute-done((bf16[48,512]{1,0:T(8,128)(2,1)S(1)}, bf16[48,512]{1,0:T(8,128)(2,1)S(1)}, u32[]{:S(2)}, u32[]{:S(2)}) %collective-permute-start.12) | collective-permute-done | bytes 49184 | tf_op jit(solution)/shard_map/ppermute | solution.py:147
  64.4 1.6 collective-permute-start.14
  66.0 2.7 %collective-permute-start.16 = (bf16[512,512]{1,0:T(8,128)(2,1)S(1)}, bf16[512,512]{1,0:T(8,128)(2,1)S(1)}, u32[]{:S(2)}, u32[]{:S(2)}) collective-permute-start(bf16[512,512]{1,0:T(8,128)(2,1)S(1)} %get-tuple-element.127), channel_id=1, source_target_pairs={{0,8},{8,0},{16,24},{24,16},{1,9},{9,1},{17,25},{25,17},{2,10},{10... | collective-permute-start | bytes 1572872 | tf_op jit(solution)/shard_map/ppermute | solution.py:147
  70.2 4.1 %place.1 = (bf16[448,2048]{1,0:T(8,128)(2,1)S(1)}, bf16[384,2048]{1,0:T(8,128)(2,1)S(1)}, bf16[384,448]{1,0:T(8,128)(2,1)S(1)}) custom-call(s32[1,3]{1,0:T(1,128)S(1)} %copy-done.1, s32[1,3]{1,0:T(1,128)S(1)} %copy-done.2, s32[1,3]{1,0:T(1,128)S(1)} %copy-done.3, bf16[576,2048]{1,0:T(8,128)(2,1)S(1)} %bitcast.6, ...), custom_call_target="tpu_custom_call" | custom-call | flops 1048576 | bytes 65536 | tf_op jit(solution)/shard_map/place/pallas_call | solution.py:300
  74.4 15.8 %collective-permute-done.17 = bf16[48,1024]{1,0:T(8,128)(2,1)S(1)} collective-permute-done((bf16[48,1024]{1,0:T(8,128)(2,1)S(1)}, bf16[48,1024]{1,0:T(8,128)(2,1)S(1)}, u32[]{:S(2)}, u32[]{:S(2)}) %collective-permute-start.17) | collective-permute-done | bytes 98336 | tf_op jit(solution)/shard_map/ppermute | solution.py:147
  91.0 1.6 collective-permute-start.25
  93.4 3.1 %collective-permute-start.19 = (bf16[1024,512]{1,0:T(8,128)(2,1)S(1)}, bf16[1024,512]{1,0:T(8,128)(2,1)S(1)}, u32[]{:S(2)}, u32[]{:S(2)}) collective-permute-start(bf16[1024,512]{1,0:T(8,128)(2,1)S(1)} %get-tuple-element.121.d8), channel_id=1, source_target_pairs={{0,16},{8,24},{16,0},{24,8},{1,17},{9,25},{17,1},{25,9},{2,18},{10... | collective-permute-start | bytes 3145736 | tf_op jit(solution)/shard_map/ppermute | solution.py:147
  96.5 6.7 %prep.1 = (bf16[2,896,1024]{2,1,0:T(8,128)(2,1)S(1)}, bf16[2,896,1024]{2,1,0:T(8,128)(2,1)S(1)}, bf16[2,896,1024]{2,1,0:T(8,128)(2,1)S(1)}, bf16[2,896,1024]{2,1,0:T(8,128)(2,1)S(1)}, f32[48,2048]{1,0:T(8,128)S(1)}) custom-call(bf16[448,2048]{1,0:T(8,128)(2,1)S(1)} %get-tuple-element.88.mine_ref, bf16[448,2048]{1,0:T(8,128)(2,1)S(1)} %collective-permute-done.20.other_ref, ...), custom_call_target="tpu_custom_call" | custom-call | flops 1048576 | bytes 65536 | tf_op jit(solution)/shard_map/prep/pallas_call | solution.py:335
  108.2 8.4 %collective-permute-done.25.far_ref = bf16[1024,512]{1,0:T(8,128)(2,1)S(1)} collective-permute-done((bf16[1024,512]{1,0:T(8,128)(2,1)S(1)}, bf16[1024,512]{1,0:T(8,128)(2,1)S(1)}, u32[]{:S(2)}, u32[]{:S(2)}) %collective-permute-start.25) | collective-permute-done | bytes 1048608 | tf_op jit(solution)/shard_map/ppermute | solution.py:147
  116.6 1.5 collective-permute-start.22
  118.1 3.3 %conv.5 = (bf16[448,256]{1,0:T(8,128)(2,1)S(1)}, bf16[448,256]{1,0:T(8,128)(2,1)S(1)}) custom-call(bf16[2,896,1024]{2,1,0:T(8,128)(2,1)S(1)} %get-tuple-element.94.rows_ref, f32[896,512]{1,0:T(8,128)S(1)} %early.6.part_ref, bf16[1024,512]{1,0:T(8,128)(2,1)S(1)} %collective-permute-done.25.far_ref, f32[48,2048]{1,0:T(8,128)S(1)} %get-tuple-element.99.small_ref), custom_call_target="tpu_custom_call" | custom-call | flops 1048576 | bytes 65536 | tf_op jit(solution)/shard_map/conv/pallas_call | solution.py:395
  121.5 3.3 %conv.4 = (bf16[448,256]{1,0:T(8,128)(2,1)S(1)}, bf16[448,256]{1,0:T(8,128)(2,1)S(1)}) custom-call(bf16[2,896,1024]{2,1,0:T(8,128)(2,1)S(1)} %get-tuple-element.91.rows_ref, f32[896,512]{1,0:T(8,128)S(1)} %early.4.part_ref, bf16[1024,512]{1,0:T(8,128)(2,1)S(1)} %collective-permute-done.23.far_ref, f32[48,2048]{1,0:T(8,128)S(1)} %get-tuple-element.99.small_ref), custom_call_target="tpu_custom_call" | custom-call | flops 1048576 | bytes 65536 | tf_op jit(solution)/shard_map/conv/pallas_call | solution.py:395
  124.9 15.7 %collective-permute-done.18.er = bf16[1024,512]{1,0:T(8,128)(2,1)S(1)} collective-permute-done((bf16[1024,512]{1,0:T(8,128)(2,1)S(1)}, bf16[1024,512]{1,0:T(8,128)(2,1)S(1)}, u32[]{:S(2)}, u32[]{:S(2)}) %collective-permute-start.18) | collective-permute-done | bytes 1048608 | tf_op jit(solution)/shard_map/ppermute | solution.py:147
  140.6 1.3 collective-permute-done.19.dr
  143.1 3.3 %conv.7 = (bf16[448,256]{1,0:T(8,128)(2,1)S(1)}, bf16[448,256]{1,0:T(8,128)(2,1)S(1)}) custom-call(bf16[2,896,1024]{2,1,0:T(8,128)(2,1)S(1)} %get-tuple-element.95.rows_ref, f32[896,512]{1,0:T(8,128)S(1)} %early.7.part_ref, bf16[1024,512]{1,0:T(8,128)(2,1)S(1)} %collective-permute-done.22.far_ref, f32[48,2048]{1,0:T(8,128)S(1)} %get-tuple-element.99.small_ref), custom_call_target="tpu_custom_call" | custom-call | flops 1048576 | bytes 65536 | tf_op jit(solution)/shard_map/conv/pallas_call | solution.py:395
  146.7 3.5 %conv.6 = (bf16[448,256]{1,0:T(8,128)(2,1)S(1)}, bf16[448,256]{1,0:T(8,128)(2,1)S(1)}) custom-call(bf16[2,896,1024]{2,1,0:T(8,128)(2,1)S(1)} %get-tuple-element.93.rows_ref, f32[896,512]{1,0:T(8,128)S(1)} %early.5.part_ref, bf16[1024,512]{1,0:T(8,128)(2,1)S(1)} %collective-permute-done.21.far_ref, f32[48,2048]{1,0:T(8,128)S(1)} %get-tuple-element.99.small_ref), custom_call_target="tpu_custom_call" | custom-call | flops 1048576 | bytes 65536 | tf_op jit(solution)/shard_map/conv/pallas_call | solution.py:395
  151.8 6.8 %finish.1 = bf16[384,2048]{1,0:T(8,128)(2,1)} custom-call(bf16[448,256]{1,0:T(8,128)(2,1)S(1)} %get-tuple-element.105.m0, bf16[448,256]{1,0:T(8,128)(2,1)S(1)} %get-tuple-element.108.m1, bf16[448,256]{1,0:T(8,128)(2,1)S(1)} %get-tuple-element.109.m2, bf16[448,256]{1,0:T(8,128)(2,1)S(1)} %get-tuple-element.112.m3, ...), custom_call_target="tpu_custom_call" | custom-call | flops 1048576 | bytes 65536 | tf_op jit(solution)/shard_map/finish/pallas_call | solution.py:456
  (99 shorter events, 17.7 us)
Async XLA Ops:
  1.6 2.8 %collective-permute-start = (bf16[64,3072]{1,0:T(8,128)(2,1)S(1)}, bf16[64,3072]{1,0:T(8,128)(2,1)S(1)}, u32[]{:S(2)}, u32[]{:S(2)}) collective-permute-start(bf16[64,3072]{1,0:T(8,128)(2,1)S(1)} %get-tuple-element.136), channel_id=1, source_target_pairs={{0,1},{1,0},{2,3},{3,2},{4,5},{5,4},{6,7},{7,6},{8,9},{9,8},{10,11... | collective-permute-start | bytes 1179656 | tf_op jit(solution)/shard_map/ppermute | solution.py:147
  4.7 23.2 %collective-permute-start.2 = (bf16[128,1536]{1,0:T(8,128)(2,1)S(1)}, bf16[128,1536]{1,0:T(8,128)(2,1)S(1)}, u32[]{:S(2)}, u32[]{:S(2)}) collective-permute-start(bf16[128,1536]{1,0:T(8,128)(2,1)S(1)} %pad_maximum_fusion.14), channel_id=1, source_target_pairs={{0,16},{8,24},{16,0},{24,8},{1,17},{9,25},{17,1},{25,9},{2,18},{10... | collective-permute-start | bytes 1179656 | tf_op jit(solution)/shard_map/ppermute | solution.py:147
  8.5 19.6 %collective-permute-start.1 = (bf16[128,1536]{1,0:T(8,128)(2,1)S(1)}, bf16[128,1536]{1,0:T(8,128)(2,1)S(1)}, u32[]{:S(2)}, u32[]{:S(2)}) collective-permute-start(bf16[128,1536]{1,0:T(8,128)(2,1)S(1)} %get-tuple-element.134), channel_id=1, source_target_pairs={{0,8},{8,0},{16,24},{24,16},{1,9},{9,1},{17,25},{25,17},{2,10},{10... | collective-permute-start | bytes 1179656 | tf_op jit(solution)/shard_map/ppermute | solution.py:147
  11.2 16.7 %collective-permute-start.4 = (bf16[48,128]{1,0:T(8,128)(2,1)S(1)}, bf16[48,128]{1,0:T(8,128)(2,1)S(1)}, u32[]{:S(2)}, u32[]{:S(2)}) collective-permute-start(bf16[48,128]{1,0:T(8,128)(2,1)S(1)} %add.7), channel_id=1, source_target_pairs={{0,8},{8,0},{16,24},{24,16},{1,9},{9,1},{17,25},{25,17},{2,10},{10... | collective-permute-start | bytes 36872 | tf_op jit(solution)/shard_map/ppermute | solution.py:147
  11.7 34.7 %collective-permute-start.5 = (bf16[192,2048]{1,0:T(8,128)(2,1)S(1)}, bf16[192,2048]{1,0:T(8,128)(2,1)S(1)}, u32[]{:S(2)}, u32[]{:S(2)}) collective-permute-start(bf16[192,2048]{1,0:T(8,128)(2,1)S(1)} %get-tuple-element.70), channel_id=1, source_target_pairs={{0,4},{4,8},{8,12},{12,16},{16,20},{20,24},{24,28},{28,0},{1,5},{5... | collective-permute-start | bytes 2359304 | tf_op jit(solution)/shard_map/ppermute | solution.py:151
  13.2 35.8 %collective-permute-start.6 = (bf16[192,2048]{1,0:T(8,128)(2,1)S(1)}, bf16[192,2048]{1,0:T(8,128)(2,1)S(1)}, u32[]{:S(2)}, u32[]{:S(2)}) collective-permute-start(bf16[192,2048]{1,0:T(8,128)(2,1)S(1)} %get-tuple-element.71), channel_id=1, source_target_pairs={{0,28},{4,0},{8,4},{12,8},{16,12},{20,16},{24,20},{28,24},{1,29},{... | collective-permute-start | bytes 2359304 | tf_op jit(solution)/shard_map/ppermute | solution.py:151
  28.1 27.3 %collective-permute-start.10 = (bf16[256,512]{1,0:T(8,128)(2,1)S(1)}, bf16[256,512]{1,0:T(8,128)(2,1)S(1)}, u32[]{:S(2)}, u32[]{:S(2)}) collective-permute-start(bf16[256,512]{1,0:T(8,128)(2,1)S(1)} %slice.101), channel_id=1, source_target_pairs={{0,8},{8,0},{16,24},{24,16},{1,9},{9,1},{17,25},{25,17},{2,10},{10... | collective-permute-start | bytes 786440 | tf_op jit(solution)/shard_map/ppermute | solution.py:147
  29.4 33.3 %collective-permute-start.9 = (bf16[256,1024]{1,0:T(8,128)(2,1)S(1)}, bf16[256,1024]{1,0:T(8,128)(2,1)S(1)}, u32[]{:S(2)}, u32[]{:S(2)}) collective-permute-start(bf16[256,1024]{1,0:T(8,128)(2,1)S(1)} %slice.100), channel_id=1, source_target_pairs={{0,2},{2,0},{1,3},{3,1},{4,6},{6,4},{5,7},{7,5},{8,10},{10,8},{9,1... | collective-permute-start | bytes 1572872 | tf_op jit(solution)/shard_map/ppermute | solution.py:147
  31.0 27.8 %collective-permute-start.8 = (bf16[256,512]{1,0:T(8,128)(2,1)S(1)}, bf16[256,512]{1,0:T(8,128)(2,1)S(1)}, u32[]{:S(2)}, u32[]{:S(2)}) collective-permute-start(bf16[256,512]{1,0:T(8,128)(2,1)S(1)} %slice.99), channel_id=1, source_target_pairs={{0,16},{8,24},{16,0},{24,8},{1,17},{9,25},{17,1},{25,9},{2,18},{10... | collective-permute-start | bytes 786440 | tf_op jit(solution)/shard_map/ppermute | solution.py:147
  49.1 8.1 %collective-permute-start.11 = (bf16[48,256]{1,0:T(8,128)(2,1)S(1)}, bf16[48,256]{1,0:T(8,128)(2,1)S(1)}, u32[]{:S(2)}, u32[]{:S(2)}) collective-permute-start(bf16[48,256]{1,0:T(8,128)(2,1)S(1)} %pad_maximum_fusion.18), channel_id=1, source_target_pairs={{0,16},{8,24},{16,0},{24,8},{1,17},{9,25},{17,1},{25,9},{2,18},{10... | collective-permute-start | bytes 73736 | tf_op jit(solution)/shard_map/ppermute | solution.py:147
  49.4 13.3 %collective-permute-start.7 = (bf16[256,1024]{1,0:T(8,128)(2,1)S(1)}, bf16[256,1024]{1,0:T(8,128)(2,1)S(1)}, u32[]{:S(2)}, u32[]{:S(2)}) collective-permute-start(bf16[256,1024]{1,0:T(8,128)(2,1)S(1)} %slice.98), channel_id=1, source_target_pairs={{0,4},{4,0},{1,5},{5,1},{2,6},{6,2},{3,7},{7,3},{8,12},{12,8},{9,1... | collective-permute-start | bytes 1572872 | tf_op jit(solution)/shard_map/ppermute | solution.py:147
  57.2 5.5 %collective-permute-start.12 = (bf16[48,512]{1,0:T(8,128)(2,1)S(1)}, bf16[48,512]{1,0:T(8,128)(2,1)S(1)}, u32[]{:S(2)}, u32[]{:S(2)}) collective-permute-start(bf16[48,512]{1,0:T(8,128)(2,1)S(1)} %pad_maximum_fusion.17), channel_id=1, source_target_pairs={{0,4},{4,0},{1,5},{5,1},{2,6},{6,2},{3,7},{7,3},{8,12},{12,8},{9,1... | collective-permute-start | bytes 147464 | tf_op jit(solution)/shard_map/ppermute | solution.py:147
  63.1 27.2 %collective-permute-start.15 = (bf16[512,1024]{1,0:T(8,128)(2,1)S(1)}, bf16[512,1024]{1,0:T(8,128)(2,1)S(1)}, u32[]{:S(2)}, u32[]{:S(2)}) collective-permute-start(bf16[512,1024]{1,0:T(8,128)(2,1)S(1)} %pad_maximum_fusion.6), channel_id=1, source_target_pairs={{0,4},{4,0},{1,5},{5,1},{2,6},{6,2},{3,7},{7,3},{8,12},{12,8},{9,1... | collective-permute-start | bytes 3145736 | tf_op jit(solution)/shard_map/ppermute | solution.py:147
  64.4 26.1 %collective-permute-start.14 = (bf16[512,1024]{1,0:T(8,128)(2,1)S(1)}, bf16[512,1024]{1,0:T(8,128)(2,1)S(1)}, u32[]{:S(2)}, u32[]{:S(2)}) collective-permute-start(bf16[512,1024]{1,0:T(8,128)(2,1)S(1)} %pad_maximum_fusion.5), channel_id=1, source_target_pairs={{0,2},{2,0},{1,3},{3,1},{4,6},{6,4},{5,7},{7,5},{8,10},{10,8},{9,1... | collective-permute-start | bytes 3145736 | tf_op jit(solution)/shard_map/ppermute | solution.py:147
  66.0 24.1 %collective-permute-start.16 = (bf16[512,512]{1,0:T(8,128)(2,1)S(1)}, bf16[512,512]{1,0:T(8,128)(2,1)S(1)}, u32[]{:S(2)}, u32[]{:S(2)}) collective-permute-start(bf16[512,512]{1,0:T(8,128)(2,1)S(1)} %get-tuple-element.127), channel_id=1, source_target_pairs={{0,8},{8,0},{16,24},{24,16},{1,9},{9,1},{17,25},{25,17},{2,10},{10... | collective-permute-start | bytes 1572872 | tf_op jit(solution)/shard_map/ppermute | solution.py:147
  68.7 21.5 %collective-permute-start.13 = (bf16[512,512]{1,0:T(8,128)(2,1)S(1)}, bf16[512,512]{1,0:T(8,128)(2,1)S(1)}, u32[]{:S(2)}, u32[]{:S(2)}) collective-permute-start(bf16[512,512]{1,0:T(8,128)(2,1)S(1)} %get-tuple-element.130), channel_id=1, source_target_pairs={{0,16},{8,24},{16,0},{24,8},{1,17},{9,25},{17,1},{25,9},{2,18},{10... | collective-permute-start | bytes 1572872 | tf_op jit(solution)/shard_map/ppermute | solution.py:147
  69.7 20.4 %collective-permute-start.17 = (bf16[48,1024]{1,0:T(8,128)(2,1)S(1)}, bf16[48,1024]{1,0:T(8,128)(2,1)S(1)}, u32[]{:S(2)}, u32[]{:S(2)}) collective-permute-start(bf16[48,1024]{1,0:T(8,128)(2,1)S(1)} %pad_maximum_fusion.16.notes_ref), channel_id=1, source_target_pairs={{0,2},{2,0},{1,3},{3,1},{4,6},{6,4},{5,7},{7,5},{8,10},{10,8},{9,1... | collective-permute-start | bytes 294920 | tf_op jit(solution)/shard_map/ppermute | solution.py:147
  90.8 5.7 %collective-permute-start.20 = (bf16[448,2048]{1,0:T(8,128)(2,1)S(1)}, bf16[448,2048]{1,0:T(8,128)(2,1)S(1)}, u32[]{:S(2)}, u32[]{:S(2)}) collective-permute-start(bf16[448,2048]{1,0:T(8,128)(2,1)S(1)} %get-tuple-element.88.mine_ref), channel_id=1, source_target_pairs={{0,1},{1,0},{2,3},{3,2},{4,5},{5,4},{6,7},{7,6},{8,9},{9,8},{10,11... | collective-permute-start | bytes 5505032 | tf_op jit(solution)/shard_map/ppermute | solution.py:147
  91.0 25.6 %collective-permute-start.25 = (bf16[1024,512]{1,0:T(8,128)(2,1)S(1)}, bf16[1024,512]{1,0:T(8,128)(2,1)S(1)}, u32[]{:S(2)}, u32[]{:S(2)}) collective-permute-start(bf16[1024,512]{1,0:T(8,128)(2,1)S(1)} %get-tuple-element.123.near_ref), channel_id=1, source_target_pairs={{0,4},{4,0},{1,5},{5,1},{2,6},{6,2},{3,7},{7,3},{8,12},{12,8},{9,1... | collective-permute-start | bytes 3145736 | tf_op jit(solution)/shard_map/ppermute | solution.py:147
  92.6 28.9 %collective-permute-start.23 = (bf16[1024,512]{1,0:T(8,128)(2,1)S(1)}, bf16[1024,512]{1,0:T(8,128)(2,1)S(1)}, u32[]{:S(2)}, u32[]{:S(2)}) collective-permute-start(bf16[1024,512]{1,0:T(8,128)(2,1)S(1)} %pad_maximum_fusion.4.near_ref), channel_id=1, source_target_pairs={{0,2},{2,0},{1,3},{3,1},{4,6},{6,4},{5,7},{7,5},{8,10},{10,8},{9,1... | collective-permute-start | bytes 3145736 | tf_op jit(solution)/shard_map/ppermute | solution.py:147
  93.3 47.3 %collective-permute-start.18 = (bf16[1024,512]{1,0:T(8,128)(2,1)S(1)}, bf16[1024,512]{1,0:T(8,128)(2,1)S(1)}, u32[]{:S(2)}, u32[]{:S(2)}) collective-permute-start(bf16[1024,512]{1,0:T(8,128)(2,1)S(1)} %get-tuple-element.119.e8), channel_id=1, source_target_pairs={{0,8},{8,0},{16,24},{24,16},{1,9},{9,1},{17,25},{25,17},{2,10},{10... | collective-permute-start | bytes 3145736 | tf_op jit(solution)/shard_map/ppermute | solution.py:147
  93.4 48.6 %collective-permute-start.19 = (bf16[1024,512]{1,0:T(8,128)(2,1)S(1)}, bf16[1024,512]{1,0:T(8,128)(2,1)S(1)}, u32[]{:S(2)}, u32[]{:S(2)}) collective-permute-start(bf16[1024,512]{1,0:T(8,128)(2,1)S(1)} %get-tuple-element.121.d8), channel_id=1, source_target_pairs={{0,16},{8,24},{16,0},{24,8},{1,17},{9,25},{17,1},{25,9},{2,18},{10... | collective-permute-start | bytes 3145736 | tf_op jit(solution)/shard_map/ppermute | solution.py:147
  107.6 34.5 %collective-permute-start.21 = (bf16[1024,512]{1,0:T(8,128)(2,1)S(1)}, bf16[1024,512]{1,0:T(8,128)(2,1)S(1)}, u32[]{:S(2)}, u32[]{:S(2)}) collective-permute-start(bf16[1024,512]{1,0:T(8,128)(2,1)S(1)} %get-tuple-element.96.near_ref), channel_id=1, source_target_pairs={{0,2},{2,0},{1,3},{3,1},{4,6},{6,4},{5,7},{7,5},{8,10},{10,8},{9,1... | collective-permute-start | bytes 3145736 | tf_op jit(solution)/shard_map/ppermute | solution.py:147
  116.6 25.5 %collective-permute-start.22 = (bf16[1024,512]{1,0:T(8,128)(2,1)S(1)}, bf16[1024,512]{1,0:T(8,128)(2,1)S(1)}, u32[]{:S(2)}, u32[]{:S(2)}) collective-permute-start(bf16[1024,512]{1,0:T(8,128)(2,1)S(1)} %pad_maximum_fusion.7.near_ref), channel_id=1, source_target_pairs={{0,4},{4,0},{1,5},{5,1},{2,6},{6,2},{3,7},{7,3},{8,12},{12,8},{9,1... | collective-permute-start | bytes 3145736 | tf_op jit(solution)/shard_map/ppermute | solution.py:147
  121.5 20.5 %collective-permute-start.26 = (bf16[448,256]{1,0:T(8,128)(2,1)S(1)}, bf16[448,256]{1,0:T(8,128)(2,1)S(1)}, u32[]{:S(2)}, u32[]{:S(2)}) collective-permute-start(bf16[448,256]{1,0:T(8,128)(2,1)S(1)} %get-tuple-element.104), channel_id=1, source_target_pairs={{0,1},{1,0},{2,3},{3,2},{4,5},{5,4},{6,7},{7,6},{8,9},{9,8},{10,11... | collective-permute-start | bytes 688136 | tf_op jit(solution)/shard_map/ppermute | solution.py:147
  140.6 1.5 collective-permute-start.24
  142.1 9.7 %collective-permute-start.29 = (bf16[1024,512]{1,0:T(8,128)(2,1)S(1)}, bf16[1024,512]{1,0:T(8,128)(2,1)S(1)}, u32[]{:S(2)}, u32[]{:S(2)}) collective-permute-start(bf16[1024,512]{1,0:T(8,128)(2,1)S(1)} %get-tuple-element.119.e8), channel_id=1, source_target_pairs={{0,1},{1,0},{2,3},{3,2},{4,5},{5,4},{6,7},{7,6},{8,9},{9,8},{10,11... | collective-permute-start | bytes 3145736 | tf_op jit(solution)/shard_map/ppermute | solution.py:147
  142.2 9.5 %collective-permute-start.30 = (bf16[1024,512]{1,0:T(8,128)(2,1)S(1)}, bf16[1024,512]{1,0:T(8,128)(2,1)S(1)}, u32[]{:S(2)}, u32[]{:S(2)}) collective-permute-start(bf16[1024,512]{1,0:T(8,128)(2,1)S(1)} %collective-permute-done.18.er), channel_id=1, source_target_pairs={{0,1},{1,0},{2,3},{3,2},{4,5},{5,4},{6,7},{7,6},{8,9},{9,8},{10,11... | collective-permute-start | bytes 3145736 | tf_op jit(solution)/shard_map/ppermute | solution.py:147
  142.6 9.2 %collective-permute-start.31 = (bf16[1024,512]{1,0:T(8,128)(2,1)S(1)}, bf16[1024,512]{1,0:T(8,128)(2,1)S(1)}, u32[]{:S(2)}, u32[]{:S(2)}) collective-permute-start(bf16[1024,512]{1,0:T(8,128)(2,1)S(1)} %get-tuple-element.121.d8), channel_id=1, source_target_pairs={{0,1},{1,0},{2,3},{3,2},{4,5},{5,4},{6,7},{7,6},{8,9},{9,8},{10,11... | collective-permute-start | bytes 3145736 | tf_op jit(solution)/shard_map/ppermute | solution.py:147
  142.8 9.0 %collective-permute-start.32 = (bf16[1024,512]{1,0:T(8,128)(2,1)S(1)}, bf16[1024,512]{1,0:T(8,128)(2,1)S(1)}, u32[]{:S(2)}, u32[]{:S(2)}) collective-permute-start(bf16[1024,512]{1,0:T(8,128)(2,1)S(1)} %collective-permute-done.19.dr), channel_id=1, source_target_pairs={{0,1},{1,0},{2,3},{3,2},{4,5},{5,4},{6,7},{7,6},{8,9},{9,8},{10,11... | collective-permute-start | bytes 3145736 | tf_op jit(solution)/shard_map/ppermute | solution.py:147
  146.5 3.8 %collective-permute-start.28 = (bf16[448,256]{1,0:T(8,128)(2,1)S(1)}, bf16[448,256]{1,0:T(8,128)(2,1)S(1)}, u32[]{:S(2)}, u32[]{:S(2)}) collective-permute-start(bf16[448,256]{1,0:T(8,128)(2,1)S(1)} %get-tuple-element.116), channel_id=1, source_target_pairs={{0,1},{1,0},{2,3},{3,2},{4,5},{5,4},{6,7},{7,6},{8,9},{9,8},{10,11... | collective-permute-start | bytes 688136 | tf_op jit(solution)/shard_map/ppermute | solution.py:147
  150.2 1.6 collective-permute-start.27
  (8 other events, 17.6 us)

commit v7 on v6

--- a/solution.py
+++ b/solution.py
@@ -140,6 +140,7 @@
 NOTES = ("z1", "z2", "y", "x")
 SMALL = 48
 TILE = 64
+SLIDE = 224
 
 
 def hop(array, name):
@@ -375,15 +376,15 @@
     def slide(out_ref, base):
         def one(step, carry):
             for tile in range(tiles):
-                total = jnp.zeros((TILE, LANE), jnp.float32)
+                total = jnp.zeros((SLIDE, LANE), jnp.float32)
                 for tap in range(KERNEL):
-                    window = gated[tile, pl.ds(base + step * TILE + tap, TILE), :]
+                    window = gated[tile, pl.ds(base + step * SLIDE + tap, SLIDE), :]
                     total = total + window * taps[tile, tap : tap + 1, :]
-                at = pl.ds(pl.multiple_of(step * TILE, TILE), TILE)
+                at = pl.ds(pl.multiple_of(step * SLIDE, SLIDE), SLIDE)
                 out_ref[at, tile * LANE : (tile + 1) * LANE] = total.astype(jnp.bfloat16)
             return carry
 
-        lax.fori_loop(0, PAD // TILE, one, 0)
+        lax.fori_loop(0, PAD // SLIDE, one, 0)
 
     slide(own_ref, 0)
     slide(other_ref, PAD)

time: 159 us -> 159 us (level)
  no operation moved by 1% of the time
where the time goes in v7:
time: 159 us; the launch traced here: 158 us
  waiting for transfers between devices  81.1 us (51%)
  Pallas kernels  36.7 us (23%)
  starting transfers between devices  36.1 us (23%)
  local copies, waits for them, and re-layouts  2.23 us (1%)
  other arithmetic  1.65 us (1%)
    ppermute x31, waiting for transfers between devices, hop(): return lax.ppermute(array, axis, pairs)  64.8 us
    ppermute x31, starting transfers between devices, hop(): return lax.ppermute(array, axis, pairs)  31.4 us
    ppermute x2, waiting for transfers between devices, turn(): lax.ppermute(array, ('z', 'y'), [(i, (i + by) % 8) for i in range(8)])  16.3 us
    pallas_call x4, Pallas kernels, conv(): pl.pallas_call(functools.partial(conv_kernel, sub), out_shape=(out, out),...  12.6 us
    pallas_call x1, Pallas kernels, finish(): pl.pallas_call(finish_kernel, out_shape=shape(RCV_DEV, D), in_specs=vmem(...  6.84 us
    pallas_call x1, Pallas kernels, prep(): pl.pallas_call(prep_kernel, out_shape=(jax.ShapeDtypeStruct((2, PAIR, HAL...  6.71 us
    ppermute x2, starting transfers between devices, turn(): lax.ppermute(array, ('z', 'y'), [(i, (i + by) % 8) for i in range(8)])  4.72 us
    pallas_call x4, Pallas kernels, early(): pl.pallas_call(early_kernel, out_shape=shape(PAIR, near.shape[1], jnp.flo...  4.44 us
  transfers between devices with their start and end apart: 33, of which 13 were waited for; matrix products, arithmetic and copies ran while one was open for 1% of the time, Pallas kernels for 19%

profile of v7, /device:TPU:0, one launch (start us, length us, event | category | flops | bytes accessed | tf_op | source)
XLA Modules:
  0.0 158.4 jit_solution(8942954953995338534)
XLA Ops:
  0.0 1.4 fusion.5
  2.4 2.0 %cut.1 = (bf16[192,2048]{1,0:T(8,128)(2,1)S(1)}, bf16[192,2048]{1,0:T(8,128)(2,1)S(1)}, bf16[48,128]{1,0:T(8,128)(2,1)S(1)}) custom-call(s32[1,3]{1,0:T(1,128)S(1)} %copy-done.1, s32[1,3]{1,0:T(1,128)S(1)} %copy-done.2, s32[1,3]{1,0:T(1,128)S(1)} %copy-done.3, bf16[576,2048]{1,0:T(8,128)(2,1)S(1)} %bitcast.5, bf16[48,128]{1,0:T(8,128)(2,1)S(1)} %pad_select_fusion.notes_ref), custom_call_target="tpu_custom_call" | custom-call | flops 1048576 | bytes 65536 | tf_op jit(solution)/shard_map/cut/pallas_call | solution.py:248
  4.7 3.7 %collective-permute-start.2 = (bf16[128,1536]{1,0:T(8,128)(2,1)S(1)}, bf16[128,1536]{1,0:T(8,128)(2,1)S(1)}, u32[]{:S(2)}, u32[]{:S(2)}) collective-permute-start(bf16[128,1536]{1,0:T(8,128)(2,1)S(1)} %pad_maximum_fusion.14), channel_id=1, source_target_pairs={{0,16},{8,24},{16,0},{24,8},{1,17},{9,25},{17,1},{25,9},{2,18},{10... | collective-permute-start | bytes 1179656 | tf_op jit(solution)/shard_map/ppermute | solution.py:148
  8.5 1.6 collective-permute-start.1
  11.7 1.5 collective-permute-start.5
  13.2 3.2 %collective-permute-start.6 = (bf16[192,2048]{1,0:T(8,128)(2,1)S(1)}, bf16[192,2048]{1,0:T(8,128)(2,1)S(1)}, u32[]{:S(2)}, u32[]{:S(2)}) collective-permute-start(bf16[192,2048]{1,0:T(8,128)(2,1)S(1)} %get-tuple-element.71), channel_id=1, source_target_pairs={{0,28},{4,0},{8,4},{12,8},{16,12},{20,16},{24,20},{28,24},{1,29},{... | collective-permute-start | bytes 2359304 | tf_op jit(solution)/shard_map/ppermute | solution.py:152
  16.5 11.5 %collective-permute-done.4 = bf16[48,128]{1,0:T(8,128)(2,1)S(1)} collective-permute-done((bf16[48,128]{1,0:T(8,128)(2,1)S(1)}, bf16[48,128]{1,0:T(8,128)(2,1)S(1)}, u32[]{:S(2)}, u32[]{:S(2)}) %collective-permute-start.4) | collective-permute-done | bytes 12320 | tf_op jit(solution)/shard_map/ppermute | solution.py:148
  29.4 1.6 collective-permute-start.9
  31.0 1.8 %collective-permute-start.8 = (bf16[256,512]{1,0:T(8,128)(2,1)S(1)}, bf16[256,512]{1,0:T(8,128)(2,1)S(1)}, u32[]{:S(2)}, u32[]{:S(2)}) collective-permute-start(bf16[256,512]{1,0:T(8,128)(2,1)S(1)} %slice.99), channel_id=1, source_target_pairs={{0,16},{8,24},{16,0},{24,8},{1,17},{9,25},{17,1},{25,9},{2,18},{10... | collective-permute-start | bytes 786440 | tf_op jit(solution)/shard_map/ppermute | solution.py:148
  32.8 13.6 %collective-permute-done.5.prev_ref = bf16[192,2048]{1,0:T(8,128)(2,1)S(1)} collective-permute-done((bf16[192,2048]{1,0:T(8,128)(2,1)S(1)}, bf16[192,2048]{1,0:T(8,128)(2,1)S(1)}, u32[]{:S(2)}, u32[]{:S(2)}) %collective-permute-start.5) | collective-permute-done | bytes 786464 | tf_op jit(solution)/shard_map/ppermute | solution.py:152
  46.4 2.7 %collective-permute-done.6.next_ref = bf16[192,2048]{1,0:T(8,128)(2,1)S(1)} collective-permute-done((bf16[192,2048]{1,0:T(8,128)(2,1)S(1)}, bf16[192,2048]{1,0:T(8,128)(2,1)S(1)}, u32[]{:S(2)}, u32[]{:S(2)}) %collective-permute-start.6) | collective-permute-done | bytes 786464 | tf_op jit(solution)/shard_map/ppermute | solution.py:152
  49.4 2.5 %collective-permute-start.7 = (bf16[256,1024]{1,0:T(8,128)(2,1)S(1)}, bf16[256,1024]{1,0:T(8,128)(2,1)S(1)}, u32[]{:S(2)}, u32[]{:S(2)}) collective-permute-start(bf16[256,1024]{1,0:T(8,128)(2,1)S(1)} %slice.98), channel_id=1, source_target_pairs={{0,4},{4,0},{1,5},{5,1},{2,6},{6,2},{3,7},{7,3},{8,12},{12,8},{9,1... | collective-permute-start | bytes 1572872 | tf_op jit(solution)/shard_map/ppermute | solution.py:148
  51.9 3.5 %collective-permute-done.10 = bf16[256,512]{1,0:T(8,128)(2,1)S(1)} collective-permute-done((bf16[256,512]{1,0:T(8,128)(2,1)S(1)}, bf16[256,512]{1,0:T(8,128)(2,1)S(1)}, u32[]{:S(2)}, u32[]{:S(2)}) %collective-permute-start.10) | collective-permute-done | bytes 262176 | tf_op jit(solution)/shard_map/ppermute | solution.py:148
  55.4 1.7 %collective-permute-done.11 = bf16[48,256]{1,0:T(8,128)(2,1)S(1)} collective-permute-done((bf16[48,256]{1,0:T(8,128)(2,1)S(1)}, bf16[48,256]{1,0:T(8,128)(2,1)S(1)}, u32[]{:S(2)}, u32[]{:S(2)}) %collective-permute-start.11) | collective-permute-done | bytes 24608 | tf_op jit(solution)/shard_map/ppermute | solution.py:148
  57.2 1.6 collective-permute-start.12
  58.8 3.9 %collective-permute-done.12 = bf16[48,512]{1,0:T(8,128)(2,1)S(1)} collective-permute-done((bf16[48,512]{1,0:T(8,128)(2,1)S(1)}, bf16[48,512]{1,0:T(8,128)(2,1)S(1)}, u32[]{:S(2)}, u32[]{:S(2)}) %collective-permute-start.12) | collective-permute-done | bytes 49184 | tf_op jit(solution)/shard_map/ppermute | solution.py:148
  64.4 1.6 collective-permute-start.14
  66.0 2.7 %collective-permute-start.16 = (bf16[512,512]{1,0:T(8,128)(2,1)S(1)}, bf16[512,512]{1,0:T(8,128)(2,1)S(1)}, u32[]{:S(2)}, u32[]{:S(2)}) collective-permute-start(bf16[512,512]{1,0:T(8,128)(2,1)S(1)} %get-tuple-element.127), channel_id=1, source_target_pairs={{0,8},{8,0},{16,24},{24,16},{1,9},{9,1},{17,25},{25,17},{2,10},{10... | collective-permute-start | bytes 1572872 | tf_op jit(solution)/shard_map/ppermute | solution.py:148
  70.2 4.1 %place.1 = (bf16[448,2048]{1,0:T(8,128)(2,1)S(1)}, bf16[384,2048]{1,0:T(8,128)(2,1)S(1)}, bf16[384,448]{1,0:T(8,128)(2,1)S(1)}) custom-call(s32[1,3]{1,0:T(1,128)S(1)} %copy-done.1, s32[1,3]{1,0:T(1,128)S(1)} %copy-done.2, s32[1,3]{1,0:T(1,128)S(1)} %copy-done.3, bf16[576,2048]{1,0:T(8,128)(2,1)S(1)} %bitcast.6, ...), custom_call_target="tpu_custom_call" | custom-call | flops 1048576 | bytes 65536 | tf_op jit(solution)/shard_map/place/pallas_call | solution.py:301
  74.4 15.8 %collective-permute-done.17 = bf16[48,1024]{1,0:T(8,128)(2,1)S(1)} collective-permute-done((bf16[48,1024]{1,0:T(8,128)(2,1)S(1)}, bf16[48,1024]{1,0:T(8,128)(2,1)S(1)}, u32[]{:S(2)}, u32[]{:S(2)}) %collective-permute-start.17) | collective-permute-done | bytes 98336 | tf_op jit(solution)/shard_map/ppermute | solution.py:148
  91.0 1.6 collective-permute-start.25
  93.4 3.1 %collective-permute-start.19 = (bf16[1024,512]{1,0:T(8,128)(2,1)S(1)}, bf16[1024,512]{1,0:T(8,128)(2,1)S(1)}, u32[]{:S(2)}, u32[]{:S(2)}) collective-permute-start(bf16[1024,512]{1,0:T(8,128)(2,1)S(1)} %get-tuple-element.121.d8), channel_id=1, source_target_pairs={{0,16},{8,24},{16,0},{24,8},{1,17},{9,25},{17,1},{25,9},{2,18},{10... | collective-permute-start | bytes 3145736 | tf_op jit(solution)/shard_map/ppermute | solution.py:148
  96.5 6.7 %prep.1 = (bf16[2,896,1024]{2,1,0:T(8,128)(2,1)S(1)}, bf16[2,896,1024]{2,1,0:T(8,128)(2,1)S(1)}, bf16[2,896,1024]{2,1,0:T(8,128)(2,1)S(1)}, bf16[2,896,1024]{2,1,0:T(8,128)(2,1)S(1)}, f32[48,2048]{1,0:T(8,128)S(1)}) custom-call(bf16[448,2048]{1,0:T(8,128)(2,1)S(1)} %get-tuple-element.88.mine_ref, bf16[448,2048]{1,0:T(8,128)(2,1)S(1)} %collective-permute-done.20.other_ref, ...), custom_call_target="tpu_custom_call" | custom-call | flops 1048576 | bytes 65536 | tf_op jit(solution)/shard_map/prep/pallas_call | solution.py:336
  108.2 8.4 %collective-permute-done.25.far_ref = bf16[1024,512]{1,0:T(8,128)(2,1)S(1)} collective-permute-done((bf16[1024,512]{1,0:T(8,128)(2,1)S(1)}, bf16[1024,512]{1,0:T(8,128)(2,1)S(1)}, u32[]{:S(2)}, u32[]{:S(2)}) %collective-permute-start.25) | collective-permute-done | bytes 1048608 | tf_op jit(solution)/shard_map/ppermute | solution.py:148
  116.6 1.5 collective-permute-start.22
  118.1 3.1 %conv.5 = (bf16[448,256]{1,0:T(8,128)(2,1)S(1)}, bf16[448,256]{1,0:T(8,128)(2,1)S(1)}) custom-call(bf16[2,896,1024]{2,1,0:T(8,128)(2,1)S(1)} %get-tuple-element.94.rows_ref, f32[896,512]{1,0:T(8,128)S(1)} %early.6.part_ref, bf16[1024,512]{1,0:T(8,128)(2,1)S(1)} %collective-permute-done.25.far_ref, f32[48,2048]{1,0:T(8,128)S(1)} %get-tuple-element.99.small_ref), custom_call_target="tpu_custom_call" | custom-call | flops 1048576 | bytes 65536 | tf_op jit(solution)/shard_map/conv/pallas_call | solution.py:396
  121.3 3.1 %conv.4 = (bf16[448,256]{1,0:T(8,128)(2,1)S(1)}, bf16[448,256]{1,0:T(8,128)(2,1)S(1)}) custom-call(bf16[2,896,1024]{2,1,0:T(8,128)(2,1)S(1)} %get-tuple-element.91.rows_ref, f32[896,512]{1,0:T(8,128)S(1)} %early.4.part_ref, bf16[1024,512]{1,0:T(8,128)(2,1)S(1)} %collective-permute-done.23.far_ref, f32[48,2048]{1,0:T(8,128)S(1)} %get-tuple-element.99.small_ref), custom_call_target="tpu_custom_call" | custom-call | flops 1048576 | bytes 65536 | tf_op jit(solution)/shard_map/conv/pallas_call | solution.py:396
  124.4 16.2 %collective-permute-done.18.er = bf16[1024,512]{1,0:T(8,128)(2,1)S(1)} collective-permute-done((bf16[1024,512]{1,0:T(8,128)(2,1)S(1)}, bf16[1024,512]{1,0:T(8,128)(2,1)S(1)}, u32[]{:S(2)}, u32[]{:S(2)}) %collective-permute-start.18) | collective-permute-done | bytes 1048608 | tf_op jit(solution)/shard_map/ppermute | solution.py:148
  140.6 1.3 collective-permute-done.19.dr
  143.1 3.1 %conv.7 = (bf16[448,256]{1,0:T(8,128)(2,1)S(1)}, bf16[448,256]{1,0:T(8,128)(2,1)S(1)}) custom-call(bf16[2,896,1024]{2,1,0:T(8,128)(2,1)S(1)} %get-tuple-element.95.rows_ref, f32[896,512]{1,0:T(8,128)S(1)} %early.7.part_ref, bf16[1024,512]{1,0:T(8,128)(2,1)S(1)} %collective-permute-done.22.far_ref, f32[48,2048]{1,0:T(8,128)S(1)} %get-tuple-element.99.small_ref), custom_call_target="tpu_custom_call" | custom-call | flops 1048576 | bytes 65536 | tf_op jit(solution)/shard_map/conv/pallas_call | solution.py:396
  146.4 3.3 %conv.6 = (bf16[448,256]{1,0:T(8,128)(2,1)S(1)}, bf16[448,256]{1,0:T(8,128)(2,1)S(1)}) custom-call(bf16[2,896,1024]{2,1,0:T(8,128)(2,1)S(1)} %get-tuple-element.93.rows_ref, f32[896,512]{1,0:T(8,128)S(1)} %early.5.part_ref, bf16[1024,512]{1,0:T(8,128)(2,1)S(1)} %collective-permute-done.21.far_ref, f32[48,2048]{1,0:T(8,128)S(1)} %get-tuple-element.99.small_ref), custom_call_target="tpu_custom_call" | custom-call | flops 1048576 | bytes 65536 | tf_op jit(solution)/shard_map/conv/pallas_call | solution.py:396
  151.3 6.8 %finish.1 = bf16[384,2048]{1,0:T(8,128)(2,1)} custom-call(bf16[448,256]{1,0:T(8,128)(2,1)S(1)} %get-tuple-element.105.m0, bf16[448,256]{1,0:T(8,128)(2,1)S(1)} %get-tuple-element.108.m1, bf16[448,256]{1,0:T(8,128)(2,1)S(1)} %get-tuple-element.109.m2, bf16[448,256]{1,0:T(8,128)(2,1)S(1)} %get-tuple-element.112.m3, ...), custom_call_target="tpu_custom_call" | custom-call | flops 1048576 | bytes 65536 | tf_op jit(solution)/shard_map/finish/pallas_call | solution.py:457
  (99 shorter events, 17.7 us)
Async XLA Ops:
  1.6 2.8 %collective-permute-start = (bf16[64,3072]{1,0:T(8,128)(2,1)S(1)}, bf16[64,3072]{1,0:T(8,128)(2,1)S(1)}, u32[]{:S(2)}, u32[]{:S(2)}) collective-permute-start(bf16[64,3072]{1,0:T(8,128)(2,1)S(1)} %get-tuple-element.136), channel_id=1, source_target_pairs={{0,1},{1,0},{2,3},{3,2},{4,5},{5,4},{6,7},{7,6},{8,9},{9,8},{10,11... | collective-permute-start | bytes 1179656 | tf_op jit(solution)/shard_map/ppermute | solution.py:148
  4.7 23.2 %collective-permute-start.2 = (bf16[128,1536]{1,0:T(8,128)(2,1)S(1)}, bf16[128,1536]{1,0:T(8,128)(2,1)S(1)}, u32[]{:S(2)}, u32[]{:S(2)}) collective-permute-start(bf16[128,1536]{1,0:T(8,128)(2,1)S(1)} %pad_maximum_fusion.14), channel_id=1, source_target_pairs={{0,16},{8,24},{16,0},{24,8},{1,17},{9,25},{17,1},{25,9},{2,18},{10... | collective-permute-start | bytes 1179656 | tf_op jit(solution)/shard_map/ppermute | solution.py:148
  8.5 19.6 %collective-permute-start.1 = (bf16[128,1536]{1,0:T(8,128)(2,1)S(1)}, bf16[128,1536]{1,0:T(8,128)(2,1)S(1)}, u32[]{:S(2)}, u32[]{:S(2)}) collective-permute-start(bf16[128,1536]{1,0:T(8,128)(2,1)S(1)} %get-tuple-element.134), channel_id=1, source_target_pairs={{0,8},{8,0},{16,24},{24,16},{1,9},{9,1},{17,25},{25,17},{2,10},{10... | collective-permute-start | bytes 1179656 | tf_op jit(solution)/shard_map/ppermute | solution.py:148
  11.2 16.7 %collective-permute-start.4 = (bf16[48,128]{1,0:T(8,128)(2,1)S(1)}, bf16[48,128]{1,0:T(8,128)(2,1)S(1)}, u32[]{:S(2)}, u32[]{:S(2)}) collective-permute-start(bf16[48,128]{1,0:T(8,128)(2,1)S(1)} %add.7), channel_id=1, source_target_pairs={{0,8},{8,0},{16,24},{24,16},{1,9},{9,1},{17,25},{25,17},{2,10},{10... | collective-permute-start | bytes 36872 | tf_op jit(solution)/shard_map/ppermute | solution.py:148
  11.7 34.7 %collective-permute-start.5 = (bf16[192,2048]{1,0:T(8,128)(2,1)S(1)}, bf16[192,2048]{1,0:T(8,128)(2,1)S(1)}, u32[]{:S(2)}, u32[]{:S(2)}) collective-permute-start(bf16[192,2048]{1,0:T(8,128)(2,1)S(1)} %get-tuple-element.70), channel_id=1, source_target_pairs={{0,4},{4,8},{8,12},{12,16},{16,20},{20,24},{24,28},{28,0},{1,5},{5... | collective-permute-start | bytes 2359304 | tf_op jit(solution)/shard_map/ppermute | solution.py:152
  13.2 35.8 %collective-permute-start.6 = (bf16[192,2048]{1,0:T(8,128)(2,1)S(1)}, bf16[192,2048]{1,0:T(8,128)(2,1)S(1)}, u32[]{:S(2)}, u32[]{:S(2)}) collective-permute-start(bf16[192,2048]{1,0:T(8,128)(2,1)S(1)} %get-tuple-element.71), channel_id=1, source_target_pairs={{0,28},{4,0},{8,4},{12,8},{16,12},{20,16},{24,20},{28,24},{1,29},{... | collective-permute-start | bytes 2359304 | tf_op jit(solution)/shard_map/ppermute | solution.py:152
  28.1 27.3 %collective-permute-start.10 = (bf16[256,512]{1,0:T(8,128)(2,1)S(1)}, bf16[256,512]{1,0:T(8,128)(2,1)S(1)}, u32[]{:S(2)}, u32[]{:S(2)}) collective-permute-start(bf16[256,512]{1,0:T(8,128)(2,1)S(1)} %slice.101), channel_id=1, source_target_pairs={{0,8},{8,0},{16,24},{24,16},{1,9},{9,1},{17,25},{25,17},{2,10},{10... | collective-permute-start | bytes 786440 | tf_op jit(solution)/shard_map/ppermute | solution.py:148
  29.4 33.3 %collective-permute-start.9 = (bf16[256,1024]{1,0:T(8,128)(2,1)S(1)}, bf16[256,1024]{1,0:T(8,128)(2,1)S(1)}, u32[]{:S(2)}, u32[]{:S(2)}) collective-permute-start(bf16[256,1024]{1,0:T(8,128)(2,1)S(1)} %slice.100), channel_id=1, source_target_pairs={{0,2},{2,0},{1,3},{3,1},{4,6},{6,4},{5,7},{7,5},{8,10},{10,8},{9,1... | collective-permute-start | bytes 1572872 | tf_op jit(solution)/shard_map/ppermute | solution.py:148
  31.0 27.8 %collective-permute-start.8 = (bf16[256,512]{1,0:T(8,128)(2,1)S(1)}, bf16[256,512]{1,0:T(8,128)(2,1)S(1)}, u32[]{:S(2)}, u32[]{:S(2)}) collective-permute-start(bf16[256,512]{1,0:T(8,128)(2,1)S(1)} %slice.99), channel_id=1, source_target_pairs={{0,16},{8,24},{16,0},{24,8},{1,17},{9,25},{17,1},{25,9},{2,18},{10... | collective-permute-start | bytes 786440 | tf_op jit(solution)/shard_map/ppermute | solution.py:148
  49.1 8.1 %collective-permute-start.11 = (bf16[48,256]{1,0:T(8,128)(2,1)S(1)}, bf16[48,256]{1,0:T(8,128)(2,1)S(1)}, u32[]{:S(2)}, u32[]{:S(2)}) collective-permute-start(bf16[48,256]{1,0:T(8,128)(2,1)S(1)} %pad_maximum_fusion.18), channel_id=1, source_target_pairs={{0,16},{8,24},{16,0},{24,8},{1,17},{9,25},{17,1},{25,9},{2,18},{10... | collective-permute-start | bytes 73736 | tf_op jit(solution)/shard_map/ppermute | solution.py:148
  49.4 13.3 %collective-permute-start.7 = (bf16[256,1024]{1,0:T(8,128)(2,1)S(1)}, bf16[256,1024]{1,0:T(8,128)(2,1)S(1)}, u32[]{:S(2)}, u32[]{:S(2)}) collective-permute-start(bf16[256,1024]{1,0:T(8,128)(2,1)S(1)} %slice.98), channel_id=1, source_target_pairs={{0,4},{4,0},{1,5},{5,1},{2,6},{6,2},{3,7},{7,3},{8,12},{12,8},{9,1... | collective-permute-start | bytes 1572872 | tf_op jit(solution)/shard_map/ppermute | solution.py:148
  57.2 5.5 %collective-permute-start.12 = (bf16[48,512]{1,0:T(8,128)(2,1)S(1)}, bf16[48,512]{1,0:T(8,128)(2,1)S(1)}, u32[]{:S(2)}, u32[]{:S(2)}) collective-permute-start(bf16[48,512]{1,0:T(8,128)(2,1)S(1)} %pad_maximum_fusion.17), channel_id=1, source_target_pairs={{0,4},{4,0},{1,5},{5,1},{2,6},{6,2},{3,7},{7,3},{8,12},{12,8},{9,1... | collective-permute-start | bytes 147464 | tf_op jit(solution)/shard_map/ppermute | solution.py:148
  63.1 27.2 %collective-permute-start.15 = (bf16[512,1024]{1,0:T(8,128)(2,1)S(1)}, bf16[512,1024]{1,0:T(8,128)(2,1)S(1)}, u32[]{:S(2)}, u32[]{:S(2)}) collective-permute-start(bf16[512,1024]{1,0:T(8,128)(2,1)S(1)} %pad_maximum_fusion.6), channel_id=1, source_target_pairs={{0,4},{4,0},{1,5},{5,1},{2,6},{6,2},{3,7},{7,3},{8,12},{12,8},{9,1... | collective-permute-start | bytes 3145736 | tf_op jit(solution)/shard_map/ppermute | solution.py:148
  64.4 26.1 %collective-permute-start.14 = (bf16[512,1024]{1,0:T(8,128)(2,1)S(1)}, bf16[512,1024]{1,0:T(8,128)(2,1)S(1)}, u32[]{:S(2)}, u32[]{:S(2)}) collective-permute-start(bf16[512,1024]{1,0:T(8,128)(2,1)S(1)} %pad_maximum_fusion.5), channel_id=1, source_target_pairs={{0,2},{2,0},{1,3},{3,1},{4,6},{6,4},{5,7},{7,5},{8,10},{10,8},{9,1... | collective-permute-start | bytes 3145736 | tf_op jit(solution)/shard_map/ppermute | solution.py:148
  66.0 24.1 %collective-permute-start.16 = (bf16[512,512]{1,0:T(8,128)(2,1)S(1)}, bf16[512,512]{1,0:T(8,128)(2,1)S(1)}, u32[]{:S(2)}, u32[]{:S(2)}) collective-permute-start(bf16[512,512]{1,0:T(8,128)(2,1)S(1)} %get-tuple-element.127), channel_id=1, source_target_pairs={{0,8},{8,0},{16,24},{24,16},{1,9},{9,1},{17,25},{25,17},{2,10},{10... | collective-permute-start | bytes 1572872 | tf_op jit(solution)/shard_map/ppermute | solution.py:148
  68.7 21.5 %collective-permute-start.13 = (bf16[512,512]{1,0:T(8,128)(2,1)S(1)}, bf16[512,512]{1,0:T(8,128)(2,1)S(1)}, u32[]{:S(2)}, u32[]{:S(2)}) collective-permute-start(bf16[512,512]{1,0:T(8,128)(2,1)S(1)} %get-tuple-element.130), channel_id=1, source_target_pairs={{0,16},{8,24},{16,0},{24,8},{1,17},{9,25},{17,1},{25,9},{2,18},{10... | collective-permute-start | bytes 1572872 | tf_op jit(solution)/shard_map/ppermute | solution.py:148
  69.7 20.4 %collective-permute-start.17 = (bf16[48,1024]{1,0:T(8,128)(2,1)S(1)}, bf16[48,1024]{1,0:T(8,128)(2,1)S(1)}, u32[]{:S(2)}, u32[]{:S(2)}) collective-permute-start(bf16[48,1024]{1,0:T(8,128)(2,1)S(1)} %pad_maximum_fusion.16.notes_ref), channel_id=1, source_target_pairs={{0,2},{2,0},{1,3},{3,1},{4,6},{6,4},{5,7},{7,5},{8,10},{10,8},{9,1... | collective-permute-start | bytes 294920 | tf_op jit(solution)/shard_map/ppermute | solution.py:148
  90.8 5.7 %collective-permute-start.20 = (bf16[448,2048]{1,0:T(8,128)(2,1)S(1)}, bf16[448,2048]{1,0:T(8,128)(2,1)S(1)}, u32[]{:S(2)}, u32[]{:S(2)}) collective-permute-start(bf16[448,2048]{1,0:T(8,128)(2,1)S(1)} %get-tuple-element.88.mine_ref), channel_id=1, source_target_pairs={{0,1},{1,0},{2,3},{3,2},{4,5},{5,4},{6,7},{7,6},{8,9},{9,8},{10,11... | collective-permute-start | bytes 5505032 | tf_op jit(solution)/shard_map/ppermute | solution.py:148
  91.0 25.6 %collective-permute-start.25 = (bf16[1024,512]{1,0:T(8,128)(2,1)S(1)}, bf16[1024,512]{1,0:T(8,128)(2,1)S(1)}, u32[]{:S(2)}, u32[]{:S(2)}) collective-permute-start(bf16[1024,512]{1,0:T(8,128)(2,1)S(1)} %get-tuple-element.123.near_ref), channel_id=1, source_target_pairs={{0,4},{4,0},{1,5},{5,1},{2,6},{6,2},{3,7},{7,3},{8,12},{12,8},{9,1... | collective-permute-start | bytes 3145736 | tf_op jit(solution)/shard_map/ppermute | solution.py:148
  92.6 28.7 %collective-permute-start.23 = (bf16[1024,512]{1,0:T(8,128)(2,1)S(1)}, bf16[1024,512]{1,0:T(8,128)(2,1)S(1)}, u32[]{:S(2)}, u32[]{:S(2)}) collective-permute-start(bf16[1024,512]{1,0:T(8,128)(2,1)S(1)} %pad_maximum_fusion.4.near_ref), channel_id=1, source_target_pairs={{0,2},{2,0},{1,3},{3,1},{4,6},{6,4},{5,7},{7,5},{8,10},{10,8},{9,1... | collective-permute-start | bytes 3145736 | tf_op jit(solution)/shard_map/ppermute | solution.py:148
  93.3 47.3 %collective-permute-start.18 = (bf16[1024,512]{1,0:T(8,128)(2,1)S(1)}, bf16[1024,512]{1,0:T(8,128)(2,1)S(1)}, u32[]{:S(2)}, u32[]{:S(2)}) collective-permute-start(bf16[1024,512]{1,0:T(8,128)(2,1)S(1)} %get-tuple-element.119.e8), channel_id=1, source_target_pairs={{0,8},{8,0},{16,24},{24,16},{1,9},{9,1},{17,25},{25,17},{2,10},{10... | collective-permute-start | bytes 3145736 | tf_op jit(solution)/shard_map/ppermute | solution.py:148
  93.4 48.6 %collective-permute-start.19 = (bf16[1024,512]{1,0:T(8,128)(2,1)S(1)}, bf16[1024,512]{1,0:T(8,128)(2,1)S(1)}, u32[]{:S(2)}, u32[]{:S(2)}) collective-permute-start(bf16[1024,512]{1,0:T(8,128)(2,1)S(1)} %get-tuple-element.121.d8), channel_id=1, source_target_pairs={{0,16},{8,24},{16,0},{24,8},{1,17},{9,25},{17,1},{25,9},{2,18},{10... | collective-permute-start | bytes 3145736 | tf_op jit(solution)/shard_map/ppermute | solution.py:148
  107.6 34.5 %collective-permute-start.21 = (bf16[1024,512]{1,0:T(8,128)(2,1)S(1)}, bf16[1024,512]{1,0:T(8,128)(2,1)S(1)}, u32[]{:S(2)}, u32[]{:S(2)}) collective-permute-start(bf16[1024,512]{1,0:T(8,128)(2,1)S(1)} %get-tuple-element.96.near_ref), channel_id=1, source_target_pairs={{0,2},{2,0},{1,3},{3,1},{4,6},{6,4},{5,7},{7,5},{8,10},{10,8},{9,1... | collective-permute-start | bytes 3145736 | tf_op jit(solution)/shard_map/ppermute | solution.py:148
  116.6 25.5 %collective-permute-start.22 = (bf16[1024,512]{1,0:T(8,128)(2,1)S(1)}, bf16[1024,512]{1,0:T(8,128)(2,1)S(1)}, u32[]{:S(2)}, u32[]{:S(2)}) collective-permute-start(bf16[1024,512]{1,0:T(8,128)(2,1)S(1)} %pad_maximum_fusion.7.near_ref), channel_id=1, source_target_pairs={{0,4},{4,0},{1,5},{5,1},{2,6},{6,2},{3,7},{7,3},{8,12},{12,8},{9,1... | collective-permute-start | bytes 3145736 | tf_op jit(solution)/shard_map/ppermute | solution.py:148
  121.2 20.7 %collective-permute-start.26 = (bf16[448,256]{1,0:T(8,128)(2,1)S(1)}, bf16[448,256]{1,0:T(8,128)(2,1)S(1)}, u32[]{:S(2)}, u32[]{:S(2)}) collective-permute-start(bf16[448,256]{1,0:T(8,128)(2,1)S(1)} %get-tuple-element.104), channel_id=1, source_target_pairs={{0,1},{1,0},{2,3},{3,2},{4,5},{5,4},{6,7},{7,6},{8,9},{9,8},{10,11... | collective-permute-start | bytes 688136 | tf_op jit(solution)/shard_map/ppermute | solution.py:148
  140.6 1.5 collective-permute-start.24
  142.1 9.2 %collective-permute-start.29 = (bf16[1024,512]{1,0:T(8,128)(2,1)S(1)}, bf16[1024,512]{1,0:T(8,128)(2,1)S(1)}, u32[]{:S(2)}, u32[]{:S(2)}) collective-permute-start(bf16[1024,512]{1,0:T(8,128)(2,1)S(1)} %get-tuple-element.119.e8), channel_id=1, source_target_pairs={{0,1},{1,0},{2,3},{3,2},{4,5},{5,4},{6,7},{7,6},{8,9},{9,8},{10,11... | collective-permute-start | bytes 3145736 | tf_op jit(solution)/shard_map/ppermute | solution.py:148
  142.2 9.1 %collective-permute-start.30 = (bf16[1024,512]{1,0:T(8,128)(2,1)S(1)}, bf16[1024,512]{1,0:T(8,128)(2,1)S(1)}, u32[]{:S(2)}, u32[]{:S(2)}) collective-permute-start(bf16[1024,512]{1,0:T(8,128)(2,1)S(1)} %collective-permute-done.18.er), channel_id=1, source_target_pairs={{0,1},{1,0},{2,3},{3,2},{4,5},{5,4},{6,7},{7,6},{8,9},{9,8},{10,11... | collective-permute-start | bytes 3145736 | tf_op jit(solution)/shard_map/ppermute | solution.py:148
  142.6 8.7 %collective-permute-start.31 = (bf16[1024,512]{1,0:T(8,128)(2,1)S(1)}, bf16[1024,512]{1,0:T(8,128)(2,1)S(1)}, u32[]{:S(2)}, u32[]{:S(2)}) collective-permute-start(bf16[1024,512]{1,0:T(8,128)(2,1)S(1)} %get-tuple-element.121.d8), channel_id=1, source_target_pairs={{0,1},{1,0},{2,3},{3,2},{4,5},{5,4},{6,7},{7,6},{8,9},{9,8},{10,11... | collective-permute-start | bytes 3145736 | tf_op jit(solution)/shard_map/ppermute | solution.py:148
  142.8 8.6 %collective-permute-start.32 = (bf16[1024,512]{1,0:T(8,128)(2,1)S(1)}, bf16[1024,512]{1,0:T(8,128)(2,1)S(1)}, u32[]{:S(2)}, u32[]{:S(2)}) collective-permute-start(bf16[1024,512]{1,0:T(8,128)(2,1)S(1)} %collective-permute-done.19.dr), channel_id=1, source_target_pairs={{0,1},{1,0},{2,3},{3,2},{4,5},{5,4},{6,7},{7,6},{8,9},{9,8},{10,11... | collective-permute-start | bytes 3145736 | tf_op jit(solution)/shard_map/ppermute | solution.py:148
  146.2 3.5 %collective-permute-start.28 = (bf16[448,256]{1,0:T(8,128)(2,1)S(1)}, bf16[448,256]{1,0:T(8,128)(2,1)S(1)}, u32[]{:S(2)}, u32[]{:S(2)}) collective-permute-start(bf16[448,256]{1,0:T(8,128)(2,1)S(1)} %get-tuple-element.116), channel_id=1, source_target_pairs={{0,1},{1,0},{2,3},{3,2},{4,5},{5,4},{6,7},{7,6},{8,9},{9,8},{10,11... | collective-permute-start | bytes 688136 | tf_op jit(solution)/shard_map/ppermute | solution.py:148
  149.8 1.6 collective-permute-start.27
  (8 other events, 17.6 us)

commit v8 on v7

--- a/solution.py
+++ b/solution.py
@@ -532,7 +532,10 @@
     in1_far, in3_far = hop(in1, "x"), hop(in3, "y")
     n1, n2, n3, n4, small = prep(spread, hop(spread, "c"), notes)
     part1, part2, part3, part4 = early(n1, in1), early(n2, in2), early(n3, in3), early(n4, in4)
-    in2, in4, small, part1, part2, part3, part4 = tie(in2, in4, small, part1, part2, part3, part4)
+    in2, in4, small, part1, part2, part3, part4, out1, out2 = tie(
+        in2, in4, small, part1, part2, part3, part4, out1, out2
+    )
+    out1_other, out2_other = hop(out1, "c"), hop(out2, "c")
     in2_far, in4_far = hop(in2, "x"), hop(in4, "y")
 
     def run(normed, which, part, far):
@@ -541,11 +544,10 @@
 
     m0, o0 = run(n1, 0, part1, in1_far)
     m2, o2 = run(n3, 2, part3, in3_far)
-    out1, out2, out1_far, out2_far, in2_far, in4_far, m0, o0, m2, o2 = tie(
-        out1, out2, out1_far, out2_far, in2_far, in4_far, m0, o0, m2, o2
-    )
-    weights = [out1, out1_far, out2, out2_far]
-    weights = weights + [hop(array, "c") for array in weights]
+    out1_other, out2_other, out1_far, out2_far, in2_far, in4_far, m0, o0, m2, o2 = tie(
+        out1_other, out2_other, out1_far, out2_far, in2_far, in4_far, m0, o0, m2, o2
+    )
+    weights = [out1, out1_far, out2, out2_far, out1_other, hop(out1_far, "c"), out2_other, hop(out2_far, "c")]
     m1, o1 = run(n2, 1, part2, in2_far)
     m3, o3 = run(n4, 3, part4, in4_far)
     mixed = finish((m0, m1, m2, m3), (o0, o1, o2, o3), small, pick, base, weights)

time: 159 us -> 181 us (1.14)
  waiting for transfers between devices: 81.1 us -> 104 us
    ppermute x31, waiting for transfers between devices: 64.8 us -> 87.3 us  [hop(): return lax.ppermute(array, axis, pairs)]
  transfers between devices with their start and end apart: 33 -> 33, of which waited for: 13 -> 14; matrix products, arithmetic and copies ran while one was open for 1% -> 1% of each run, Pallas kernels for 19% -> 17%
where the time goes in v8:
time: 181 us; the launch traced here: 180 us
  waiting for transfers between devices  104 us (57%)
  Pallas kernels  36.7 us (20%)
  starting transfers between devices  35.7 us (20%)
  local copies, waits for them, and re-layouts  2.23 us (1%)
    ppermute x31, waiting for transfers between devices, hop(): return lax.ppermute(array, axis, pairs)  87.3 us
    ppermute x31, starting transfers between devices, hop(): return lax.ppermute(array, axis, pairs)  31 us
    ppermute x2, waiting for transfers between devices, turn(): lax.ppermute(array, ('z', 'y'), [(i, (i + by) % 8) for i in range(8)])  16.3 us
    pallas_call x4, Pallas kernels, conv(): pl.pallas_call(functools.partial(conv_kernel, sub), out_shape=(out, out),...  12.6 us
    pallas_call x1, Pallas kernels, finish(): pl.pallas_call(finish_kernel, out_shape=shape(RCV_DEV, D), in_specs=vmem(...  6.84 us
    pallas_call x1, Pallas kernels, prep(): pl.pallas_call(prep_kernel, out_shape=(jax.ShapeDtypeStruct((2, PAIR, HAL...  6.71 us
    ppermute x2, starting transfers between devices, turn(): lax.ppermute(array, ('z', 'y'), [(i, (i + by) % 8) for i in range(8)])  4.72 us
    pallas_call x4, Pallas kernels, early(): pl.pallas_call(early_kernel, out_shape=shape(PAIR, near.shape[1], jnp.flo...  4.44 us
  transfers between devices with their start and end apart: 33, of which 14 were waited for; matrix products, arithmetic and copies ran while one was open for 1% of the time, Pallas kernels for 17%

profile of v8, /device:TPU:0, one launch (start us, length us, event | category | flops | bytes accessed | tf_op | source)
XLA Modules:
  0.0 180.5 jit_solution(1967618203055866249)
XLA Ops:
  0.0 1.4 fusion.5
  2.4 2.0 %cut.1 = (bf16[192,2048]{1,0:T(8,128)(2,1)S(1)}, bf16[192,2048]{1,0:T(8,128)(2,1)S(1)}, bf16[48,128]{1,0:T(8,128)(2,1)S(1)}) custom-call(s32[1,3]{1,0:T(1,128)S(1)} %copy-done.1, s32[1,3]{1,0:T(1,128)S(1)} %copy-done.2, s32[1,3]{1,0:T(1,128)S(1)} %copy-done.3, bf16[576,2048]{1,0:T(8,128)(2,1)S(1)} %bitcast.5, bf16[48,128]{1,0:T(8,128)(2,1)S(1)} %pad_select_fusion.notes_ref), custom_call_target="tpu_custom_call" | custom-call | flops 1048576 | bytes 65536 | tf_op jit(solution)/shard_map/cut/pallas_call | solution.py:248
  4.7 3.7 %collective-permute-start.2 = (bf16[128,1536]{1,0:T(8,128)(2,1)S(1)}, bf16[128,1536]{1,0:T(8,128)(2,1)S(1)}, u32[]{:S(2)}, u32[]{:S(2)}) collective-permute-start(bf16[128,1536]{1,0:T(8,128)(2,1)S(1)} %pad_maximum_fusion.14), channel_id=1, source_target_pairs={{0,16},{8,24},{16,0},{24,8},{1,17},{9,25},{17,1},{25,9},{2,18},{10... | collective-permute-start | bytes 1179656 | tf_op jit(solution)/shard_map/ppermute | solution.py:148
  8.5 1.6 collective-permute-start.1
  11.7 1.5 collective-permute-start.5
  13.2 3.2 %collective-permute-start.6 = (bf16[192,2048]{1,0:T(8,128)(2,1)S(1)}, bf16[192,2048]{1,0:T(8,128)(2,1)S(1)}, u32[]{:S(2)}, u32[]{:S(2)}) collective-permute-start(bf16[192,2048]{1,0:T(8,128)(2,1)S(1)} %get-tuple-element.73), channel_id=1, source_target_pairs={{0,28},{4,0},{8,4},{12,8},{16,12},{20,16},{24,20},{28,24},{1,29},{... | collective-permute-start | bytes 2359304 | tf_op jit(solution)/shard_map/ppermute | solution.py:152
  16.5 11.5 %collective-permute-done.4 = bf16[48,128]{1,0:T(8,128)(2,1)S(1)} collective-permute-done((bf16[48,128]{1,0:T(8,128)(2,1)S(1)}, bf16[48,128]{1,0:T(8,128)(2,1)S(1)}, u32[]{:S(2)}, u32[]{:S(2)}) %collective-permute-start.4) | collective-permute-done | bytes 12320 | tf_op jit(solution)/shard_map/ppermute | solution.py:148
  28.1 1.2 collective-permute-start.10
  29.4 1.6 collective-permute-start.9
  31.0 1.8 collective-permute-start.8
  32.8 13.6 %collective-permute-done.5.prev_ref = bf16[192,2048]{1,0:T(8,128)(2,1)S(1)} collective-permute-done((bf16[192,2048]{1,0:T(8,128)(2,1)S(1)}, bf16[192,2048]{1,0:T(8,128)(2,1)S(1)}, u32[]{:S(2)}, u32[]{:S(2)}) %collective-permute-start.5) | collective-permute-done | bytes 786464 | tf_op jit(solution)/shard_map/ppermute | solution.py:152
  46.4 2.7 %collective-permute-done.6.next_ref = bf16[192,2048]{1,0:T(8,128)(2,1)S(1)} collective-permute-done((bf16[192,2048]{1,0:T(8,128)(2,1)S(1)}, bf16[192,2048]{1,0:T(8,128)(2,1)S(1)}, u32[]{:S(2)}, u32[]{:S(2)}) %collective-permute-start.6) | collective-permute-done | bytes 786464 | tf_op jit(solution)/shard_map/ppermute | solution.py:152
  49.4 2.5 %collective-permute-start.7 = (bf16[256,1024]{1,0:T(8,128)(2,1)S(1)}, bf16[256,1024]{1,0:T(8,128)(2,1)S(1)}, u32[]{:S(2)}, u32[]{:S(2)}) collective-permute-start(bf16[256,1024]{1,0:T(8,128)(2,1)S(1)} %slice.98), channel_id=1, source_target_pairs={{0,4},{4,0},{1,5},{5,1},{2,6},{6,2},{3,7},{7,3},{8,12},{12,8},{9,1... | collective-permute-start | bytes 1572872 | tf_op jit(solution)/shard_map/ppermute | solution.py:148
  51.9 3.5 %collective-permute-done.10 = bf16[256,512]{1,0:T(8,128)(2,1)S(1)} collective-permute-done((bf16[256,512]{1,0:T(8,128)(2,1)S(1)}, bf16[256,512]{1,0:T(8,128)(2,1)S(1)}, u32[]{:S(2)}, u32[]{:S(2)}) %collective-permute-start.10) | collective-permute-done | bytes 262176 | tf_op jit(solution)/shard_map/ppermute | solution.py:148
  55.4 1.7 collective-permute-done.11
  57.2 1.6 collective-permute-start.12
  58.8 3.9 %collective-permute-done.12 = bf16[48,512]{1,0:T(8,128)(2,1)S(1)} collective-permute-done((bf16[48,512]{1,0:T(8,128)(2,1)S(1)}, bf16[48,512]{1,0:T(8,128)(2,1)S(1)}, u32[]{:S(2)}, u32[]{:S(2)}) %collective-permute-start.12) | collective-permute-done | bytes 49184 | tf_op jit(solution)/shard_map/ppermute | solution.py:148
  64.4 1.6 collective-permute-start.14
  66.0 2.7 %collective-permute-start.16 = (bf16[512,512]{1,0:T(8,128)(2,1)S(1)}, bf16[512,512]{1,0:T(8,128)(2,1)S(1)}, u32[]{:S(2)}, u32[]{:S(2)}) collective-permute-start(bf16[512,512]{1,0:T(8,128)(2,1)S(1)} %get-tuple-element.131), channel_id=1, source_target_pairs={{0,8},{8,0},{16,24},{24,16},{1,9},{9,1},{17,25},{25,17},{2,10},{10... | collective-permute-start | bytes 1572872 | tf_op jit(solution)/shard_map/ppermute | solution.py:148
  70.2 4.1 %place.1 = (bf16[448,2048]{1,0:T(8,128)(2,1)S(1)}, bf16[384,2048]{1,0:T(8,128)(2,1)S(1)}, bf16[384,448]{1,0:T(8,128)(2,1)S(1)}) custom-call(s32[1,3]{1,0:T(1,128)S(1)} %copy-done.1, s32[1,3]{1,0:T(1,128)S(1)} %copy-done.2, s32[1,3]{1,0:T(1,128)S(1)} %copy-done.3, bf16[576,2048]{1,0:T(8,128)(2,1)S(1)} %bitcast.6, ...), custom_call_target="tpu_custom_call" | custom-call | flops 1048576 | bytes 65536 | tf_op jit(solution)/shard_map/place/pallas_call | solution.py:301
  74.4 15.8 %collective-permute-done.17 = bf16[48,1024]{1,0:T(8,128)(2,1)S(1)} collective-permute-done((bf16[48,1024]{1,0:T(8,128)(2,1)S(1)}, bf16[48,1024]{1,0:T(8,128)(2,1)S(1)}, u32[]{:S(2)}, u32[]{:S(2)}) %collective-permute-start.17) | collective-permute-done | bytes 98336 | tf_op jit(solution)/shard_map/ppermute | solution.py:148
  91.0 1.6 collective-permute-start.27
  93.4 3.1 %collective-permute-start.22 = (bf16[1024,512]{1,0:T(8,128)(2,1)S(1)}, bf16[1024,512]{1,0:T(8,128)(2,1)S(1)}, u32[]{:S(2)}, u32[]{:S(2)}) collective-permute-start(bf16[1024,512]{1,0:T(8,128)(2,1)S(1)} %get-tuple-element.99.d8), channel_id=1, source_target_pairs={{0,16},{8,24},{16,0},{24,8},{1,17},{9,25},{17,1},{25,9},{2,18},{10... | collective-permute-start | bytes 3145736 | tf_op jit(solution)/shard_map/ppermute | solution.py:148
  96.5 6.7 %prep.1 = (bf16[2,896,1024]{2,1,0:T(8,128)(2,1)S(1)}, bf16[2,896,1024]{2,1,0:T(8,128)(2,1)S(1)}, bf16[2,896,1024]{2,1,0:T(8,128)(2,1)S(1)}, bf16[2,896,1024]{2,1,0:T(8,128)(2,1)S(1)}, f32[48,2048]{1,0:T(8,128)S(1)}) custom-call(bf16[448,2048]{1,0:T(8,128)(2,1)S(1)} %get-tuple-element.89.mine_ref, bf16[448,2048]{1,0:T(8,128)(2,1)S(1)} %collective-permute-done.18.other_ref, ...), custom_call_target="tpu_custom_call" | custom-call | flops 1048576 | bytes 65536 | tf_op jit(solution)/shard_map/prep/pallas_call | solution.py:336
  107.7 8.9 %collective-permute-done.27.far_ref = bf16[1024,512]{1,0:T(8,128)(2,1)S(1)} collective-permute-done((bf16[1024,512]{1,0:T(8,128)(2,1)S(1)}, bf16[1024,512]{1,0:T(8,128)(2,1)S(1)}, u32[]{:S(2)}, u32[]{:S(2)}) %collective-permute-start.27) | collective-permute-done | bytes 1048608 | tf_op jit(solution)/shard_map/ppermute | solution.py:148
  118.4 22.2 %collective-permute-done.21.er = bf16[1024,512]{1,0:T(8,128)(2,1)S(1)} collective-permute-done((bf16[1024,512]{1,0:T(8,128)(2,1)S(1)}, bf16[1024,512]{1,0:T(8,128)(2,1)S(1)}, u32[]{:S(2)}, u32[]{:S(2)}) %collective-permute-start.21) | collective-permute-done | bytes 1048608 | tf_op jit(solution)/shard_map/ppermute | solution.py:148
  141.6 3.1 %conv.5 = (bf16[448,256]{1,0:T(8,128)(2,1)S(1)}, bf16[448,256]{1,0:T(8,128)(2,1)S(1)}) custom-call(bf16[2,896,1024]{2,1,0:T(8,128)(2,1)S(1)} %get-tuple-element.95.rows_ref, f32[896,512]{1,0:T(8,128)S(1)} %early.6.part_ref, bf16[1024,512]{1,0:T(8,128)(2,1)S(1)} %collective-permute-done.27.far_ref, f32[48,2048]{1,0:T(8,128)S(1)} %get-tuple-element.103.small_ref), custom_call_target="tpu_custom_call" | custom-call | flops 1048576 | bytes 65536 | tf_op jit(solution)/shard_map/conv/pallas_call | solution.py:396
  144.8 3.1 %conv.4 = (bf16[448,256]{1,0:T(8,128)(2,1)S(1)}, bf16[448,256]{1,0:T(8,128)(2,1)S(1)}) custom-call(bf16[2,896,1024]{2,1,0:T(8,128)(2,1)S(1)} %get-tuple-element.92.rows_ref, f32[896,512]{1,0:T(8,128)S(1)} %early.4.part_ref, bf16[1024,512]{1,0:T(8,128)(2,1)S(1)} %collective-permute-done.25.far_ref, f32[48,2048]{1,0:T(8,128)S(1)} %get-tuple-element.103.small_ref), custom_call_target="tpu_custom_call" | custom-call | flops 1048576 | bytes 65536 | tf_op jit(solution)/shard_map/conv/pallas_call | solution.py:396
  149.6 15.2 %collective-permute-done.24.far_ref = bf16[1024,512]{1,0:T(8,128)(2,1)S(1)} collective-permute-done((bf16[1024,512]{1,0:T(8,128)(2,1)S(1)}, bf16[1024,512]{1,0:T(8,128)(2,1)S(1)}, u32[]{:S(2)}, u32[]{:S(2)}) %collective-permute-start.24) | collective-permute-done | bytes 1048608 | tf_op jit(solution)/shard_map/ppermute | solution.py:148
  165.3 3.1 %conv.7 = (bf16[448,256]{1,0:T(8,128)(2,1)S(1)}, bf16[448,256]{1,0:T(8,128)(2,1)S(1)}) custom-call(bf16[2,896,1024]{2,1,0:T(8,128)(2,1)S(1)} %get-tuple-element.97.rows_ref, f32[896,512]{1,0:T(8,128)S(1)} %early.7.part_ref, bf16[1024,512]{1,0:T(8,128)(2,1)S(1)} %collective-permute-done.24.far_ref, f32[48,2048]{1,0:T(8,128)S(1)} %get-tuple-element.103.small_ref), custom_call_target="tpu_custom_call" | custom-call | flops 1048576 | bytes 65536 | tf_op jit(solution)/shard_map/conv/pallas_call | solution.py:396
  168.4 3.3 %conv.6 = (bf16[448,256]{1,0:T(8,128)(2,1)S(1)}, bf16[448,256]{1,0:T(8,128)(2,1)S(1)}) custom-call(bf16[2,896,1024]{2,1,0:T(8,128)(2,1)S(1)} %get-tuple-element.94.rows_ref, f32[896,512]{1,0:T(8,128)S(1)} %early.5.part_ref, bf16[1024,512]{1,0:T(8,128)(2,1)S(1)} %collective-permute-done.23.far_ref, f32[48,2048]{1,0:T(8,128)S(1)} %get-tuple-element.103.small_ref), custom_call_target="tpu_custom_call" | custom-call | flops 1048576 | bytes 65536 | tf_op jit(solution)/shard_map/conv/pallas_call | solution.py:396
  173.4 6.8 %finish.1 = bf16[384,2048]{1,0:T(8,128)(2,1)} custom-call(bf16[448,256]{1,0:T(8,128)(2,1)S(1)} %get-tuple-element.109.m0, bf16[448,256]{1,0:T(8,128)(2,1)S(1)} %get-tuple-element.112.m1, bf16[448,256]{1,0:T(8,128)(2,1)S(1)} %get-tuple-element.113.m2, bf16[448,256]{1,0:T(8,128)(2,1)S(1)} %get-tuple-element.116.m3, ...), custom_call_target="tpu_custom_call" | custom-call | flops 1048576 | bytes 65536 | tf_op jit(solution)/shard_map/finish/pallas_call | solution.py:457
  (99 shorter events, 19.7 us)
Async XLA Ops:
  1.6 2.8 %collective-permute-start = (bf16[64,3072]{1,0:T(8,128)(2,1)S(1)}, bf16[64,3072]{1,0:T(8,128)(2,1)S(1)}, u32[]{:S(2)}, u32[]{:S(2)}) collective-permute-start(bf16[64,3072]{1,0:T(8,128)(2,1)S(1)} %get-tuple-element.140), channel_id=1, source_target_pairs={{0,1},{1,0},{2,3},{3,2},{4,5},{5,4},{6,7},{7,6},{8,9},{9,8},{10,11... | collective-permute-start | bytes 1179656 | tf_op jit(solution)/shard_map/ppermute | solution.py:148
  4.7 23.2 %collective-permute-start.2 = (bf16[128,1536]{1,0:T(8,128)(2,1)S(1)}, bf16[128,1536]{1,0:T(8,128)(2,1)S(1)}, u32[]{:S(2)}, u32[]{:S(2)}) collective-permute-start(bf16[128,1536]{1,0:T(8,128)(2,1)S(1)} %pad_maximum_fusion.14), channel_id=1, source_target_pairs={{0,16},{8,24},{16,0},{24,8},{1,17},{9,25},{17,1},{25,9},{2,18},{10... | collective-permute-start | bytes 1179656 | tf_op jit(solution)/shard_map/ppermute | solution.py:148
  8.5 19.6 %collective-permute-start.1 = (bf16[128,1536]{1,0:T(8,128)(2,1)S(1)}, bf16[128,1536]{1,0:T(8,128)(2,1)S(1)}, u32[]{:S(2)}, u32[]{:S(2)}) collective-permute-start(bf16[128,1536]{1,0:T(8,128)(2,1)S(1)} %get-tuple-element.138), channel_id=1, source_target_pairs={{0,8},{8,0},{16,24},{24,16},{1,9},{9,1},{17,25},{25,17},{2,10},{10... | collective-permute-start | bytes 1179656 | tf_op jit(solution)/shard_map/ppermute | solution.py:148
  11.2 16.7 %collective-permute-start.4 = (bf16[48,128]{1,0:T(8,128)(2,1)S(1)}, bf16[48,128]{1,0:T(8,128)(2,1)S(1)}, u32[]{:S(2)}, u32[]{:S(2)}) collective-permute-start(bf16[48,128]{1,0:T(8,128)(2,1)S(1)} %add.7), channel_id=1, source_target_pairs={{0,8},{8,0},{16,24},{24,16},{1,9},{9,1},{17,25},{25,17},{2,10},{10... | collective-permute-start | bytes 36872 | tf_op jit(solution)/shard_map/ppermute | solution.py:148
  11.7 34.7 %collective-permute-start.5 = (bf16[192,2048]{1,0:T(8,128)(2,1)S(1)}, bf16[192,2048]{1,0:T(8,128)(2,1)S(1)}, u32[]{:S(2)}, u32[]{:S(2)}) collective-permute-start(bf16[192,2048]{1,0:T(8,128)(2,1)S(1)} %get-tuple-element.72), channel_id=1, source_target_pairs={{0,4},{4,8},{8,12},{12,16},{16,20},{20,24},{24,28},{28,0},{1,5},{5... | collective-permute-start | bytes 2359304 | tf_op jit(solution)/shard_map/ppermute | solution.py:152
  13.2 35.8 %collective-permute-start.6 = (bf16[192,2048]{1,0:T(8,128)(2,1)S(1)}, bf16[192,2048]{1,0:T(8,128)(2,1)S(1)}, u32[]{:S(2)}, u32[]{:S(2)}) collective-permute-start(bf16[192,2048]{1,0:T(8,128)(2,1)S(1)} %get-tuple-element.73), channel_id=1, source_target_pairs={{0,28},{4,0},{8,4},{12,8},{16,12},{20,16},{24,20},{28,24},{1,29},{... | collective-permute-start | bytes 2359304 | tf_op jit(solution)/shard_map/ppermute | solution.py:152
  28.1 27.3 %collective-permute-start.10 = (bf16[256,512]{1,0:T(8,128)(2,1)S(1)}, bf16[256,512]{1,0:T(8,128)(2,1)S(1)}, u32[]{:S(2)}, u32[]{:S(2)}) collective-permute-start(bf16[256,512]{1,0:T(8,128)(2,1)S(1)} %slice.101), channel_id=1, source_target_pairs={{0,8},{8,0},{16,24},{24,16},{1,9},{9,1},{17,25},{25,17},{2,10},{10... | collective-permute-start | bytes 786440 | tf_op jit(solution)/shard_map/ppermute | solution.py:148
  29.4 33.3 %collective-permute-start.9 = (bf16[256,1024]{1,0:T(8,128)(2,1)S(1)}, bf16[256,1024]{1,0:T(8,128)(2,1)S(1)}, u32[]{:S(2)}, u32[]{:S(2)}) collective-permute-start(bf16[256,1024]{1,0:T(8,128)(2,1)S(1)} %slice.100), channel_id=1, source_target_pairs={{0,2},{2,0},{1,3},{3,1},{4,6},{6,4},{5,7},{7,5},{8,10},{10,8},{9,1... | collective-permute-start | bytes 1572872 | tf_op jit(solution)/shard_map/ppermute | solution.py:148
  31.0 27.8 %collective-permute-start.8 = (bf16[256,512]{1,0:T(8,128)(2,1)S(1)}, bf16[256,512]{1,0:T(8,128)(2,1)S(1)}, u32[]{:S(2)}, u32[]{:S(2)}) collective-permute-start(bf16[256,512]{1,0:T(8,128)(2,1)S(1)} %slice.99), channel_id=1, source_target_pairs={{0,16},{8,24},{16,0},{24,8},{1,17},{9,25},{17,1},{25,9},{2,18},{10... | collective-permute-start | bytes 786440 | tf_op jit(solution)/shard_map/ppermute | solution.py:148
  49.1 8.1 %collective-permute-start.11 = (bf16[48,256]{1,0:T(8,128)(2,1)S(1)}, bf16[48,256]{1,0:T(8,128)(2,1)S(1)}, u32[]{:S(2)}, u32[]{:S(2)}) collective-permute-start(bf16[48,256]{1,0:T(8,128)(2,1)S(1)} %pad_maximum_fusion.18), channel_id=1, source_target_pairs={{0,16},{8,24},{16,0},{24,8},{1,17},{9,25},{17,1},{25,9},{2,18},{10... | collective-permute-start | bytes 73736 | tf_op jit(solution)/shard_map/ppermute | solution.py:148
  49.4 13.3 %collective-permute-start.7 = (bf16[256,1024]{1,0:T(8,128)(2,1)S(1)}, bf16[256,1024]{1,0:T(8,128)(2,1)S(1)}, u32[]{:S(2)}, u32[]{:S(2)}) collective-permute-start(bf16[256,1024]{1,0:T(8,128)(2,1)S(1)} %slice.98), channel_id=1, source_target_pairs={{0,4},{4,0},{1,5},{5,1},{2,6},{6,2},{3,7},{7,3},{8,12},{12,8},{9,1... | collective-permute-start | bytes 1572872 | tf_op jit(solution)/shard_map/ppermute | solution.py:148
  57.2 5.5 %collective-permute-start.12 = (bf16[48,512]{1,0:T(8,128)(2,1)S(1)}, bf16[48,512]{1,0:T(8,128)(2,1)S(1)}, u32[]{:S(2)}, u32[]{:S(2)}) collective-permute-start(bf16[48,512]{1,0:T(8,128)(2,1)S(1)} %pad_maximum_fusion.17), channel_id=1, source_target_pairs={{0,4},{4,0},{1,5},{5,1},{2,6},{6,2},{3,7},{7,3},{8,12},{12,8},{9,1... | collective-permute-start | bytes 147464 | tf_op jit(solution)/shard_map/ppermute | solution.py:148
  63.1 27.2 %collective-permute-start.15 = (bf16[512,1024]{1,0:T(8,128)(2,1)S(1)}, bf16[512,1024]{1,0:T(8,128)(2,1)S(1)}, u32[]{:S(2)}, u32[]{:S(2)}) collective-permute-start(bf16[512,1024]{1,0:T(8,128)(2,1)S(1)} %pad_maximum_fusion.6), channel_id=1, source_target_pairs={{0,4},{4,0},{1,5},{5,1},{2,6},{6,2},{3,7},{7,3},{8,12},{12,8},{9,1... | collective-permute-start | bytes 3145736 | tf_op jit(solution)/shard_map/ppermute | solution.py:148
  64.4 26.1 %collective-permute-start.14 = (bf16[512,1024]{1,0:T(8,128)(2,1)S(1)}, bf16[512,1024]{1,0:T(8,128)(2,1)S(1)}, u32[]{:S(2)}, u32[]{:S(2)}) collective-permute-start(bf16[512,1024]{1,0:T(8,128)(2,1)S(1)} %pad_maximum_fusion.5), channel_id=1, source_target_pairs={{0,2},{2,0},{1,3},{3,1},{4,6},{6,4},{5,7},{7,5},{8,10},{10,8},{9,1... | collective-permute-start | bytes 3145736 | tf_op jit(solution)/shard_map/ppermute | solution.py:148
  66.0 24.1 %collective-permute-start.16 = (bf16[512,512]{1,0:T(8,128)(2,1)S(1)}, bf16[512,512]{1,0:T(8,128)(2,1)S(1)}, u32[]{:S(2)}, u32[]{:S(2)}) collective-permute-start(bf16[512,512]{1,0:T(8,128)(2,1)S(1)} %get-tuple-element.131), channel_id=1, source_target_pairs={{0,8},{8,0},{16,24},{24,16},{1,9},{9,1},{17,25},{25,17},{2,10},{10... | collective-permute-start | bytes 1572872 | tf_op jit(solution)/shard_map/ppermute | solution.py:148
  68.7 21.5 %collective-permute-start.13 = (bf16[512,512]{1,0:T(8,128)(2,1)S(1)}, bf16[512,512]{1,0:T(8,128)(2,1)S(1)}, u32[]{:S(2)}, u32[]{:S(2)}) collective-permute-start(bf16[512,512]{1,0:T(8,128)(2,1)S(1)} %get-tuple-element.134), channel_id=1, source_target_pairs={{0,16},{8,24},{16,0},{24,8},{1,17},{9,25},{17,1},{25,9},{2,18},{10... | collective-permute-start | bytes 1572872 | tf_op jit(solution)/shard_map/ppermute | solution.py:148
  69.7 20.4 %collective-permute-start.17 = (bf16[48,1024]{1,0:T(8,128)(2,1)S(1)}, bf16[48,1024]{1,0:T(8,128)(2,1)S(1)}, u32[]{:S(2)}, u32[]{:S(2)}) collective-permute-start(bf16[48,1024]{1,0:T(8,128)(2,1)S(1)} %pad_maximum_fusion.16.notes_ref), channel_id=1, source_target_pairs={{0,2},{2,0},{1,3},{3,1},{4,6},{6,4},{5,7},{7,5},{8,10},{10,8},{9,1... | collective-permute-start | bytes 294920 | tf_op jit(solution)/shard_map/ppermute | solution.py:148
  90.8 5.7 %collective-permute-start.18 = (bf16[448,2048]{1,0:T(8,128)(2,1)S(1)}, bf16[448,2048]{1,0:T(8,128)(2,1)S(1)}, u32[]{:S(2)}, u32[]{:S(2)}) collective-permute-start(bf16[448,2048]{1,0:T(8,128)(2,1)S(1)} %get-tuple-element.89.mine_ref), channel_id=1, source_target_pairs={{0,1},{1,0},{2,3},{3,2},{4,5},{5,4},{6,7},{7,6},{8,9},{9,8},{10,11... | collective-permute-start | bytes 5505032 | tf_op jit(solution)/shard_map/ppermute | solution.py:148
  91.0 25.6 %collective-permute-start.27 = (bf16[1024,512]{1,0:T(8,128)(2,1)S(1)}, bf16[1024,512]{1,0:T(8,128)(2,1)S(1)}, u32[]{:S(2)}, u32[]{:S(2)}) collective-permute-start(bf16[1024,512]{1,0:T(8,128)(2,1)S(1)} %get-tuple-element.128.near_ref), channel_id=1, source_target_pairs={{0,4},{4,0},{1,5},{5,1},{2,6},{6,2},{3,7},{7,3},{8,12},{12,8},{9,1... | collective-permute-start | bytes 3145736 | tf_op jit(solution)/shard_map/ppermute | solution.py:148
  92.6 25.3 %collective-permute-start.25 = (bf16[1024,512]{1,0:T(8,128)(2,1)S(1)}, bf16[1024,512]{1,0:T(8,128)(2,1)S(1)}, u32[]{:S(2)}, u32[]{:S(2)}) collective-permute-start(bf16[1024,512]{1,0:T(8,128)(2,1)S(1)} %pad_maximum_fusion.4.near_ref), channel_id=1, source_target_pairs={{0,2},{2,0},{1,3},{3,1},{4,6},{6,4},{5,7},{7,5},{8,10},{10,8},{9,1... | collective-permute-start | bytes 3145736 | tf_op jit(solution)/shard_map/ppermute | solution.py:148
  93.3 47.3 %collective-permute-start.21 = (bf16[1024,512]{1,0:T(8,128)(2,1)S(1)}, bf16[1024,512]{1,0:T(8,128)(2,1)S(1)}, u32[]{:S(2)}, u32[]{:S(2)}) collective-permute-start(bf16[1024,512]{1,0:T(8,128)(2,1)S(1)} %get-tuple-element.98.e8), channel_id=1, source_target_pairs={{0,8},{8,0},{16,24},{24,16},{1,9},{9,1},{17,25},{25,17},{2,10},{10... | collective-permute-start | bytes 3145736 | tf_op jit(solution)/shard_map/ppermute | solution.py:148
  93.4 51.3 %collective-permute-start.22 = (bf16[1024,512]{1,0:T(8,128)(2,1)S(1)}, bf16[1024,512]{1,0:T(8,128)(2,1)S(1)}, u32[]{:S(2)}, u32[]{:S(2)}) collective-permute-start(bf16[1024,512]{1,0:T(8,128)(2,1)S(1)} %get-tuple-element.99.d8), channel_id=1, source_target_pairs={{0,16},{8,24},{16,0},{24,8},{1,17},{9,25},{17,1},{25,9},{2,18},{10... | collective-permute-start | bytes 3145736 | tf_op jit(solution)/shard_map/ppermute | solution.py:148
  107.6 42.0 %collective-permute-start.19 = (bf16[1024,512]{1,0:T(8,128)(2,1)S(1)}, bf16[1024,512]{1,0:T(8,128)(2,1)S(1)}, u32[]{:S(2)}, u32[]{:S(2)}) collective-permute-start(bf16[1024,512]{1,0:T(8,128)(2,1)S(1)} %get-tuple-element.98.e8), channel_id=1, source_target_pairs={{0,1},{1,0},{2,3},{3,2},{4,5},{5,4},{6,7},{7,6},{8,9},{9,8},{10,11... | collective-permute-start | bytes 3145736 | tf_op jit(solution)/shard_map/ppermute | solution.py:148
  116.6 33.0 %collective-permute-start.20 = (bf16[1024,512]{1,0:T(8,128)(2,1)S(1)}, bf16[1024,512]{1,0:T(8,128)(2,1)S(1)}, u32[]{:S(2)}, u32[]{:S(2)}) collective-permute-start(bf16[1024,512]{1,0:T(8,128)(2,1)S(1)} %get-tuple-element.99.d8), channel_id=1, source_target_pairs={{0,1},{1,0},{2,3},{3,2},{4,5},{5,4},{6,7},{7,6},{8,9},{9,8},{10,11... | collective-permute-start | bytes 3145736 | tf_op jit(solution)/shard_map/ppermute | solution.py:148
  117.8 31.8 %collective-permute-start.23 = (bf16[1024,512]{1,0:T(8,128)(2,1)S(1)}, bf16[1024,512]{1,0:T(8,128)(2,1)S(1)}, u32[]{:S(2)}, u32[]{:S(2)}) collective-permute-start(bf16[1024,512]{1,0:T(8,128)(2,1)S(1)} %get-tuple-element.100.near_ref), channel_id=1, source_target_pairs={{0,2},{2,0},{1,3},{3,1},{4,6},{6,4},{5,7},{7,5},{8,10},{10,8},{9,1... | collective-permute-start | bytes 3145736 | tf_op jit(solution)/shard_map/ppermute | solution.py:148
  140.6 24.1 %collective-permute-start.24 = (bf16[1024,512]{1,0:T(8,128)(2,1)S(1)}, bf16[1024,512]{1,0:T(8,128)(2,1)S(1)}, u32[]{:S(2)}, u32[]{:S(2)}) collective-permute-start(bf16[1024,512]{1,0:T(8,128)(2,1)S(1)} %pad_maximum_fusion.7.near_ref), channel_id=1, source_target_pairs={{0,4},{4,0},{1,5},{5,1},{2,6},{6,2},{3,7},{7,3},{8,12},{12,8},{9,1... | collective-permute-start | bytes 3145736 | tf_op jit(solution)/shard_map/ppermute | solution.py:148
  144.7 3.2 %collective-permute-start.28 = (bf16[448,256]{1,0:T(8,128)(2,1)S(1)}, bf16[448,256]{1,0:T(8,128)(2,1)S(1)}, u32[]{:S(2)}, u32[]{:S(2)}) collective-permute-start(bf16[448,256]{1,0:T(8,128)(2,1)S(1)} %get-tuple-element.108), channel_id=1, source_target_pairs={{0,1},{1,0},{2,3},{3,2},{4,5},{5,4},{6,7},{7,6},{8,9},{9,8},{10,11... | collective-permute-start | bytes 688136 | tf_op jit(solution)/shard_map/ppermute | solution.py:148
  147.9 1.7 collective-permute-start.26
  164.8 8.7 %collective-permute-start.31 = (bf16[1024,512]{1,0:T(8,128)(2,1)S(1)}, bf16[1024,512]{1,0:T(8,128)(2,1)S(1)}, u32[]{:S(2)}, u32[]{:S(2)}) collective-permute-start(bf16[1024,512]{1,0:T(8,128)(2,1)S(1)} %collective-permute-done.21.er), channel_id=1, source_target_pairs={{0,1},{1,0},{2,3},{3,2},{4,5},{5,4},{6,7},{7,6},{8,9},{9,8},{10,11... | collective-permute-start | bytes 3145736 | tf_op jit(solution)/shard_map/ppermute | solution.py:148
  164.8 8.7 %collective-permute-start.32 = (bf16[1024,512]{1,0:T(8,128)(2,1)S(1)}, bf16[1024,512]{1,0:T(8,128)(2,1)S(1)}, u32[]{:S(2)}, u32[]{:S(2)}) collective-permute-start(bf16[1024,512]{1,0:T(8,128)(2,1)S(1)} %collective-permute-done.22.dr), channel_id=1, source_target_pairs={{0,1},{1,0},{2,3},{3,2},{4,5},{5,4},{6,7},{7,6},{8,9},{9,8},{10,11... | collective-permute-start | bytes 3145736 | tf_op jit(solution)/shard_map/ppermute | solution.py:148
  168.4 4.0 %collective-permute-start.30 = (bf16[448,256]{1,0:T(8,128)(2,1)S(1)}, bf16[448,256]{1,0:T(8,128)(2,1)S(1)}, u32[]{:S(2)}, u32[]{:S(2)}) collective-permute-start(bf16[448,256]{1,0:T(8,128)(2,1)S(1)} %get-tuple-element.120), channel_id=1, source_target_pairs={{0,1},{1,0},{2,3},{3,2},{4,5},{5,4},{6,7},{7,6},{8,9},{9,8},{10,11... | collective-permute-start | bytes 688136 | tf_op jit(solution)/shard_map/ppermute | solution.py:148
  171.8 1.7 collective-permute-start.29
  (8 other events, 17.6 us)
